TPU v7x, 32 devices: a whole 2x2x4 slice. The times are simulated.
32 devices in a mesh: ctx: 4 (over x, core), ep: 8 (over z, y).
Axes of the slice: x: 2, y: 2, z: 4, core: 2. Of those that a mesh axis runs over, the one named last changes fastest.
Arguments:
- layer_input: bfloat16 [8, 1024, 2048], P('ep', 'ctx'), may hold values from -6 to 6
- attn_gain: float32 [2048], replicated, may hold values from 0.1 to 1.9
- q_weight: bfloat16 [2048, 4096], P('ep'), may hold values from -0.125 to 0.125
- key_matrix: bfloat16 [2048, 512], P('ep'), may hold values from -0.125 to 0.125
- value_matrix: bfloat16 [2048, 512], P('ep'), may hold values from -0.125 to 0.125
- o_weight: bfloat16 [4096, 2048], P('ep'), may hold values from -1 to 1
- q_gain: float32 [128], replicated, may hold values from 0.1 to 1.9
- key_norm_gain: float32 [128], replicated, may hold values from 0.1 to 1.9
- ffn_gain: float32 [2048], replicated, may hold values from 0.1 to 1.9
- router_weight: bfloat16 [2048, 32], P('ep'), may hold values from -0.0625 to 0.0625
- gate_weight: bfloat16 [32, 2048, 768], P(('ctx', 'ep')), may hold values from -0.125 to 0.125
- up_weight: bfloat16 [32, 2048, 768], P(('ctx', 'ep')), may hold values from -0.125 to 0.125
- down_weight: bfloat16 [32, 768, 2048], P(('ctx', 'ep')), may hold values from -0.875 to 0.875
- routes: int32 [8, 1024, 8], P('ep', 'ctx'), may hold values from 0 to 31, all different within a row; in each aligned block of 256 rows (0 to 255, 256 to 511, ..., all dimensions but the last counted through in order) at most 80 rows name the same one
- out_grad: bfloat16 [8, 1024, 2048], P('ep', 'ctx'), may hold values from -6 to 6
Outputs:
- layer_output: bfloat16 [8, 1024, 2048], P('ep', 'ctx')
- input_grad: float32 [8, 1024, 2048], P('ep', 'ctx')
- attn_gain_grad: float32 [2048], replicated
- q_weight_grad: float32 [2048, 4096], P(('ctx', 'ep'))
- k_weight_grad: float32 [2048, 512], P(('ctx', 'ep'))
- v_weight_grad: float32 [2048, 512], P(('ctx', 'ep'))
- o_weight_grad: float32 [4096, 2048], P(('ctx', 'ep'))
- q_gain_grad: float32 [128], replicated
- k_gain_grad: float32 [128], replicated
- ffn_gain_grad: float32 [2048], replicated
- router_weight_grad: float32 [2048, 32], P(('ctx', 'ep'))
- gate_weight_grad: float32 [32, 2048, 768], P(('ctx', 'ep'))
- up_weight_grad: float32 [32, 2048, 768], P(('ctx', 'ep'))
- down_weight_grad: float32 [32, 768, 2048], P(('ctx', 'ep'))
Inputs may be any that keep to these rules, and one draw needn't show every extreme that they name: `routes`: each token names 8 different experts. Among the 256 tokens of one device (one block of 256 positions of one sequence) no expert is named more than 80 times, a bound that some block reaches in some such blocks.
All inputs are finite; a program needn't handle non-finite values.
Results may differ from a plain program's by a relative error of at most 0.02.
Values may be sent and summed in bfloat16 or wider, within the bound.
No kernel may reach another device: no remote copies, remote signals or barrier semaphores. Data moves between devices by JAX's collectives and lax.ppermute only.
A program may use at most 384 MiB of HBM per device.

v0:
```python
import jax
import jax.numpy as jnp
from jax import lax
from jax.sharding import PartitionSpec as P

QUERY_HEADS = 32
KEY_VALUE_HEADS = 4
HEAD_DIM = 128
TOP = 8


EPSILON = 1e-06
ROPE_BASE = 1000000.0


def norm_rows(value, gain):
    return value * lax.rsqrt(jnp.mean(value * value, axis=-1, keepdims=True) + EPSILON) * gain


def rotate(value, token_positions):
    half_width = value.shape[-1] // 2
    frequency = ROPE_BASE ** (-jnp.arange(half_width).astype(jnp.float32) * 2.0 / value.shape[-1])
    angles = token_positions[:, None] * frequency[None, :]
    cosine = jnp.cos(angles)[:, None, :]
    sine_part = jnp.sin(angles)[:, None, :]
    front_half = value[..., :half_width]
    back_half = value[..., half_width:]
    return jnp.concatenate(
        [front_half * cosine - back_half * sine_part, back_half * cosine + front_half * sine_part],
        axis=-1,
    )


def head_prepare(projected_rows, gain, token_positions, head_count):
    shaped = projected_rows.reshape(projected_rows.shape[0], head_count, -1)
    return rotate(norm_rows(shaped, gain), token_positions)


def soft_rows(value_rows):
    row_max = jnp.max(value_rows, axis=-1, keepdims=True)
    shifted = jnp.exp(value_rows - row_max)
    return shifted / jnp.sum(shifted, axis=-1, keepdims=True)


def route_gates(score_logits, picker):
    router = soft_rows(score_logits)
    picked = jnp.sum(picker * router[..., None, :], axis=-1)
    return picked / jnp.sum(picked, axis=-1, keepdims=True)


def on_device(
    layer_input,
    attn_gain,
    q_weight,
    key_matrix,
    value_matrix,
    o_weight,
    q_gain,
    key_norm_gain,
    ffn_gain,
    router_weight,
    gate_weight,
    up_weight,
    down_weight,
    routes,
    out_grad,
):
    block_row_span = layer_input.shape[1]
    model_width = layer_input.shape[2]
    query_group_width = QUERY_HEADS // KEY_VALUE_HEADS
    score_scale = HEAD_DIM ** (-0.5)
    ctx_index = lax.axis_index("ctx")
    ctx_count = lax.axis_size("ctx")
    seq_length = block_row_span * ctx_count
    query_pos = ctx_index * block_row_span + jnp.arange(block_row_span, dtype=jnp.int32)
    token_positions = query_pos.astype(jnp.float32)
    visible = jnp.arange(seq_length, dtype=jnp.int32)[None, :] <= query_pos[:, None]
    input_full = layer_input[0].astype(jnp.float32)
    normed_one, norm_one_pull = jax.vjp(norm_rows, input_full, attn_gain)
    h_one = normed_one.astype(jnp.bfloat16)
    query_full, key_full, value_full, output_full, router_complete = (
        lax.all_gather(q_weight, "ep", axis=0, tiled=True),
        lax.all_gather(key_matrix, "ep", axis=0, tiled=True),
        lax.all_gather(value_matrix, "ep", axis=0, tiled=True),
        lax.all_gather(o_weight, "ep", axis=0, tiled=True),
        lax.all_gather(router_weight, "ep", axis=0, tiled=True),
    )
    query_projected = jnp.dot(h_one, query_full, preferred_element_type=jnp.float32)
    key_projected = jnp.dot(h_one, key_full, preferred_element_type=jnp.float32)
    value_projected = jnp.dot(h_one, value_full, preferred_element_type=jnp.float32)
    query_rotated, q_pull = jax.vjp(
        lambda projected_rows, gain_vector_row: head_prepare(
            projected_rows, gain_vector_row, token_positions, QUERY_HEADS
        ),
        query_projected,
        q_gain,
    )
    k_rot, k_pull = jax.vjp(
        lambda projected_rows, gain_vector_row: head_prepare(
            projected_rows, gain_vector_row, token_positions, KEY_VALUE_HEADS
        ),
        key_projected,
        key_norm_gain,
    )
    query_rows = query_rotated.astype(jnp.bfloat16).reshape(
        block_row_span, KEY_VALUE_HEADS, query_group_width, HEAD_DIM
    )
    keys_local = k_rot.astype(jnp.bfloat16)
    value_rows_local = value_projected.astype(jnp.bfloat16).reshape(
        block_row_span, KEY_VALUE_HEADS, HEAD_DIM
    )
    keys_all, values_all = (
        lax.all_gather(keys_local, "ctx", axis=0, tiled=True),
        lax.all_gather(value_rows_local, "ctx", axis=0, tiled=True),
    )

    def scores_of(current_head_index):
        raw_scores = (
            jnp.einsum(
                "cgd,kd->gck",
                query_rows[:, current_head_index],
                keys_all[:, current_head_index],
                preferred_element_type=jnp.float32,
            )
            * score_scale
        )
        return jnp.where(visible[None], raw_scores, -1e30)

    outputs = []
    log_totals = []
    for current_head_index in range(KEY_VALUE_HEADS):
        scores = scores_of(current_head_index)
        row_max = jnp.max(scores, axis=-1, keepdims=True)
        shifted = jnp.exp(scores - row_max)
        row_total = jnp.sum(shifted, axis=-1, keepdims=True)
        prob_low = (shifted / row_total).astype(jnp.bfloat16)
        log_totals.append(row_max + jnp.log(row_total))
        outputs.append(
            jnp.einsum(
                "gck,kd->cgd",
                prob_low,
                values_all[:, current_head_index],
                preferred_element_type=jnp.float32,
            )
        )
    attn_low = (
        jnp.stack(outputs, axis=1)
        .reshape(block_row_span, QUERY_HEADS * HEAD_DIM)
        .astype(jnp.bfloat16)
    )
    branch = jnp.dot(attn_low, output_full, preferred_element_type=jnp.float32)
    resid = input_full + branch
    normed_two, norm_two_pull = jax.vjp(norm_rows, resid, ffn_gain)
    hidden_second = normed_two.astype(jnp.bfloat16)
    score_logits = jnp.dot(hidden_second, router_complete, preferred_element_type=jnp.float32)
    local_routes = routes[0]
    experts = router_complete.shape[1]
    picker = (
        local_routes[:, :, None] == jnp.arange(experts, dtype=jnp.int32)[None, None, :]
    ).astype(jnp.float32)
    gates, gate_pull = jax.vjp(lambda logits_in: route_gates(logits_in, picker), score_logits)
    flat_routes = local_routes.reshape(-1)
    route_count = flat_routes.shape[0]
    expert_hits = (flat_routes[:, None] == jnp.arange(experts, dtype=jnp.int32)[None, :]).astype(
        jnp.int32
    )
    route_rank = jnp.sum((jnp.cumsum(expert_hits, axis=0) - 1) * expert_hits, axis=1)
    capacity = block_row_span * TOP * 5 // (4 * experts)
    slot_index = flat_routes * capacity + route_rank
    sources = (
        jnp.full((experts * capacity,), route_count, jnp.int32)
        .at[slot_index]
        .set(jnp.arange(route_count, dtype=jnp.int32))
    )
    padded_two = jnp.concatenate([hidden_second, jnp.zeros((1, model_width), jnp.bfloat16)], axis=0)
    sending = padded_two[sources // TOP].reshape(experts, capacity, model_width)
    arrived = lax.all_to_all(sending, ("ctx", "ep"), split_axis=0, concat_axis=0, tiled=True)
    expert_rows = arrived.reshape(-1, model_width)
    gate_proj = jnp.dot(expert_rows, gate_weight[0], preferred_element_type=jnp.float32)
    up_proj = jnp.dot(expert_rows, up_weight[0], preferred_element_type=jnp.float32)
    gate_sigmoid = jax.nn.sigmoid(gate_proj)
    hidden = (gate_proj * gate_sigmoid * up_proj).astype(jnp.bfloat16)
    expert_out = jnp.dot(hidden, down_weight[0], preferred_element_type=jnp.float32).astype(
        jnp.bfloat16
    )
    returned = lax.all_to_all(
        expert_out.reshape(experts, capacity, model_width),
        ("ctx", "ep"),
        split_axis=0,
        concat_axis=0,
        tiled=True,
    )
    per_route = returned.reshape(-1, model_width)[slot_index].reshape(
        block_row_span, TOP, model_width
    )
    mixed_out = resid + jnp.einsum("ct,ctd->cd", gates, per_route.astype(jnp.float32))
    grad_out = out_grad[0].astype(jnp.float32)
    grad_gates = jnp.einsum("cd,ctd->ct", grad_out, per_route.astype(jnp.float32))
    grad_routed = (
        (gates[:, :, None] * grad_out[:, None, :])
        .astype(jnp.bfloat16)
        .reshape(route_count, model_width)
    )
    padded_grad = jnp.concatenate([grad_routed, jnp.zeros((1, model_width), jnp.bfloat16)], axis=0)
    grad_sending = padded_grad[sources].reshape(experts, capacity, model_width)
    grad_arrived = lax.all_to_all(
        grad_sending, ("ctx", "ep"), split_axis=0, concat_axis=0, tiled=True
    ).reshape(-1, model_width)
    grad_hidden = jnp.dot(grad_arrived, down_weight[0].T, preferred_element_type=jnp.float32)
    down_part = jnp.dot(hidden.T, grad_arrived, preferred_element_type=jnp.float32)
    grad_up = (grad_hidden * gate_proj * gate_sigmoid).astype(jnp.bfloat16)
    grad_gate = (
        grad_hidden * up_proj * gate_sigmoid * (1.0 + gate_proj * (1.0 - gate_sigmoid))
    ).astype(jnp.bfloat16)
    gate_part = jnp.dot(expert_rows.T, grad_gate, preferred_element_type=jnp.float32)
    up_part = jnp.dot(expert_rows.T, grad_up, preferred_element_type=jnp.float32)
    grad_copy = (
        jnp.dot(grad_gate, gate_weight[0].T, preferred_element_type=jnp.float32)
        + jnp.dot(grad_up, up_weight[0].T, preferred_element_type=jnp.float32)
    ).astype(jnp.bfloat16)
    grad_back = lax.all_to_all(
        grad_copy.reshape(experts, capacity, model_width),
        ("ctx", "ep"),
        split_axis=0,
        concat_axis=0,
        tiled=True,
    )
    grad_two = jnp.sum(
        grad_back.reshape(-1, model_width)[slot_index]
        .reshape(block_row_span, TOP, model_width)
        .astype(jnp.float32),
        axis=1,
    )
    (grad_logits,) = gate_pull(grad_gates)
    logit_low = grad_logits.astype(jnp.bfloat16)
    grad_two = grad_two + jnp.dot(logit_low, router_complete.T, preferred_element_type=jnp.float32)
    grad_resid, ffn_gain_part = norm_two_pull(grad_two)
    grad_resid = grad_resid + grad_out
    branch_low = grad_resid.astype(jnp.bfloat16)
    grad_attn = (
        jnp.dot(branch_low, output_full.T, preferred_element_type=jnp.float32)
        .astype(jnp.bfloat16)
        .reshape(block_row_span, KEY_VALUE_HEADS, query_group_width, HEAD_DIM)
    )
    query_terms = []
    key_terms = []
    value_terms = []
    for current_head_index in range(KEY_VALUE_HEADS):
        scores = scores_of(current_head_index)
        probs = jnp.exp(scores - log_totals[current_head_index])
        prob_low = probs.astype(jnp.bfloat16)
        grad_probs = jnp.einsum(
            "cgd,kd->gck",
            grad_attn[:, current_head_index],
            values_all[:, current_head_index],
            preferred_element_type=jnp.float32,
        )
        value_terms.append(
            jnp.einsum(
                "gck,cgd->kd",
                prob_low,
                grad_attn[:, current_head_index],
                preferred_element_type=jnp.float32,
            )
        )
        inner = jnp.sum(probs * grad_probs, axis=-1, keepdims=True)
        grad_scores = (probs * (grad_probs - inner)).astype(jnp.bfloat16)
        query_terms.append(
            jnp.einsum(
                "gck,kd->cgd",
                grad_scores,
                keys_all[:, current_head_index],
                preferred_element_type=jnp.float32,
            )
            * score_scale
        )
        key_terms.append(
            jnp.einsum(
                "gck,cgd->kd",
                grad_scores,
                query_rows[:, current_head_index],
                preferred_element_type=jnp.float32,
            )
            * score_scale
        )
    key_grad, value_gradient = (
        lax.psum_scatter(
            jnp.stack(key_terms, axis=1).astype(jnp.bfloat16),
            "ctx",
            scatter_dimension=0,
            tiled=True,
        ).astype(jnp.float32),
        lax.psum_scatter(
            jnp.stack(value_terms, axis=1).astype(jnp.bfloat16),
            "ctx",
            scatter_dimension=0,
            tiled=True,
        ).astype(jnp.float32),
    )
    grad_query = jnp.stack(query_terms, axis=1).reshape(block_row_span, QUERY_HEADS, HEAD_DIM)
    q_back, q_gain_part = q_pull(grad_query)
    k_back, k_gain_part = k_pull(key_grad)
    q_back_low = q_back.astype(jnp.bfloat16)
    k_back_low = k_back.astype(jnp.bfloat16)
    value_backward_reduced = value_gradient.reshape(
        block_row_span, KEY_VALUE_HEADS * HEAD_DIM
    ).astype(jnp.bfloat16)
    grad_one = jnp.dot(q_back_low, query_full.T, preferred_element_type=jnp.float32)
    grad_one = grad_one + jnp.dot(k_back_low, key_full.T, preferred_element_type=jnp.float32)
    grad_one = grad_one + jnp.dot(
        value_backward_reduced, value_full.T, preferred_element_type=jnp.float32
    )
    grad_input, attn_gain_part = norm_one_pull(grad_one)
    input_grad = (grad_resid + grad_input)[None]
    gain_totals = lax.psum((attn_gain_part, q_gain_part, k_gain_part, ffn_gain_part), ("ctx", "ep"))
    q_part = jnp.dot(h_one.T, q_back_low, preferred_element_type=jnp.float32)
    k_part = jnp.dot(h_one.T, k_back_low, preferred_element_type=jnp.float32)
    v_part = jnp.dot(h_one.T, value_backward_reduced, preferred_element_type=jnp.float32)
    o_part = jnp.dot(attn_low.T, branch_low, preferred_element_type=jnp.float32)
    router_part = jnp.dot(hidden_second.T, logit_low, preferred_element_type=jnp.float32)
    summed_grads = (
        lax.psum_scatter(q_part, ("ctx", "ep"), scatter_dimension=0, tiled=True),
        lax.psum_scatter(k_part, ("ctx", "ep"), scatter_dimension=0, tiled=True),
        lax.psum_scatter(v_part, ("ctx", "ep"), scatter_dimension=0, tiled=True),
        lax.psum_scatter(o_part, ("ctx", "ep"), scatter_dimension=0, tiled=True),
        lax.psum_scatter(router_part, ("ctx", "ep"), scatter_dimension=0, tiled=True),
    )
    return (
        mixed_out.astype(jnp.bfloat16)[None],
        input_grad,
        gain_totals[0],
        summed_grads[0],
        summed_grads[1],
        summed_grads[2],
        summed_grads[3],
        gain_totals[1],
        gain_totals[2],
        gain_totals[3],
        summed_grads[4],
        gate_part[None],
        up_part[None],
        down_part[None],
    )


def solution(mesh):
    placed = (
        P("ep", "ctx", None),
        P(),
        P("ep", None),
        P("ep", None),
        P("ep", None),
        P("ep", None),
        P(),
        P(),
        P(),
        P("ep", None),
        P(("ctx", "ep"), None, None),
        P(("ctx", "ep"), None, None),
        P(("ctx", "ep"), None, None),
        P("ep", "ctx", None),
        P("ep", "ctx", None),
    )
    return jax.shard_map(
        on_device,
        mesh=mesh,
        in_specs=placed,
        out_specs=(
            P("ep", "ctx", None),
            P("ep", "ctx", None),
            P(),
            P(("ctx", "ep"), None),
            P(("ctx", "ep"), None),
            P(("ctx", "ep"), None),
            P(("ctx", "ep"), None),
            P(),
            P(),
            P(),
            P(("ctx", "ep"), None),
            P(("ctx", "ep"), None, None),
            P(("ctx", "ep"), None, None),
            P(("ctx", "ep"), None, None),
        ),
        check_vma=False,
    )
```

profile of v0, /device:TPU:0, one launch (start us, length us, event | category | flops | bytes accessed | tf_op | source)
XLA Modules:
  0.0 3680.9 jit_solution(17481950690440425078)
XLA Ops:
  11.4 50.8 %all-gather.11.cloned.1.call-done = bf16[2048,512]{1,0:T(8,128)(2,1)} async-done(((bf16[256,512]{1,0:T(8,128)(2,1)}), bf16[2048,512]{1,0:T(8,128)(2,1)}) %all-gather.11.cloned.1.call-update) | async-done | bytes 2097168 | tf_op jit(solution)/shard_map/all_gather | solution.py:83
  62.2 3.9 copy.135
  70.7 41.4 %all-gather.7.cloned.1.call-done = bf16[2048,512]{1,0:T(8,128)(2,1)} async-done(((bf16[256,512]{1,0:T(8,128)(2,1)}), bf16[2048,512]{1,0:T(8,128)(2,1)}) %all-gather.7.cloned.1.call-update) | async-done | bytes 2097168 | tf_op jit(solution)/shard_map/all_gather | solution.py:84
  118.8 16.0 reduce-window.6
  141.3 8.1 scatter_custom_fusion
  150.2 190.2 %all-gather.15.cloned.1.call-done = bf16[2048,4096]{1,0:T(8,128)(2,1)} async-done(((bf16[256,4096]{1,0:T(8,128)(2,1)}), bf16[2048,4096]{1,0:T(8,128)(2,1)}) %all-gather.15.cloned.1.call-update) | async-done | bytes 16777232 | tf_op jit(solution)/shard_map/all_gather | solution.py:82
  340.4 22.5 copy.136
  362.9 9.2 multiply_reduce_fusion.2
  384.0 3.4 fusion.194
  387.9 5.5 fusion.193
  401.6 4.6 fusion.18
  407.4 5.7 fusion.98
  413.2 5.2 fusion.95
  424.2 181.8 %all-gather.17.cloned.1.call-done = bf16[4096,2048]{1,0:T(8,128)(2,1)} async-done(((bf16[512,2048]{1,0:T(8,128)(2,1)}), bf16[4096,2048]{1,0:T(8,128)(2,1)}) %all-gather.17.cloned.1.call-update) | async-done | bytes 16777232 | tf_op jit(solution)/shard_map/all_gather | solution.py:85
  605.9 11.2 multiply_reduce_fusion.5
  620.8 21.5 gather_fusion
  642.3 3.8 all-to-all-start
  646.1 249.8 %all_gather.27 = bf16[2048,32]{0,1:T(8,128)(2,1)S(1)} all-gather(bf16[256,32]{0,1:T(8,128)(2,1)S(1)} %copy-done.96), channel_id=1, replica_groups=mesh['ctx'=4,'ep'=8] {'ep'}, dimensions={0}, use_global_device_ids=true | all-gather | bytes 147456 | tf_op jit(solution)/shard_map/all_gather | solution.py:86
  903.1 5.8 fusion
  908.9 8.4 concatenate.24
  917.3 24.6 gather_fusion.2
  942.0 3.7 all-to-all-start.2
  945.7 14.0 fusion.46
  959.7 13.0 fusion.50
  972.7 209.1 %all-to-all-done.2 = bf16[32,80,2048]{2,1,0:T(8,128)(2,1)} async-done(((bf16[32,80,2048]{2,1,0:T(8,128)(2,1)}), bf16[32,80,2048]{2,1,0:T(8,128)(2,1)}, u32[]{:S(2)}, u32[]{:S(2)}) %all-to-all-start.2) | async-done | bytes 10485792 | tf_op jit(solution)/shard_map/all_to_all | solution.py:206
  1181.8 20.0 multiply_convert_fusion
  1201.8 13.4 convolution_convert_fusion
  1215.2 4.0 all-to-all-start.1
  1219.2 13.6 fusion.48
  1232.8 16.5 add_convert_fusion
  1249.3 206.0 %all-to-all-done.1 = bf16[32,80,2048]{2,1,0:T(8,128)(2,1)} async-done(((bf16[32,80,2048]{2,1,0:T(8,128)(2,1)}), bf16[32,80,2048]{2,1,0:T(8,128)(2,1)}, u32[]{:S(2)}, u32[]{:S(2)}) %all-to-all-start.1) | async-done | bytes 10485792 | tf_op jit(solution)/shard_map/all_to_all | solution.py:186
  1455.4 3.9 all-to-all-start.3
  1459.8 21.9 gather_fusion.1
  1481.7 8.7 fusion.13
  1490.7 7.0 fusion.15
  1497.7 197.8 %all-to-all-done.3 = bf16[32,80,2048]{2,1,0:T(8,128)(2,1)} async-done(((bf16[32,80,2048]{2,1,0:T(8,128)(2,1)}), bf16[32,80,2048]{2,1,0:T(8,128)(2,1)}, u32[]{:S(2)}, u32[]{:S(2)}) %all-to-all-start.3) | async-done | bytes 10485792 | tf_op jit(solution)/shard_map/all_to_all | solution.py:221
  1695.5 21.8 gather_fusion.3
  1717.4 11.4 convert_reduce_fusion
  1732.0 3.5 fusion.65
  1735.5 12.7 fusion.70
  1750.8 5.5 fusion.119
  1762.6 5.6 fusion.7
  1768.3 4.7 fusion.9
  1776.8 5.0 fusion.4
  1781.8 4.6 fusion.6
  1788.4 5.1 fusion.1
  1793.5 4.5 fusion.3
  1799.6 5.1 fusion.10
  1804.7 4.6 fusion.12
  1818.9 15.2 reduce-scatter.10.cloned.1.call-done
  1840.1 14.8 fusion.153
  1869.4 13.8 fusion.137
  1883.3 14.1 convolution_bitcast_fusion
  1897.4 13.4 convolution_bitcast_fusion.1
  1910.8 13.4 convolution_bitcast_fusion.2
  1924.2 12.5 fusion.196
  1936.6 34.8 reduce-scatter.22.cloned.1.call-done
  1975.4 4.0 fusion.60
  1979.4 40.9 %all-reduce.6 = (f32[2048]{0:T(1024)}, f32[128]{0:T(128)}, f32[128]{0:T(128)}, f32[2048]{0:T(1024)}) all-reduce(f32[2048]{0:T(1024)S(1)} %get-tuple-element.18, f32[128]{0:T(128)S(1)} %get-tuple-element.14, f32[128]{0:T(128)S(1)} %get-tuple-element.20, f32[2048]{0:T(1024)S(1)} %copy-done.77), channel_id=1, replica_groups=mesh['ctx'=4,'ep'=8] {'ctx','ep'}, use_global_device_ids=true, to_apply=%region_37.38 | all-reduce | flops 4352 | bytes 34816 | tf_op jit(solution)/shard_map/psum | solution.py:315
  2020.4 4.4 fusion.67
  2024.8 90.0 %reduce-scatter.18.cloned.1.call-done = f32[64,512]{1,0:T(8,128)} async-done(((f32[2048,512]{1,0:T(8,128)}), f32[64,512]{1,0:T(8,128)}) %reduce-scatter.18.cloned.1.call-update) | async-done | bytes 131088 | tf_op jit(solution)/shard_map/reduce_scatter | solution.py:324
  2114.7 144.1 %reduce-scatter.16.cloned.1.call-done = f32[64,512]{1,0:T(8,128)} async-done(((f32[2048,512]{1,0:T(8,128)}), f32[64,512]{1,0:T(8,128)}) %reduce-scatter.16.cloned.1.call-update) | async-done | bytes 131088 | tf_op jit(solution)/shard_map/reduce_scatter | solution.py:323
  2258.9 706.3 %reduce-scatter.20.cloned.1.call-done = f32[128,2048]{1,0:T(8,128)} async-done(((f32[4096,2048]{1,0:T(8,128)}), f32[128,2048]{1,0:T(8,128)}) %reduce-scatter.20.cloned.1.call-update) | async-done | bytes 1048592 | tf_op jit(solution)/shard_map/reduce_scatter | solution.py:325
  2965.2 708.9 %reduce-scatter.14.cloned.1.call-done = f32[64,4096]{1,0:T(8,128)} async-done(((f32[2048,4096]{1,0:T(8,128)}), f32[64,4096]{1,0:T(8,128)}) %reduce-scatter.14.cloned.1.call-update) | async-done | bytes 1048592 | tf_op jit(solution)/shard_map/reduce_scatter | solution.py:322
  (401 shorter events, 113.9 us)
Async XLA Ops:
  7.2 1174.6 %copy-start = (bf16[1,768,2048]{2,1,0:T(8,128)(2,1)S(1)}, bf16[1,768,2048]{2,1,0:T(8,128)(2,1)}, u32[]{:S(2)}) copy-start(bf16[1,768,2048]{2,1,0:T(8,128)(2,1)} %param.27) | copy-start | bytes 9437188
  7.2 58.9 %copy-start.48 = (f32[2048]{0:T(1024)S(1)}, f32[2048]{0:T(1024)}, u32[]{:S(2)}) copy-start(f32[2048]{0:T(1024)} %param.16) | copy-start | bytes 24580
  7.2 55.0 %all-gather.11.cloned.1.call-start = ((), (), s32[]{:S(2)}) async-start(), calls=%async_computation.13 | async-start | bytes 2359296 | tf_op jit(solution)/shard_map/all_gather | solution.py:83
  7.9 104.2 %all-gather.7.cloned.1.call-start = ((), (), s32[]{:S(2)}) async-start(), calls=%async_computation.11 | async-start | bytes 2359296 | tf_op jit(solution)/shard_map/all_gather | solution.py:84
  8.7 331.7 %all-gather.15.cloned.1.call-start = ((), (), s32[]{:S(2)}) async-start(), calls=%async_computation.15 | async-start | bytes 18874368 | tf_op jit(solution)/shard_map/all_gather | solution.py:82
  9.4 374.6 %all-gather.13.cloned.1.call-start = ((), (), s32[]{:S(2)}) async-start(), calls=%async_computation.14 | async-start | bytes 1310720 | tf_op jit(solution)/shard_map/all_gather | solution.py:113
  11.0 55.1 %copy-start.99 = (f32[256]{0:T(256)}, f32[256]{0:T(256)S(1)}, u32[]{:S(2)}) copy-start(f32[256]{0:T(256)S(1)} %fusion.61) | copy-start | bytes 3076
  11.0 57.8 %copy-start.60 = (f32[256]{0:T(256)}, f32[256]{0:T(256)S(1)}, u32[]{:S(2)}) copy-start(f32[256]{0:T(256)S(1)} %fusion.174) | copy-start | bytes 3076
  11.4 361.5 %copy-start.40 = (f32[256,64]{0,1:T(8,128)}, f32[256,64]{0,1:T(8,128)S(1)}, u32[]{:S(2)}) copy-start(f32[256,64]{0,1:T(8,128)S(1)} %get-tuple-element.52) | copy-start | bytes 196612
  11.4 361.5 %copy-start.42 = (f32[256,64]{0,1:T(8,128)}, f32[256,64]{0,1:T(8,128)S(1)}, u32[]{:S(2)}) copy-start(f32[256,64]{0,1:T(8,128)S(1)} %get-tuple-element.53) | copy-start | bytes 196612
  69.9 46.4 %copy-start.56 = (s32[1,256,8]{1,2,0:T(8,128)S(1)}, s32[1,256,8]{1,2,0:T(8,128)}, u32[]{:S(2)}) copy-start(s32[1,256,8]{1,2,0:T(8,128)} %param.28) | copy-start | bytes 24580
  70.6 336.7 %all-gather.9.cloned.1.call-start = ((), (), s32[]{:S(2)}) async-start(), calls=%async_computation.12 | async-start | bytes 1310720 | tf_op jit(solution)/shard_map/all_gather | solution.py:114
  115.7 490.3 %all-gather.17.cloned.1.call-start = ((), (), s32[]{:S(2)}) async-start(), calls=%async_computation.16 | async-start | bytes 18874368 | tf_op jit(solution)/shard_map/all_gather | solution.py:85
  362.9 9.3 copy-start.105
  387.9 12.5 copy-start.2
  387.9 25.2 copy-start.65
  393.4 25.0 copy-start.67
  395.2 10.9 copy-start.4
  395.2 24.9 copy-start.69
  396.8 10.6 copy-start.71
  401.6 11.6 copy-start.84
  406.1 12.3 copy-start.82
  407.3 12.9 copy-start.80
  407.4 11.1 slice-start.12
  605.9 12.5 copy-start.62
  617.2 25.2 copy-start.101
  617.2 25.1 copy-start.92
  642.3 299.6 %all-to-all-start = ((bf16[32,80,2048]{2,1,0:T(8,128)(2,1)}), bf16[32,80,2048]{2,1,0:T(8,128)(2,1)}, u32[]{:S(2)}, u32[]{:S(2)}) async-start(bf16[32,80,2048]{2,1,0:T(8,128)(2,1)} %bitcast.476), calls=%async_computation | async-start | bytes 20971520 | tf_op jit(solution)/shard_map/all_to_all | solution.py:177
  942.0 239.8 %all-to-all-start.2 = ((bf16[32,80,2048]{2,1,0:T(8,128)(2,1)}), bf16[32,80,2048]{2,1,0:T(8,128)(2,1)}, u32[]{:S(2)}, u32[]{:S(2)}) async-start(bf16[32,80,2048]{2,1,0:T(8,128)(2,1)} %bitcast.477), calls=%async_computation.2 | async-start | bytes 20971520 | tf_op jit(solution)/shard_map/all_to_all | solution.py:206
  945.7 14.0 copy-start.108
  1215.2 240.2 %all-to-all-start.1 = ((bf16[32,80,2048]{2,1,0:T(8,128)(2,1)}), bf16[32,80,2048]{2,1,0:T(8,128)(2,1)}, u32[]{:S(2)}, u32[]{:S(2)}) async-start(bf16[32,80,2048]{2,1,0:T(8,128)(2,1)} %bitcast.484), calls=%async_computation.1 | async-start | bytes 20971520 | tf_op jit(solution)/shard_map/all_to_all | solution.py:186
  1455.4 240.0 %all-to-all-start.3 = ((bf16[32,80,2048]{2,1,0:T(8,128)(2,1)}), bf16[32,80,2048]{2,1,0:T(8,128)(2,1)}, u32[]{:S(2)}, u32[]{:S(2)}) async-start(bf16[32,80,2048]{2,1,0:T(8,128)(2,1)} %bitcast.483), calls=%async_computation.3 | async-start | bytes 20971520 | tf_op jit(solution)/shard_map/all_to_all | solution.py:221
  1459.3 354.8 %reduce-scatter.12.cloned.1.call-start = ((), (), s32[]{:S(2)}) async-start(), calls=%async_computation.18 | async-start | bytes 1310720 | tf_op jit(solution)/shard_map/reduce_scatter | solution.py:293
  1459.8 21.9 copy-start.35
  1481.7 8.8 copy-start.57
  1481.7 8.9 copy-start.51
  1481.7 8.9 copy-start.91
  1717.3 11.5 copy-start.107
  1717.3 11.5 copy-start.20
  1717.3 11.5 copy-start.45
  1717.3 11.5 copy-start.63
  1717.3 11.5 copy-start.64
  1717.4 11.5 copy-start.93
  1748.2 9.5 slice-start.14
  1762.6 71.5 %reduce-scatter.10.cloned.1.call-start = ((), (), s32[]{:S(2)}) async-start(), calls=%async_computation.17 | async-start | bytes 1310720 | tf_op jit(solution)/shard_map/reduce_scatter | solution.py:287
  1762.6 14.1 slice-start.10
  1776.8 11.7 slice-start.4
  1788.4 11.2 slice-start
  1812.4 159.0 %reduce-scatter.22.cloned.1.call-start = ((), (), s32[]{:S(2)}) async-start(), calls=%async_computation.23 | async-start | bytes 1081344
  1814.1 300.7 %reduce-scatter.18.cloned.1.call-start = ((), (), s32[]{:S(2)}) async-start(), calls=%async_computation.21 | async-start | bytes 4325376 | tf_op jit(solution)/shard_map/reduce_scatter | solution.py:324
  1818.8 16.3 copy-start.41
  1818.8 16.3 copy-start.43
  1818.8 16.4 copy-start.28
  1818.8 16.4 copy-start.74
  1818.8 16.4 copy-start.104
  1818.8 16.6 copy-start.98
  1818.9 440.0 %reduce-scatter.16.cloned.1.call-start = ((), (), s32[]{:S(2)}) async-start(), calls=%async_computation.20 | async-start | bytes 4325376 | tf_op jit(solution)/shard_map/reduce_scatter | solution.py:323
  1838.5 1126.7 %reduce-scatter.20.cloned.1.call-start = ((), (), s32[]{:S(2)}) async-start(), calls=%async_computation.22 | async-start | bytes 34603008 | tf_op jit(solution)/shard_map/reduce_scatter | solution.py:325
  1854.9 1819.3 %reduce-scatter.14.cloned.1.call-start = ((), (), s32[]{:S(2)}) async-start(), calls=%async_computation.19 | async-start | bytes 34603008 | tf_op jit(solution)/shard_map/reduce_scatter | solution.py:322
  1883.3 14.1 copy-start.111
  1897.4 13.4 copy-start.110
  1924.2 48.7 %copy-start.24 = (bf16[2048,512]{1,0:T(8,128)(2,1)S(1)}, bf16[2048,512]{1,0:T(8,128)(2,1)}, u32[]{:S(2)}) copy-start(bf16[2048,512]{1,0:T(8,128)(2,1)} %all-gather.11.cloned.1.call-done) | copy-start | bytes 6291460
  1975.4 44.9 %copy-start.100 = (f32[256]{0:T(256)S(1)}, f32[256]{0:T(256)}, u32[]{:S(2)}) copy-start(f32[256]{0:T(256)} %copy-done.99) | copy-start | bytes 3076
  1975.4 1698.7 %copy-start.1 = (bf16[1,768,2048]{2,1,0:T(8,128)(2,1)S(1)}, bf16[1,768,2048]{2,1,0:T(8,128)(2,1)}, u32[]{:S(2)}) copy-start(bf16[1,768,2048]{2,1,0:T(8,128)(2,1)} %param.27) | copy-start | bytes 9437188
  (81 other events, 301.8 us)
Sparse Core Ops, SparseCore 0:
  10.2 51.9 all-gather.10
  64.3 47.7 all-gather.6
  114.3 226.1 all-gather.14
  342.4 15.0 all-gather.12
  359.4 16.8 all-gather.8
  378.3 227.6 all-gather.16
  1762.7 21.4 reduce-scatter.11
  1812.6 21.5 reduce-scatter.9
  1836.4 135.0 reduce-scatter.21
  1974.2 140.4 reduce-scatter.17
  2117.7 141.1 reduce-scatter.15
  2261.7 703.4 reduce-scatter.19
  2968.2 705.8 reduce-scatter.13
where the time goes:
time: 3690 us; the launch traced here: 3680 us
  waiting for transfers between devices  2780 us (75%)
  matrix products  315 us (9%)
  blocking collectives  291 us (8%)
  local copies, waits for them, and re-layouts  169 us (5%)
  other arithmetic  94.6 us (3%)
    reduce_scatter x1, waiting for transfers between devices, on_device(): lax.psum_scatter(q_part, ('ctx', 'ep'), scatter_dimension=0, tiled=True)  709 us
    reduce_scatter x1, waiting for transfers between devices, on_device(): lax.psum_scatter(o_part, ('ctx', 'ep'), scatter_dimension=0, tiled=True)  706 us
    all_gather x1, blocking collectives, on_device(): lax.all_gather(router_weight, 'ep', axis=0, tiled=True)  250 us
    all_to_all x1, waiting for transfers between devices, on_device(): lax.all_to_all(grad_sending, ('ctx', 'ep'), split_axis=0, concat_axis=0,...  209 us
    all_to_all x1, waiting for transfers between devices, on_device(): lax.all_to_all(expert_out.reshape(experts, capacity, model_width), ('ctx'...  206 us
    all_to_all x1, waiting for transfers between devices, on_device(): lax.all_to_all(grad_copy.reshape(experts, capacity, model_width), ('ctx',...  198 us
    all_gather x1, waiting for transfers between devices, on_device(): lax.all_gather(q_weight, 'ep', axis=0, tiled=True)  190 us
    all_gather x1, waiting for transfers between devices, on_device(): lax.all_gather(o_weight, 'ep', axis=0, tiled=True)  182 us
  transfers between devices with their start and end apart: 17, of which 13 were waited for; matrix products, arithmetic and copies ran while one was open for 12% of the time, Pallas kernels for 0%

commit v1 on v0

v1 whole, which is shorter than its diff:
```python
import math

import jax
import jax.numpy as jnp
from jax import lax
from jax.experimental import pallas as pl
from jax.experimental.pallas import tpu as pltpu
from jax.sharding import PartitionSpec as P

QUERY_HEADS = 32
KEY_VALUE_HEADS = 4
HEAD_DIM = 128
TOP = 8
BLOCK = 256

EPSILON = 1e-06
ROPE_BASE = 1000000.0
LOG2_E = 1.4426950408889634
F32 = jnp.float32
BF16 = jnp.bfloat16
AXES = ("ctx", "ep")
HIGHEST = lax.Precision.HIGHEST
WINDOW = {"x": 3, "y": 3, "z": 2}


def mm(a, b):
    return jnp.dot(a, b, preferred_element_type=F32)


def mm_t(a, b):
    return lax.dot_general(a, b, (((1,), (1,)), ((), ())), preferred_element_type=F32)


def t_mm(a, b):
    return lax.dot_general(a, b, (((0,), (0,)), ((), ())), preferred_element_type=F32)


def half_turn(v):
    return pltpu.roll(v, HEAD_DIM // 2, 1)


def head_norm(v, gain):
    scale = lax.rsqrt(jnp.mean(v * v, axis=-1, keepdims=True) + EPSILON)
    return v * scale * gain


def head_norm_back(v, gain, dy):
    scale = lax.rsqrt(jnp.mean(v * v, axis=-1, keepdims=True) + EPSILON)
    lifted = gain * dy
    inner = jnp.mean(v * lifted, axis=-1, keepdims=True)
    return (
        scale * lifted - v * (scale * scale * scale * inner),
        jnp.sum(v * scale * dy, axis=0, keepdims=True),
    )


def diagonal_mask():
    key_at = lax.broadcasted_iota(jnp.int32, (BLOCK, BLOCK), 0)
    query_at = lax.broadcasted_iota(jnp.int32, (BLOCK, BLOCK), 1)
    return key_at <= query_at


def attend_kernel(
    q_ref, k_ref, v_ref, cos_ref, sin_ref, qg_ref, kg_ref,
    out_ref, qr_ref, kr_ref, lse_ref, keys, values_t,
):
    blocks = q_ref.shape[0] // BLOCK
    coefficient = LOG2_E * HEAD_DIM ** (-0.5)

    @pl.when(pl.program_id(0) == 0)
    def _():
        normed = head_norm(k_ref[...], kg_ref[...])
        turned = (normed * cos_ref[...] + half_turn(normed) * sin_ref[...]).astype(BF16)
        keys[...] = turned
        kr_ref[...] = turned
        values_t[...] = v_ref[...].T.astype(BF16)

    normed = head_norm(q_ref[...], qg_ref[...])
    queries = (normed * cos_ref[...] + half_turn(normed) * sin_ref[...]).astype(BF16)
    qr_ref[...] = queries
    visible = diagonal_mask()
    for i in range(blocks):
        low, high = i * BLOCK, (i + 1) * BLOCK
        q_i = queries[low:high]
        s_in = jnp.where(visible, mm_t(keys[low:high, :], q_i) * coefficient, -1e30)
        top = jnp.max(s_in, axis=0, keepdims=True)
        if i:
            s_off = mm_t(keys[:low, :], q_i) * coefficient
            top = jnp.maximum(top, jnp.max(s_off, axis=0, keepdims=True))
        p_in = jnp.exp2(s_in - top)
        total = jnp.sum(p_in, axis=0, keepdims=True)
        mixed = mm(values_t[:, low:high], p_in.astype(BF16))
        if i:
            p_off = jnp.exp2(s_off - top)
            total = total + jnp.sum(p_off, axis=0, keepdims=True)
            mixed = mixed + mm(values_t[:, :low], p_off.astype(BF16))
        out_ref[low:high, :] = (mixed * (1.0 / total)).T.astype(BF16)
        lse_ref[0, :, low:high] = top + jnp.log2(total)


def attend_back_kernel(
    qr_ref, q_ref, do_ref, out_ref, lse_ref, kr_ref, k_ref, v_ref, cos_ref, sin_ref, qg_ref, kg_ref,
    grad_ref, qgain_ref, kgain_ref, keys_t, values, dk, dv, dq,
):
    step = pl.program_id(0)
    heads = pl.num_programs(0) - 2
    blocks = q_ref.shape[0] // BLOCK
    scale = HEAD_DIM ** (-0.5)
    coefficient = LOG2_E * scale

    @pl.when(step == 0)
    def _():
        keys_t[...] = kr_ref[...].astype(F32).T.astype(BF16)
        values[...] = v_ref[...].astype(BF16)
        dk[...] = jnp.zeros_like(dk)
        dv[...] = jnp.zeros_like(dv)
        qgain_ref[...] = jnp.zeros_like(qgain_ref)

    def turn_back(v):
        return v * cos_ref[...] - half_turn(v) * sin_ref[...]

    @pl.when(step < heads)
    def _():
        delta = jnp.sum((do_ref[...].astype(F32) * out_ref[...].astype(F32)).T, axis=0, keepdims=True)
        visible = diagonal_mask()
        for i in range(blocks):
            low, high = i * BLOCK, (i + 1) * BLOCK
            q_i = qr_ref[low:high, :]
            do_i = do_ref[low:high, :]
            lse_i = lse_ref[0, :, low:high]
            delta_i = delta[:, low:high]

            def part(first, last, masked):
                p = jnp.exp2(mm_t(kr_ref[first:last, :], q_i) * coefficient - lse_i)
                if masked:
                    p = jnp.where(visible, p, 0.0)
                dp = mm_t(values[first:last, :], do_i)
                dv[first:last, :] += mm(p.astype(BF16), do_i)
                ds = (p * (dp - delta_i)).astype(BF16)
                dk[first:last, :] += mm(ds, q_i)
                return mm(keys_t[:, first:last], ds)

            turned = part(low, high, True)
            if i:
                turned = turned + part(0, low, False)
            dq[low:high, :] = turned.T * scale
        back, gain_part = head_norm_back(q_ref[...], qg_ref[...], turn_back(dq[...]))
        grad_ref[...] = back.astype(BF16)
        qgain_ref[...] += gain_part

    @pl.when(step == heads)
    def _():
        back, gain_part = head_norm_back(k_ref[...], kg_ref[...], turn_back(dk[...] * scale))
        grad_ref[...] = back.astype(BF16)
        kgain_ref[...] = gain_part

    @pl.when(step == heads + 1)
    def _():
        grad_ref[...] = dv[...].astype(BF16)


def attend(qkv, cos, sin, q_gain, k_gain, heads):
    length = qkv.shape[0]
    column = lambda at: pl.BlockSpec((length, HEAD_DIM), lambda h: (0, at))
    moving = pl.BlockSpec((length, HEAD_DIM), lambda h: (0, h))
    fixed = pl.BlockSpec((length, HEAD_DIM), lambda h: (0, 0))
    row = pl.BlockSpec((1, HEAD_DIM), lambda h: (0, 0))
    pairs = heads * length * length
    return pl.pallas_call(
        attend_kernel,
        grid=(heads,),
        in_specs=[moving, column(heads), column(heads + 1), fixed, fixed, row, row],
        out_specs=[moving, moving, fixed, pl.BlockSpec((1, 1, length), lambda h: (h, 0, 0))],
        out_shape=[
            jax.ShapeDtypeStruct((length, heads * HEAD_DIM), BF16),
            jax.ShapeDtypeStruct((length, heads * HEAD_DIM), BF16),
            jax.ShapeDtypeStruct((length, HEAD_DIM), BF16),
            jax.ShapeDtypeStruct((heads, 1, length), F32),
        ],
        scratch_shapes=[pltpu.VMEM((length, HEAD_DIM), BF16), pltpu.VMEM((HEAD_DIM, length), BF16)],
        compiler_params=pltpu.CompilerParams(vmem_limit_bytes=40 * 1024 * 1024),
        cost_estimate=pl.CostEstimate(
            flops=2 * pairs * HEAD_DIM, bytes_accessed=10 * length * heads * HEAD_DIM, transcendentals=pairs // 2
        ),
        name="attend",
    )(qkv, qkv, qkv, cos, sin, q_gain, k_gain)


def attend_back(qkv, turned_q, turned_k, out, lse, grad_out, cos, sin, q_gain, k_gain, heads):
    length = qkv.shape[0]
    column = lambda at: pl.BlockSpec((length, HEAD_DIM), lambda h: (0, at))
    moving = pl.BlockSpec((length, HEAD_DIM), lambda h: (0, jnp.minimum(h, heads - 1)))
    fixed = pl.BlockSpec((length, HEAD_DIM), lambda h: (0, 0))
    row = pl.BlockSpec((1, HEAD_DIM), lambda h: (0, 0))
    pairs = heads * length * length
    return pl.pallas_call(
        attend_back_kernel,
        grid=(heads + 2,),
        in_specs=[
            moving, moving, moving, moving,
            pl.BlockSpec((1, 1, length), lambda h: (jnp.minimum(h, heads - 1), 0, 0)),
            fixed, column(heads), column(heads + 1), fixed, fixed, row, row,
        ],
        out_specs=[pl.BlockSpec((length, HEAD_DIM), lambda h: (0, h)), row, row],
        out_shape=[
            jax.ShapeDtypeStruct((length, (heads + 2) * HEAD_DIM), BF16),
            jax.ShapeDtypeStruct((1, HEAD_DIM), F32),
            jax.ShapeDtypeStruct((1, HEAD_DIM), F32),
        ],
        scratch_shapes=[
            pltpu.VMEM((HEAD_DIM, length), BF16),
            pltpu.VMEM((length, HEAD_DIM), BF16),
            pltpu.VMEM((length, HEAD_DIM), F32),
            pltpu.VMEM((length, HEAD_DIM), F32),
            pltpu.VMEM((length, HEAD_DIM), F32),
        ],
        compiler_params=pltpu.CompilerParams(vmem_limit_bytes=40 * 1024 * 1024),
        cost_estimate=pl.CostEstimate(
            flops=5 * pairs * HEAD_DIM, bytes_accessed=14 * length * heads * HEAD_DIM, transcendentals=pairs // 2
        ),
        name="attend_back",
    )(turned_q, qkv, grad_out, out, lse, turned_k, qkv, qkv, cos, sin, q_gain, k_gain)


def norm_back(v, scale, gain, dy):
    lifted = gain * dy
    inner = jnp.mean(v * lifted, axis=-1, keepdims=True)
    return scale * lifted - v * (scale * scale * scale * inner), jnp.sum(v * scale * dy, axis=0)


def layer(
    nctx, nep,
    layer_input, attn_gain, q_weight, key_matrix, value_matrix, o_weight, q_gain, key_norm_gain,
    ffn_gain, router_weight, gate_weight, up_weight, down_weight, routes, out_grad,
):
    rows, width = layer_input.shape[1:]
    devices = nctx * nep
    nz = nep // 2
    np_ = nctx * 2
    nb = nctx
    experts = devices
    capacity = rows * TOP * 5 // (4 * experts)
    length = rows * nctx
    heads = QUERY_HEADS // nctx
    q_cols = heads * HEAD_DIM
    at_ctx = lax.axis_index("ctx")
    at_ep = lax.axis_index("ep")

    lanes = {"x": [], "y": [], "z": [], "core": []}

    def after(v, *done):
        return lax.optimization_barrier((v, *done))[0]

    def swap(v, by_ctx, by_ep, window=True):
        if by_ctx == 0 and by_ep == 0:
            return v
        taken = [name for name, used in (("x", by_ctx >> 1), ("y", by_ep & 1), ("z", by_ep >> 1)) if used]
        if window:
            ahead = [lanes[name][-WINDOW[name]] for name in taken if len(lanes[name]) >= WINDOW[name]]
            if ahead:
                v = after(v, *ahead)
        pairs = [(i, ((i // nep) ^ by_ctx) * nep + ((i % nep) ^ by_ep)) for i in range(devices)]
        got = lax.ppermute(v, AXES, pairs)
        if window:
            for name in taken or ["core"]:
                lanes[name].append(got)
        return got

    def to_plane(v):
        n = v.shape[0] // nb
        half = n // 2
        got = [v[:n]] + [swap(v[b * n : (b + 1) * n], b & ~1, b & 1) for b in range(1, nb)]
        other = swap(jnp.concatenate([g[half:] for g in got], axis=0), 1, 0)
        return jnp.concatenate([g[:half] for g in got] + [other], axis=0)

    def from_plane(v):
        half = v.shape[0] // np_
        other = swap(v[nb * half :], 1, 0)
        sent = [jnp.concatenate([u[b * half : (b + 1) * half] for u in (v, other)], axis=0) for b in range(nb)]
        return jnp.concatenate([sent[0]] + [swap(sent[b], b & ~1, b & 1) for b in range(1, nb)], axis=0)

    def gather_z(piece, window=True):
        return [swap(piece, 0, 2 * j, window) for j in range(nz)]

    def gather_y(far, window=True):
        deep = far[0].shape[0]
        whole = jnp.zeros((nep * deep, far[0].shape[1]), far[0].dtype)
        for j in range(nz):
            for ry in range(2):
                part = swap(far[j], 0, ry, window)
                whole = lax.dynamic_update_slice(whole, part, ((at_ep ^ (2 * j + ry)) * deep, 0))
        return whole

    def sum_all(v):
        for by_ctx, by_ep in [(0, 1 << b) for b in range(nep.bit_length() - 1)] + [(1 << b, 0) for b in range(nctx.bit_length() - 1)]:
            v = v + swap(v, by_ctx, by_ep, False)
        return v

    def gather_ctx(piece):
        deep = piece.shape[0]
        whole = jnp.zeros((nctx * deep, piece.shape[1]), piece.dtype)
        for hi in range(0, nctx, 2):
            far = swap(piece, hi, 0)
            for lo in range(2):
                part = swap(far, lo, 0)
                whole = lax.dynamic_update_slice(whole, part, ((at_ctx ^ (hi + lo)) * deep, 0))
        return whole

    def scatter_ctx(block_of):
        held = {}
        for hi in reversed(range(0, nctx, 2)):
            arrived = swap(block_of(hi + 1).astype(BF16), 1, 0)
            held[hi] = block_of(hi) + arrived.astype(F32)
        total = held[0]
        for hi in range(2, nctx, 2):
            total = total + swap(held[hi].astype(BF16), hi, 0).astype(F32)
        return total

    def own_rows(v, m):
        return lax.dynamic_slice_in_dim(v, (at_ctx ^ m) * rows, rows, 0)

    x = layer_input[0].astype(F32)
    scale_one = lax.rsqrt(jnp.mean(x * x, axis=-1, keepdims=True) + EPSILON)
    h_one = (x * scale_one * attn_gain).astype(BF16)
    o_cols = width // nctx
    far_o = gather_z(lax.dynamic_slice_in_dim(o_weight, at_ctx * o_cols, o_cols, 1))
    qkv_piece = jnp.concatenate(
        [
            lax.dynamic_slice_in_dim(q_weight, at_ctx * q_cols, q_cols, 1),
            lax.dynamic_slice_in_dim(key_matrix, at_ctx * HEAD_DIM, HEAD_DIM, 1),
            lax.dynamic_slice_in_dim(value_matrix, at_ctx * HEAD_DIM, HEAD_DIM, 1),
        ],
        axis=1,
    )
    far_qkv = gather_z(qkv_piece)
    h_full = gather_ctx(h_one)
    o_all = gather_y(far_o)
    qkv_weight = gather_y(far_qkv)
    o_rows = jnp.zeros((q_cols, width), BF16)
    for m in range(nctx):
        there = at_ctx ^ m
        part = swap(lax.dynamic_slice_in_dim(o_all, there * q_cols, q_cols, 0), m, 0)
        o_rows = lax.dynamic_update_slice(o_rows, part, (0, there * o_cols))

    local_routes = after(routes[0], far_o[1])
    token = jnp.arange(rows, dtype=jnp.int32)
    upto = (token[:, None] <= token[None, :]).astype(BF16)
    slots = jnp.arange(capacity, dtype=jnp.int32).astype(F32)

    def slot_table(hits):
        rank = mm(hits.astype(BF16), upto) - 1.0
        return ((rank[:, None, :] == slots[None, :, None]) & (hits[:, None, :] > 0)).astype(BF16)

    plane_steps = jnp.arange(np_, dtype=jnp.int32)
    plane_chip, plane_core = plane_steps >> 1, plane_steps & 1
    plane_experts = (at_ctx ^ (plane_chip & ~1) ^ plane_core) * nep + (at_ep ^ (plane_chip & 1))
    routes_t = local_routes.T
    tables = []
    for j in range(nz):
        there = swap(routes_t, 0, 2 * j, False)
        hits = jnp.sum((there[None] == plane_experts[:, None, None]).astype(F32), axis=1)
        tables.append(slot_table(hits).reshape(np_ * capacity, rows))
    expert_ids = jnp.arange(experts, dtype=jnp.int32)
    picker_t = jnp.sum((routes_t[None] == expert_ids[:, None, None]).astype(F32), axis=1)
    picker = picker_t.T
    steps = jnp.arange(devices, dtype=jnp.int32)
    step_j, step_r = steps // np_, steps % np_
    step_chip, step_core = step_r % nb, step_r // nb
    step_source = (at_ctx ^ (step_chip & ~1) ^ step_core) * nep + (at_ep ^ (2 * step_j) ^ (step_chip & 1))
    reorder = (step_source[:, None] == steps[None, :]).astype(F32)

    def to_experts(v):
        arrived = lax.all_to_all(v, AXES, split_axis=0, concat_axis=0, tiled=True)
        return jnp.dot(reorder, arrived, precision=HIGHEST)

    def from_experts(v):
        ordered = jnp.dot(reorder.T, v, precision=HIGHEST)
        return lax.all_to_all(ordered, AXES, split_axis=0, concat_axis=0, tiled=True)

    expert_table = slot_table(to_experts(picker_t))

    def send(j, tokens):
        return to_plane(mm(tables[j], tokens).astype(BF16))

    def bring(j, made):
        total = t_mm(tables[j], from_plane(made))
        return swap(total.astype(BF16), 0, 2 * j).astype(F32) if j else total

    grad_out = out_grad[0]
    far_g = gather_z(grad_out)
    arrived_g = [send(0, far_g[0])]
    early_y, early_xy = lanes["y"][-2:]
    arrived_g.append(send(1, far_g[1]))
    router_full = gather_y(gather_z(after(router_weight, far_qkv[1]), False), False)
    qkv = mm(h_full, qkv_weight)

    frequency = ROPE_BASE ** (-jnp.arange(HEAD_DIM // 2).astype(F32) * 2.0 / HEAD_DIM)
    angles = jnp.arange(length).astype(F32)[:, None] * frequency[None, :]
    cosine, sine = jnp.cos(angles), jnp.sin(angles)
    cos_full = jnp.concatenate([cosine, cosine], axis=1)
    sin_full = jnp.concatenate([-sine, sine], axis=1)
    q_gain_row, k_gain_row = q_gain[None, :], key_norm_gain[None, :]
    attn, turned_q, turned_k, lse = attend(after(qkv, early_y), cos_full, sin_full, q_gain_row, k_gain_row, heads)
    attn = after(attn, early_xy)
    branch = scatter_ctx(lambda m: mm(own_rows(attn, m), o_rows))
    arrived_g += [send(j, far_g[j]) for j in range(2, nz)]

    resid = x + branch
    scale_two = lax.rsqrt(jnp.mean(resid * resid, axis=-1, keepdims=True) + EPSILON)
    h_two = (resid * scale_two * ffn_gain).astype(BF16)
    logits = mm(h_two, router_full)
    shifted = jnp.exp(logits - jnp.max(logits, axis=-1, keepdims=True))
    router = shifted / jnp.sum(shifted, axis=-1, keepdims=True)
    picked_total = jnp.sum(picker * router, axis=-1, keepdims=True)
    gates = picker * router / picked_total

    gate_up = jnp.concatenate([gate_weight[0], up_weight[0]], axis=1)
    down = down_weight[0]
    ff = down.shape[0]
    row_gates = jnp.sum(expert_table.astype(F32) * to_experts(gates.T)[:, None, :], axis=-1)
    row_gates = row_gates.reshape(nz, np_ * capacity, 1)
    far_h = gather_z(h_two)
    arrived_h, posted = [], []
    for j in range(nz):
        arrived_h.append(send(j, far_h[j]))
        posted.append(lanes["y"][-2])
    hidden_all, grad_gate_all, grad_up_all, grad_copies, dots = [], [], [], [], []

    def expert(j, *done):
        h_j = after(arrived_h[j], *done)
        grad_down = mm_t(arrived_g[j], down)
        both = mm(h_j, gate_up)
        gate_proj, up_proj = both[:, :ff], both[:, ff:]
        sigmoid = jax.nn.sigmoid(gate_proj)
        hidden = gate_proj * sigmoid * up_proj
        dots.append(jnp.sum(hidden * grad_down, axis=-1).reshape(np_, capacity))
        weighted = grad_down * row_gates[j]
        grad_up = (weighted * gate_proj * sigmoid).astype(BF16)
        grad_gate = (weighted * up_proj * sigmoid * (1.0 + gate_proj * (1.0 - sigmoid))).astype(BF16)
        grad_copies.append(mm_t(jnp.concatenate([grad_gate, grad_up], axis=1), gate_up).astype(BF16))
        hidden_all.append((hidden * row_gates[j]).astype(BF16))
        grad_gate_all.append(grad_gate)
        grad_up_all.append(grad_up)

    for j in range(nz - 1):
        expert(j, posted[j + 1])
    order = [*range(1, nz), 0]
    returned, marks = [], []
    for j in order:
        if j == nz - 1:
            expert(j, lanes["core"][-1])
        returned.append(bring(j, grad_copies[j]))
        marks.append(lanes["y"][-2])
    grad_two = sum(returned)
    joined_h = jnp.concatenate(arrived_h, axis=0)
    gate_part = t_mm(joined_h, after(jnp.concatenate(grad_gate_all, axis=0), marks[0]))
    up_part = t_mm(joined_h, after(jnp.concatenate(grad_up_all, axis=0), marks[1]))
    down_part = t_mm(after(jnp.concatenate(hidden_all, axis=0), marks[2]), jnp.concatenate(arrived_g, axis=0))
    outs = {j: mm(after(hidden_all[j], marks[2]), down).astype(BF16) for j in range(nz)}
    mixed = resid + bring(1, outs[1])

    slot_dots = jnp.concatenate(dots, axis=0)
    token_dots = jnp.sum(expert_table.astype(F32) * slot_dots[:, :, None], axis=1)
    grad_gates = from_experts(token_dots).T
    grad_pick = picker * (grad_gates - jnp.sum(grad_gates * gates, axis=-1, keepdims=True)) / picked_total
    grad_logits = router * (grad_pick - jnp.sum(router * grad_pick, axis=-1, keepdims=True))
    logit_low = grad_logits.astype(BF16)
    grad_two = grad_two + mm_t(logit_low, router_full)
    grad_resid, ffn_gain_part = norm_back(resid, scale_two, ffn_gain, grad_two)
    grad_resid = grad_resid + grad_out.astype(F32)
    router_part = t_mm(logit_low, h_two)
    branch_full = gather_ctx(grad_resid.astype(BF16))
    for j in range(2, nz):
        mixed = mixed + bring(j, outs[j])
    grad_attn = mm_t(branch_full, o_rows).astype(BF16)
    def scatter_ep(term):
        total, first = None, None
        for j in reversed(range(nz)):
            arrived = swap(term(j, 1).astype(BF16), 0, 1)
            first = arrived if first is None else first
            near = term(j, 0) + arrived.astype(F32)
            if j:
                near = swap(near.astype(BF16), 0, 2 * j).astype(F32)
            total = near if total is None else total + near
        return total, first

    o_own = q_cols // nep
    own_width = width // devices
    o_part = t_mm(attn, branch_full)
    router_part = t_mm(logit_low, h_two).reshape(experts, nctx, nep, own_width)
    router_rows = experts * nctx * own_width // width

    def o_term(j, ry):
        there = at_ep ^ (2 * j + ry)
        block = lax.dynamic_slice_in_dim(o_part, there * o_own, o_own, 0)
        router_block = lax.dynamic_slice_in_dim(router_part, there, 1, 2).reshape(router_rows, width)
        return jnp.concatenate([block, router_block], axis=0)

    o_sum, o_first = scatter_ep(o_term)
    o_grad = o_sum[:o_own]
    router_sum = o_sum[o_own:].reshape(experts, nctx, own_width).transpose(1, 2, 0)
    grad_qkv, q_gain_part, k_gain_part = attend_back(
        qkv, turned_q, turned_k, attn, lse, after(grad_attn, o_first), cos_full, sin_full, q_gain_row, k_gain_row, heads
    )
    qkv_part = t_mm(h_full, grad_qkv).reshape(nctx, nep, own_width, -1)

    def qkv_term(j, ry):
        return lax.dynamic_slice_in_dim(qkv_part, at_ep ^ (2 * j + ry), 1, 1)[:, 0]

    qkv_sum, qkv_first = scatter_ep(qkv_term)
    late_qkv = after(grad_qkv, qkv_first)
    grad_one = scatter_ctx(lambda m: mm_t(own_rows(late_qkv, m), qkv_weight))
    grad_input, attn_gain_part = norm_back(x, scale_one, attn_gain, grad_one)
    input_grad = grad_resid + grad_input
    late = sum_all(jnp.concatenate([attn_gain_part, ffn_gain_part, q_gain_part[0], k_gain_part[0]]))

    mixed = mixed + bring(0, outs[0])
    last = jnp.concatenate([qkv_sum, router_sum], axis=2).astype(BF16)
    last = lax.all_to_all(last, "ctx", split_axis=0, concat_axis=0, tiled=True).astype(F32)
    qkv_grad = last
    router_grad = jnp.sum(last[:, :, q_cols + 2 * HEAD_DIM :], axis=0)

    def columns(first, last):
        return jnp.concatenate([qkv_grad[c, :, first:last] for c in range(nctx)], axis=1)

    return (
        mixed.astype(BF16)[None],
        input_grad[None],
        late[:width],
        columns(0, q_cols),
        columns(q_cols, q_cols + HEAD_DIM),
        columns(q_cols + HEAD_DIM, q_cols + 2 * HEAD_DIM),
        o_grad,
        late[2 * width : 2 * width + HEAD_DIM],
        late[2 * width + HEAD_DIM :],
        late[width : 2 * width],
        router_grad,
        gate_part[None],
        up_part[None],
        down_part[None],
    )


def solution(mesh):
    nctx, nep = mesh.shape["ctx"], mesh.shape["ep"]
    tokens = P("ep", "ctx", None)
    own = P(("ctx", "ep"), None)
    expert = P(("ctx", "ep"), None, None)
    by_rows = P("ep", None)

    def on_device(*arrays):
        return layer(nctx, nep, *arrays)

    return jax.shard_map(
        on_device,
        mesh=mesh,
        in_specs=(
            tokens, P(), by_rows, by_rows, by_rows, by_rows, P(), P(), P(), by_rows,
            expert, expert, expert, tokens, tokens,
        ),
        out_specs=(
            tokens, tokens, P(), own, own, own, own, P(), P(), P(), own, expert, expert, expert,
        ),
        check_vma=False,
    )
```

time: 3690 us -> 1160 us (0.31)
  waiting for transfers between devices: 2780 us -> 367 us
  blocking collectives: 291 us -> 0 us
  starting transfers between devices: 15.9 us -> 271 us
  matrix products: 315 us -> 196 us
  Pallas kernels: 0 us -> 41.8 us
    reduce_scatter x6 -> x0, waiting for transfers between devices: 1660 us -> none  [the longest x1 709 us: on_device(): lax.psum_scatter(q_part, ('ctx', 'ep'), scatter_dimension=0, tiled=True)]
    all_to_all x4, waiting for transfers between devices: 613 us -> 1.19 us  [the longest x2 1.18 us: to_experts(): arrived = lax.all_to_all(v, AXES, split_axis=0, concat_axis=0, tiled=True)]
    all_gather x6 -> x0, waiting for transfers between devices: 464 us -> none  [the longest x1 190 us: on_device(): lax.all_gather(q_weight, 'ep', axis=0, tiled=True)]
    ppermute x0 -> x134, waiting for transfers between devices: none -> 366 us  [swap(): got = lax.ppermute(v, AXES, pairs)]
    all_gather x1 -> x0, blocking collectives: 250 us -> none  [on_device(): lax.all_gather(router_weight, 'ep', axis=0, tiled=True)]
    ppermute x0 -> x134, starting transfers between devices: none -> 236 us  [swap(): got = lax.ppermute(v, AXES, pairs)]
    dot_general x49 -> x58, matrix products: 314 us -> 196 us  [the longest x14 74.3 us: t_mm(): lax.dot_general(a, b, (((0,), (0,)), ((), ())), preferred_element_type=F32)]
    gather x4 -> x0, local copies, waits for them, and re-layouts: 89.9 us -> none  [the longest x1 24.6 us: on_device(): grad_sending = padded_grad[sources].reshape(experts, capacity, model_width)]
  transfers between devices with their start and end apart: 17 -> 138, of which waited for: 13 -> 39; matrix products, arithmetic and copies ran while one was open for 12% -> 38% of each run, Pallas kernels for 0% -> 4%
where the time goes in v1:
time: 1160 us; the launch traced here: 1150 us
  waiting for transfers between devices  367 us (32%)
  starting transfers between devices  271 us (23%)
  local copies, waits for them, and re-layouts  198 us (17%)
  matrix products  196 us (17%)
  other arithmetic  74.4 us (6%)
  Pallas kernels  41.8 us (4%)
    ppermute x134, waiting for transfers between devices, swap(): got = lax.ppermute(v, AXES, pairs)  366 us
    ppermute x134, starting transfers between devices, swap(): got = lax.ppermute(v, AXES, pairs)  236 us
    unnamed x429, local copies, waits for them, and re-layouts  99.5 us
    dot_general x14, matrix products, t_mm(): lax.dot_general(a, b, (((0,), (0,)), ((), ())), preferred_element_type=F32)  74.3 us
    dot_general x14, matrix products, mm_t(): lax.dot_general(a, b, (((1,), (1,)), ((), ())), preferred_element_type=F32)  66.8 us
    dot_general x27, matrix products, mm(): return jnp.dot(a, b, preferred_element_type=F32)  54.5 us
    all_to_all x2, starting transfers between devices, to_experts(): arrived = lax.all_to_all(v, AXES, split_axis=0, concat_axis=0, tiled=True)  25.3 us
    pallas_call x1, Pallas kernels, attend_back(): pl.pallas_call(attend_back_kernel, grid=(heads + 2,), in_specs=[moving, m...  24 us
  transfers between devices with their start and end apart: 138, of which 39 were waited for; matrix products, arithmetic and copies ran while one was open for 38% of the time, Pallas kernels for 4%

profile of v1, /device:TPU:0, one launch (start us, length us, event | category | flops | bytes accessed | tf_op | source)
XLA Modules:
  0.0 1152.7 jit_solution(16528799411615139791)
XLA Ops:
  55.1 7.4 collective-permute-done.10
  63.9 9.4 collective-permute-done.4
  88.6 9.4 collective-permute-done.51
  100.9 3.4 collective-permute-start.53
  125.4 4.3 collective-permute-done.9
  136.6 13.7 %collective-permute-done.14 = bf16[256,1280]{1,0:T(8,128)(2,1)S(1)} collective-permute-done((bf16[256,1280]{1,0:T(8,128)(2,1)S(1)}, bf16[256,1280]{1,0:T(8,128)(2,1)S(1)}, u32[]{:S(2)}, u32[]{:S(2)}) %collective-permute-start.14) | collective-permute-done | bytes 655392 | tf_op jit(solution)/shard_map/ppermute | solution.py:263
  152.2 9.8 collective-permute-done.16
  164.2 8.2 fusion.136.q_ref.k_ref.v_ref
  172.4 4.1 collective-permute-done.17
  176.5 10.3 collective-permute-start.29
  187.8 17.8 %attend.1 = (bf16[1024,1024]{1,0:T(8,128)(2,1)S(1)}, bf16[1024,1024]{1,0:T(8,128)(2,1)S(1)}, bf16[1024,128]{1,0:T(8,128)(2,1)S(1)}, f32[8,1,1024]{2,1,0:T(1,128)S(1)}) custom-call(f32[1024,1280]{1,0:T(8,128)S(1)} %fusion.136.q_ref.k_ref.v_ref, f32[1024,1280]{1,0:T(8,128)S(1)} %fusion.136.q_ref.k_ref.v_ref, f32[1024,1280]{1,0:T(8,128)S(1)} %fusion.136.q_ref.k_ref.v_ref, ...), custom_call_target="tpu_custom_call" | custom-call | flops 2147483648 | bytes 10485760 | tf_op jit(solution)/shard_map/attend/pallas_call | solution.py:169
  219.1 31.1 %collective-permute-done.26 = bf16[256,2048]{1,0:T(8,128)(2,1)S(1)} collective-permute-done((bf16[256,2048]{1,0:T(8,128)(2,1)S(1)}, bf16[256,2048]{1,0:T(8,128)(2,1)S(1)}, u32[]{:S(2)}, u32[]{:S(2)}) %collective-permute-start.26) | collective-permute-done | bytes 1048608 | tf_op jit(solution)/shard_map/ppermute | solution.py:263
  258.8 17.0 %collective-permute-done.30 = bf16[256,2048]{1,0:T(8,128)(2,1)S(1)} collective-permute-done((bf16[256,2048]{1,0:T(8,128)(2,1)S(1)}, bf16[256,2048]{1,0:T(8,128)(2,1)S(1)}, u32[]{:S(2)}, u32[]{:S(2)}) %collective-permute-start.30) | collective-permute-done | bytes 1048608 | tf_op jit(solution)/shard_map/ppermute | solution.py:263
  280.1 13.4 %collective-permute-done.33 = bf16[160,2048]{1,0:T(8,128)(2,1)S(1)} collective-permute-done((bf16[160,2048]{1,0:T(8,128)(2,1)S(1)}, bf16[160,2048]{1,0:T(8,128)(2,1)S(1)}, u32[]{:S(2)}, u32[]{:S(2)}) %collective-permute-start.33) | collective-permute-done | bytes 655392 | tf_op jit(solution)/shard_map/ppermute | solution.py:263
  303.2 23.5 %collective-permute-done.24 = bf16[256,2048]{1,0:T(8,128)(2,1)S(1)} collective-permute-done((bf16[256,2048]{1,0:T(8,128)(2,1)S(1)}, bf16[256,2048]{1,0:T(8,128)(2,1)S(1)}, u32[]{:S(2)}, u32[]{:S(2)}) %collective-permute-start.24) | collective-permute-done | bytes 1048608 | tf_op jit(solution)/shard_map/ppermute | solution.py:263
  333.9 22.2 %all-to-all-start.1 = ((f32[32,1,256]{2,1,0:T(1,128)}), f32[32,1,256]{2,1,0:T(1,128)S(1)}, u32[]{:S(2)}, u32[]{:S(2)}) async-start(f32[32,1,256]{2,1,0:T(1,128)} %copy.60), calls=%async_computation.1 | async-start | bytes 65536 | tf_op jit(solution)/shard_map/all_to_all | solution.py:373
  382.8 7.3 collective-permute-done.42
  400.3 4.9 collective-permute-done.35
  406.6 41.9 %collective-permute-done.46 = bf16[256,2048]{1,0:T(8,128)(2,1)S(1)} collective-permute-done((bf16[256,2048]{1,0:T(8,128)(2,1)S(1)}, bf16[256,2048]{1,0:T(8,128)(2,1)S(1)}, u32[]{:S(2)}, u32[]{:S(2)}) %collective-permute-start.46) | collective-permute-done | bytes 1048608 | tf_op jit(solution)/shard_map/ppermute | solution.py:263
  454.0 9.4 collective-permute-done.37
  490.5 4.3 fusion.109
  494.8 4.9 multiply_convert_fusion.5
  499.8 7.7 convolution_convert_fusion.3
  524.9 4.2 fusion.112
  529.1 4.1 multiply_convert_fusion.7
  533.2 4.9 convolution_convert_fusion.5
  560.6 6.0 fusion.111
  574.8 4.1 multiply_convert_fusion.11
  578.9 4.6 convolution_convert_fusion.7
  586.0 16.0 %collective-permute-done.84 = bf16[160,2048]{1,0:T(8,128)(2,1)} collective-permute-done((bf16[160,2048]{1,0:T(8,128)(2,1)}, bf16[160,2048]{1,0:T(8,128)(2,1)}, u32[]{:S(2)}, u32[]{:S(2)}) %collective-permute-start.84) | collective-permute-done | bytes 655392 | tf_op jit(solution)/shard_map/ppermute | solution.py:263
  608.0 3.9 convolution_convert_fusion.17
  612.5 3.4 constant_dynamic-update-slice_fusion.32
  616.0 6.1 fusion.110
  622.1 4.1 multiply_convert_fusion.9
  626.2 4.5 convolution_convert_fusion.6
  644.8 5.0 all-to-all-start.2
  657.2 14.3 %convolution_bitcast_fusion.2 = f32[1,2048,768]{2,1,0:T(8,128)} fusion(bf16[2560,2048]{1,0:T(8,128)(2,1)} %get-tuple-element.413, bf16[2560,768]{1,0:T(8,128)(2,1)} %pad_maximum_fusion.1), kind=kOutput, calls=%fused_computation.11 | convolution fusion | flops 8053063680 | bytes 20709376 | tf_op jit(solution)/shard_map/dot_general | solution.py:35
  679.1 4.3 constant_dynamic-slice_fusion.5
  706.5 3.7 convolution_convert_fusion.20
  714.7 13.6 %convolution_bitcast_fusion.1 = f32[1,2048,768]{2,1,0:T(8,128)} fusion(bf16[2560,2048]{1,0:T(8,128)(2,1)} %get-tuple-element.413, bf16[2560,768]{1,0:T(8,128)(2,1)S(1)} %copy-done.39), kind=kOutput, calls=%fused_computation.10 | convolution fusion | flops 8053063680 | bytes 20709376 | tf_op jit(solution)/shard_map/dot_general | solution.py:35
  735.4 24.0 %collective-permute-done.73 = bf16[160,2048]{1,0:T(8,128)(2,1)S(1)} collective-permute-done((bf16[160,2048]{1,0:T(8,128)(2,1)S(1)}, bf16[160,2048]{1,0:T(8,128)(2,1)S(1)}, u32[]{:S(2)}, u32[]{:S(2)}) %collective-permute-start.73) | collective-permute-done | bytes 655392 | tf_op jit(solution)/shard_map/ppermute | solution.py:263
  773.3 13.2 %convolution_bitcast_fusion = f32[1,768,2048]{2,1,0:T(8,128)} fusion(bf16[2560,768]{1,0:T(8,128)(2,1)S(1)} %copy-done.38, bf16[2560,2048]{1,0:T(8,128)(2,1)} %get-tuple-element.405), kind=kOutput, calls=%fused_computation.9 | convolution fusion | flops 8053063680 | bytes 20709376 | tf_op jit(solution)/shard_map/dot_general | solution.py:35
  809.6 8.4 collective-permute-done.78
  819.8 21.9 %collective-permute-done.88 = bf16[160,2048]{1,0:T(8,128)(2,1)S(1)} collective-permute-done((bf16[160,2048]{1,0:T(8,128)(2,1)S(1)}, bf16[160,2048]{1,0:T(8,128)(2,1)S(1)}, u32[]{:S(2)}, u32[]{:S(2)}) %collective-permute-start.88) | collective-permute-done | bytes 655392 | tf_op jit(solution)/shard_map/ppermute | solution.py:263
  842.0 12.0 %collective-permute-done.79 = bf16[160,2048]{1,0:T(8,128)(2,1)S(1)} collective-permute-done((bf16[160,2048]{1,0:T(8,128)(2,1)S(1)}, bf16[160,2048]{1,0:T(8,128)(2,1)S(1)}, u32[]{:S(2)}, u32[]{:S(2)}) %collective-permute-start.79) | collective-permute-done | bytes 655392 | tf_op jit(solution)/shard_map/ppermute | solution.py:263
  859.0 22.2 %collective-permute-start.90 = (bf16[256,2048]{1,0:T(8,128)(2,1)}, bf16[256,2048]{1,0:T(8,128)(2,1)S(1)}, u32[]{:S(2)}, u32[]{:S(2)}) collective-permute-start(bf16[256,2048]{1,0:T(8,128)(2,1)} %convolution_convert_fusion.21), channel_id=1, source_target_pairs={{0,2},{1,3},{2,0},{3,1},{4,6},{5,7},{6,4},{7,5},{8,10},{9,11},{10,... | collective-permute-start | bytes 3145736 | tf_op jit(solution)/shard_map/ppermute | solution.py:263
  886.6 21.8 %collective-permute-start.99 = (bf16[256,2048]{1,0:T(8,128)(2,1)}, bf16[256,2048]{1,0:T(8,128)(2,1)S(1)}, u32[]{:S(2)}, u32[]{:S(2)}) collective-permute-start(bf16[256,2048]{1,0:T(8,128)(2,1)} %convolution_convert_fusion.19), channel_id=1, source_target_pairs={{0,4},{1,5},{2,6},{3,7},{4,0},{5,1},{6,2},{7,3},{8,12},{9,13},{10,... | collective-permute-start | bytes 3145736 | tf_op jit(solution)/shard_map/ppermute | solution.py:263
  910.3 5.0 fusion.138
  915.3 4.8 convolution_convert_fusion.26.do_ref
  931.9 4.4 collective-permute-done.109
  937.2 24.0 %attend_back.1 = (bf16[1024,1280]{1,0:T(8,128)(2,1)S(1)}, f32[1,128]{1,0:T(1,128)S(1)}, f32[1,128]{1,0:T(1,128)S(1)}) custom-call(bf16[1024,1024]{1,0:T(8,128)(2,1)S(1)} %copy-done.9, f32[1024,1280]{1,0:T(8,128)} %copy-done.1, bf16[1024,1024]{1,0:T(8,128)(2,1)S(1)} %convolution_convert_fusion.26.do_ref, bf16[1024,1024]{1,0:T(8,128)(2,1)S(1)} %copy-done.7, ...), custom_call_target="tpu_custom_call" | custom-call | flops 5368709120 | bytes 14680064 | tf_op jit(solution)/shard_map/attend_back/pallas_call | solution.py:196
  961.2 6.1 fusion.139
  970.7 6.8 collective-permute-done.99
  984.2 9.1 collective-permute-done.129
  993.8 30.5 %collective-permute-start.130 = (bf16[132,2048]{1,0:T(8,128)(2,1)S(1)}, bf16[132,2048]{1,0:T(8,128)(2,1)S(1)}, u32[]{:S(2)}, u32[]{:S(2)}) collective-permute-start(bf16[132,2048]{1,0:T(8,128)(2,1)S(1)} %fusion.45), channel_id=1, source_target_pairs={{0,2},{1,3},{2,0},{3,1},{4,6},{5,7},{6,4},{7,5},{8,10},{9,11},{10,... | collective-permute-start | bytes 1622024 | tf_op jit(solution)/shard_map/ppermute | solution.py:263
  1024.4 4.0 convolution_convert_fusion.24
  1028.5 5.1 convolution_convert_fusion.25
  1038.4 23.0 %collective-permute-done.127 = bf16[132,2048]{1,0:T(8,128)(2,1)S(1)} collective-permute-done((bf16[132,2048]{1,0:T(8,128)(2,1)S(1)}, bf16[132,2048]{1,0:T(8,128)(2,1)S(1)}, u32[]{:S(2)}, u32[]{:S(2)}) %collective-permute-start.127) | collective-permute-done | bytes 540704 | tf_op jit(solution)/shard_map/ppermute | solution.py:263
  1064.1 5.0 fusion.16
  1080.8 11.8 %collective-permute-start.131 = (bf16[4,64,1280]{2,1,0:T(8,128)(2,1)S(1)}, bf16[4,64,1280]{2,1,0:T(8,128)(2,1)S(1)}, u32[]{:S(2)}, u32[]{:S(2)}) collective-permute-start(bf16[4,64,1280]{2,1,0:T(8,128)(2,1)S(1)} %copy-done.91), channel_id=1, source_target_pairs={{0,4},{1,5},{2,6},{3,7},{4,0},{5,1},{6,2},{7,3},{8,12},{9,13},{10,... | collective-permute-start | bytes 1966088 | tf_op jit(solution)/shard_map/ppermute | solution.py:263
  1094.9 14.9 %collective-permute-done.121 = bf16[256,2048]{1,0:T(8,128)(2,1)} collective-permute-done((bf16[256,2048]{1,0:T(8,128)(2,1)}, bf16[256,2048]{1,0:T(8,128)(2,1)}, u32[]{:S(2)}, u32[]{:S(2)}) %collective-permute-start.121) | collective-permute-done | bytes 1048608 | tf_op jit(solution)/shard_map/ppermute | solution.py:263
  1109.9 6.5 fusion.21
  1127.3 4.2 all-to-all-start.3
  1134.7 7.9 fusion.26
  (903 shorter events, 459.7 us)
Async XLA Ops:
  8.2 37.2 %collective-permute-start.6 = (bf16[512,512]{1,0:T(8,128)(2,1)}, bf16[512,512]{1,0:T(8,128)(2,1)}, u32[]{:S(2)}, u32[]{:S(2)}) collective-permute-start(bf16[512,512]{1,0:T(8,128)(2,1)} %get-tuple-element.127), channel_id=1, source_target_pairs={{0,4},{1,5},{2,6},{3,7},{4,0},{5,1},{6,2},{7,3},{8,12},{9,13},{10,... | collective-permute-start | bytes 1572872 | tf_op jit(solution)/shard_map/ppermute | solution.py:263
  18.4 36.5 %collective-permute-start.1 = (bf16[256,2048]{1,0:T(8,128)(2,1)}, bf16[256,2048]{1,0:T(8,128)(2,1)}, u32[]{:S(2)}, u32[]{:S(2)}) collective-permute-start(bf16[256,2048]{1,0:T(8,128)(2,1)} %get-tuple-element.273), channel_id=1, source_target_pairs={{0,16},{1,17},{2,18},{3,19},{4,20},{5,21},{6,22},{7,23},{8,24},{9,... | collective-permute-start | bytes 3145736 | tf_op jit(solution)/shard_map/ppermute | solution.py:263
  45.5 37.6 %collective-permute-start = (bf16[256,2048]{1,0:T(8,128)(2,1)}, bf16[256,2048]{1,0:T(8,128)(2,1)}, u32[]{:S(2)}, u32[]{:S(2)}) collective-permute-start(bf16[256,2048]{1,0:T(8,128)(2,1)} %get-tuple-element.273), channel_id=1, source_target_pairs={{0,8},{1,9},{2,10},{3,11},{4,12},{5,13},{6,14},{7,15},{8,0},{9,1},... | collective-permute-start | bytes 3145736 | tf_op jit(solution)/shard_map/ppermute | solution.py:263
  62.5 53.2 %collective-permute-start.13 = (bf16[512,512]{1,0:T(8,128)(2,1)}, bf16[512,512]{1,0:T(8,128)(2,1)S(1)}, u32[]{:S(2)}, u32[]{:S(2)}) collective-permute-start(bf16[512,512]{1,0:T(8,128)(2,1)} %collective-permute-done.10), channel_id=1, source_target_pairs={{0,1},{1,0},{2,3},{3,2},{4,5},{5,4},{6,7},{7,6},{8,9},{9,8},{10,11... | collective-permute-start | bytes 1572872 | tf_op jit(solution)/shard_map/ppermute | solution.py:263
  73.3 48.2 %collective-permute-start.11 = (bf16[256,1280]{1,0:T(8,128)(2,1)}, bf16[256,1280]{1,0:T(8,128)(2,1)S(1)}, u32[]{:S(2)}, u32[]{:S(2)}) collective-permute-start(bf16[256,1280]{1,0:T(8,128)(2,1)} %get-tuple-element.131), channel_id=1, source_target_pairs={{0,4},{1,5},{2,6},{3,7},{4,0},{5,1},{6,2},{7,3},{8,12},{9,13},{10,... | collective-permute-start | bytes 1966088 | tf_op jit(solution)/shard_map/ppermute | solution.py:263
  77.8 45.2 %collective-permute-start.5 = (bf16[256,1280]{1,0:T(8,128)(2,1)}, bf16[256,1280]{1,0:T(8,128)(2,1)S(1)}, u32[]{:S(2)}, u32[]{:S(2)}) collective-permute-start(bf16[256,1280]{1,0:T(8,128)(2,1)} %get-tuple-element.131), channel_id=1, source_target_pairs={{0,1},{1,0},{2,3},{3,2},{4,5},{5,4},{6,7},{7,6},{8,9},{9,8},{10,11... | collective-permute-start | bytes 1966088 | tf_op jit(solution)/shard_map/ppermute | solution.py:263
  121.5 84.1 %collective-permute-start.38 = (bf16[160,2048]{1,0:T(8,128)(2,1)}, bf16[160,2048]{1,0:T(8,128)(2,1)S(1)}, u32[]{:S(2)}, u32[]{:S(2)}) collective-permute-start(bf16[160,2048]{1,0:T(8,128)(2,1)} %get-tuple-element.150), channel_id=1, source_target_pairs={{0,16},{1,17},{2,18},{3,19},{4,20},{5,21},{6,22},{7,23},{8,24},{9,... | collective-permute-start | bytes 1966088 | tf_op jit(solution)/shard_map/ppermute | solution.py:263
  123.1 83.8 %collective-permute-start.18 = (bf16[1024,512]{1,0:T(8,128)(2,1)S(1)}, bf16[1024,512]{1,0:T(8,128)(2,1)}, u32[]{:S(2)}, u32[]{:S(2)}) collective-permute-start(bf16[1024,512]{1,0:T(8,128)(2,1)S(1)} %get-tuple-element.306), channel_id=1, source_target_pairs={{0,16},{1,17},{2,18},{3,19},{4,20},{5,21},{6,22},{7,23},{8,24},{9,... | collective-permute-start | bytes 3145736 | tf_op jit(solution)/shard_map/ppermute | solution.py:263
  129.6 81.5 %collective-permute-start.21 = (bf16[1024,512]{1,0:T(8,128)(2,1)S(1)}, bf16[1024,512]{1,0:T(8,128)(2,1)}, u32[]{:S(2)}, u32[]{:S(2)}) collective-permute-start(bf16[1024,512]{1,0:T(8,128)(2,1)S(1)} %get-tuple-element.303), channel_id=1, source_target_pairs={{0,24},{1,25},{2,26},{3,27},{4,28},{5,29},{6,30},{7,31},{8,16},{9,... | collective-permute-start | bytes 3145736 | tf_op jit(solution)/shard_map/ppermute | solution.py:263
  150.4 57.9 %collective-permute-start.20 = (bf16[1024,512]{1,0:T(8,128)(2,1)S(1)}, bf16[1024,512]{1,0:T(8,128)(2,1)}, u32[]{:S(2)}, u32[]{:S(2)}) collective-permute-start(bf16[1024,512]{1,0:T(8,128)(2,1)S(1)} %get-tuple-element.304), channel_id=1, source_target_pairs={{0,8},{1,9},{2,10},{3,11},{4,12},{5,13},{6,14},{7,15},{8,0},{9,1},... | collective-permute-start | bytes 3145736 | tf_op jit(solution)/shard_map/ppermute | solution.py:263
  176.5 36.0 %collective-permute-start.29 = (bf16[256,2048]{1,0:T(8,128)(2,1)S(1)}, bf16[256,2048]{1,0:T(8,128)(2,1)}, u32[]{:S(2)}, u32[]{:S(2)}) collective-permute-start(bf16[256,2048]{1,0:T(8,128)(2,1)S(1)} %bitcast.306), channel_id=1, source_target_pairs={{0,2},{1,3},{2,0},{3,1},{4,6},{5,7},{6,4},{7,5},{8,10},{9,11},{10,... | collective-permute-start | bytes 3145736 | tf_op jit(solution)/shard_map/ppermute | solution.py:263
  205.6 44.6 %collective-permute-start.26 = (bf16[256,2048]{1,0:T(8,128)(2,1)S(1)}, bf16[256,2048]{1,0:T(8,128)(2,1)S(1)}, u32[]{:S(2)}, u32[]{:S(2)}) collective-permute-start(bf16[256,2048]{1,0:T(8,128)(2,1)S(1)} %bitcast.307), channel_id=1, source_target_pairs={{0,4},{1,5},{2,6},{3,7},{4,0},{5,1},{6,2},{7,3},{8,12},{9,13},{10,... | collective-permute-start | bytes 3145736 | tf_op jit(solution)/shard_map/ppermute | solution.py:263
  206.8 45.3 %collective-permute-start.19 = (bf16[160,2048]{1,0:T(8,128)(2,1)}, bf16[160,2048]{1,0:T(8,128)(2,1)S(1)}, u32[]{:S(2)}, u32[]{:S(2)}) collective-permute-start(bf16[160,2048]{1,0:T(8,128)(2,1)} %get-tuple-element.137), channel_id=1, source_target_pairs={{0,17},{1,16},{2,19},{3,18},{4,21},{5,20},{6,23},{7,22},{8,25},{9,... | collective-permute-start | bytes 1966088 | tf_op jit(solution)/shard_map/ppermute | solution.py:263
  215.6 42.7 %collective-permute-start.40 = (bf16[160,2048]{1,0:T(8,128)(2,1)S(1)}, bf16[160,2048]{1,0:T(8,128)(2,1)S(1)}, u32[]{:S(2)}, u32[]{:S(2)}) collective-permute-start(bf16[160,2048]{1,0:T(8,128)(2,1)S(1)} %get-tuple-element.152), channel_id=1, source_target_pairs={{0,1},{1,0},{2,3},{3,2},{4,5},{5,4},{6,7},{7,6},{8,9},{9,8},{10,11... | collective-permute-start | bytes 1966088 | tf_op jit(solution)/shard_map/ppermute | solution.py:263
  217.1 39.2 %collective-permute-start.32 = (bf16[160,2048]{1,0:T(8,128)(2,1)S(1)}, bf16[160,2048]{1,0:T(8,128)(2,1)S(1)}, u32[]{:S(2)}, u32[]{:S(2)}) collective-permute-start(bf16[160,2048]{1,0:T(8,128)(2,1)S(1)} %get-tuple-element.144), channel_id=1, source_target_pairs={{0,16},{1,17},{2,18},{3,19},{4,20},{5,21},{6,22},{7,23},{8,24},{9,... | collective-permute-start | bytes 1966088 | tf_op jit(solution)/shard_map/ppermute | solution.py:263
  217.7 41.1 %collective-permute-start.39 = (bf16[160,2048]{1,0:T(8,128)(2,1)S(1)}, bf16[160,2048]{1,0:T(8,128)(2,1)S(1)}, u32[]{:S(2)}, u32[]{:S(2)}) collective-permute-start(bf16[160,2048]{1,0:T(8,128)(2,1)S(1)} %get-tuple-element.151), channel_id=1, source_target_pairs={{0,17},{1,16},{2,19},{3,18},{4,21},{5,20},{6,23},{7,22},{8,25},{9,... | collective-permute-start | bytes 1966088 | tf_op jit(solution)/shard_map/ppermute | solution.py:263
  255.0 41.9 %collective-permute-start.80 = (bf16[320,2048]{1,0:T(8,128)(2,1)S(1)}, bf16[320,2048]{1,0:T(8,128)(2,1)S(1)}, u32[]{:S(2)}, u32[]{:S(2)}) collective-permute-start(bf16[320,2048]{1,0:T(8,128)(2,1)S(1)} %pad_maximum_fusion.10), channel_id=1, source_target_pairs={{0,8},{1,9},{2,10},{3,11},{4,12},{5,13},{6,14},{7,15},{8,0},{9,1},... | collective-permute-start | bytes 3932168 | tf_op jit(solution)/shard_map/ppermute | solution.py:263
  256.4 37.6 %collective-permute-start.23 = (bf16[256,2048]{1,0:T(8,128)(2,1)S(1)}, bf16[256,2048]{1,0:T(8,128)(2,1)S(1)}, u32[]{:S(2)}, u32[]{:S(2)}) collective-permute-start(bf16[256,2048]{1,0:T(8,128)(2,1)S(1)} %convolution_convert_fusion.22), channel_id=1, source_target_pairs={{0,8},{1,9},{2,10},{3,11},{4,12},{5,13},{6,14},{7,15},{8,0},{9,1},... | collective-permute-start | bytes 3145736 | tf_op jit(solution)/shard_map/ppermute | solution.py:263
  258.8 44.3 %collective-permute-start.22 = (bf16[256,2048]{1,0:T(8,128)(2,1)S(1)}, bf16[256,2048]{1,0:T(8,128)(2,1)S(1)}, u32[]{:S(2)}, u32[]{:S(2)}) collective-permute-start(bf16[256,2048]{1,0:T(8,128)(2,1)S(1)} %convolution_convert_fusion.23), channel_id=1, source_target_pairs={{0,8},{1,9},{2,10},{3,11},{4,12},{5,13},{6,14},{7,15},{8,0},{9,1},... | collective-permute-start | bytes 3145736 | tf_op jit(solution)/shard_map/ppermute | solution.py:263
  279.5 81.8 %collective-permute-start.41 = (bf16[160,2048]{1,0:T(8,128)(2,1)}, bf16[160,2048]{1,0:T(8,128)(2,1)}, u32[]{:S(2)}, u32[]{:S(2)}) collective-permute-start(bf16[160,2048]{1,0:T(8,128)(2,1)} %get-tuple-element.153), channel_id=1, source_target_pairs={{0,17},{1,16},{2,19},{3,18},{4,21},{5,20},{6,23},{7,22},{8,25},{9,... | collective-permute-start | bytes 1966088 | tf_op jit(solution)/shard_map/ppermute | solution.py:263
  293.5 81.6 %collective-permute-start.48 = (bf16[160,2048]{1,0:T(8,128)(2,1)}, bf16[160,2048]{1,0:T(8,128)(2,1)}, u32[]{:S(2)}, u32[]{:S(2)}) collective-permute-start(bf16[160,2048]{1,0:T(8,128)(2,1)} %get-tuple-element.159), channel_id=1, source_target_pairs={{0,1},{1,0},{2,3},{3,2},{4,5},{5,4},{6,7},{7,6},{8,9},{9,8},{10,11... | collective-permute-start | bytes 1966088 | tf_op jit(solution)/shard_map/ppermute | solution.py:263
  303.2 61.8 %collective-permute-start.70 = (bf16[320,2048]{1,0:T(8,128)(2,1)}, bf16[320,2048]{1,0:T(8,128)(2,1)}, u32[]{:S(2)}, u32[]{:S(2)}) collective-permute-start(bf16[320,2048]{1,0:T(8,128)(2,1)} %pad_maximum_fusion.9), channel_id=1, source_target_pairs={{0,8},{1,9},{2,10},{3,11},{4,12},{5,13},{6,14},{7,15},{8,0},{9,1},... | collective-permute-start | bytes 3932168 | tf_op jit(solution)/shard_map/ppermute | solution.py:263
  359.9 34.7 %collective-permute-start.27 = (bf16[256,2048]{1,0:T(8,128)(2,1)}, bf16[256,2048]{1,0:T(8,128)(2,1)}, u32[]{:S(2)}, u32[]{:S(2)}) collective-permute-start(bf16[256,2048]{1,0:T(8,128)(2,1)} %copy-done.18), channel_id=1, source_target_pairs={{0,2},{1,3},{2,0},{3,1},{4,6},{5,7},{6,4},{7,5},{8,10},{9,11},{10,... | collective-permute-start | bytes 3145736 | tf_op jit(solution)/shard_map/ppermute | solution.py:263
  376.6 71.9 %collective-permute-start.46 = (bf16[256,2048]{1,0:T(8,128)(2,1)S(1)}, bf16[256,2048]{1,0:T(8,128)(2,1)S(1)}, u32[]{:S(2)}, u32[]{:S(2)}) collective-permute-start(bf16[256,2048]{1,0:T(8,128)(2,1)S(1)} %copy-done.19), channel_id=1, source_target_pairs={{0,4},{1,5},{2,6},{3,7},{4,0},{5,1},{6,2},{7,3},{8,12},{9,13},{10,... | collective-permute-start | bytes 3145736 | tf_op jit(solution)/shard_map/ppermute | solution.py:263
  382.0 85.1 %collective-permute-start.65 = (bf16[320,2048]{1,0:T(8,128)(2,1)S(1)}, bf16[320,2048]{1,0:T(8,128)(2,1)S(1)}, u32[]{:S(2)}, u32[]{:S(2)}) collective-permute-start(bf16[320,2048]{1,0:T(8,128)(2,1)S(1)} %pad_maximum_fusion.7), channel_id=1, source_target_pairs={{0,8},{1,9},{2,10},{3,11},{4,12},{5,13},{6,14},{7,15},{8,0},{9,1},... | collective-permute-start | bytes 3932168 | tf_op jit(solution)/shard_map/ppermute | solution.py:263
  390.1 61.8 %collective-permute-start.49 = (bf16[160,2048]{1,0:T(8,128)(2,1)S(1)}, bf16[160,2048]{1,0:T(8,128)(2,1)S(1)}, u32[]{:S(2)}, u32[]{:S(2)}) collective-permute-start(bf16[160,2048]{1,0:T(8,128)(2,1)S(1)} %copy-done.108), channel_id=1, source_target_pairs={{0,17},{1,16},{2,19},{3,18},{4,21},{5,20},{6,23},{7,22},{8,25},{9,... | collective-permute-start | bytes 1966088 | tf_op jit(solution)/shard_map/ppermute | solution.py:263
  394.6 83.3 %collective-permute-start.59 = (bf16[256,2048]{1,0:T(8,128)(2,1)S(1)}, bf16[256,2048]{1,0:T(8,128)(2,1)S(1)}, u32[]{:S(2)}, u32[]{:S(2)}) collective-permute-start(bf16[256,2048]{1,0:T(8,128)(2,1)S(1)} %copy-done.19), channel_id=1, source_target_pairs={{0,6},{1,7},{2,4},{3,5},{4,2},{5,3},{6,0},{7,1},{8,14},{9,15},{10,... | collective-permute-start | bytes 3145736 | tf_op jit(solution)/shard_map/ppermute | solution.py:263
  405.2 78.2 %collective-permute-start.44 = (bf16[160,2048]{1,0:T(8,128)(2,1)S(1)}, bf16[160,2048]{1,0:T(8,128)(2,1)S(1)}, u32[]{:S(2)}, u32[]{:S(2)}) collective-permute-start(bf16[160,2048]{1,0:T(8,128)(2,1)S(1)} %get-tuple-element.156), channel_id=1, source_target_pairs={{0,17},{1,16},{2,19},{3,18},{4,21},{5,20},{6,23},{7,22},{8,25},{9,... | collective-permute-start | bytes 1966088 | tf_op jit(solution)/shard_map/ppermute | solution.py:263
  477.9 43.3 %collective-permute-start.66 = (bf16[160,2048]{1,0:T(8,128)(2,1)}, bf16[160,2048]{1,0:T(8,128)(2,1)}, u32[]{:S(2)}, u32[]{:S(2)}) collective-permute-start(bf16[160,2048]{1,0:T(8,128)(2,1)} %get-tuple-element.169), channel_id=1, source_target_pairs={{0,17},{1,16},{2,19},{3,18},{4,21},{5,20},{6,23},{7,22},{8,25},{9,... | collective-permute-start | bytes 1966088 | tf_op jit(solution)/shard_map/ppermute | solution.py:263
  482.3 75.1 %collective-permute-start.63 = (bf16[160,2048]{1,0:T(8,128)(2,1)}, bf16[160,2048]{1,0:T(8,128)(2,1)}, u32[]{:S(2)}, u32[]{:S(2)}) collective-permute-start(bf16[160,2048]{1,0:T(8,128)(2,1)} %get-tuple-element.168), channel_id=1, source_target_pairs={{0,17},{1,16},{2,19},{3,18},{4,21},{5,20},{6,23},{7,22},{8,25},{9,... | collective-permute-start | bytes 1966088 | tf_op jit(solution)/shard_map/ppermute | solution.py:263
  483.4 71.9 %collective-permute-start.61 = (bf16[160,2048]{1,0:T(8,128)(2,1)}, bf16[160,2048]{1,0:T(8,128)(2,1)}, u32[]{:S(2)}, u32[]{:S(2)}) collective-permute-start(bf16[160,2048]{1,0:T(8,128)(2,1)} %get-tuple-element.166), channel_id=1, source_target_pairs={{0,16},{1,17},{2,18},{3,19},{4,20},{5,21},{6,22},{7,23},{8,24},{9,... | collective-permute-start | bytes 1966088 | tf_op jit(solution)/shard_map/ppermute | solution.py:263
  508.8 44.3 %collective-permute-start.60 = (bf16[160,2048]{1,0:T(8,128)(2,1)}, bf16[160,2048]{1,0:T(8,128)(2,1)}, u32[]{:S(2)}, u32[]{:S(2)}) collective-permute-start(bf16[160,2048]{1,0:T(8,128)(2,1)} %get-tuple-element.165), channel_id=1, source_target_pairs={{0,1},{1,0},{2,3},{3,2},{4,5},{5,4},{6,7},{7,6},{8,9},{9,8},{10,11... | collective-permute-start | bytes 1966088 | tf_op jit(solution)/shard_map/ppermute | solution.py:263
  560.6 51.9 %collective-permute-start.64 = (bf16[320,2048]{1,0:T(8,128)(2,1)}, bf16[320,2048]{1,0:T(8,128)(2,1)}, u32[]{:S(2)}, u32[]{:S(2)}) collective-permute-start(bf16[320,2048]{1,0:T(8,128)(2,1)} %pad_maximum_fusion.6), channel_id=1, source_target_pairs={{0,8},{1,9},{2,10},{3,11},{4,12},{5,13},{6,14},{7,15},{8,0},{9,1},... | collective-permute-start | bytes 3932168 | tf_op jit(solution)/shard_map/ppermute | solution.py:263
  569.6 36.4 %collective-permute-start.72 = (bf16[160,2048]{1,0:T(8,128)(2,1)}, bf16[160,2048]{1,0:T(8,128)(2,1)}, u32[]{:S(2)}, u32[]{:S(2)}) collective-permute-start(bf16[160,2048]{1,0:T(8,128)(2,1)} %pad_maximum_fusion.16), channel_id=1, source_target_pairs={{0,17},{1,16},{2,19},{3,18},{4,21},{5,20},{6,23},{7,22},{8,25},{9,... | collective-permute-start | bytes 1966088 | tf_op jit(solution)/shard_map/ppermute | solution.py:263
  611.9 157.9 %collective-permute-start.97 = (bf16[256,2048]{1,0:T(8,128)(2,1)}, bf16[256,2048]{1,0:T(8,128)(2,1)}, u32[]{:S(2)}, u32[]{:S(2)}) collective-permute-start(bf16[256,2048]{1,0:T(8,128)(2,1)} %convolution_convert_fusion.17), channel_id=1, source_target_pairs={{0,2},{1,3},{2,0},{3,1},{4,6},{5,7},{6,4},{7,5},{8,10},{9,11},{10,... | collective-permute-start | bytes 3145736 | tf_op jit(solution)/shard_map/ppermute | solution.py:263
  638.6 89.7 %collective-permute-start.69 = (bf16[320,2048]{1,0:T(8,128)(2,1)}, bf16[320,2048]{1,0:T(8,128)(2,1)}, u32[]{:S(2)}, u32[]{:S(2)}) collective-permute-start(bf16[320,2048]{1,0:T(8,128)(2,1)} %slice.872), channel_id=1, source_target_pairs={{0,8},{1,9},{2,10},{3,11},{4,12},{5,13},{6,14},{7,15},{8,0},{9,1},... | collective-permute-start | bytes 3932168 | tf_op jit(solution)/shard_map/ppermute | solution.py:263
  641.8 58.5 %collective-permute-start.76 = (bf16[160,2048]{1,0:T(8,128)(2,1)}, bf16[160,2048]{1,0:T(8,128)(2,1)}, u32[]{:S(2)}, u32[]{:S(2)}) collective-permute-start(bf16[160,2048]{1,0:T(8,128)(2,1)} %pad_maximum_fusion.20), channel_id=1, source_target_pairs={{0,1},{1,0},{2,3},{3,2},{4,5},{5,4},{6,7},{7,6},{8,9},{9,8},{10,11... | collective-permute-start | bytes 1966088 | tf_op jit(solution)/shard_map/ppermute | solution.py:263
  651.8 50.6 %collective-permute-start.75 = (bf16[160,2048]{1,0:T(8,128)(2,1)}, bf16[160,2048]{1,0:T(8,128)(2,1)}, u32[]{:S(2)}, u32[]{:S(2)}) collective-permute-start(bf16[160,2048]{1,0:T(8,128)(2,1)} %pad_maximum_fusion.19), channel_id=1, source_target_pairs={{0,16},{1,17},{2,18},{3,19},{4,20},{5,21},{6,22},{7,23},{8,24},{9,... | collective-permute-start | bytes 1966088 | tf_op jit(solution)/shard_map/ppermute | solution.py:263
  655.7 48.7 %collective-permute-start.85 = (bf16[160,2048]{1,0:T(8,128)(2,1)}, bf16[160,2048]{1,0:T(8,128)(2,1)}, u32[]{:S(2)}, u32[]{:S(2)}) collective-permute-start(bf16[160,2048]{1,0:T(8,128)(2,1)} %pad_maximum_fusion.24), channel_id=1, source_target_pairs={{0,17},{1,16},{2,19},{3,18},{4,21},{5,20},{6,23},{7,22},{8,25},{9,... | collective-permute-start | bytes 1966088 | tf_op jit(solution)/shard_map/ppermute | solution.py:263
  710.3 83.4 %collective-permute-start.89 = (bf16[256,2048]{1,0:T(8,128)(2,1)}, bf16[256,2048]{1,0:T(8,128)(2,1)S(1)}, u32[]{:S(2)}, u32[]{:S(2)}) collective-permute-start(bf16[256,2048]{1,0:T(8,128)(2,1)} %convolution_convert_fusion.20), channel_id=1, source_target_pairs={{0,4},{1,5},{2,6},{3,7},{4,0},{5,1},{6,2},{7,3},{8,12},{9,13},{10,... | collective-permute-start | bytes 3145736 | tf_op jit(solution)/shard_map/ppermute | solution.py:263
  731.6 35.8 %collective-permute-start.77 = (bf16[160,2048]{1,0:T(8,128)(2,1)S(1)}, bf16[160,2048]{1,0:T(8,128)(2,1)S(1)}, u32[]{:S(2)}, u32[]{:S(2)}) collective-permute-start(bf16[160,2048]{1,0:T(8,128)(2,1)S(1)} %pad_maximum_fusion.18), channel_id=1, source_target_pairs={{0,17},{1,16},{2,19},{3,18},{4,21},{5,20},{6,23},{7,22},{8,25},{9,... | collective-permute-start | bytes 1966088 | tf_op jit(solution)/shard_map/ppermute | solution.py:263
  799.8 81.5 %collective-permute-start.107 = (bf16[256,2048]{1,0:T(8,128)(2,1)S(1)}, bf16[256,2048]{1,0:T(8,128)(2,1)S(1)}, u32[]{:S(2)}, u32[]{:S(2)}) collective-permute-start(bf16[256,2048]{1,0:T(8,128)(2,1)S(1)} %get-tuple-element.200), channel_id=1, source_target_pairs={{0,8},{1,9},{2,10},{3,11},{4,12},{5,13},{6,14},{7,15},{8,0},{9,1},... | collective-permute-start | bytes 3145736 | tf_op jit(solution)/shard_map/ppermute | solution.py:263
  799.9 59.2 %collective-permute-start.102 = (bf16[256,2048]{1,0:T(8,128)(2,1)S(1)}, bf16[256,2048]{1,0:T(8,128)(2,1)S(1)}, u32[]{:S(2)}, u32[]{:S(2)}) collective-permute-start(bf16[256,2048]{1,0:T(8,128)(2,1)S(1)} %get-tuple-element.200), channel_id=1, source_target_pairs={{0,16},{1,17},{2,18},{3,19},{4,20},{5,21},{6,22},{7,23},{8,24},{9,... | collective-permute-start | bytes 3145736 | tf_op jit(solution)/shard_map/ppermute | solution.py:263
  803.4 38.3 %collective-permute-start.88 = (bf16[160,2048]{1,0:T(8,128)(2,1)S(1)}, bf16[160,2048]{1,0:T(8,128)(2,1)S(1)}, u32[]{:S(2)}, u32[]{:S(2)}) collective-permute-start(bf16[160,2048]{1,0:T(8,128)(2,1)S(1)} %pad_maximum_fusion.22), channel_id=1, source_target_pairs={{0,17},{1,16},{2,19},{3,18},{4,21},{5,20},{6,23},{7,22},{8,25},{9,... | collective-permute-start | bytes 1966088 | tf_op jit(solution)/shard_map/ppermute | solution.py:263
  804.7 49.3 %collective-permute-start.79 = (bf16[160,2048]{1,0:T(8,128)(2,1)S(1)}, bf16[160,2048]{1,0:T(8,128)(2,1)S(1)}, u32[]{:S(2)}, u32[]{:S(2)}) collective-permute-start(bf16[160,2048]{1,0:T(8,128)(2,1)S(1)} %pad_maximum_fusion.21), channel_id=1, source_target_pairs={{0,16},{1,17},{2,18},{3,19},{4,20},{5,21},{6,22},{7,23},{8,24},{9,... | collective-permute-start | bytes 1966088 | tf_op jit(solution)/shard_map/ppermute | solution.py:263
  818.1 39.2 %collective-permute-start.94 = (bf16[160,2048]{1,0:T(8,128)(2,1)S(1)}, bf16[160,2048]{1,0:T(8,128)(2,1)S(1)}, u32[]{:S(2)}, u32[]{:S(2)}) collective-permute-start(bf16[160,2048]{1,0:T(8,128)(2,1)S(1)} %pad_maximum_fusion.28), channel_id=1, source_target_pairs={{0,1},{1,0},{2,3},{3,2},{4,5},{5,4},{6,7},{7,6},{8,9},{9,8},{10,11... | collective-permute-start | bytes 1966088 | tf_op jit(solution)/shard_map/ppermute | solution.py:263
  841.7 41.4 %collective-permute-start.96 = (bf16[160,2048]{1,0:T(8,128)(2,1)S(1)}, bf16[160,2048]{1,0:T(8,128)(2,1)S(1)}, u32[]{:S(2)}, u32[]{:S(2)}) collective-permute-start(bf16[160,2048]{1,0:T(8,128)(2,1)S(1)} %pad_maximum_fusion.32), channel_id=1, source_target_pairs={{0,17},{1,16},{2,19},{3,18},{4,21},{5,20},{6,23},{7,22},{8,25},{9,... | collective-permute-start | bytes 1966088 | tf_op jit(solution)/shard_map/ppermute | solution.py:263
  859.0 70.2 %collective-permute-start.90 = (bf16[256,2048]{1,0:T(8,128)(2,1)}, bf16[256,2048]{1,0:T(8,128)(2,1)S(1)}, u32[]{:S(2)}, u32[]{:S(2)}) collective-permute-start(bf16[256,2048]{1,0:T(8,128)(2,1)} %convolution_convert_fusion.21), channel_id=1, source_target_pairs={{0,2},{1,3},{2,0},{3,1},{4,6},{5,7},{6,4},{7,5},{8,10},{9,11},{10,... | collective-permute-start | bytes 3145736 | tf_op jit(solution)/shard_map/ppermute | solution.py:263
  883.1 42.8 %collective-permute-start.104 = (bf16[160,2048]{1,0:T(8,128)(2,1)S(1)}, bf16[160,2048]{1,0:T(8,128)(2,1)S(1)}, u32[]{:S(2)}, u32[]{:S(2)}) collective-permute-start(bf16[160,2048]{1,0:T(8,128)(2,1)S(1)} %pad_maximum_fusion.35), channel_id=1, source_target_pairs={{0,17},{1,16},{2,19},{3,18},{4,21},{5,20},{6,23},{7,22},{8,25},{9,... | collective-permute-start | bytes 1966088 | tf_op jit(solution)/shard_map/ppermute | solution.py:263
  886.6 90.9 %collective-permute-start.99 = (bf16[256,2048]{1,0:T(8,128)(2,1)}, bf16[256,2048]{1,0:T(8,128)(2,1)S(1)}, u32[]{:S(2)}, u32[]{:S(2)}) collective-permute-start(bf16[256,2048]{1,0:T(8,128)(2,1)} %convolution_convert_fusion.19), channel_id=1, source_target_pairs={{0,4},{1,5},{2,6},{3,7},{4,0},{5,1},{6,2},{7,3},{8,12},{9,13},{10,... | collective-permute-start | bytes 3145736 | tf_op jit(solution)/shard_map/ppermute | solution.py:263
  921.7 46.8 %collective-permute-start.117 = (bf16[132,2048]{1,0:T(8,128)(2,1)}, bf16[132,2048]{1,0:T(8,128)(2,1)S(1)}, u32[]{:S(2)}, u32[]{:S(2)}) collective-permute-start(bf16[132,2048]{1,0:T(8,128)(2,1)} %pad_maximum_fusion.42), channel_id=1, source_target_pairs={{0,1},{1,0},{2,3},{3,2},{4,5},{5,4},{6,7},{7,6},{8,9},{9,8},{10,11... | collective-permute-start | bytes 1622024 | tf_op jit(solution)/shard_map/ppermute | solution.py:263
  925.8 55.5 %collective-permute-start.110 = (bf16[132,2048]{1,0:T(8,128)(2,1)}, bf16[132,2048]{1,0:T(8,128)(2,1)}, u32[]{:S(2)}, u32[]{:S(2)}) collective-permute-start(bf16[132,2048]{1,0:T(8,128)(2,1)} %pad_maximum_fusion.40), channel_id=1, source_target_pairs={{0,1},{1,0},{2,3},{3,2},{4,5},{5,4},{6,7},{7,6},{8,9},{9,8},{10,11... | collective-permute-start | bytes 1622024 | tf_op jit(solution)/shard_map/ppermute | solution.py:263
  929.3 64.5 %collective-permute-start.105 = (bf16[256,2048]{1,0:T(8,128)(2,1)}, bf16[256,2048]{1,0:T(8,128)(2,1)S(1)}, u32[]{:S(2)}, u32[]{:S(2)}) collective-permute-start(bf16[256,2048]{1,0:T(8,128)(2,1)} %convolution_convert_fusion.16), channel_id=1, source_target_pairs={{0,6},{1,7},{2,4},{3,5},{4,2},{5,3},{6,0},{7,1},{8,14},{9,15},{10,... | collective-permute-start | bytes 3145736 | tf_op jit(solution)/shard_map/ppermute | solution.py:263
  936.4 47.8 %collective-permute-start.114 = (bf16[132,2048]{1,0:T(8,128)(2,1)}, bf16[132,2048]{1,0:T(8,128)(2,1)}, u32[]{:S(2)}, u32[]{:S(2)}) collective-permute-start(bf16[132,2048]{1,0:T(8,128)(2,1)} %pad_maximum_fusion.41), channel_id=1, source_target_pairs={{0,1},{1,0},{2,3},{3,2},{4,5},{5,4},{6,7},{7,6},{8,9},{9,8},{10,11... | collective-permute-start | bytes 1622024 | tf_op jit(solution)/shard_map/ppermute | solution.py:263
  969.3 55.0 %collective-permute-start.118 = (bf16[4,64,1280]{2,1,0:T(8,128)(2,1)S(1)}, bf16[4,64,1280]{2,1,0:T(8,128)(2,1)S(1)}, u32[]{:S(2)}, u32[]{:S(2)}) collective-permute-start(bf16[4,64,1280]{2,1,0:T(8,128)(2,1)S(1)} %get-tuple-element.219), channel_id=1, source_target_pairs={{0,1},{1,0},{2,3},{3,2},{4,5},{5,4},{6,7},{7,6},{8,9},{9,8},{10,11... | collective-permute-start | bytes 1966088 | tf_op jit(solution)/shard_map/ppermute | solution.py:263
  981.4 95.9 %collective-permute-start.113 = (bf16[160,2048]{1,0:T(8,128)(2,1)}, bf16[160,2048]{1,0:T(8,128)(2,1)}, u32[]{:S(2)}, u32[]{:S(2)}) collective-permute-start(bf16[160,2048]{1,0:T(8,128)(2,1)} %pad_maximum_fusion.37), channel_id=1, source_target_pairs={{0,16},{1,17},{2,18},{3,19},{4,20},{5,21},{6,22},{7,23},{8,24},{9,... | collective-permute-start | bytes 1966088 | tf_op jit(solution)/shard_map/ppermute | solution.py:263
  984.1 49.4 %collective-permute-start.111 = (bf16[4,64,1280]{2,1,0:T(8,128)(2,1)S(1)}, bf16[4,64,1280]{2,1,0:T(8,128)(2,1)S(1)}, u32[]{:S(2)}, u32[]{:S(2)}) collective-permute-start(bf16[4,64,1280]{2,1,0:T(8,128)(2,1)S(1)} %get-tuple-element.212), channel_id=1, source_target_pairs={{0,1},{1,0},{2,3},{3,2},{4,5},{5,4},{6,7},{7,6},{8,9},{9,8},{10,11... | collective-permute-start | bytes 1966088 | tf_op jit(solution)/shard_map/ppermute | solution.py:263
  993.3 41.9 %collective-permute-start.115 = (bf16[4,64,1280]{2,1,0:T(8,128)(2,1)S(1)}, bf16[4,64,1280]{2,1,0:T(8,128)(2,1)S(1)}, u32[]{:S(2)}, u32[]{:S(2)}) collective-permute-start(bf16[4,64,1280]{2,1,0:T(8,128)(2,1)S(1)} %get-tuple-element.216), channel_id=1, source_target_pairs={{0,1},{1,0},{2,3},{3,2},{4,5},{5,4},{6,7},{7,6},{8,9},{9,8},{10,11... | collective-permute-start | bytes 1966088 | tf_op jit(solution)/shard_map/ppermute | solution.py:263
  993.8 75.3 %collective-permute-start.130 = (bf16[132,2048]{1,0:T(8,128)(2,1)S(1)}, bf16[132,2048]{1,0:T(8,128)(2,1)S(1)}, u32[]{:S(2)}, u32[]{:S(2)}) collective-permute-start(bf16[132,2048]{1,0:T(8,128)(2,1)S(1)} %fusion.45), channel_id=1, source_target_pairs={{0,2},{1,3},{2,0},{3,1},{4,6},{5,7},{6,4},{7,5},{8,10},{9,11},{10,... | collective-permute-start | bytes 1622024 | tf_op jit(solution)/shard_map/ppermute | solution.py:263
  1035.2 36.6 %collective-permute-start.112 = (bf16[160,2048]{1,0:T(8,128)(2,1)S(1)}, bf16[160,2048]{1,0:T(8,128)(2,1)S(1)}, u32[]{:S(2)}, u32[]{:S(2)}) collective-permute-start(bf16[160,2048]{1,0:T(8,128)(2,1)S(1)} %copy-done.104), channel_id=1, source_target_pairs={{0,1},{1,0},{2,3},{3,2},{4,5},{5,4},{6,7},{7,6},{8,9},{9,8},{10,11... | collective-permute-start | bytes 1966088 | tf_op jit(solution)/shard_map/ppermute | solution.py:263
  1061.4 33.5 %collective-permute-start.119 = (bf16[256,2048]{1,0:T(8,128)(2,1)}, bf16[256,2048]{1,0:T(8,128)(2,1)}, u32[]{:S(2)}, u32[]{:S(2)}) collective-permute-start(bf16[256,2048]{1,0:T(8,128)(2,1)} %convolution_convert_fusion.25), channel_id=1, source_target_pairs={{0,8},{1,9},{2,10},{3,11},{4,12},{5,13},{6,14},{7,15},{8,0},{9,1},... | collective-permute-start | bytes 3145736 | tf_op jit(solution)/shard_map/ppermute | solution.py:263
  1071.7 38.1 %collective-permute-start.121 = (bf16[256,2048]{1,0:T(8,128)(2,1)}, bf16[256,2048]{1,0:T(8,128)(2,1)}, u32[]{:S(2)}, u32[]{:S(2)}) collective-permute-start(bf16[256,2048]{1,0:T(8,128)(2,1)} %fusion.16), channel_id=1, source_target_pairs={{0,16},{1,17},{2,18},{3,19},{4,20},{5,21},{6,22},{7,23},{8,24},{9,... | collective-permute-start | bytes 3145736 | tf_op jit(solution)/shard_map/ppermute | solution.py:263
  1077.2 43.1 %collective-permute-start.133 = (bf16[4,64,1280]{2,1,0:T(8,128)(2,1)}, bf16[4,64,1280]{2,1,0:T(8,128)(2,1)S(1)}, u32[]{:S(2)}, u32[]{:S(2)}) collective-permute-start(bf16[4,64,1280]{2,1,0:T(8,128)(2,1)} %get-tuple-element.230), channel_id=1, source_target_pairs={{0,1},{1,0},{2,3},{3,2},{4,5},{5,4},{6,7},{7,6},{8,9},{9,8},{10,11... | collective-permute-start | bytes 1966088 | tf_op jit(solution)/shard_map/ppermute | solution.py:263
  1080.8 40.4 %collective-permute-start.131 = (bf16[4,64,1280]{2,1,0:T(8,128)(2,1)S(1)}, bf16[4,64,1280]{2,1,0:T(8,128)(2,1)S(1)}, u32[]{:S(2)}, u32[]{:S(2)}) collective-permute-start(bf16[4,64,1280]{2,1,0:T(8,128)(2,1)S(1)} %copy-done.91), channel_id=1, source_target_pairs={{0,4},{1,5},{2,6},{3,7},{4,0},{5,1},{6,2},{7,3},{8,12},{9,13},{10,... | collective-permute-start | bytes 1966088 | tf_op jit(solution)/shard_map/ppermute | solution.py:263
  (257 other events, 5788.6 us)

commit v2 on v1

v2 whole, which is shorter than its diff:
```python
import math

import jax
import jax.numpy as jnp
from jax import lax
from jax.experimental import pallas as pl
from jax.experimental.pallas import tpu as pltpu
from jax.sharding import PartitionSpec as P

QUERY_HEADS = 32
KEY_VALUE_HEADS = 4
HEAD_DIM = 128
TOP = 8
BLOCK = 256

EPSILON = 1e-06
ROPE_BASE = 1000000.0
LOG2_E = 1.4426950408889634
F32 = jnp.float32
BF16 = jnp.bfloat16
AXES = ("ctx", "ep")
HIGHEST = lax.Precision.HIGHEST


def mm(a, b):
    return jnp.dot(a, b, preferred_element_type=F32)


def mm_t(a, b):
    return lax.dot_general(a, b, (((1,), (1,)), ((), ())), preferred_element_type=F32)


def t_mm(a, b):
    return lax.dot_general(a, b, (((0,), (0,)), ((), ())), preferred_element_type=F32)


LIGHT = pl.CostEstimate(flops=1, bytes_accessed=1, transcendentals=0)
VMEM_MOST = 56 * 1024 * 1024


def half_turn(v):
    return pltpu.roll(v, HEAD_DIM // 2, 1)


def head_norm(v, gain):
    scale = lax.rsqrt(jnp.mean(v * v, axis=-1, keepdims=True) + EPSILON)
    return v * scale * gain


def head_norm_back(v, gain, dy):
    scale = lax.rsqrt(jnp.mean(v * v, axis=-1, keepdims=True) + EPSILON)
    lifted = gain * dy
    inner = jnp.mean(v * lifted, axis=-1, keepdims=True)
    return (
        scale * lifted - v * (scale * scale * scale * inner),
        jnp.sum(v * scale * dy, axis=0, keepdims=True),
    )


def diagonal_mask():
    key_at = lax.broadcasted_iota(jnp.int32, (BLOCK, BLOCK), 0)
    query_at = lax.broadcasted_iota(jnp.int32, (BLOCK, BLOCK), 1)
    return key_at <= query_at


def attend_kernel(
    q_ref, k_ref, v_ref, cos_ref, sin_ref, qg_ref, kg_ref,
    out_ref, qr_ref, kr_ref, lse_ref, keys, values_t,
):
    blocks = q_ref.shape[0] // BLOCK
    coefficient = LOG2_E * HEAD_DIM ** (-0.5)

    @pl.when(pl.program_id(0) == 0)
    def _():
        normed = head_norm(k_ref[...], kg_ref[...])
        turned = (normed * cos_ref[...] + half_turn(normed) * sin_ref[...]).astype(BF16)
        keys[...] = turned
        kr_ref[...] = turned
        values_t[...] = v_ref[...].T.astype(BF16)

    normed = head_norm(q_ref[...], qg_ref[...])
    queries = (normed * cos_ref[...] + half_turn(normed) * sin_ref[...]).astype(BF16)
    qr_ref[...] = queries
    visible = diagonal_mask()
    for i in range(blocks):
        low, high = i * BLOCK, (i + 1) * BLOCK
        q_i = queries[low:high]
        s_in = jnp.where(visible, mm_t(keys[low:high, :], q_i) * coefficient, -1e30)
        top = jnp.max(s_in, axis=0, keepdims=True)
        if i:
            s_off = mm_t(keys[:low, :], q_i) * coefficient
            top = jnp.maximum(top, jnp.max(s_off, axis=0, keepdims=True))
        p_in = jnp.exp2(s_in - top)
        total = jnp.sum(p_in, axis=0, keepdims=True)
        mixed = mm(values_t[:, low:high], p_in.astype(BF16))
        if i:
            p_off = jnp.exp2(s_off - top)
            total = total + jnp.sum(p_off, axis=0, keepdims=True)
            mixed = mixed + mm(values_t[:, :low], p_off.astype(BF16))
        out_ref[low:high, :] = (mixed * (1.0 / total)).T.astype(BF16)
        lse_ref[0, :, low:high] = top + jnp.log2(total)


def attend_back_kernel(
    qr_ref, q_ref, do_ref, out_ref, lse_ref, kr_ref, k_ref, v_ref, cos_ref, sin_ref, qg_ref, kg_ref,
    grad_ref, qgain_ref, kgain_ref, keys_t, values, dk, dv, dq,
):
    step = pl.program_id(0)
    heads = pl.num_programs(0) - 2
    blocks = q_ref.shape[0] // BLOCK
    scale = HEAD_DIM ** (-0.5)
    coefficient = LOG2_E * scale

    @pl.when(step == 0)
    def _():
        keys_t[...] = kr_ref[...].astype(F32).T.astype(BF16)
        values[...] = v_ref[...].astype(BF16)
        dk[...] = jnp.zeros_like(dk)
        dv[...] = jnp.zeros_like(dv)
        qgain_ref[...] = jnp.zeros_like(qgain_ref)

    def turn_back(v):
        return v * cos_ref[...] - half_turn(v) * sin_ref[...]

    @pl.when(step < heads)
    def _():
        delta = jnp.sum((do_ref[...].astype(F32) * out_ref[...].astype(F32)).T, axis=0, keepdims=True)
        visible = diagonal_mask()
        for i in range(blocks):
            low, high = i * BLOCK, (i + 1) * BLOCK
            q_i = qr_ref[low:high, :]
            do_i = do_ref[low:high, :]
            lse_i = lse_ref[0, :, low:high]
            delta_i = delta[:, low:high]

            def part(first, last, masked):
                p = jnp.exp2(mm_t(kr_ref[first:last, :], q_i) * coefficient - lse_i)
                if masked:
                    p = jnp.where(visible, p, 0.0)
                dp = mm_t(values[first:last, :], do_i)
                dv[first:last, :] += mm(p.astype(BF16), do_i)
                ds = (p * (dp - delta_i)).astype(BF16)
                dk[first:last, :] += mm(ds, q_i)
                return mm(keys_t[:, first:last], ds)

            turned = part(low, high, True)
            if i:
                turned = turned + part(0, low, False)
            dq[low:high, :] = turned.T * scale
        back, gain_part = head_norm_back(q_ref[...], qg_ref[...], turn_back(dq[...]))
        grad_ref[...] = back.astype(BF16)
        qgain_ref[...] += gain_part

    @pl.when(step == heads)
    def _():
        back, gain_part = head_norm_back(k_ref[...], kg_ref[...], turn_back(dk[...] * scale))
        grad_ref[...] = back.astype(BF16)
        kgain_ref[...] = gain_part

    @pl.when(step == heads + 1)
    def _():
        grad_ref[...] = dv[...].astype(BF16)


def attend(qkv, cos, sin, q_gain, k_gain, heads):
    length = qkv.shape[0]
    column = lambda at: pl.BlockSpec((length, HEAD_DIM), lambda h: (0, at))
    moving = pl.BlockSpec((length, HEAD_DIM), lambda h: (0, h))
    fixed = pl.BlockSpec((length, HEAD_DIM), lambda h: (0, 0))
    row = pl.BlockSpec((1, HEAD_DIM), lambda h: (0, 0))
    return pl.pallas_call(
        attend_kernel,
        grid=(heads,),
        in_specs=[moving, column(heads), column(heads + 1), fixed, fixed, row, row],
        out_specs=[moving, moving, fixed, pl.BlockSpec((1, 1, length), lambda h: (h, 0, 0))],
        out_shape=[
            jax.ShapeDtypeStruct((length, heads * HEAD_DIM), BF16),
            jax.ShapeDtypeStruct((length, heads * HEAD_DIM), BF16),
            jax.ShapeDtypeStruct((length, HEAD_DIM), BF16),
            jax.ShapeDtypeStruct((heads, 1, length), F32),
        ],
        scratch_shapes=[pltpu.VMEM((length, HEAD_DIM), BF16), pltpu.VMEM((HEAD_DIM, length), BF16)],
        compiler_params=pltpu.CompilerParams(vmem_limit_bytes=40 * 1024 * 1024),
        cost_estimate=LIGHT,
        name="attend",
    )(qkv, qkv, qkv, cos, sin, q_gain, k_gain)


def attend_back(qkv, turned_q, turned_k, out, lse, grad_out, cos, sin, q_gain, k_gain, heads):
    length = qkv.shape[0]
    column = lambda at: pl.BlockSpec((length, HEAD_DIM), lambda h: (0, at))
    moving = pl.BlockSpec((length, HEAD_DIM), lambda h: (0, jnp.minimum(h, heads - 1)))
    fixed = pl.BlockSpec((length, HEAD_DIM), lambda h: (0, 0))
    row = pl.BlockSpec((1, HEAD_DIM), lambda h: (0, 0))
    return pl.pallas_call(
        attend_back_kernel,
        grid=(heads + 2,),
        in_specs=[
            moving, moving, moving, moving,
            pl.BlockSpec((1, 1, length), lambda h: (jnp.minimum(h, heads - 1), 0, 0)),
            fixed, column(heads), column(heads + 1), fixed, fixed, row, row,
        ],
        out_specs=[pl.BlockSpec((length, HEAD_DIM), lambda h: (0, h)), row, row],
        out_shape=[
            jax.ShapeDtypeStruct((length, (heads + 2) * HEAD_DIM), BF16),
            jax.ShapeDtypeStruct((1, HEAD_DIM), F32),
            jax.ShapeDtypeStruct((1, HEAD_DIM), F32),
        ],
        scratch_shapes=[
            pltpu.VMEM((HEAD_DIM, length), BF16),
            pltpu.VMEM((length, HEAD_DIM), BF16),
            pltpu.VMEM((length, HEAD_DIM), F32),
            pltpu.VMEM((length, HEAD_DIM), F32),
            pltpu.VMEM((length, HEAD_DIM), F32),
        ],
        compiler_params=pltpu.CompilerParams(vmem_limit_bytes=40 * 1024 * 1024),
        cost_estimate=LIGHT,
        name="attend_back",
    )(turned_q, qkv, grad_out, out, lse, turned_k, qkv, qkv, cos, sin, q_gain, k_gain)


def select_kernel(n_parts, table, *refs):
    parts, outs = refs[:n_parts], refs[n_parts:]
    deep = outs[0].shape[0]
    first = 0
    for part in parts:
        for at in range(0, part.shape[1], 1024):
            wide = min(1024, part.shape[1] - at)
            rows = mm(table[...], part[:, at : at + wide]).astype(BF16)
            for b, out in enumerate(outs):
                out[:, first : first + wide] = rows[b * deep : (b + 1) * deep]
            first += wide


def select(table, parts, chips):
    width, deep = sum(v.shape[1] for v in parts), table.shape[0] // chips
    return pl.pallas_call(
        lambda *refs: select_kernel(len(parts), *refs),
        out_shape=[jax.ShapeDtypeStruct((deep, width), BF16)] * chips,
        compiler_params=pltpu.CompilerParams(vmem_limit_bytes=VMEM_MOST),
        cost_estimate=LIGHT,
        name="select",
    )(table, *parts)


def combine_kernel(n_pieces, table, *refs):
    pieces, outs = refs[:n_pieces], refs[n_pieces:]
    deep, width = outs[0].shape
    for first in range(0, width, 512):
        at = slice(first, min(first + 512, width))
        rows = jnp.concatenate([p[:, at] for p in pieces], axis=0)
        total = t_mm(table[...], rows)
        for i, out in enumerate(outs):
            out[:, at] = total[i * deep : (i + 1) * deep].astype(out.dtype)


def combine(table, pieces, dtype, shares):
    shape = (table.shape[1] // shares, pieces[0].shape[1])
    return pl.pallas_call(
        lambda *refs: combine_kernel(len(pieces), *refs),
        out_shape=[jax.ShapeDtypeStruct(shape, dtype)] * shares,
        compiler_params=pltpu.CompilerParams(vmem_limit_bytes=VMEM_MOST),
        cost_estimate=LIGHT,
        name="combine",
    )(table, *pieces)


def pack_kernel(chips, near, other, *outs):
    deep = outs[0].shape[0] // 2
    first = 0
    for group in (outs[:chips], outs[chips:]):
        at = slice(first, first + group[0].shape[1])
        for b, out in enumerate(group):
            out[:deep, :] = near[b * deep : (b + 1) * deep, at]
            out[deep:, :] = other[b * deep : (b + 1) * deep, at]
        first = at.stop


def pack(near, other, chips, width):
    deep, first = 2 * near.shape[0] // chips, near.shape[1] - width
    got = pl.pallas_call(
        lambda *refs: pack_kernel(chips, *refs),
        out_shape=[jax.ShapeDtypeStruct((deep, n), BF16) for n in (first, width) for _ in range(chips)],
        compiler_params=pltpu.CompilerParams(vmem_limit_bytes=VMEM_MOST),
        cost_estimate=LIGHT,
        name="pack",
    )(near, other)
    return got[:chips], got[chips:]


def expert_kernel(chips, ff_tiles, n_in, *refs):
    h_in, g_in = refs[: chips + 1], refs[chips + 1 : 2 * chips + 2]
    gate_c, up_c, down_r, gate_r, up_r, down_c, router, picks, marks = refs[2 * chips + 2 : 2 * chips + 11]
    results = refs[n_in : n_in + 2]
    h_all, g_all, hid_all, gg_all, gu_all, scale, dots = refs[n_in + 2 :]
    step = pl.program_id(0)
    deep = h_in[0].shape[0] // 2
    half = chips * deep
    wide, out_wide = gate_c.shape[1], down_c.shape[1]
    width = h_in[0].shape[1]

    @pl.when(step == 0)
    def _():
        for arrived, joined in ((h_in, h_all), (g_in, g_all)):
            for b in range(chips):
                joined[b * deep : (b + 1) * deep, :] = arrived[b][:deep, :]
            joined[half:, :] = arrived[chips][...]
        dots[...] = jnp.zeros_like(dots)
        logits = mm(h_all[...], router[...])
        picked = picks[...] > 0
        top = jnp.max(jnp.where(picked, logits, -1e30), axis=-1, keepdims=True)
        weight = jnp.where(picked, jnp.exp(logits - top), 0.0)
        total = jnp.sum(weight, axis=-1, keepdims=True)
        own = jnp.sum(weight * marks[0:1, : logits.shape[1]], axis=-1, keepdims=True)
        scale[...] = own / jnp.where(total > 0, total, 1.0)

    @pl.when(step < ff_tiles)
    def _():
        gate_proj = mm(h_all[...], gate_c[...])
        up_proj = mm(h_all[...], up_c[...])
        grad_hidden = mm_t(g_all[...], down_r[...])
        at = pl.ds(pl.multiple_of(step * wide, wide), wide)
        sigmoid = jax.nn.sigmoid(gate_proj)
        turned = gate_proj * sigmoid
        hidden = turned * up_proj
        dots[...] += jnp.sum(hidden * grad_hidden, axis=-1, keepdims=True)
        weighted = grad_hidden * scale[...]
        hid_all[:, at] = (hidden * scale[...]).astype(BF16)
        gu_all[:, at] = (weighted * turned).astype(BF16)
        gg_all[:, at] = (weighted * up_proj * (sigmoid + turned * (1.0 - sigmoid))).astype(BF16)

    @pl.when(step >= ff_tiles)
    def _():
        back = (mm_t(gg_all[...], gate_r[...]) + mm_t(gu_all[...], up_r[...])).astype(BF16)
        made = mm(hid_all[...], down_c[...]).astype(BF16)
        at = pl.multiple_of((step - ff_tiles) * out_wide, out_wide)
        behind = pl.multiple_of(at + width + marks.shape[1], 128)
        for core in range(2):
            results[core][:, pl.ds(at, out_wide)] = back[core * half : (core + 1) * half]
            results[core][:, pl.ds(behind, out_wide)] = made[core * half : (core + 1) * half]

    @pl.when(step == ff_tiles)
    def _():
        high = dots[...].astype(BF16).astype(F32)
        tagged = (high * marks[1:2, :] + (dots[...] - high) * marks[2:3, :]).astype(BF16)
        for core in range(2):
            results[core][:, width : width + marks.shape[1]] = tagged[core * half : (core + 1) * half]


def expert_step(j, steps, h_in, g_in, gate, up, down, router, picks, marks, joined):
    chips, (deep, width), ff = len(h_in) - 1, h_in[0].shape, down.shape[0]
    rows, extra = chips * deep, marks.shape[1]
    half = rows // 2
    ff_tile, out_tile = min(256, ff), min(512, width)
    ff_tiles, out_tiles = ff // ff_tile, width // out_tile
    first = lambda i: jnp.minimum(i, ff_tiles - 1)
    second = lambda i: jnp.maximum(i - ff_tiles, 0)
    whole = lambda shape: pl.BlockSpec(shape, lambda i: (0, 0))
    here = lambda n: pl.BlockSpec((rows, n), lambda i: (j, 0))
    in_specs = ([whole((deep, width))] * chips + [whole((half, width))]) * 2 + [
        pl.BlockSpec((width, ff_tile), lambda i: (0, first(i))),
        pl.BlockSpec((width, ff_tile), lambda i: (0, first(i))),
        pl.BlockSpec((ff_tile, width), lambda i: (first(i), 0)),
        pl.BlockSpec((out_tile, ff), lambda i: (second(i), 0)),
        pl.BlockSpec((out_tile, ff), lambda i: (second(i), 0)),
        pl.BlockSpec((ff, out_tile), lambda i: (0, second(i))),
        whole(router.shape),
        pl.BlockSpec((rows, picks.shape[1]), lambda i: (j, 0)),
        whole(marks.shape),
    ]
    args = [*h_in, *g_in, gate, up, down, gate, up, down, router, picks, marks]
    aliases = {}
    if joined:
        aliases = {len(args) + i: 2 + i for i in range(len(joined))}
        args += joined
        in_specs += [pl.BlockSpec(memory_space=pl.ANY)] * len(joined)
    got = pl.pallas_call(
        lambda *refs: expert_kernel(chips, ff_tiles, len(args), *refs),
        grid=(ff_tiles + out_tiles,),
        in_specs=in_specs,
        out_specs=[whole((half, 2 * width + extra))] * 2
        + [here(width), here(width), here(ff), here(ff), here(ff)],
        out_shape=[jax.ShapeDtypeStruct((half, 2 * width + extra), BF16)] * 2
        + [jax.ShapeDtypeStruct((steps * rows, n), BF16) for n in (width, width, ff, ff, ff)],
        scratch_shapes=[pltpu.VMEM((rows, 1), F32), pltpu.VMEM((rows, 1), F32)],
        input_output_aliases=aliases,
        compiler_params=pltpu.CompilerParams(vmem_limit_bytes=VMEM_MOST),
        cost_estimate=LIGHT,
        name="expert",
    )(*args)
    return got[:2], list(got[2:])


def picks_kernel(capacity, own, routes, upto, out):
    top, sources, rows = routes.shape
    lanes = out.shape[1]
    hits = jnp.zeros((sources, rows), F32)
    for i in range(top):
        hits = hits + (routes[i] == own[0:1, 0:1]).astype(F32)
    rank = jnp.where(hits > 0, mm(hits.astype(BF16), upto[...]) - 1.0, -1.0)
    slot = lax.broadcasted_iota(jnp.int32, (capacity, rows), 0).astype(F32)
    lane = lax.broadcasted_iota(jnp.int32, (lanes, rows), 0)
    for source in range(sources):
        table = (rank[source : source + 1] == slot).astype(BF16)
        named = jnp.zeros((lanes, rows), F32)
        for i in range(top):
            named = named + (routes[i, source : source + 1, :] == lane).astype(F32)
        out[source * capacity : (source + 1) * capacity, :] = mm_t(table, named.astype(BF16)).astype(BF16)


def pick_rows(own, routes, upto, capacity, lanes):
    return pl.pallas_call(
        lambda *refs: picks_kernel(capacity, *refs),
        out_shape=jax.ShapeDtypeStruct((routes.shape[1] * capacity, lanes), BF16),
        compiler_params=pltpu.CompilerParams(vmem_limit_bytes=VMEM_MOST),
        cost_estimate=LIGHT,
        name="picks",
    )(own, routes, upto)


def product_kernel(kind, dtype, a, b, *rest):
    out = rest[-1]
    dims = {"nn": ((1,), (0,)), "nt": ((1,), (1,)), "tn": ((0,), (0,))}[kind]
    made = lax.dot_general(a[...], b[...], (dims, ((), ())), preferred_element_type=F32)
    if len(rest) == 2:
        made = made + rest[0][...].astype(F32)
    out[...] = made.astype(dtype)


def product(a, b, kind, dtype, tile, plus=None):
    m, n = a.shape[1 if kind == "tn" else 0], b.shape[0 if kind == "nt" else 1]
    tile = min(tile, m if kind == "tn" else n)
    whole = lambda v: pl.BlockSpec(v.shape, lambda i: (0, 0))
    if kind == "tn":
        specs = [pl.BlockSpec((a.shape[0], tile), lambda i: (0, i)), whole(b)]
        out_spec = pl.BlockSpec((tile, n), lambda i: (i, 0))
    else:
        b_spec = pl.BlockSpec((b.shape[0], tile), lambda i: (0, i))
        if kind == "nt":
            b_spec = pl.BlockSpec((tile, b.shape[1]), lambda i: (i, 0))
        specs = [whole(a), b_spec]
        out_spec = pl.BlockSpec((m, tile), lambda i: (0, i))
    args = [a, b] if plus is None else [a, b, plus]
    return pl.pallas_call(
        lambda *refs: product_kernel(kind, dtype, *refs),
        grid=((m if kind == "tn" else n) // tile,),
        in_specs=specs if plus is None else [*specs, out_spec],
        out_specs=out_spec,
        out_shape=jax.ShapeDtypeStruct((m, n), dtype),
        compiler_params=pltpu.CompilerParams(vmem_limit_bytes=VMEM_MOST),
        cost_estimate=LIGHT,
        name="product",
    )(*args)


def second_norm_kernel(held, arrived, x, gain, resid, normed, scale):
    total = x[...].astype(F32) + held[...] + arrived[...].astype(F32)
    factor = lax.rsqrt(jnp.mean(total * total, axis=-1, keepdims=True) + EPSILON)
    resid[...] = total
    normed[...] = (total * factor * gain[...]).astype(BF16)
    scale[...] = factor


def route_kernel(experts, h, router_weight, picker, router, gates, total):
    logits = mm(h[...], router_weight[...])
    real = lax.broadcasted_iota(jnp.int32, logits.shape, 1) < experts
    logits = jnp.where(real, logits, -1e30)
    shifted = jnp.where(real, jnp.exp(logits - jnp.max(logits, axis=-1, keepdims=True)), 0.0)
    probs = shifted / jnp.sum(shifted, axis=-1, keepdims=True)
    picked = picker[...] * probs
    picked_total = jnp.sum(picked, axis=-1, keepdims=True)
    router[...] = probs
    gates[...] = picked / picked_total
    total[...] = picked_total


def norm_back(v, scale, gain, dy):
    lifted = gain * dy
    inner = jnp.mean(v * lifted, axis=-1, keepdims=True)
    return scale * lifted - v * (scale * scale * scale * inner), jnp.sum(v * scale * dy, axis=0, keepdims=True)


def second_back_kernel(experts, n_homes, n_whole, *refs):
    homes = refs[:n_homes]
    gates, router, picker, total, router_weight, resid, scale, gain, grad_out = refs[n_homes : n_homes + 9]
    grad_resid, low, logit_low, gain_part = refs[n_homes + 9 :]
    width, lanes = resid.shape[1], router.shape[1]
    arrived = homes[0][...]
    for home in homes[1 : 1 + n_whole]:
        arrived = arrived + home[...].astype(F32)
    for upper, lower in zip(homes[1 + n_whole :: 2], homes[2 + n_whole :: 2]):
        arrived = arrived + jnp.where(pl.program_id(0) == 0, upper[...].astype(F32), lower[...].astype(F32))
    tags = arrived[:, width:]
    if tags.shape[1] == lanes:
        dots = tags + pltpu.roll(tags, lanes - experts, 1)
    else:
        dots = tags[:, :lanes] + tags[:, lanes : 2 * lanes]
    probs, chosen = router[...], picker[...]
    dots = jnp.where(chosen > 0, dots, 0.0)
    grad_pick = chosen * (dots - jnp.sum(dots * gates[...], axis=-1, keepdims=True)) / total[...]
    grad_logits = probs * (grad_pick - jnp.sum(probs * grad_pick, axis=-1, keepdims=True))
    logit_low[...] = grad_logits.astype(BF16)
    grad_two = arrived[:, :width] + mm_t(grad_logits.astype(BF16), router_weight[...])
    back, part = norm_back(resid[...], scale[...], gain[...], grad_two)
    back = back + grad_out[...].astype(F32)
    grad_resid[...] = back
    low[...] = back.astype(BF16)
    gain_part[...] = jnp.where(pl.program_id(0) == 0, 0.0, gain_part[...]) + part


def first_back_kernel(held, arrived, x, scale, gain, grad_resid, input_grad, gain_part):
    dy = held[...] + arrived[...].astype(F32)
    back, part = norm_back(x[...].astype(F32), scale[...], gain[...], dy)
    input_grad[...] = grad_resid[...] + back
    gain_part[...] = jnp.where(pl.program_id(0) == 0, 0.0, gain_part[...]) + part


def by_rows(kernel, args, outs, name, step=128):
    rows = args[0].shape[0]

    def spec(shape):
        if shape[0] == rows:
            return pl.BlockSpec((step, shape[1]), lambda i: (i, 0))
        return pl.BlockSpec(shape, lambda i: (0, 0))

    return pl.pallas_call(
        kernel,
        grid=(rows // step,),
        in_specs=[spec(v.shape) for v in args],
        out_specs=[spec(v.shape) for v in outs],
        out_shape=outs,
        compiler_params=pltpu.CompilerParams(vmem_limit_bytes=VMEM_MOST),
        cost_estimate=LIGHT,
        name=name,
    )(*args)


def layer(
    nctx, nep,
    layer_input, attn_gain, q_weight, key_matrix, value_matrix, o_weight, q_gain, key_norm_gain,
    ffn_gain, router_weight, gate_weight, up_weight, down_weight, routes, out_grad,
):
    rows, width = layer_input.shape[1:]
    devices = nctx * nep
    nz = nep // 2
    np_ = nctx * 2
    nb = nctx
    experts = devices
    capacity = -(-rows * TOP * 5 // (4 * experts) // 16) * 16
    length = rows * nctx
    heads = QUERY_HEADS // nctx
    q_cols = heads * HEAD_DIM
    at_ctx = lax.axis_index("ctx")
    at_ep = lax.axis_index("ep")

    due = {}
    clock = 0

    def after(v, *done):
        return lax.optimization_barrier((v, *done))[0] if done else v

    def now(v):
        return after(v, *due.get(clock, []))

    def tick():
        nonlocal clock
        clock += 1

    def swap(v, by_ctx, by_ep, rounds=1):
        if by_ctx == 0 and by_ep == 0:
            return v
        pairs = [(i, ((i // nep) ^ by_ctx) * nep + ((i % nep) ^ by_ep)) for i in range(devices)]
        got = lax.ppermute(now(v) if rounds else v, AXES, pairs)
        if rounds:
            due.setdefault(clock + rounds, []).append(got)
        return got

    def did(v):
        due.setdefault(clock + 1, []).append(v)
        return v

    def swap_z(v, j, rounds=1):
        return swap(v, 0, 2 * j, rounds)

    def sum_all(v):
        bits = [(1 << b, 0) for b in range(nctx.bit_length() - 1)] + [(0, 1 << b) for b in range(nep.bit_length() - 1)]
        for by_ctx, by_ep in bits:
            v = v + swap(v, by_ctx, by_ep, 0)
        return v

    def place(pieces, at, axis=0):
        size = pieces[0].shape[axis]
        shape = list(pieces[0].shape)
        shape[axis] = size * len(pieces)
        whole = after(jnp.zeros(shape, pieces[0].dtype), pieces[-1])
        for i, piece in enumerate(pieces):
            whole = lax.dynamic_update_slice_in_dim(whole, piece, at(i) * size, axis)
        return whole

    def place_ep(far, near):
        return place([v for j in range(nz) for v in (far[j], near[j])], lambda i: at_ep ^ i)

    def own_rows(v, m):
        return lax.dynamic_slice_in_dim(v, (at_ctx ^ m) * rows, rows, 0)

    z_first, z_second = range(1, nz // 2 + 1), range(nz // 2 + 1, nz)
    groups = [list(range(q * nz // 4, (q + 1) * nz // 4)) for q in range(4)]

    x = layer_input[0].astype(F32)
    scale_one = lax.rsqrt(jnp.mean(x * x, axis=-1, keepdims=True) + EPSILON)
    h_one = (x * scale_one * attn_gain).astype(BF16)
    o_cols = width // nctx
    o_piece = lax.dynamic_slice_in_dim(o_weight, at_ctx * o_cols, o_cols, 1)
    qkv_piece = jnp.concatenate(
        [
            lax.dynamic_slice_in_dim(q_weight, at_ctx * q_cols, q_cols, 1),
            lax.dynamic_slice_in_dim(key_matrix, at_ctx * HEAD_DIM, HEAD_DIM, 1),
            lax.dynamic_slice_in_dim(value_matrix, at_ctx * HEAD_DIM, HEAD_DIM, 1),
        ],
        axis=1,
    )
    router_deep = router_weight.size // o_cols
    o_deep = o_piece.shape[0]
    o_piece = jnp.concatenate([o_piece, router_weight.reshape(router_deep, o_cols)])
    far_o, near_o, far_w, near_w = {0: o_piece}, {}, {0: qkv_piece}, {}
    for j in z_first:
        far_o[j] = swap_z(o_piece, j)
    near_o[0] = swap(o_piece, 0, 1)
    near_w[0] = swap(qkv_piece, 0, 1)
    h_pieces = [h_one, None, swap(h_one, 2, 0, 3), None]
    routes_t = routes[0].T
    there = [routes_t] + [None] * (nz - 1)
    for j in groups[1]:
        there[j] = swap_z(routes_t, j)
    tick()

    for j in z_second:
        far_o[j] = swap_z(o_piece, j)
    for j in z_first:
        near_o[j] = swap(far_o[j], 0, 1)
    h_pieces[1] = swap(h_one, 1, 0)
    for j in groups[2]:
        there[j] = swap_z(routes_t, j)
    tick()

    for j in z_first:
        far_w[j] = swap_z(qkv_piece, j)
    for j in z_second:
        near_o[j] = swap(far_o[j], 0, 1)
    for j in groups[0][1:] + groups[3]:
        there[j] = swap_z(routes_t, j)
    tick()

    h_pieces[3] = swap(h_pieces[2], 1, 0)
    for j in z_second:
        far_w[j] = swap_z(qkv_piece, j)
    for j in z_first:
        near_w[j] = swap(far_w[j], 0, 1)
    o_all = now(place_ep(far_o, near_o)).reshape(nep, o_deep + router_deep, o_cols)
    o_part_of = nep // nctx

    def o_block(m):
        block = lax.dynamic_slice(o_all, ((at_ctx ^ m) * o_part_of, 0, 0), (o_part_of, o_deep, o_cols))
        return block.reshape(q_cols, o_cols)

    o_pieces = {0: o_block(0), 2: swap(o_block(2), 2, 0)}
    router_full = o_all[:, o_deep:].reshape(width, experts)
    token = jnp.arange(rows, dtype=jnp.int32)
    upto = (token[:, None] <= token[None, :]).astype(BF16)
    slots = jnp.arange(capacity, dtype=jnp.int32).astype(F32)

    def slot_table(hits):
        rank = mm(hits.astype(BF16), upto) - 1.0
        return ((rank[:, None, :] == slots[None, :, None]) & (hits[:, None, :] > 0)).astype(BF16)

    places = jnp.arange(np_, dtype=jnp.int32)
    plane_experts = (at_ctx ^ (places >> 1 & ~1) ^ (places & 1)) * nep + (at_ep ^ (places >> 1 & 1))
    tables = []
    for j in range(nz):
        hits = jnp.sum((now(there[j])[None] == plane_experts[:, None, None]).astype(F32), axis=1)
        tables.append(slot_table(hits).reshape(np_ * capacity, rows))
    lane_ids = jnp.arange(-(-experts // 128) * 128, dtype=jnp.int32)
    picker = jnp.sum((routes[0][:, :, None] == lane_ids).astype(F32), axis=1)

    def pick(far, q):
        return {j: [did(v) for v in select(tables[j], [now(v) for v in far[j]], nb)] for j in groups[q]}

    def fetch(v, far, q, *parts):
        half = width // 2
        for j in groups[q]:
            if j and len(parts) == 2:
                far[j] = [swap_z(v, j)]
            elif j:
                far.setdefault(j, []).append(swap_z(v[:, parts[0] * half : (parts[0] + 1) * half], j))

    def post(pieces, got, q, *bs, rounds=1):
        for j in groups[q]:
            for b in bs:
                got.setdefault(j, [pieces[j][0]] + [None] * (nb - 1))[b] = swap(pieces[j][b], b & ~1, b & 1, rounds)

    def share(got, q):
        half = np_ * capacity // 2 // nb
        for j in groups[q]:
            got[j].append(swap(jnp.concatenate([v[half:] for v in got[j]], axis=0), 1, 0))

    def share_back(made, q):
        for j in groups[q]:
            made[j] = [made[j][0], swap(made[j][1], 1, 0)]

    def packed(made, q):
        for j in groups[q]:
            copies[j], outs[j] = pack(now(made[j][0]), made[j][1], nb, width)
            did(copies[j][0])

    def gather(pieces, q, shares=2):
        total = {}
        for j in groups[q]:
            ready = [now(pieces[j][0]), *pieces[j][1:]]
            total[j] = combine(tables[j], ready, BF16, shares) if j else combine(tables[j], ready, F32, 1)
            for v in total[j]:
                did(v)
        return total

    def home(total, kept, part, rounds=1):
        for j, v in total.items():
            if j:
                kept.setdefault(j, [None] * len(v))[part] = swap_z(v[part], j, rounds)
            else:
                kept[j] = v

    grad_out = out_grad[0]
    far_g, got_g = {0: [grad_out]}, {}
    tick()

    for j in z_second:
        near_w[j] = swap(far_w[j], 0, 1)
    fetch(grad_out, far_g, 2, 0)
    fetch(grad_out, far_g, 0, 0, 1)
    picked_g0 = pick(far_g, 0)
    frequency = ROPE_BASE ** (-jnp.arange(HEAD_DIM // 2).astype(F32) * 2.0 / HEAD_DIM)
    angles = jnp.arange(length).astype(F32)[:, None] * frequency[None, :]
    cosine, sine = jnp.cos(angles), jnp.sin(angles)
    cos_full = jnp.concatenate([cosine, cosine], axis=1)
    sin_full = jnp.concatenate([-sine, sine], axis=1)
    q_gain_row, k_gain_row = q_gain[None, :], key_norm_gain[None, :]
    h_full = place(h_pieces, lambda i: at_ctx ^ i)
    flat_routes = now(jnp.concatenate(there))
    plane_routes = [flat_routes] + [swap(flat_routes, b & ~1, b & 1) for b in range(1, nb)]
    tick()

    o_pieces[3] = swap(o_block(3), 3, 0)
    o_pieces[1] = swap(o_block(1), 1, 0)
    post(picked_g0, got_g, 0, 1)
    fetch(grad_out, far_g, 2, 1)
    fetch(grad_out, far_g, 3, 0)
    qkv_weight = place_ep(far_w, near_w)
    qkv = mm(h_full, now(qkv_weight))
    attn, turned_q, turned_k, lse = attend(qkv, cos_full, sin_full, q_gain_row, k_gain_row, heads)
    did(attn)
    tick()

    router_wide = jnp.pad(router_full, ((0, 0), (0, lane_ids.shape[0] - experts)))
    fetch(grad_out, far_g, 3, 1)
    picked_g2 = pick(far_g, 2)
    o_rows = place([o_pieces[m] for m in range(nctx)], lambda i: at_ctx ^ i, 1)
    attn = now(attn)
    held = {}
    for hi in reversed(range(0, nctx, 2)):
        sent = swap(mm(own_rows(attn, hi + 1), o_rows).astype(BF16), 1, 0)
        held[hi] = did(mm(own_rows(attn, hi), o_rows) + sent.astype(F32))
    branch_far = swap(held[2].astype(BF16), 2, 0)
    tick()

    post(picked_g0, got_g, 0, 2, 3)
    post(picked_g2, got_g, 2, 1)
    shape = jax.ShapeDtypeStruct
    resid, h_two, scale_two = by_rows(
        second_norm_kernel,
        [held[0], now(branch_far), layer_input[0], ffn_gain[None]],
        [shape((rows, width), F32), shape((rows, width), BF16), shape((rows, 1), F32)],
        "second_norm",
    )
    far_h, got_h = {0: [h_two]}, {}
    fetch(h_two, far_h, 2, 0)
    fetch(h_two, far_h, 0, 0, 1)
    picked_h = pick(far_h, 0)
    tick()

    post(picked_h, got_h, 0, 1, 2, 3)
    share(got_g, 0)
    fetch(h_two, far_h, 2, 1)
    here_routes = now(jnp.stack(plane_routes))
    all_routes = jnp.stack([here_routes, swap(here_routes, 1, 0)])
    picked_g3 = pick(far_g, 3)
    gate, up, down = gate_weight[0], up_weight[0], down_weight[0]
    results, copies, outs, joined = {}, {}, {}, None

    def expert(q):
        nonlocal joined
        for j in groups[q]:
            h_in = [now(got_h[j][0]), *got_h[j][1:]]
            results[j], joined = expert_step(
                j, nz, h_in, got_g[j], gate, up, down, router_wide, picks, marks, joined
            )
            did(results[j][0])

    tick()

    post(picked_g2, got_g, 2, 2, 3)
    post(picked_g3, got_g, 3, 1)
    fetch(h_two, far_h, 3, 0)
    share(got_h, 0)
    picked_h2 = pick(far_h, 2)
    at_device = at_ctx * nep + at_ep
    all_routes = now(all_routes).reshape(2, nb, nz, TOP, rows).transpose(3, 2, 0, 1, 4)
    all_routes = all_routes.reshape(TOP, devices, rows)
    own_id = jnp.full((1, 128), at_device, jnp.int32)
    picks = did(pick_rows(own_id, all_routes, upto, capacity, lane_ids.shape[0]))
    extra = -(-2 * experts // 128) * 128
    extra_ids = jnp.arange(extra, dtype=jnp.int32)
    marks = jnp.stack([extra_ids == at_device, extra_ids == at_device, extra_ids == at_device + experts]).astype(F32)
    lanes = lane_ids.shape[0]
    router, gates, picked_total = by_rows(
        lambda *refs: route_kernel(experts, *refs),
        [now(h_two), router_wide, picker],
        [shape((rows, lanes), F32), shape((rows, lanes), F32), shape((rows, 1), F32)],
        "route",
    )
    did(gates)
    tick()
    post(picked_h2, got_h, 2, 1, 2, 3)
    share(got_g, 2)
    fetch(h_two, far_h, 3, 1)
    expert(0)
    tick()
    post(picked_g3, got_g, 3, 2, 3)
    fetch(grad_out, far_g, 1, 0, 1)
    picked_h3 = pick(far_h, 3)
    share(got_h, 2)
    share_back(results, 0)
    tick()
    post(picked_h3, got_h, 3, 1, 2, 3)
    share(got_g, 3)
    fetch(h_two, far_h, 1, 0, 1)
    picked_g1 = pick(far_g, 1)
    expert(2)
    tick()
    post(picked_g1, got_g, 1, 1, 2, 3)
    share(got_h, 3)
    share_back(results, 2)
    picked_h1 = pick(far_h, 1)
    packed(results, 0)
    tick()
    post(picked_h1, got_h, 1, 1, 2, 3)
    share(got_g, 1)
    expert(3)
    packed(results, 2)
    back, made = {}, {}
    tick()

    post(copies, back, 2, 1, 2, 3)
    share(got_h, 1)
    share_back(results, 3)
    packed(results, 3)
    tick()
    post(copies, back, 3, 1, 2, 3)
    total_2 = gather(back, 2)
    homes = {}
    home(total_2, homes, 0)
    for j in groups[1]:
        got_h[j][0] = after(got_h[j][0], *total_2[groups[2][-1]])
    expert(1)
    tick()
    post(copies, back, 0, 1, 2, 3)
    home(total_2, homes, 1)
    total_3 = gather(back, 3)
    share_back(results, 1)
    packed(results, 1)
    joined_h, joined_g, hidden_all, grad_gate_all, grad_up_all = joined
    gate_part = did(product(joined_h, now(grad_gate_all), "tn", F32, 512))
    tick()
    post(copies, back, 1, 1, 2, 3)
    home(total_3, homes, 0)
    total_0 = gather(back, 0, 1)
    up_part = did(product(joined_h, now(grad_up_all), "tn", F32, 512))
    tick()

    home(total_3, homes, 1)
    home(gather(back, 1, 1), homes, 0)
    home(total_0, homes, 0)
    post(outs, made, 3, 1, 2, 3)
    down_part = did(product(now(hidden_all), joined_g, "tn", F32, 256))
    tick()

    post(outs, made, 2, 1, 2, 3, rounds=2)
    whole = [homes[j][0] for j in sorted(homes) if j and len(homes[j]) == 1]
    homes = [now(homes[0][0]), *whole, *[v for j in sorted(homes) if len(homes[j]) == 2 for v in homes[j]]]
    grad_resid, low, logit_low, ffn_gain_part = by_rows(
        lambda *refs: second_back_kernel(experts, len(homes), len(whole), *refs),
        [*homes, gates, router, picker, picked_total, router_wide, resid, scale_two, ffn_gain[None], grad_out],
        [shape((rows, width), F32), shape((rows, width), BF16), shape((rows, lanes), BF16), shape((1, width), F32)],
        "second_back",
    )
    did(low)
    homes = {}
    total_3 = gather(made, 3)
    home(total_3, homes, 0)
    tick()
    low_pieces = [low, swap(low, 1, 0), swap(low, 2, 0), None]
    home(total_3, homes, 1)
    tick()
    low_pieces[3] = swap(low_pieces[2], 1, 0)
    total_2 = gather(made, 2)
    tick()

    post(outs, made, 1, 1, 2, 3)
    home(total_2, homes, 0)
    branch_full = now(place(low_pieces, lambda i: at_ctx ^ i))
    o_own = q_cols // nep
    own_width = width // devices
    o_part = product(attn, branch_full, "tn", F32, 256)
    router_part = t_mm(logit_low, h_two)[:experts].reshape(experts, nctx, nep, own_width)
    router_rows = experts * nctx * own_width // width

    def o_term(j, ry):
        place_of = at_ep ^ (2 * j + ry)
        block = lax.dynamic_slice_in_dim(o_part, place_of * o_own, o_own, 0)
        router_block = lax.dynamic_slice_in_dim(router_part, place_of, 1, 2).reshape(router_rows, width)
        return jnp.concatenate([block, router_block], axis=0)

    last_steps = list(reversed(range(nz)))
    o_sent = {j: did(o_term(j, 1).astype(BF16)) for j in last_steps}
    grad_attn = did(product(branch_full, o_rows, "nt", BF16, 512))
    tick()

    o_near = {j: swap(o_sent[j], 0, 1) for j in last_steps}
    home(total_2, homes, 1)
    total_1 = gather(made, 1, 1)
    grad_qkv, q_gain_part, k_gain_part = attend_back(
        qkv, turned_q, turned_k, attn, lse, now(grad_attn), cos_full, sin_full, q_gain_row, k_gain_row, heads
    )
    did(grad_qkv)
    tick()

    post(outs, made, 0, 1, 2, 3)
    o_far = {}
    o_mid = {j: (o_term(j, 0) + now(o_near[j]).astype(F32)).astype(BF16) for j in last_steps[:-1]}
    for j in last_steps[: nz // 4]:
        o_far[j] = swap_z(o_mid[j], j)
    qkv_part = product(h_full, now(grad_qkv), "tn", F32, 512).reshape(nctx, nep, own_width, -1)

    def qkv_term(j, ry):
        return lax.dynamic_slice_in_dim(qkv_part, at_ep ^ (2 * j + ry), 1, 1)[:, 0]

    qkv_sent = {j: did(qkv_term(j, 1).astype(BF16)) for j in last_steps}
    one_term = lambda m, plus, dtype: product(
        own_rows(grad_qkv, m), qkv_weight, "nt", dtype, 1024, plus
    )
    sent = [did(one_term(m, None, BF16)) for m in (3, 1)]
    tick()

    first_steps, other_steps = last_steps[::2], last_steps[1::2]
    qkv_near = {j: swap(qkv_sent[j], 0, 1) for j in first_steps}
    sent = [swap(v, 1, 0) for v in sent]
    for j in last_steps[nz // 4 : -1]:
        o_far[j] = swap_z(o_mid[j], j)
    held = [did(one_term(0, sent[1], F32)), did(one_term(2, sent[0], BF16))]
    tick()

    qkv_near.update({j: swap(qkv_sent[j], 0, 1) for j in other_steps})
    one_far = swap(held[1], 2, 0)
    qkv_mid = lambda j: (qkv_term(j, 0) + now(qkv_near[j]).astype(F32)).astype(BF16)
    qkv_far = {j: swap_z(qkv_mid(j), j) for j in last_steps[: nz // 4]}
    home(total_1, homes, 0)
    total_0 = gather(made, 0, 1)
    o_sum = o_term(0, 0) + o_near[0].astype(F32)
    for j in range(1, nz):
        o_sum = o_sum + now(o_far[j]).astype(F32)
    o_grad = did(o_sum[:o_own])
    router_sum = did(o_sum[o_own:].reshape(experts, nctx, own_width).transpose(1, 2, 0))
    tick()

    qkv_far.update({j: swap_z(qkv_mid(j), j) for j in last_steps[nz // 4 : -1]})
    home(total_0, homes, 0)
    input_grad, attn_gain_part = by_rows(
        first_back_kernel,
        [held[0], now(one_far), layer_input[0], scale_one, attn_gain[None], grad_resid],
        [shape((rows, width), F32), shape((1, width), F32)],
        "first_back",
    )
    did(input_grad)
    tick()

    qkv_sum = qkv_term(0, 0) + qkv_near[0].astype(F32)
    for j in range(1, nz):
        qkv_sum = qkv_sum + now(qkv_far[j]).astype(F32)
    last = jnp.concatenate([qkv_sum, router_sum], axis=2).astype(BF16)
    last_block = lambda m: lax.dynamic_index_in_dim(last, at_ctx ^ m, 0)
    last = place([swap(last_block(m), m, 0) for m in range(nctx)], lambda i: at_ctx ^ i).astype(F32)
    late = sum_all(jnp.concatenate([attn_gain_part[0], ffn_gain_part[0], q_gain_part[0], k_gain_part[0]]))
    qkv_grad = last
    router_grad = jnp.sum(last[:, :, q_cols + 2 * HEAD_DIM :], axis=0)
    mixed = resid
    for j in sorted(homes):
        mixed = mixed + jnp.concatenate(homes[j]).astype(F32)

    def columns(first, last):
        return jnp.concatenate([qkv_grad[c, :, first:last] for c in range(nctx)], axis=1)

    return (
        mixed.astype(BF16)[None],
        input_grad[None],
        late[:width],
        columns(0, q_cols),
        columns(q_cols, q_cols + HEAD_DIM),
        columns(q_cols + HEAD_DIM, q_cols + 2 * HEAD_DIM),
        o_grad,
        late[2 * width : 2 * width + HEAD_DIM],
        late[2 * width + HEAD_DIM :],
        late[width : 2 * width],
        router_grad,
        gate_part[None],
        up_part[None],
        down_part[None],
    )


def solution(mesh):
    nctx, nep = mesh.shape["ctx"], mesh.shape["ep"]
    tokens = P("ep", "ctx", None)
    own = P(("ctx", "ep"), None)
    expert = P(("ctx", "ep"), None, None)
    split_rows = P("ep", None)

    def on_device(*arrays):
        return layer(nctx, nep, *arrays)

    return jax.shard_map(
        on_device,
        mesh=mesh,
        in_specs=(
            tokens, P(), split_rows, split_rows, split_rows, split_rows, P(), P(), P(), split_rows,
            expert, expert, expert, tokens, tokens,
        ),
        out_specs=(
            tokens, tokens, P(), own, own, own, own, P(), P(), P(), own, expert, expert, expert,
        ),
        check_vma=False,
    )
```

time: 1160 us -> 1070 us (0.922)
  Pallas kernels: 41.8 us -> 342 us
  matrix products: 196 us -> 18.1 us
  starting transfers between devices: 271 us -> 137 us
  local copies, waits for them, and re-layouts: 198 us -> 78.9 us
  waiting for transfers between devices: 367 us -> 433 us
  other arithmetic: 74.4 us -> 40.9 us
    pallas_call x0 -> x39, Pallas kernels: none -> 302 us  [the longest x4 107 us: expert_step(): pl.pallas_call(lambda *refs: expert_kernel(chips, ff_tiles, len(args), *r...]
    ppermute x134 -> x138, starting transfers between devices: 236 us -> 137 us  [swap(): got = lax.ppermute(now(v) if rounds else v, AXES, pairs)]
    unnamed x429 -> x270, local copies, waits for them, and re-layouts: 99.5 us -> 20.3 us
    dot_general x14 -> x1, matrix products: 74.3 us -> 1.14 us  [t_mm(): lax.dot_general(a, b, (((0,), (0,)), ((), ())), preferred_element_type=F32)]
    dot_general x17 -> x0, matrix products: 67.4 us -> none  [the longest x14 66.8 us: mm_t(): lax.dot_general(a, b, (((1,), (1,)), ((), ())), preferred_element_type=F32)]
    ppermute x134 -> x138, waiting for transfers between devices: 366 us -> 433 us  [swap(): got = lax.ppermute(now(v) if rounds else v, AXES, pairs)]
    dot_general x27 -> x9, matrix products: 54.5 us -> 17 us  [mm(): return jnp.dot(a, b, preferred_element_type=F32)]
    all_to_all x4 -> x0, starting transfers between devices: 34.5 us -> none  [the longest x2 25.3 us: to_experts(): arrived = lax.all_to_all(v, AXES, split_axis=0, concat_axis=0, tiled=True)]
  transfers between devices with their start and end apart: 138 -> 138, of which waited for: 39 -> 57; matrix products, arithmetic and copies ran while one was open for 38% -> 9% of each run, Pallas kernels for 4% -> 30%
where the time goes in v2:
time: 1070 us; the launch traced here: 1050 us
  waiting for transfers between devices  433 us (40%)
  Pallas kernels  342 us (32%)
  starting transfers between devices  137 us (13%)
  local copies, waits for them, and re-layouts  78.9 us (7%)
  other arithmetic  40.9 us (4%)
  matrix products  18.1 us (2%)
    ppermute x138, waiting for transfers between devices, swap(): got = lax.ppermute(now(v) if rounds else v, AXES, pairs)  433 us
    ppermute x138, starting transfers between devices, swap(): got = lax.ppermute(now(v) if rounds else v, AXES, pairs)  137 us
    pallas_call x4, Pallas kernels, expert_step(): pl.pallas_call(lambda *refs: expert_kernel(chips, ff_tiles, len(args), *r...  107 us
    pallas_call x10, Pallas kernels, product(): pl.pallas_call(lambda *refs: product_kernel(kind, dtype, *refs), grid=((m...  87.8 us
    pallas_call x8, Pallas kernels, combine(): pl.pallas_call(lambda *refs: combine_kernel(len(pieces), *refs), out_shap...  32.4 us
    pallas_call x8, Pallas kernels, select(): pl.pallas_call(lambda *refs: select_kernel(len(parts), *refs), out_shape=...  29.6 us
    pallas_call x1, Pallas kernels, attend_back(): pl.pallas_call(attend_back_kernel, grid=(heads + 2,), in_specs=[moving, m...  23.6 us
  transfers between devices with their start and end apart: 138, of which 57 were waited for; matrix products, arithmetic and copies ran while one was open for 9% of the time, Pallas kernels for 30%

profile of v2, /device:TPU:0, one launch (start us, length us, event | category | flops | bytes accessed | tf_op | source)
XLA Modules:
  0.0 1053.9 jit_solution(669060026782581415)
XLA Ops:
  15.9 15.2 %collective-permute-done.5 = s32[8,256]{1,0:T(8,128)S(1)} collective-permute-done((s32[8,256]{1,0:T(8,128)S(1)}, s32[8,256]{1,0:T(8,128)S(1)}, u32[]{:S(2)}, u32[]{:S(2)}) %collective-permute-start.5) | collective-permute-done | bytes 8224 | tf_op jit(solution)/shard_map/ppermute | solution.py:573
  43.6 20.4 %collective-permute-done.10 = s32[8,256]{1,0:T(8,128)S(1)} collective-permute-done((s32[8,256]{1,0:T(8,128)S(1)}, s32[8,256]{1,0:T(8,128)S(1)}, u32[]{:S(2)}, u32[]{:S(2)}) %collective-permute-start.10) | collective-permute-done | bytes 8224 | tf_op jit(solution)/shard_map/ppermute | solution.py:573
  73.9 5.3 collective-permute-done.13
  88.8 10.3 collective-permute-done.11
  110.1 9.2 collective-permute-done.16
  119.2 4.4 collective-permute-done.17
  123.6 13.7 %collective-permute-done.18 = bf16[256,1280]{1,0:T(8,128)(2,1)S(1)} collective-permute-done((bf16[256,1280]{1,0:T(8,128)(2,1)S(1)}, bf16[256,1280]{1,0:T(8,128)(2,1)S(1)}, u32[]{:S(2)}, u32[]{:S(2)}) %collective-permute-start.18) | collective-permute-done | bytes 655392 | tf_op jit(solution)/shard_map/ppermute | solution.py:573
  147.0 4.6 select.9
  151.6 13.9 %collective-permute-done.21.refs_1_ = bf16[256,1024]{1,0:T(8,128)(2,1)S(1)} collective-permute-done((bf16[256,1024]{1,0:T(8,128)(2,1)}, bf16[256,1024]{1,0:T(8,128)(2,1)S(1)}, u32[]{:S(2)}, u32[]{:S(2)}) %collective-permute-start.21) | collective-permute-done | bytes 524320 | tf_op jit(solution)/shard_map/ppermute | solution.py:573
  172.3 5.8 fusion.55.q_ref.k_ref.v_ref
  178.2 17.2 %attend.1 = (bf16[1024,1024]{1,0:T(8,128)(2,1)S(1)}, bf16[1024,1024]{1,0:T(8,128)(2,1)S(1)}, bf16[1024,128]{1,0:T(8,128)(2,1)S(1)}, f32[8,1,1024]{2,1,0:T(1,128)S(1)}) custom-call(f32[1024,1280]{1,0:T(8,128)S(1)} %fusion.55.q_ref.k_ref.v_ref, f32[1024,1280]{1,0:T(8,128)S(1)} %fusion.55.q_ref.k_ref.v_ref, f32[1024,1280]{1,0:T(8,128)S(1)} %fusion.55.q_ref.k_ref.v_ref, ...), custom_call_target="tpu_custom_call" | custom-call | flops 1 | bytes 1 | tf_op jit(solution)/shard_map/attend/pallas_call | solution.py:171
  195.5 16.1 %collective-permute-done.28.refs_2_ = bf16[256,1024]{1,0:T(8,128)(2,1)S(1)} collective-permute-done((bf16[256,1024]{1,0:T(8,128)(2,1)}, bf16[256,1024]{1,0:T(8,128)(2,1)S(1)}, u32[]{:S(2)}, u32[]{:S(2)}) %collective-permute-start.28) | collective-permute-done | bytes 524320 | tf_op jit(solution)/shard_map/ppermute | solution.py:573
  226.9 4.8 convolution_add_fusion.1.held
  231.7 5.1 collective-permute-done.33.refs_2_
  236.8 9.0 collective-permute-done.32.arrived
  249.2 4.1 second_norm.1
  259.2 5.4 collective-permute-done.35.refs_8_
  264.6 11.2 %collective-permute-done.34.refs_7_ = bf16[160,2048]{1,0:T(8,128)(2,1)S(1)} collective-permute-done((bf16[160,2048]{1,0:T(8,128)(2,1)}, bf16[160,2048]{1,0:T(8,128)(2,1)S(1)}, u32[]{:S(2)}, u32[]{:S(2)}) %collective-permute-start.34) | collective-permute-done | bytes 655392 | tf_op jit(solution)/shard_map/ppermute | solution.py:573
  287.2 11.7 %collective-permute-done.40.refs_3_ = bf16[160,2048]{1,0:T(8,128)(2,1)S(1)} collective-permute-done((bf16[160,2048]{1,0:T(8,128)(2,1)}, bf16[160,2048]{1,0:T(8,128)(2,1)S(1)}, u32[]{:S(2)}, u32[]{:S(2)}) %collective-permute-start.40) | collective-permute-done | bytes 655392 | tf_op jit(solution)/shard_map/ppermute | solution.py:573
  298.9 12.1 %collective-permute-done.39.refs_2_ = bf16[160,2048]{1,0:T(8,128)(2,1)S(1)} collective-permute-done((bf16[160,2048]{1,0:T(8,128)(2,1)}, bf16[160,2048]{1,0:T(8,128)(2,1)S(1)}, u32[]{:S(2)}, u32[]{:S(2)}) %collective-permute-start.39) | collective-permute-done | bytes 655392 | tf_op jit(solution)/shard_map/ppermute | solution.py:573
  332.4 6.3 picks.1.refs_17_
  339.7 6.5 collective-permute-done.44.refs_7_
  354.1 26.7 %expert.4 = (bf16[320,4224]{1,0:T(8,128)(2,1)}, bf16[320,4224]{1,0:T(8,128)(2,1)}, bf16[2560,2048]{1,0:T(8,128)(2,1)}, bf16[2560,2048]{1,0:T(8,128)(2,1)}, bf16[...) custom-call(bf16[160,2048]{1,0:T(8,128)(2,1)} %get-tuple-element.410.refs_0_, ...), custom_call_target="tpu_custom_call" | custom-call | flops 1 | bytes 1 | tf_op jit(solution)/shard_map/expert/pallas_call | solution.py:377
  390.8 12.3 %collective-permute-done.55.refs_8_ = bf16[160,2048]{1,0:T(8,128)(2,1)S(1)} collective-permute-done((bf16[160,2048]{1,0:T(8,128)(2,1)}, bf16[160,2048]{1,0:T(8,128)(2,1)S(1)}, u32[]{:S(2)}, u32[]{:S(2)}) %collective-permute-start.55) | collective-permute-done | bytes 655392 | tf_op jit(solution)/shard_map/ppermute | solution.py:573
  403.2 13.1 %collective-permute-done.54.refs_7_ = bf16[160,2048]{1,0:T(8,128)(2,1)} collective-permute-done((bf16[160,2048]{1,0:T(8,128)(2,1)}, bf16[160,2048]{1,0:T(8,128)(2,1)}, u32[]{:S(2)}, u32[]{:S(2)}) %collective-permute-start.54) | collective-permute-done | bytes 655392 | tf_op jit(solution)/shard_map/ppermute | solution.py:573
  427.4 26.7 %expert.5 = (bf16[320,4224]{1,0:T(8,128)(2,1)}, bf16[320,4224]{1,0:T(8,128)(2,1)}, bf16[2560,2048]{1,0:T(8,128)(2,1)}, bf16[2560,2048]{1,0:T(8,128)(2,1)}, bf16[...) custom-call(bf16[160,2048]{1,0:T(8,128)(2,1)} %get-tuple-element.440, ...), custom_call_target="tpu_custom_call", output_to_operand_aliasing={{2}: (19, {}), {3}: (20, {}), {4}: (21, {}), {5}: (22, {}),... | custom-call | flops 1 | bytes 1 | tf_op jit(solution)/shard_map/expert/pallas_call | solution.py:377
  465.0 5.0 pack.4
  470.1 6.6 collective-permute-done.66.refs_8_
  476.7 12.5 %collective-permute-done.65.refs_7_ = bf16[160,2048]{1,0:T(8,128)(2,1)S(1)} collective-permute-done((bf16[160,2048]{1,0:T(8,128)(2,1)}, bf16[160,2048]{1,0:T(8,128)(2,1)S(1)}, u32[]{:S(2)}, u32[]{:S(2)}) %collective-permute-start.65) | collective-permute-done | bytes 655392 | tf_op jit(solution)/shard_map/ppermute | solution.py:573
  494.8 5.0 pack.5
  499.8 26.6 %expert.6 = (bf16[320,4224]{1,0:T(8,128)(2,1)}, bf16[320,4224]{1,0:T(8,128)(2,1)}, bf16[2560,2048]{1,0:T(8,128)(2,1)}, bf16[2560,2048]{1,0:T(8,128)(2,1)}, bf16[...) custom-call(bf16[160,2048]{1,0:T(8,128)(2,1)} %get-tuple-element.463, ...), custom_call_target="tpu_custom_call", output_to_operand_aliasing={{2}: (19, {}), {3}: (20, {}), {4}: (21, {}), {5}: (22, {}),... | custom-call | flops 1 | bytes 1 | tf_op jit(solution)/shard_map/expert/pallas_call | solution.py:377
  535.2 5.1 pack.6
  540.3 9.5 collective-permute-done.76.refs_4_
  549.8 13.5 %collective-permute-done.75.refs_3_ = bf16[160,2176]{1,0:T(8,128)(2,1)} collective-permute-done((bf16[160,2176]{1,0:T(8,128)(2,1)}, bf16[160,2176]{1,0:T(8,128)(2,1)}, u32[]{:S(2)}, u32[]{:S(2)}) %collective-permute-start.75) | collective-permute-done | bytes 696352 | tf_op jit(solution)/shard_map/ppermute | solution.py:573
  572.5 26.9 %expert.7 = (bf16[320,4224]{1,0:T(8,128)(2,1)}, bf16[320,4224]{1,0:T(8,128)(2,1)}, bf16[2560,2048]{1,0:T(8,128)(2,1)}, bf16[2560,2048]{1,0:T(8,128)(2,1)}, bf16[...) custom-call(bf16[160,2048]{1,0:T(8,128)(2,1)} %get-tuple-element.498, ...), custom_call_target="tpu_custom_call", output_to_operand_aliasing={{2}: (19, {}), {3}: (20, {}), {4}: (21, {}), {5}: (22, {}),... | custom-call | flops 1 | bytes 1 | tf_op jit(solution)/shard_map/expert/pallas_call | solution.py:377
  604.9 13.1 %product.10 = f32[2048,768]{1,0:T(8,128)} custom-call(bf16[2560,2048]{1,0:T(8,128)(2,1)} %get-tuple-element.518.refs_0_, bf16[2560,768]{1,0:T(8,128)(2,1)} %get-tuple-element.520.refs_1_), custom_call_target="tpu_custom_call" | custom-call | flops 1 | bytes 1 | tf_op jit(solution)/shard_map/product/pallas_call | solution.py:444
  623.5 5.0 pack.7
  638.7 13.3 %product.11 = f32[2048,768]{1,0:T(8,128)} custom-call(bf16[2560,2048]{1,0:T(8,128)(2,1)} %get-tuple-element.518.refs_0_, bf16[2560,768]{1,0:T(8,128)(2,1)} %get-tuple-element.530.refs_1_), custom_call_target="tpu_custom_call" | custom-call | flops 1 | bytes 1 | tf_op jit(solution)/shard_map/product/pallas_call | solution.py:444
  652.0 4.3 combine.10.refs_0_
  656.4 10.3 collective-permute-done.88.refs_3_
  679.1 14.5 %product.12 = f32[768,2048]{1,0:T(8,128)} custom-call(bf16[2560,768]{1,0:T(8,128)(2,1)} %get-tuple-element.541.refs_0_, bf16[2560,2048]{1,0:T(8,128)(2,1)} %get-tuple-element.542.refs_1_), custom_call_target="tpu_custom_call" | custom-call | flops 1 | bytes 1 | tf_op jit(solution)/shard_map/product/pallas_call | solution.py:444
  693.6 18.4 %collective-permute-done.91.refs_5_ = bf16[128,2176]{1,0:T(8,128)(2,1)S(1)} collective-permute-done((bf16[128,2176]{1,0:T(8,128)(2,1)S(1)}, bf16[128,2176]{1,0:T(8,128)(2,1)S(1)}, u32[]{:S(2)}, u32[]{:S(2)}) %collective-permute-start.91) | collective-permute-done | bytes 557088 | tf_op jit(solution)/shard_map/ppermute | solution.py:573
  720.3 6.8 second_back.1
  727.1 4.7 collective-permute-done.96
  737.3 34.5 %collective-permute-done.99.refs_3_ = bf16[160,2048]{1,0:T(8,128)(2,1)} collective-permute-done((bf16[160,2048]{1,0:T(8,128)(2,1)S(1)}, bf16[160,2048]{1,0:T(8,128)(2,1)}, u32[]{:S(2)}, u32[]{:S(2)}) %collective-permute-start.99) | collective-permute-done | bytes 655392 | tf_op jit(solution)/shard_map/ppermute | solution.py:573
  786.2 9.2 product.14
  807.0 8.7 product.13.do_ref
  817.5 5.6 collective-permute-done.107
  823.1 7.5 collective-permute-done.105.refs_3_
  840.6 23.6 %attend_back.1 = (bf16[1024,1280]{1,0:T(8,128)(2,1)S(1)}, f32[1,128]{1,0:T(1,128)S(1)}, f32[1,128]{1,0:T(1,128)S(1)}) custom-call(bf16[1024,1024]{1,0:T(8,128)(2,1)S(1)} %copy-done.8, f32[1024,1280]{1,0:T(8,128)} %copy-done.2, bf16[1024,1024]{1,0:T(8,128)(2,1)S(1)} %copy-done.6, bf16[1024,1024]{1,0:T(8,128)(2,1)S(1)} %copy-done.5, ...), custom_call_target="tpu_custom_call" | custom-call | flops 1 | bytes 1 | tf_op jit(solution)/shard_map/attend_back/pallas_call | solution.py:195
  864.2 4.7 combine.14
  870.9 11.0 %collective-permute-done.108 = bf16[132,2048]{1,0:T(8,128)(2,1)} collective-permute-done((bf16[132,2048]{1,0:T(8,128)(2,1)}, bf16[132,2048]{1,0:T(8,128)(2,1)}, u32[]{:S(2)}, u32[]{:S(2)}) %collective-permute-start.108) | collective-permute-done | bytes 540704 | tf_op jit(solution)/shard_map/ppermute | solution.py:573
  890.2 4.4 product.17
  894.7 4.4 product.16
  899.1 10.4 product.15
  909.5 4.2 fusion.20
  923.6 4.6 product.19
  929.2 5.1 product.18.held
  934.3 12.0 %collective-permute-done.122 = bf16[132,2048]{1,0:T(8,128)(2,1)S(1)} collective-permute-done((bf16[132,2048]{1,0:T(8,128)(2,1)S(1)}, bf16[132,2048]{1,0:T(8,128)(2,1)S(1)}, u32[]{:S(2)}, u32[]{:S(2)}) %collective-permute-start.122) | collective-permute-done | bytes 540704 | tf_op jit(solution)/shard_map/ppermute | solution.py:573
  956.7 4.2 combine.15
  963.8 24.1 %collective-permute-done.127 = bf16[4,64,1280]{2,1,0:T(8,128)(2,1)S(1)} collective-permute-done((bf16[4,64,1280]{2,1,0:T(8,128)(2,1)}, bf16[4,64,1280]{2,1,0:T(8,128)(2,1)S(1)}, u32[]{:S(2)}, u32[]{:S(2)}) %collective-permute-start.127) | collective-permute-done | bytes 655392 | tf_op jit(solution)/shard_map/ppermute | solution.py:573
  987.9 4.6 first_back.1
  1013.3 23.5 %collective-permute-done.132 = f32[4352]{0:T(1024)S(1)} collective-permute-done((f32[4352]{0:T(1024)S(1)}, f32[4352]{0:T(1024)S(1)}, u32[]{:S(2)}, u32[]{:S(2)}) %collective-permute-start.132) | collective-permute-done | bytes 17440 | tf_op jit(solution)/shard_map/ppermute | solution.py:573
  1041.9 4.5 collective-permute-done.135
  (706 shorter events, 347.6 us)
Async XLA Ops:
  70.2 30.8 %collective-permute-start.12 = (bf16[256,1280]{1,0:T(8,128)(2,1)}, bf16[256,1280]{1,0:T(8,128)(2,1)S(1)}, u32[]{:S(2)}, u32[]{:S(2)}) collective-permute-start(bf16[256,1280]{1,0:T(8,128)(2,1)} %copy-done.79), channel_id=1, source_target_pairs={{0,4},{1,5},{2,6},{3,7},{4,0},{5,1},{6,2},{7,3},{8,12},{9,13},{10,... | collective-permute-start | bytes 1966088 | tf_op jit(solution)/shard_map/ppermute | solution.py:573
  103.1 34.1 %collective-permute-start.19 = (bf16[1024,512]{1,0:T(8,128)(2,1)S(1)}, bf16[1024,512]{1,0:T(8,128)(2,1)S(1)}, u32[]{:S(2)}, u32[]{:S(2)}) collective-permute-start(bf16[1024,512]{1,0:T(8,128)(2,1)S(1)} %bitcast.229), channel_id=1, source_target_pairs={{0,16},{1,17},{2,18},{3,19},{4,20},{5,21},{6,22},{7,23},{8,24},{9,... | collective-permute-start | bytes 3145736 | tf_op jit(solution)/shard_map/ppermute | solution.py:573
  106.0 31.2 %collective-permute-start.15 = (bf16[256,2048]{1,0:T(8,128)(2,1)}, bf16[256,2048]{1,0:T(8,128)(2,1)S(1)}, u32[]{:S(2)}, u32[]{:S(2)}) collective-permute-start(bf16[256,2048]{1,0:T(8,128)(2,1)} %collective-permute-done), channel_id=1, source_target_pairs={{0,8},{1,9},{2,10},{3,11},{4,12},{5,13},{6,14},{7,15},{8,0},{9,1},... | collective-permute-start | bytes 3145736 | tf_op jit(solution)/shard_map/ppermute | solution.py:573
  106.6 30.7 %collective-permute-start.18 = (bf16[256,1280]{1,0:T(8,128)(2,1)S(1)}, bf16[256,1280]{1,0:T(8,128)(2,1)S(1)}, u32[]{:S(2)}, u32[]{:S(2)}) collective-permute-start(bf16[256,1280]{1,0:T(8,128)(2,1)S(1)} %collective-permute-done.12), channel_id=1, source_target_pairs={{0,1},{1,0},{2,3},{3,2},{4,5},{5,4},{6,7},{7,6},{8,9},{9,8},{10,11... | collective-permute-start | bytes 1966088 | tf_op jit(solution)/shard_map/ppermute | solution.py:573
  167.1 44.4 %collective-permute-start.28 = (bf16[256,1024]{1,0:T(8,128)(2,1)}, bf16[256,1024]{1,0:T(8,128)(2,1)S(1)}, u32[]{:S(2)}, u32[]{:S(2)}) collective-permute-start(bf16[256,1024]{1,0:T(8,128)(2,1)} %get-tuple-element.362), channel_id=1, source_target_pairs={{0,4},{1,5},{2,6},{3,7},{4,0},{5,1},{6,2},{7,3},{8,12},{9,13},{10,... | collective-permute-start | bytes 1572872 | tf_op jit(solution)/shard_map/ppermute | solution.py:573
  167.2 44.3 %collective-permute-start.27 = (bf16[160,2048]{1,0:T(8,128)(2,1)}, bf16[160,2048]{1,0:T(8,128)(2,1)S(1)}, u32[]{:S(2)}, u32[]{:S(2)}) collective-permute-start(bf16[160,2048]{1,0:T(8,128)(2,1)} %get-tuple-element.354), channel_id=1, source_target_pairs={{0,1},{1,0},{2,3},{3,2},{4,5},{5,4},{6,7},{7,6},{8,9},{9,8},{10,11... | collective-permute-start | bytes 1966088 | tf_op jit(solution)/shard_map/ppermute | solution.py:573
  171.3 40.3 %collective-permute-start.26 = (bf16[1024,512]{1,0:T(8,128)(2,1)S(1)}, bf16[1024,512]{1,0:T(8,128)(2,1)S(1)}, u32[]{:S(2)}, u32[]{:S(2)}) collective-permute-start(bf16[1024,512]{1,0:T(8,128)(2,1)S(1)} %bitcast.228), channel_id=1, source_target_pairs={{0,8},{1,9},{2,10},{3,11},{4,12},{5,13},{6,14},{7,15},{8,0},{9,1},... | collective-permute-start | bytes 3145736 | tf_op jit(solution)/shard_map/ppermute | solution.py:573
  171.5 40.0 %collective-permute-start.25 = (bf16[1024,512]{1,0:T(8,128)(2,1)S(1)}, bf16[1024,512]{1,0:T(8,128)(2,1)S(1)}, u32[]{:S(2)}, u32[]{:S(2)}) collective-permute-start(bf16[1024,512]{1,0:T(8,128)(2,1)S(1)} %bitcast.227), channel_id=1, source_target_pairs={{0,24},{1,25},{2,26},{3,27},{4,28},{5,29},{6,30},{7,31},{8,16},{9,... | collective-permute-start | bytes 3145736 | tf_op jit(solution)/shard_map/ppermute | solution.py:573
  247.7 31.7 %collective-permute-start.36 = (bf16[160,2048]{1,0:T(8,128)(2,1)}, bf16[160,2048]{1,0:T(8,128)(2,1)S(1)}, u32[]{:S(2)}, u32[]{:S(2)}) collective-permute-start(bf16[160,2048]{1,0:T(8,128)(2,1)} %get-tuple-element.378), channel_id=1, source_target_pairs={{0,1},{1,0},{2,3},{3,2},{4,5},{5,4},{6,7},{7,6},{8,9},{9,8},{10,11... | collective-permute-start | bytes 1966088 | tf_op jit(solution)/shard_map/ppermute | solution.py:573
  279.4 33.9 %collective-permute-start.41 = (bf16[320,2048]{1,0:T(8,128)(2,1)}, bf16[320,2048]{1,0:T(8,128)(2,1)S(1)}, u32[]{:S(2)}, u32[]{:S(2)}) collective-permute-start(bf16[320,2048]{1,0:T(8,128)(2,1)} %pad_maximum_fusion), channel_id=1, source_target_pairs={{0,8},{1,9},{2,10},{3,11},{4,12},{5,13},{6,14},{7,15},{8,0},{9,1},... | collective-permute-start | bytes 3932168 | tf_op jit(solution)/shard_map/ppermute | solution.py:573
  314.4 34.0 %collective-permute-start.48 = (bf16[320,2048]{1,0:T(8,128)(2,1)}, bf16[320,2048]{1,0:T(8,128)(2,1)}, u32[]{:S(2)}, u32[]{:S(2)}) collective-permute-start(bf16[320,2048]{1,0:T(8,128)(2,1)} %pad_maximum_fusion.1), channel_id=1, source_target_pairs={{0,8},{1,9},{2,10},{3,11},{4,12},{5,13},{6,14},{7,15},{8,0},{9,1},... | collective-permute-start | bytes 3932168 | tf_op jit(solution)/shard_map/ppermute | solution.py:573
  315.3 30.9 %collective-permute-start.44 = (bf16[160,2048]{1,0:T(8,128)(2,1)}, bf16[160,2048]{1,0:T(8,128)(2,1)}, u32[]{:S(2)}, u32[]{:S(2)}) collective-permute-start(bf16[160,2048]{1,0:T(8,128)(2,1)} %get-tuple-element.396), channel_id=1, source_target_pairs={{0,16},{1,17},{2,18},{3,19},{4,20},{5,21},{6,22},{7,23},{8,24},{9,... | collective-permute-start | bytes 1966088 | tf_op jit(solution)/shard_map/ppermute | solution.py:573
  316.8 31.5 %collective-permute-start.46 = (bf16[160,2048]{1,0:T(8,128)(2,1)}, bf16[160,2048]{1,0:T(8,128)(2,1)S(1)}, u32[]{:S(2)}, u32[]{:S(2)}) collective-permute-start(bf16[160,2048]{1,0:T(8,128)(2,1)} %get-tuple-element.398), channel_id=1, source_target_pairs={{0,1},{1,0},{2,3},{3,2},{4,5},{5,4},{6,7},{7,6},{8,9},{9,8},{10,11... | collective-permute-start | bytes 1966088 | tf_op jit(solution)/shard_map/ppermute | solution.py:573
  348.4 32.5 %collective-permute-start.52 = (bf16[320,2048]{1,0:T(8,128)(2,1)}, bf16[320,2048]{1,0:T(8,128)(2,1)}, u32[]{:S(2)}, u32[]{:S(2)}) collective-permute-start(bf16[320,2048]{1,0:T(8,128)(2,1)} %pad_maximum_fusion.2), channel_id=1, source_target_pairs={{0,8},{1,9},{2,10},{3,11},{4,12},{5,13},{6,14},{7,15},{8,0},{9,1},... | collective-permute-start | bytes 3932168 | tf_op jit(solution)/shard_map/ppermute | solution.py:573
  348.4 32.3 %collective-permute-start.51 = (bf16[160,2048]{1,0:T(8,128)(2,1)}, bf16[160,2048]{1,0:T(8,128)(2,1)S(1)}, u32[]{:S(2)}, u32[]{:S(2)}) collective-permute-start(bf16[160,2048]{1,0:T(8,128)(2,1)} %get-tuple-element.414), channel_id=1, source_target_pairs={{0,17},{1,16},{2,19},{3,18},{4,21},{5,20},{6,23},{7,22},{8,25},{9,... | collective-permute-start | bytes 1966088 | tf_op jit(solution)/shard_map/ppermute | solution.py:573
  349.8 31.0 %collective-permute-start.50 = (bf16[160,2048]{1,0:T(8,128)(2,1)}, bf16[160,2048]{1,0:T(8,128)(2,1)S(1)}, u32[]{:S(2)}, u32[]{:S(2)}) collective-permute-start(bf16[160,2048]{1,0:T(8,128)(2,1)} %get-tuple-element.413), channel_id=1, source_target_pairs={{0,16},{1,17},{2,18},{3,19},{4,20},{5,21},{6,22},{7,23},{8,24},{9,... | collective-permute-start | bytes 1966088 | tf_op jit(solution)/shard_map/ppermute | solution.py:573
  381.7 36.7 %collective-permute-start.58 = (bf16[320,4224]{1,0:T(8,128)(2,1)}, bf16[320,4224]{1,0:T(8,128)(2,1)S(1)}, u32[]{:S(2)}, u32[]{:S(2)}) collective-permute-start(bf16[320,4224]{1,0:T(8,128)(2,1)} %get-tuple-element.428), channel_id=1, source_target_pairs={{0,8},{1,9},{2,10},{3,11},{4,12},{5,13},{6,14},{7,15},{8,0},{9,1},... | collective-permute-start | bytes 8110088 | tf_op jit(solution)/shard_map/ppermute | solution.py:573
  384.1 34.3 %collective-permute-start.57 = (bf16[320,2048]{1,0:T(8,128)(2,1)}, bf16[320,2048]{1,0:T(8,128)(2,1)}, u32[]{:S(2)}, u32[]{:S(2)}) collective-permute-start(bf16[320,2048]{1,0:T(8,128)(2,1)} %pad_maximum_fusion.3), channel_id=1, source_target_pairs={{0,8},{1,9},{2,10},{3,11},{4,12},{5,13},{6,14},{7,15},{8,0},{9,1},... | collective-permute-start | bytes 3932168 | tf_op jit(solution)/shard_map/ppermute | solution.py:573
  384.4 34.0 %collective-permute-start.56 = (bf16[256,2048]{1,0:T(8,128)(2,1)S(1)}, bf16[256,2048]{1,0:T(8,128)(2,1)}, u32[]{:S(2)}, u32[]{:S(2)}) collective-permute-start(bf16[256,2048]{1,0:T(8,128)(2,1)S(1)} %bitcast.222), channel_id=1, source_target_pairs={{0,2},{1,3},{2,0},{3,1},{4,6},{5,7},{6,4},{7,5},{8,10},{9,11},{10,... | collective-permute-start | bytes 3145736 | tf_op jit(solution)/shard_map/ppermute | solution.py:573
  418.4 35.7 %collective-permute-start.62 = (bf16[320,2048]{1,0:T(8,128)(2,1)}, bf16[320,2048]{1,0:T(8,128)(2,1)}, u32[]{:S(2)}, u32[]{:S(2)}) collective-permute-start(bf16[320,2048]{1,0:T(8,128)(2,1)} %pad_maximum_fusion.4), channel_id=1, source_target_pairs={{0,8},{1,9},{2,10},{3,11},{4,12},{5,13},{6,14},{7,15},{8,0},{9,1},... | collective-permute-start | bytes 3932168 | tf_op jit(solution)/shard_map/ppermute | solution.py:573
  418.5 35.6 %collective-permute-start.63 = (bf16[256,2048]{1,0:T(8,128)(2,1)S(1)}, bf16[256,2048]{1,0:T(8,128)(2,1)}, u32[]{:S(2)}, u32[]{:S(2)}) collective-permute-start(bf16[256,2048]{1,0:T(8,128)(2,1)S(1)} %copy-done.17), channel_id=1, source_target_pairs={{0,2},{1,3},{2,0},{3,1},{4,6},{5,7},{6,4},{7,5},{8,10},{9,11},{10,... | collective-permute-start | bytes 3145736 | tf_op jit(solution)/shard_map/ppermute | solution.py:573
  420.3 33.8 %collective-permute-start.61 = (bf16[160,2048]{1,0:T(8,128)(2,1)}, bf16[160,2048]{1,0:T(8,128)(2,1)S(1)}, u32[]{:S(2)}, u32[]{:S(2)}) collective-permute-start(bf16[160,2048]{1,0:T(8,128)(2,1)} %get-tuple-element.431), channel_id=1, source_target_pairs={{0,17},{1,16},{2,19},{3,18},{4,21},{5,20},{6,23},{7,22},{8,25},{9,... | collective-permute-start | bytes 1966088 | tf_op jit(solution)/shard_map/ppermute | solution.py:573
  421.4 32.7 %collective-permute-start.60 = (bf16[160,2048]{1,0:T(8,128)(2,1)}, bf16[160,2048]{1,0:T(8,128)(2,1)S(1)}, u32[]{:S(2)}, u32[]{:S(2)}) collective-permute-start(bf16[160,2048]{1,0:T(8,128)(2,1)} %get-tuple-element.430), channel_id=1, source_target_pairs={{0,16},{1,17},{2,18},{3,19},{4,20},{5,21},{6,22},{7,23},{8,24},{9,... | collective-permute-start | bytes 1966088 | tf_op jit(solution)/shard_map/ppermute | solution.py:573
  422.6 31.5 %collective-permute-start.59 = (bf16[160,2048]{1,0:T(8,128)(2,1)}, bf16[160,2048]{1,0:T(8,128)(2,1)}, u32[]{:S(2)}, u32[]{:S(2)}) collective-permute-start(bf16[160,2048]{1,0:T(8,128)(2,1)} %get-tuple-element.429), channel_id=1, source_target_pairs={{0,1},{1,0},{2,3},{3,2},{4,5},{5,4},{6,7},{7,6},{8,9},{9,8},{10,11... | collective-permute-start | bytes 1966088 | tf_op jit(solution)/shard_map/ppermute | solution.py:573
  455.2 35.9 %collective-permute-start.68 = (bf16[320,4224]{1,0:T(8,128)(2,1)}, bf16[320,4224]{1,0:T(8,128)(2,1)S(1)}, u32[]{:S(2)}, u32[]{:S(2)}) collective-permute-start(bf16[320,4224]{1,0:T(8,128)(2,1)} %get-tuple-element.457), channel_id=1, source_target_pairs={{0,8},{1,9},{2,10},{3,11},{4,12},{5,13},{6,14},{7,15},{8,0},{9,1},... | collective-permute-start | bytes 8110088 | tf_op jit(solution)/shard_map/ppermute | solution.py:573
  457.5 33.6 %collective-permute-start.67 = (bf16[320,2048]{1,0:T(8,128)(2,1)}, bf16[320,2048]{1,0:T(8,128)(2,1)}, u32[]{:S(2)}, u32[]{:S(2)}) collective-permute-start(bf16[320,2048]{1,0:T(8,128)(2,1)} %pad_maximum_fusion.5), channel_id=1, source_target_pairs={{0,8},{1,9},{2,10},{3,11},{4,12},{5,13},{6,14},{7,15},{8,0},{9,1},... | collective-permute-start | bytes 3932168 | tf_op jit(solution)/shard_map/ppermute | solution.py:573
  491.1 35.3 %collective-permute-start.72 = (bf16[320,2048]{1,0:T(8,128)(2,1)}, bf16[320,2048]{1,0:T(8,128)(2,1)}, u32[]{:S(2)}, u32[]{:S(2)}) collective-permute-start(bf16[320,2048]{1,0:T(8,128)(2,1)} %pad_maximum_fusion.6), channel_id=1, source_target_pairs={{0,8},{1,9},{2,10},{3,11},{4,12},{5,13},{6,14},{7,15},{8,0},{9,1},... | collective-permute-start | bytes 3932168 | tf_op jit(solution)/shard_map/ppermute | solution.py:573
  491.2 35.2 %collective-permute-start.71 = (bf16[160,2048]{1,0:T(8,128)(2,1)}, bf16[160,2048]{1,0:T(8,128)(2,1)}, u32[]{:S(2)}, u32[]{:S(2)}) collective-permute-start(bf16[160,2048]{1,0:T(8,128)(2,1)} %get-tuple-element.472), channel_id=1, source_target_pairs={{0,17},{1,16},{2,19},{3,18},{4,21},{5,20},{6,23},{7,22},{8,25},{9,... | collective-permute-start | bytes 1966088 | tf_op jit(solution)/shard_map/ppermute | solution.py:573
  492.4 34.0 %collective-permute-start.70 = (bf16[160,2048]{1,0:T(8,128)(2,1)}, bf16[160,2048]{1,0:T(8,128)(2,1)}, u32[]{:S(2)}, u32[]{:S(2)}) collective-permute-start(bf16[160,2048]{1,0:T(8,128)(2,1)} %get-tuple-element.471), channel_id=1, source_target_pairs={{0,16},{1,17},{2,18},{3,19},{4,20},{5,21},{6,22},{7,23},{8,24},{9,... | collective-permute-start | bytes 1966088 | tf_op jit(solution)/shard_map/ppermute | solution.py:573
  493.6 32.9 %collective-permute-start.69 = (bf16[160,2048]{1,0:T(8,128)(2,1)}, bf16[160,2048]{1,0:T(8,128)(2,1)}, u32[]{:S(2)}, u32[]{:S(2)}) collective-permute-start(bf16[160,2048]{1,0:T(8,128)(2,1)} %get-tuple-element.470), channel_id=1, source_target_pairs={{0,1},{1,0},{2,3},{3,2},{4,5},{5,4},{6,7},{7,6},{8,9},{9,8},{10,11... | collective-permute-start | bytes 1966088 | tf_op jit(solution)/shard_map/ppermute | solution.py:573
  529.7 34.3 %collective-permute-start.77 = (bf16[320,2048]{1,0:T(8,128)(2,1)S(1)}, bf16[320,2048]{1,0:T(8,128)(2,1)}, u32[]{:S(2)}, u32[]{:S(2)}) collective-permute-start(bf16[320,2048]{1,0:T(8,128)(2,1)S(1)} %pad_maximum_fusion.7), channel_id=1, source_target_pairs={{0,8},{1,9},{2,10},{3,11},{4,12},{5,13},{6,14},{7,15},{8,0},{9,1},... | collective-permute-start | bytes 3932168 | tf_op jit(solution)/shard_map/ppermute | solution.py:573
  531.3 32.0 %collective-permute-start.75 = (bf16[160,2176]{1,0:T(8,128)(2,1)}, bf16[160,2176]{1,0:T(8,128)(2,1)}, u32[]{:S(2)}, u32[]{:S(2)}) collective-permute-start(bf16[160,2176]{1,0:T(8,128)(2,1)} %get-tuple-element.483), channel_id=1, source_target_pairs={{0,16},{1,17},{2,18},{3,19},{4,20},{5,21},{6,22},{7,23},{8,24},{9,... | collective-permute-start | bytes 2088968 | tf_op jit(solution)/shard_map/ppermute | solution.py:573
  532.5 31.4 %collective-permute-start.74 = (bf16[160,2176]{1,0:T(8,128)(2,1)}, bf16[160,2176]{1,0:T(8,128)(2,1)}, u32[]{:S(2)}, u32[]{:S(2)}) collective-permute-start(bf16[160,2176]{1,0:T(8,128)(2,1)} %get-tuple-element.481), channel_id=1, source_target_pairs={{0,1},{1,0},{2,3},{3,2},{4,5},{5,4},{6,7},{7,6},{8,9},{9,8},{10,11... | collective-permute-start | bytes 2088968 | tf_op jit(solution)/shard_map/ppermute | solution.py:573
  564.0 35.5 %collective-permute-start.80 = (bf16[160,2176]{1,0:T(8,128)(2,1)}, bf16[160,2176]{1,0:T(8,128)(2,1)S(1)}, u32[]{:S(2)}, u32[]{:S(2)}) collective-permute-start(bf16[160,2176]{1,0:T(8,128)(2,1)} %get-tuple-element.492), channel_id=1, source_target_pairs={{0,17},{1,16},{2,19},{3,18},{4,21},{5,20},{6,23},{7,22},{8,25},{9,... | collective-permute-start | bytes 2088968 | tf_op jit(solution)/shard_map/ppermute | solution.py:573
  565.1 34.4 %collective-permute-start.79 = (bf16[160,2176]{1,0:T(8,128)(2,1)}, bf16[160,2176]{1,0:T(8,128)(2,1)S(1)}, u32[]{:S(2)}, u32[]{:S(2)}) collective-permute-start(bf16[160,2176]{1,0:T(8,128)(2,1)} %get-tuple-element.490), channel_id=1, source_target_pairs={{0,16},{1,17},{2,18},{3,19},{4,20},{5,21},{6,22},{7,23},{8,24},{9,... | collective-permute-start | bytes 2088968 | tf_op jit(solution)/shard_map/ppermute | solution.py:573
  566.2 33.2 %collective-permute-start.78 = (bf16[160,2176]{1,0:T(8,128)(2,1)}, bf16[160,2176]{1,0:T(8,128)(2,1)S(1)}, u32[]{:S(2)}, u32[]{:S(2)}) collective-permute-start(bf16[160,2176]{1,0:T(8,128)(2,1)} %get-tuple-element.488), channel_id=1, source_target_pairs={{0,1},{1,0},{2,3},{3,2},{4,5},{5,4},{6,7},{7,6},{8,9},{9,8},{10,11... | collective-permute-start | bytes 2088968 | tf_op jit(solution)/shard_map/ppermute | solution.py:573
  599.6 30.8 %collective-permute-start.84 = (bf16[160,2176]{1,0:T(8,128)(2,1)}, bf16[160,2176]{1,0:T(8,128)(2,1)}, u32[]{:S(2)}, u32[]{:S(2)}) collective-permute-start(bf16[160,2176]{1,0:T(8,128)(2,1)} %get-tuple-element.509), channel_id=1, source_target_pairs={{0,17},{1,16},{2,19},{3,18},{4,21},{5,20},{6,23},{7,22},{8,25},{9,... | collective-permute-start | bytes 2088968 | tf_op jit(solution)/shard_map/ppermute | solution.py:573
  600.6 32.6 %collective-permute-start.83 = (bf16[160,2176]{1,0:T(8,128)(2,1)}, bf16[160,2176]{1,0:T(8,128)(2,1)}, u32[]{:S(2)}, u32[]{:S(2)}) collective-permute-start(bf16[160,2176]{1,0:T(8,128)(2,1)} %get-tuple-element.507), channel_id=1, source_target_pairs={{0,16},{1,17},{2,18},{3,19},{4,20},{5,21},{6,22},{7,23},{8,24},{9,... | collective-permute-start | bytes 2088968 | tf_op jit(solution)/shard_map/ppermute | solution.py:573
  602.0 31.8 %collective-permute-start.82 = (bf16[160,2176]{1,0:T(8,128)(2,1)}, bf16[160,2176]{1,0:T(8,128)(2,1)}, u32[]{:S(2)}, u32[]{:S(2)}) collective-permute-start(bf16[160,2176]{1,0:T(8,128)(2,1)} %get-tuple-element.505), channel_id=1, source_target_pairs={{0,1},{1,0},{2,3},{3,2},{4,5},{5,4},{6,7},{7,6},{8,9},{9,8},{10,11... | collective-permute-start | bytes 2088968 | tf_op jit(solution)/shard_map/ppermute | solution.py:573
  634.7 32.1 %collective-permute-start.88 = (bf16[160,2176]{1,0:T(8,128)(2,1)}, bf16[160,2176]{1,0:T(8,128)(2,1)S(1)}, u32[]{:S(2)}, u32[]{:S(2)}) collective-permute-start(bf16[160,2176]{1,0:T(8,128)(2,1)} %get-tuple-element.525), channel_id=1, source_target_pairs={{0,16},{1,17},{2,18},{3,19},{4,20},{5,21},{6,22},{7,23},{8,24},{9,... | collective-permute-start | bytes 2088968 | tf_op jit(solution)/shard_map/ppermute | solution.py:573
  636.1 31.3 %collective-permute-start.87 = (bf16[160,2176]{1,0:T(8,128)(2,1)}, bf16[160,2176]{1,0:T(8,128)(2,1)S(1)}, u32[]{:S(2)}, u32[]{:S(2)}) collective-permute-start(bf16[160,2176]{1,0:T(8,128)(2,1)} %get-tuple-element.523), channel_id=1, source_target_pairs={{0,1},{1,0},{2,3},{3,2},{4,5},{5,4},{6,7},{7,6},{8,9},{9,8},{10,11... | collective-permute-start | bytes 2088968 | tf_op jit(solution)/shard_map/ppermute | solution.py:573
  672.4 39.6 %collective-permute-start.92 = (bf16[256,2176]{1,0:T(8,128)(2,1)}, bf16[256,2176]{1,0:T(8,128)(2,1)S(1)}, u32[]{:S(2)}, u32[]{:S(2)}) collective-permute-start(bf16[256,2176]{1,0:T(8,128)(2,1)} %combine.11), channel_id=1, source_target_pairs={{0,2},{1,3},{2,0},{3,1},{4,6},{5,7},{6,4},{7,5},{8,10},{9,11},{10,... | collective-permute-start | bytes 3342344 | tf_op jit(solution)/shard_map/ppermute | solution.py:573
  674.1 37.9 %collective-permute-start.95 = (bf16[160,2048]{1,0:T(8,128)(2,1)}, bf16[160,2048]{1,0:T(8,128)(2,1)S(1)}, u32[]{:S(2)}, u32[]{:S(2)}) collective-permute-start(bf16[160,2048]{1,0:T(8,128)(2,1)} %get-tuple-element.539), channel_id=1, source_target_pairs={{0,17},{1,16},{2,19},{3,18},{4,21},{5,20},{6,23},{7,22},{8,25},{9,... | collective-permute-start | bytes 1966088 | tf_op jit(solution)/shard_map/ppermute | solution.py:573
  675.4 36.6 %collective-permute-start.94 = (bf16[160,2048]{1,0:T(8,128)(2,1)}, bf16[160,2048]{1,0:T(8,128)(2,1)S(1)}, u32[]{:S(2)}, u32[]{:S(2)}) collective-permute-start(bf16[160,2048]{1,0:T(8,128)(2,1)} %get-tuple-element.537), channel_id=1, source_target_pairs={{0,16},{1,17},{2,18},{3,19},{4,20},{5,21},{6,22},{7,23},{8,24},{9,... | collective-permute-start | bytes 1966088 | tf_op jit(solution)/shard_map/ppermute | solution.py:573
  676.8 35.2 %collective-permute-start.93 = (bf16[160,2048]{1,0:T(8,128)(2,1)S(1)}, bf16[160,2048]{1,0:T(8,128)(2,1)S(1)}, u32[]{:S(2)}, u32[]{:S(2)}) collective-permute-start(bf16[160,2048]{1,0:T(8,128)(2,1)S(1)} %copy-done.128), channel_id=1, source_target_pairs={{0,1},{1,0},{2,3},{3,2},{4,5},{5,4},{6,7},{7,6},{8,9},{9,8},{10,11... | collective-permute-start | bytes 1966088 | tf_op jit(solution)/shard_map/ppermute | solution.py:573
  677.6 34.3 %collective-permute-start.91 = (bf16[128,2176]{1,0:T(8,128)(2,1)S(1)}, bf16[128,2176]{1,0:T(8,128)(2,1)S(1)}, u32[]{:S(2)}, u32[]{:S(2)}) collective-permute-start(bf16[128,2176]{1,0:T(8,128)(2,1)S(1)} %copy-done.129), channel_id=1, source_target_pairs={{0,6},{1,7},{2,4},{3,5},{4,2},{5,3},{6,0},{7,1},{8,14},{9,15},{10,... | collective-permute-start | bytes 1671176 | tf_op jit(solution)/shard_map/ppermute | solution.py:573
  731.9 39.9 %collective-permute-start.101 = (bf16[256,2048]{1,0:T(8,128)(2,1)}, bf16[256,2048]{1,0:T(8,128)(2,1)}, u32[]{:S(2)}, u32[]{:S(2)}) collective-permute-start(bf16[256,2048]{1,0:T(8,128)(2,1)} %get-tuple-element.553), channel_id=1, source_target_pairs={{0,8},{1,9},{2,10},{3,11},{4,12},{5,13},{6,14},{7,15},{8,0},{9,1},... | collective-permute-start | bytes 3145736 | tf_op jit(solution)/shard_map/ppermute | solution.py:573
  731.9 39.9 %collective-permute-start.97 = (bf16[256,2048]{1,0:T(8,128)(2,1)}, bf16[256,2048]{1,0:T(8,128)(2,1)}, u32[]{:S(2)}, u32[]{:S(2)}) collective-permute-start(bf16[256,2048]{1,0:T(8,128)(2,1)} %get-tuple-element.553), channel_id=1, source_target_pairs={{0,16},{1,17},{2,18},{3,19},{4,20},{5,21},{6,22},{7,23},{8,24},{9,... | collective-permute-start | bytes 3145736 | tf_op jit(solution)/shard_map/ppermute | solution.py:573
  732.7 39.1 %collective-permute-start.99 = (bf16[160,2048]{1,0:T(8,128)(2,1)S(1)}, bf16[160,2048]{1,0:T(8,128)(2,1)}, u32[]{:S(2)}, u32[]{:S(2)}) collective-permute-start(bf16[160,2048]{1,0:T(8,128)(2,1)S(1)} %copy-done.124), channel_id=1, source_target_pairs={{0,16},{1,17},{2,18},{3,19},{4,20},{5,21},{6,22},{7,23},{8,24},{9,... | collective-permute-start | bytes 1966088 | tf_op jit(solution)/shard_map/ppermute | solution.py:573
  733.9 37.9 %collective-permute-start.98 = (bf16[160,2048]{1,0:T(8,128)(2,1)S(1)}, bf16[160,2048]{1,0:T(8,128)(2,1)}, u32[]{:S(2)}, u32[]{:S(2)}) collective-permute-start(bf16[160,2048]{1,0:T(8,128)(2,1)S(1)} %copy-done.123), channel_id=1, source_target_pairs={{0,1},{1,0},{2,3},{3,2},{4,5},{5,4},{6,7},{7,6},{8,9},{9,8},{10,11... | collective-permute-start | bytes 1966088 | tf_op jit(solution)/shard_map/ppermute | solution.py:573
  736.3 35.5 %collective-permute-start.102 = (bf16[128,2048]{1,0:T(8,128)(2,1)S(1)}, bf16[128,2048]{1,0:T(8,128)(2,1)}, u32[]{:S(2)}, u32[]{:S(2)}) collective-permute-start(bf16[128,2048]{1,0:T(8,128)(2,1)S(1)} %copy-done.131), channel_id=1, source_target_pairs={{0,6},{1,7},{2,4},{3,5},{4,2},{5,3},{6,0},{7,1},{8,14},{9,15},{10,... | collective-permute-start | bytes 1572872 | tf_op jit(solution)/shard_map/ppermute | solution.py:573
  831.2 37.7 %collective-permute-start.111 = (bf16[132,2048]{1,0:T(8,128)(2,1)}, bf16[132,2048]{1,0:T(8,128)(2,1)S(1)}, u32[]{:S(2)}, u32[]{:S(2)}) collective-permute-start(bf16[132,2048]{1,0:T(8,128)(2,1)} %pad_maximum_fusion.13), channel_id=1, source_target_pairs={{0,1},{1,0},{2,3},{3,2},{4,5},{5,4},{6,7},{7,6},{8,9},{9,8},{10,11... | collective-permute-start | bytes 1622024 | tf_op jit(solution)/shard_map/ppermute | solution.py:573
  832.1 36.8 %collective-permute-start.110 = (bf16[132,2048]{1,0:T(8,128)(2,1)}, bf16[132,2048]{1,0:T(8,128)(2,1)}, u32[]{:S(2)}, u32[]{:S(2)}) collective-permute-start(bf16[132,2048]{1,0:T(8,128)(2,1)} %pad_maximum_fusion.12), channel_id=1, source_target_pairs={{0,1},{1,0},{2,3},{3,2},{4,5},{5,4},{6,7},{7,6},{8,9},{9,8},{10,11... | collective-permute-start | bytes 1622024 | tf_op jit(solution)/shard_map/ppermute | solution.py:573
  833.3 37.6 %collective-permute-start.109 = (bf16[132,2048]{1,0:T(8,128)(2,1)}, bf16[132,2048]{1,0:T(8,128)(2,1)}, u32[]{:S(2)}, u32[]{:S(2)}) collective-permute-start(bf16[132,2048]{1,0:T(8,128)(2,1)} %pad_maximum_fusion.11), channel_id=1, source_target_pairs={{0,1},{1,0},{2,3},{3,2},{4,5},{5,4},{6,7},{7,6},{8,9},{9,8},{10,11... | collective-permute-start | bytes 1622024 | tf_op jit(solution)/shard_map/ppermute | solution.py:573
  834.1 47.8 %collective-permute-start.108 = (bf16[132,2048]{1,0:T(8,128)(2,1)}, bf16[132,2048]{1,0:T(8,128)(2,1)}, u32[]{:S(2)}, u32[]{:S(2)}) collective-permute-start(bf16[132,2048]{1,0:T(8,128)(2,1)} %pad_maximum_fusion.10), channel_id=1, source_target_pairs={{0,1},{1,0},{2,3},{3,2},{4,5},{5,4},{6,7},{7,6},{8,9},{9,8},{10,11... | collective-permute-start | bytes 1622024 | tf_op jit(solution)/shard_map/ppermute | solution.py:573
  835.3 33.6 %collective-permute-start.112 = (bf16[128,2048]{1,0:T(8,128)(2,1)}, bf16[128,2048]{1,0:T(8,128)(2,1)}, u32[]{:S(2)}, u32[]{:S(2)}) collective-permute-start(bf16[128,2048]{1,0:T(8,128)(2,1)} %get-tuple-element.584), channel_id=1, source_target_pairs={{0,4},{1,5},{2,6},{3,7},{4,0},{5,1},{6,2},{7,3},{8,12},{9,13},{10,... | collective-permute-start | bytes 1572872 | tf_op jit(solution)/shard_map/ppermute | solution.py:573
  883.1 30.6 %collective-permute-start.116 = (bf16[132,2048]{1,0:T(8,128)(2,1)S(1)}, bf16[132,2048]{1,0:T(8,128)(2,1)S(1)}, u32[]{:S(2)}, u32[]{:S(2)}) collective-permute-start(bf16[132,2048]{1,0:T(8,128)(2,1)S(1)} %fusion.10), channel_id=1, source_target_pairs={{0,6},{1,7},{2,4},{3,5},{4,2},{5,3},{6,0},{7,1},{8,14},{9,15},{10,... | collective-permute-start | bytes 1622024 | tf_op jit(solution)/shard_map/ppermute | solution.py:573
  948.9 38.9 %collective-permute-start.124 = (bf16[256,2048]{1,0:T(8,128)(2,1)}, bf16[256,2048]{1,0:T(8,128)(2,1)}, u32[]{:S(2)}, u32[]{:S(2)}) collective-permute-start(bf16[256,2048]{1,0:T(8,128)(2,1)} %product.19), channel_id=1, source_target_pairs={{0,16},{1,17},{2,18},{3,19},{4,20},{5,21},{6,22},{7,23},{8,24},{9,... | collective-permute-start | bytes 3145736 | tf_op jit(solution)/shard_map/ppermute | solution.py:573
  949.6 38.3 %collective-permute-start.123 = (bf16[256,2048]{1,0:T(8,128)(2,1)}, bf16[256,2048]{1,0:T(8,128)(2,1)}, u32[]{:S(2)}, u32[]{:S(2)}) collective-permute-start(bf16[256,2048]{1,0:T(8,128)(2,1)} %combine.14), channel_id=1, source_target_pairs={{0,2},{1,3},{2,0},{3,1},{4,6},{5,7},{6,4},{7,5},{8,10},{9,11},{10,... | collective-permute-start | bytes 3145736 | tf_op jit(solution)/shard_map/ppermute | solution.py:573
  951.9 35.9 %collective-permute-start.127 = (bf16[4,64,1280]{2,1,0:T(8,128)(2,1)}, bf16[4,64,1280]{2,1,0:T(8,128)(2,1)S(1)}, u32[]{:S(2)}, u32[]{:S(2)}) collective-permute-start(bf16[4,64,1280]{2,1,0:T(8,128)(2,1)} %fusion.9), channel_id=1, source_target_pairs={{0,6},{1,7},{2,4},{3,5},{4,2},{5,3},{6,0},{7,1},{8,14},{9,15},{10,... | collective-permute-start | bytes 1966088 | tf_op jit(solution)/shard_map/ppermute | solution.py:573
  953.7 34.1 %collective-permute-start.126 = (bf16[4,64,1280]{2,1,0:T(8,128)(2,1)}, bf16[4,64,1280]{2,1,0:T(8,128)(2,1)}, u32[]{:S(2)}, u32[]{:S(2)}) collective-permute-start(bf16[4,64,1280]{2,1,0:T(8,128)(2,1)} %get-tuple-element.608), channel_id=1, source_target_pairs={{0,1},{1,0},{2,3},{3,2},{4,5},{5,4},{6,7},{7,6},{8,9},{9,8},{10,11... | collective-permute-start | bytes 1966088 | tf_op jit(solution)/shard_map/ppermute | solution.py:573
  954.5 33.3 %collective-permute-start.125 = (bf16[4,64,1280]{2,1,0:T(8,128)(2,1)}, bf16[4,64,1280]{2,1,0:T(8,128)(2,1)}, u32[]{:S(2)}, u32[]{:S(2)}) collective-permute-start(bf16[4,64,1280]{2,1,0:T(8,128)(2,1)} %get-tuple-element.607), channel_id=1, source_target_pairs={{0,1},{1,0},{2,3},{3,2},{4,5},{5,4},{6,7},{7,6},{8,9},{9,8},{10,11... | collective-permute-start | bytes 1966088 | tf_op jit(solution)/shard_map/ppermute | solution.py:573
  1005.1 32.3 %collective-permute-start.133 = (bf16[4,64,1280]{2,1,0:T(8,128)(2,1)S(1)}, bf16[4,64,1280]{2,1,0:T(8,128)(2,1)S(1)}, u32[]{:S(2)}, u32[]{:S(2)}) collective-permute-start(bf16[4,64,1280]{2,1,0:T(8,128)(2,1)S(1)} %get-tuple-element.622), channel_id=1, source_target_pairs={{0,2},{1,3},{2,0},{3,1},{4,6},{5,7},{6,4},{7,5},{8,10},{9,11},{10,... | collective-permute-start | bytes 1966088 | tf_op jit(solution)/shard_map/ppermute | solution.py:573
  1007.0 30.4 %collective-permute-start.134 = (bf16[4,64,1280]{2,1,0:T(8,128)(2,1)S(1)}, bf16[4,64,1280]{2,1,0:T(8,128)(2,1)S(1)}, u32[]{:S(2)}, u32[]{:S(2)}) collective-permute-start(bf16[4,64,1280]{2,1,0:T(8,128)(2,1)S(1)} %get-tuple-element.624), channel_id=1, source_target_pairs={{0,4},{1,5},{2,6},{3,7},{4,0},{5,1},{6,2},{7,3},{8,12},{9,13},{10,... | collective-permute-start | bytes 1966088 | tf_op jit(solution)/shard_map/ppermute | solution.py:573
  (213 other events, 3278.2 us)

commit v3 on v2

--- a/solution.py
+++ b/solution.py
@@ -582,8 +582,7 @@
     def swap_z(v, j, rounds=1):
         return swap(v, 0, 2 * j, rounds)
 
-    def sum_all(v):
-        bits = [(1 << b, 0) for b in range(nctx.bit_length() - 1)] + [(0, 1 << b) for b in range(nep.bit_length() - 1)]
+    def sum_over(v, bits):
         for by_ctx, by_ep in bits:
             v = v + swap(v, by_ctx, by_ep, 0)
         return v
@@ -685,13 +684,13 @@
     def pick(far, q):
         return {j: [did(v) for v in select(tables[j], [now(v) for v in far[j]], nb)] for j in groups[q]}
 
-    def fetch(v, far, q, *parts):
+    def fetch(v, far, q, *parts, rounds=1):
         half = width // 2
         for j in groups[q]:
             if j and len(parts) == 2:
-                far[j] = [swap_z(v, j)]
+                far[j] = [swap_z(v, j, rounds)]
             elif j:
-                far.setdefault(j, []).append(swap_z(v[:, parts[0] * half : (parts[0] + 1) * half], j))
+                far.setdefault(j, []).append(swap_z(v[:, parts[0] * half : (parts[0] + 1) * half], j, rounds))
 
     def post(pieces, got, q, *bs, rounds=1):
         for j in groups[q]:
@@ -752,7 +751,8 @@
     o_pieces[1] = swap(o_block(1), 1, 0)
     post(picked_g0, got_g, 0, 1)
     fetch(grad_out, far_g, 2, 1)
-    fetch(grad_out, far_g, 3, 0)
+    behind = after(grad_out, far_g[groups[2][-1]][-1])
+    fetch(behind, far_g, 3, 0, rounds=2)
     qkv_weight = place_ep(far_w, near_w)
     qkv = mm(h_full, now(qkv_weight))
     attn, turned_q, turned_k, lse = attend(qkv, cos_full, sin_full, q_gain_row, k_gain_row, heads)
@@ -760,7 +760,7 @@
     tick()
 
     router_wide = jnp.pad(router_full, ((0, 0), (0, lane_ids.shape[0] - experts)))
-    fetch(grad_out, far_g, 3, 1)
+    fetch(grad_out, far_g, 3, 1, rounds=2)
     picked_g2 = pick(far_g, 2)
     o_rows = place([o_pieces[m] for m in range(nctx)], lambda i: at_ctx ^ i, 1)
     attn = now(attn)
@@ -873,26 +873,24 @@
     tick()
     post(copies, back, 0, 1, 2, 3)
     home(total_2, homes, 1)
-    total_3 = gather(back, 3)
+    total_3 = gather(back, 3, 1)
     share_back(results, 1)
     packed(results, 1)
     joined_h, joined_g, hidden_all, grad_gate_all, grad_up_all = joined
     gate_part = did(product(joined_h, now(grad_gate_all), "tn", F32, 512))
     tick()
     post(copies, back, 1, 1, 2, 3)
-    home(total_3, homes, 0)
+    home(total_3, homes, 0, 2)
     total_0 = gather(back, 0, 1)
     up_part = did(product(joined_h, now(grad_up_all), "tn", F32, 512))
     tick()
 
-    home(total_3, homes, 1)
     home(gather(back, 1, 1), homes, 0)
     home(total_0, homes, 0)
     post(outs, made, 3, 1, 2, 3)
     down_part = did(product(now(hidden_all), joined_g, "tn", F32, 256))
     tick()
 
-    post(outs, made, 2, 1, 2, 3, rounds=2)
     whole = [homes[j][0] for j in sorted(homes) if j and len(homes[j]) == 1]
     homes = [now(homes[0][0]), *whole, *[v for j in sorted(homes) if len(homes[j]) == 2 for v in homes[j]]]
     grad_resid, low, logit_low, ffn_gain_part = by_rows(
@@ -903,18 +901,19 @@
     )
     did(low)
     homes = {}
-    total_3 = gather(made, 3)
-    home(total_3, homes, 0)
+    total_3 = gather(made, 3, 1)
+    home(total_3, homes, 0, 2)
     tick()
     low_pieces = [low, swap(low, 1, 0), swap(low, 2, 0), None]
-    home(total_3, homes, 1)
+    post(outs, made, 2, 1)
+    post(outs, made, 1, 1)
     tick()
     low_pieces[3] = swap(low_pieces[2], 1, 0)
-    total_2 = gather(made, 2)
-    tick()
-
-    post(outs, made, 1, 1, 2, 3)
-    home(total_2, homes, 0)
+    post(outs, made, 2, 2, 3, rounds=2)
+    post(outs, made, 1, 2, rounds=2)
+    post(outs, made, 0, 1, rounds=2)
+    tick()
+
     branch_full = now(place(low_pieces, lambda i: at_ctx ^ i))
     o_own = q_cols // nep
     own_width = width // devices
@@ -931,18 +930,23 @@
     last_steps = list(reversed(range(nz)))
     o_sent = {j: did(o_term(j, 1).astype(BF16)) for j in last_steps}
     grad_attn = did(product(branch_full, o_rows, "nt", BF16, 512))
-    tick()
-
-    o_near = {j: swap(o_sent[j], 0, 1) for j in last_steps}
-    home(total_2, homes, 1)
-    total_1 = gather(made, 1, 1)
+    for j in groups[2]:
+        made[j][0] = after(made[j][0], grad_attn)
+    total_2 = gather(made, 2, 1)
+    home(total_2, homes, 0, 2)
+    tick()
+
+    o_near = {j: swap(o_sent[j], 0, 1) for j in last_steps[:-1]}
+    post(outs, made, 0, 2)
     grad_qkv, q_gain_part, k_gain_part = attend_back(
         qkv, turned_q, turned_k, attn, lse, now(grad_attn), cos_full, sin_full, q_gain_row, k_gain_row, heads
     )
     did(grad_qkv)
     tick()
 
-    post(outs, made, 0, 1, 2, 3)
+    post(outs, made, 1, 3)
+    post(outs, made, 0, 3)
+    o_near[0] = swap(o_sent[0], 0, 1)
     o_far = {}
     o_mid = {j: (o_term(j, 0) + now(o_near[j]).astype(F32)).astype(BF16) for j in last_steps[:-1]}
     for j in last_steps[: nz // 4]:
@@ -964,6 +968,7 @@
     sent = [swap(v, 1, 0) for v in sent]
     for j in last_steps[nz // 4 : -1]:
         o_far[j] = swap_z(o_mid[j], j)
+    total_1, total_0 = gather(made, 1, 1), gather(made, 0, 1)
     held = [did(one_term(0, sent[1], F32)), did(one_term(2, sent[0], BF16))]
     tick()
 
@@ -972,23 +977,24 @@
     qkv_mid = lambda j: (qkv_term(j, 0) + now(qkv_near[j]).astype(F32)).astype(BF16)
     qkv_far = {j: swap_z(qkv_mid(j), j) for j in last_steps[: nz // 4]}
     home(total_1, homes, 0)
-    total_0 = gather(made, 0, 1)
     o_sum = o_term(0, 0) + o_near[0].astype(F32)
     for j in range(1, nz):
         o_sum = o_sum + now(o_far[j]).astype(F32)
     o_grad = did(o_sum[:o_own])
     router_sum = did(o_sum[o_own:].reshape(experts, nctx, own_width).transpose(1, 2, 0))
-    tick()
-
-    qkv_far.update({j: swap_z(qkv_mid(j), j) for j in last_steps[nz // 4 : -1]})
-    home(total_0, homes, 0)
     input_grad, attn_gain_part = by_rows(
         first_back_kernel,
-        [held[0], now(one_far), layer_input[0], scale_one, attn_gain[None], grad_resid],
+        [held[0], one_far, layer_input[0], scale_one, attn_gain[None], grad_resid],
         [shape((rows, width), F32), shape((1, width), F32)],
         "first_back",
     )
     did(input_grad)
+    tick()
+
+    qkv_far.update({j: swap_z(qkv_mid(j), j) for j in last_steps[nz // 4 : -1]})
+    home(total_0, homes, 0)
+    late = jnp.concatenate([now(attn_gain_part)[0], ffn_gain_part[0], q_gain_part[0], k_gain_part[0]])
+    late = did(sum_over(late, [(1 << b, 0) for b in range(nctx.bit_length() - 1)] + [(0, 1)]))
     tick()
 
     qkv_sum = qkv_term(0, 0) + qkv_near[0].astype(F32)
@@ -997,7 +1003,7 @@
     last = jnp.concatenate([qkv_sum, router_sum], axis=2).astype(BF16)
     last_block = lambda m: lax.dynamic_index_in_dim(last, at_ctx ^ m, 0)
     last = place([swap(last_block(m), m, 0) for m in range(nctx)], lambda i: at_ctx ^ i).astype(F32)
-    late = sum_all(jnp.concatenate([attn_gain_part[0], ffn_gain_part[0], q_gain_part[0], k_gain_part[0]]))
+    late = sum_over(now(late), [(0, 2 << b) for b in range(nz.bit_length() - 1)])
     qkv_grad = last
     router_grad = jnp.sum(last[:, :, q_cols + 2 * HEAD_DIM :], axis=0)
     mixed = resid

time: 1070 us -> 1030 us (0.963)
  waiting for transfers between devices: 433 us -> 381 us
    ppermute x138 -> x135, waiting for transfers between devices: 433 us -> 381 us  [swap(): got = lax.ppermute(now(v) if rounds else v, AXES, pairs)]
    ppermute x138 -> x135, starting transfers between devices: 137 us -> 141 us  [swap(): got = lax.ppermute(now(v) if rounds else v, AXES, pairs)]
    unnamed x270 -> x242, local copies, waits for them, and re-layouts: 20.3 us -> 23.9 us
  transfers between devices with their start and end apart: 138 -> 135, of which waited for: 57 -> 54; matrix products, arithmetic and copies ran while one was open for 9% -> 12% of each run, Pallas kernels for 30% -> 33%
where the time goes in v3:
time: 1030 us; the launch traced here: 1020 us
  waiting for transfers between devices  381 us (37%)
  Pallas kernels  340 us (33%)
  starting transfers between devices  141 us (14%)
  local copies, waits for them, and re-layouts  88.9 us (9%)
  other arithmetic  43.1 us (4%)
  matrix products  19.7 us (2%)
    ppermute x135, waiting for transfers between devices, swap(): got = lax.ppermute(now(v) if rounds else v, AXES, pairs)  381 us
    ppermute x135, starting transfers between devices, swap(): got = lax.ppermute(now(v) if rounds else v, AXES, pairs)  141 us
    pallas_call x4, Pallas kernels, expert_step(): pl.pallas_call(lambda *refs: expert_kernel(chips, ff_tiles, len(args), *r...  107 us
    pallas_call x10, Pallas kernels, product(): pl.pallas_call(lambda *refs: product_kernel(kind, dtype, *refs), grid=((m...  87.8 us
    pallas_call x8, Pallas kernels, combine(): pl.pallas_call(lambda *refs: combine_kernel(len(pieces), *refs), out_shap...  31.9 us
    pallas_call x8, Pallas kernels, select(): pl.pallas_call(lambda *refs: select_kernel(len(parts), *refs), out_shape=...  28.3 us
    dynamic_update_slice x28, local copies, waits for them, and re-layouts, place(): whole = lax.dynamic_update_slice_in_dim(whole, piece, at(i) * size, axis)  24.7 us
    unnamed x242, local copies, waits for them, and re-layouts  23.9 us
  transfers between devices with their start and end apart: 135, of which 54 were waited for; matrix products, arithmetic and copies ran while one was open for 12% of the time, Pallas kernels for 33%

profile of v3, /device:TPU:0, one launch (start us, length us, event | category | flops | bytes accessed | tf_op | source)
XLA Modules:
  0.0 1017.6 jit_solution(6993952848751597605)
XLA Ops:
  15.7 15.3 %collective-permute-done.5 = s32[8,256]{1,0:T(8,128)S(1)} collective-permute-done((s32[8,256]{1,0:T(8,128)}, s32[8,256]{1,0:T(8,128)S(1)}, u32[]{:S(2)}, u32[]{:S(2)}) %collective-permute-start.5) | collective-permute-done | bytes 8224 | tf_op jit(solution)/shard_map/ppermute | solution.py:573
  43.6 20.4 %collective-permute-done.10 = s32[8,256]{1,0:T(8,128)S(1)} collective-permute-done((s32[8,256]{1,0:T(8,128)S(1)}, s32[8,256]{1,0:T(8,128)S(1)}, u32[]{:S(2)}, u32[]{:S(2)}) %collective-permute-start.10) | collective-permute-done | bytes 8224 | tf_op jit(solution)/shard_map/ppermute | solution.py:573
  73.9 5.3 collective-permute-done.13
  88.8 10.3 %collective-permute-done.11 = bf16[256,1280]{1,0:T(8,128)(2,1)S(1)} collective-permute-done((bf16[256,1280]{1,0:T(8,128)(2,1)}, bf16[256,1280]{1,0:T(8,128)(2,1)S(1)}, u32[]{:S(2)}, u32[]{:S(2)}) %collective-permute-start.11) | collective-permute-done | bytes 655392 | tf_op jit(solution)/shard_map/ppermute | solution.py:573
  110.2 6.9 collective-permute-done.16
  120.7 13.7 %collective-permute-done.18 = bf16[256,1280]{1,0:T(8,128)(2,1)S(1)} collective-permute-done((bf16[256,1280]{1,0:T(8,128)(2,1)S(1)}, bf16[256,1280]{1,0:T(8,128)(2,1)S(1)}, u32[]{:S(2)}, u32[]{:S(2)}) %collective-permute-start.18) | collective-permute-done | bytes 655392 | tf_op jit(solution)/shard_map/ppermute | solution.py:573
  152.0 10.8 %collective-permute-done.21.refs_1_ = bf16[256,1024]{1,0:T(8,128)(2,1)} collective-permute-done((bf16[256,1024]{1,0:T(8,128)(2,1)}, bf16[256,1024]{1,0:T(8,128)(2,1)}, u32[]{:S(2)}, u32[]{:S(2)}) %collective-permute-start.21) | collective-permute-done | bytes 524320 | tf_op jit(solution)/shard_map/ppermute | solution.py:573
  170.5 7.6 fusion.55.q_ref.k_ref.v_ref
  178.1 17.2 %attend.1 = (bf16[1024,1024]{1,0:T(8,128)(2,1)S(1)}, bf16[1024,1024]{1,0:T(8,128)(2,1)S(1)}, bf16[1024,128]{1,0:T(8,128)(2,1)S(1)}, f32[8,1,1024]{2,1,0:T(1,128)S(1)}) custom-call(f32[1024,1280]{1,0:T(8,128)S(1)} %fusion.55.q_ref.k_ref.v_ref, f32[1024,1280]{1,0:T(8,128)S(1)} %fusion.55.q_ref.k_ref.v_ref, f32[1024,1280]{1,0:T(8,128)S(1)} %fusion.55.q_ref.k_ref.v_ref, ...), custom_call_target="tpu_custom_call" | custom-call | flops 1 | bytes 1 | tf_op jit(solution)/shard_map/attend/pallas_call | solution.py:171
  210.5 4.8 convolution_add_fusion.1.held
  215.3 5.7 collective-permute-done.32.refs_1_
  221.0 9.0 collective-permute-done.31.arrived
  234.9 4.1 second_norm.1
  248.8 12.6 %collective-permute-done.34.refs_7_ = bf16[160,2048]{1,0:T(8,128)(2,1)S(1)} collective-permute-done((bf16[160,2048]{1,0:T(8,128)(2,1)}, bf16[160,2048]{1,0:T(8,128)(2,1)S(1)}, u32[]{:S(2)}, u32[]{:S(2)}) %collective-permute-start.34) | collective-permute-done | bytes 655392 | tf_op jit(solution)/shard_map/ppermute | solution.py:573
  262.7 17.3 %collective-permute-done.37.refs_1_ = bf16[256,1024]{1,0:T(8,128)(2,1)S(1)} collective-permute-done((bf16[256,1024]{1,0:T(8,128)(2,1)S(1)}, bf16[256,1024]{1,0:T(8,128)(2,1)S(1)}, u32[]{:S(2)}, u32[]{:S(2)}) %collective-permute-start.37) | collective-permute-done | bytes 524320 | tf_op jit(solution)/shard_map/ppermute | solution.py:573
  287.9 11.7 %collective-permute-done.40.refs_3_ = bf16[160,2048]{1,0:T(8,128)(2,1)S(1)} collective-permute-done((bf16[160,2048]{1,0:T(8,128)(2,1)}, bf16[160,2048]{1,0:T(8,128)(2,1)S(1)}, u32[]{:S(2)}, u32[]{:S(2)}) %collective-permute-start.40) | collective-permute-done | bytes 655392 | tf_op jit(solution)/shard_map/ppermute | solution.py:573
  299.6 13.4 %collective-permute-done.39.refs_2_ = bf16[160,2048]{1,0:T(8,128)(2,1)S(1)} collective-permute-done((bf16[160,2048]{1,0:T(8,128)(2,1)}, bf16[160,2048]{1,0:T(8,128)(2,1)S(1)}, u32[]{:S(2)}, u32[]{:S(2)}) %collective-permute-start.39) | collective-permute-done | bytes 655392 | tf_op jit(solution)/shard_map/ppermute | solution.py:573
  330.7 6.3 picks.1.refs_17_
  341.0 5.9 collective-permute-done.44.refs_7_
  354.7 26.6 %expert.4 = (bf16[320,4224]{1,0:T(8,128)(2,1)}, bf16[320,4224]{1,0:T(8,128)(2,1)}, bf16[2560,2048]{1,0:T(8,128)(2,1)}, bf16[2560,2048]{1,0:T(8,128)(2,1)}, bf16[...) custom-call(bf16[160,2048]{1,0:T(8,128)(2,1)} %get-tuple-element.405.refs_0_, ...), custom_call_target="tpu_custom_call" | custom-call | flops 1 | bytes 1 | tf_op jit(solution)/shard_map/expert/pallas_call | solution.py:377
  392.2 12.4 %collective-permute-done.55.refs_8_ = bf16[160,2048]{1,0:T(8,128)(2,1)S(1)} collective-permute-done((bf16[160,2048]{1,0:T(8,128)(2,1)}, bf16[160,2048]{1,0:T(8,128)(2,1)S(1)}, u32[]{:S(2)}, u32[]{:S(2)}) %collective-permute-start.55) | collective-permute-done | bytes 655392 | tf_op jit(solution)/shard_map/ppermute | solution.py:573
  404.6 13.0 %collective-permute-done.54.refs_7_ = bf16[160,2048]{1,0:T(8,128)(2,1)} collective-permute-done((bf16[160,2048]{1,0:T(8,128)(2,1)}, bf16[160,2048]{1,0:T(8,128)(2,1)}, u32[]{:S(2)}, u32[]{:S(2)}) %collective-permute-start.54) | collective-permute-done | bytes 655392 | tf_op jit(solution)/shard_map/ppermute | solution.py:573
  428.7 26.7 %expert.5 = (bf16[320,4224]{1,0:T(8,128)(2,1)}, bf16[320,4224]{1,0:T(8,128)(2,1)}, bf16[2560,2048]{1,0:T(8,128)(2,1)}, bf16[2560,2048]{1,0:T(8,128)(2,1)}, bf16[...) custom-call(bf16[160,2048]{1,0:T(8,128)(2,1)} %get-tuple-element.435, ...), custom_call_target="tpu_custom_call", output_to_operand_aliasing={{2}: (19, {}), {3}: (20, {}), {4}: (21, {}), {5}: (22, {}),... | custom-call | flops 1 | bytes 1 | tf_op jit(solution)/shard_map/expert/pallas_call | solution.py:377
  466.3 5.0 pack.4
  471.2 6.7 collective-permute-done.66.refs_8_
  477.9 12.5 %collective-permute-done.65.refs_7_ = bf16[160,2048]{1,0:T(8,128)(2,1)S(1)} collective-permute-done((bf16[160,2048]{1,0:T(8,128)(2,1)}, bf16[160,2048]{1,0:T(8,128)(2,1)S(1)}, u32[]{:S(2)}, u32[]{:S(2)}) %collective-permute-start.65) | collective-permute-done | bytes 655392 | tf_op jit(solution)/shard_map/ppermute | solution.py:573
  496.0 5.0 pack.5
  501.0 26.8 %expert.6 = (bf16[320,4224]{1,0:T(8,128)(2,1)}, bf16[320,4224]{1,0:T(8,128)(2,1)}, bf16[2560,2048]{1,0:T(8,128)(2,1)}, bf16[2560,2048]{1,0:T(8,128)(2,1)}, bf16[...) custom-call(bf16[160,2048]{1,0:T(8,128)(2,1)} %get-tuple-element.463, ...), custom_call_target="tpu_custom_call", output_to_operand_aliasing={{2}: (19, {}), {3}: (20, {}), {4}: (21, {}), {5}: (22, {}),... | custom-call | flops 1 | bytes 1 | tf_op jit(solution)/shard_map/expert/pallas_call | solution.py:377
  536.6 5.0 pack.6
  541.7 7.8 collective-permute-done.73.refs_2_
  551.3 14.3 %collective-permute-done.75.refs_4_ = bf16[160,2176]{1,0:T(8,128)(2,1)} collective-permute-done((bf16[160,2176]{1,0:T(8,128)(2,1)}, bf16[160,2176]{1,0:T(8,128)(2,1)}, u32[]{:S(2)}, u32[]{:S(2)}) %collective-permute-start.75) | collective-permute-done | bytes 696352 | tf_op jit(solution)/shard_map/ppermute | solution.py:573
  569.1 3.9 combine.8
  573.9 26.9 %expert.7 = (bf16[320,4224]{1,0:T(8,128)(2,1)}, bf16[320,4224]{1,0:T(8,128)(2,1)}, bf16[2560,2048]{1,0:T(8,128)(2,1)}, bf16[2560,2048]{1,0:T(8,128)(2,1)}, bf16[...) custom-call(bf16[160,2048]{1,0:T(8,128)(2,1)} %get-tuple-element.484, ...), custom_call_target="tpu_custom_call", output_to_operand_aliasing={{2}: (19, {}), {3}: (20, {}), {4}: (21, {}), {5}: (22, {}),... | custom-call | flops 1 | bytes 1 | tf_op jit(solution)/shard_map/expert/pallas_call | solution.py:377
  607.4 13.1 %product.10 = f32[2048,768]{1,0:T(8,128)} custom-call(bf16[2560,2048]{1,0:T(8,128)(2,1)} %get-tuple-element.512.refs_0_, bf16[2560,768]{1,0:T(8,128)(2,1)} %get-tuple-element.514.refs_1_), custom_call_target="tpu_custom_call" | custom-call | flops 1 | bytes 1 | tf_op jit(solution)/shard_map/product/pallas_call | solution.py:444
  620.6 3.9 combine.9
  626.1 5.0 pack.7
  641.6 13.3 %product.11 = f32[2048,768]{1,0:T(8,128)} custom-call(bf16[2560,2048]{1,0:T(8,128)(2,1)} %get-tuple-element.512.refs_0_, bf16[2560,768]{1,0:T(8,128)(2,1)} %get-tuple-element.524.refs_1_), custom_call_target="tpu_custom_call" | custom-call | flops 1 | bytes 1 | tf_op jit(solution)/shard_map/product/pallas_call | solution.py:444
  654.9 4.4 combine.10.refs_0_
  659.3 10.2 %collective-permute-done.90.refs_4_ = bf16[160,2176]{1,0:T(8,128)(2,1)S(1)} collective-permute-done((bf16[160,2176]{1,0:T(8,128)(2,1)}, bf16[160,2176]{1,0:T(8,128)(2,1)S(1)}, u32[]{:S(2)}, u32[]{:S(2)}) %collective-permute-start.90) | collective-permute-done | bytes 696352 | tf_op jit(solution)/shard_map/ppermute | solution.py:573
  670.4 3.9 combine.11
  679.6 14.5 %product.12 = f32[768,2048]{1,0:T(8,128)} custom-call(bf16[2560,768]{1,0:T(8,128)(2,1)} %get-tuple-element.534.refs_0_, bf16[2560,2048]{1,0:T(8,128)(2,1)} %get-tuple-element.535.refs_1_), custom_call_target="tpu_custom_call" | custom-call | flops 1 | bytes 1 | tf_op jit(solution)/shard_map/product/pallas_call | solution.py:444
  695.2 11.0 %collective-permute-done.94.refs_4_ = bf16[160,2048]{1,0:T(8,128)(2,1)} collective-permute-done((bf16[160,2048]{1,0:T(8,128)(2,1)}, bf16[160,2048]{1,0:T(8,128)(2,1)}, u32[]{:S(2)}, u32[]{:S(2)}) %collective-permute-start.94) | collective-permute-done | bytes 655392 | tf_op jit(solution)/shard_map/ppermute | solution.py:573
  706.2 4.2 combine.12
  712.2 6.7 second_back.1
  722.4 15.6 %collective-permute-done.98.refs_2_ = bf16[160,2048]{1,0:T(8,128)(2,1)} collective-permute-done((bf16[160,2048]{1,0:T(8,128)(2,1)S(1)}, bf16[160,2048]{1,0:T(8,128)(2,1)}, u32[]{:S(2)}, u32[]{:S(2)}) %collective-permute-start.98) | collective-permute-done | bytes 655392 | tf_op jit(solution)/shard_map/ppermute | solution.py:573
  738.0 13.7 %collective-permute-done.99.refs_2_ = bf16[160,2048]{1,0:T(8,128)(2,1)} collective-permute-done((bf16[160,2048]{1,0:T(8,128)(2,1)S(1)}, bf16[160,2048]{1,0:T(8,128)(2,1)}, u32[]{:S(2)}, u32[]{:S(2)}) %collective-permute-start.99) | collective-permute-done | bytes 655392 | tf_op jit(solution)/shard_map/ppermute | solution.py:573
  769.9 8.5 product.13.do_ref
  778.4 9.3 product.14
  794.3 4.0 collective-permute-start.103
  812.9 23.6 %attend_back.1 = (bf16[1024,1280]{1,0:T(8,128)(2,1)S(1)}, f32[1,128]{1,0:T(1,128)S(1)}, f32[1,128]{1,0:T(1,128)S(1)}) custom-call(bf16[1024,1024]{1,0:T(8,128)(2,1)S(1)} %copy-done.8, f32[1024,1280]{1,0:T(8,128)} %copy-done.2, bf16[1024,1024]{1,0:T(8,128)(2,1)S(1)} %copy-done.6, bf16[1024,1024]{1,0:T(8,128)(2,1)S(1)} %copy-done.5, ...), custom_call_target="tpu_custom_call" | custom-call | flops 1 | bytes 1 | tf_op jit(solution)/shard_map/attend_back/pallas_call | solution.py:195
  837.7 5.1 collective-permute-done.108
  852.4 4.4 product.16
  856.9 4.4 product.17
  861.3 10.5 %product.15 = f32[2048,1280]{1,0:T(8,128)} custom-call(bf16[1024,2048]{1,0:T(8,128)(2,1)} %constant_dynamic-update-slice_fusion.27.refs_0_, bf16[1024,1280]{1,0:T(8,128)(2,1)} %copy-done.3), custom_call_target="tpu_custom_call" | custom-call | flops 1 | bytes 1 | tf_op jit(solution)/shard_map/product/pallas_call | solution.py:444
  871.8 4.2 fusion.20
  875.9 10.0 collective-permute-done.112
  898.4 4.1 combine.14
  902.5 4.9 product.18.held
  908.3 4.8 product.19
  913.2 5.8 collective-permute-done.118
  933.9 13.0 %collective-permute-done.121.arrived = bf16[256,2048]{1,0:T(8,128)(2,1)S(1)} collective-permute-done((bf16[256,2048]{1,0:T(8,128)(2,1)}, bf16[256,2048]{1,0:T(8,128)(2,1)S(1)}, u32[]{:S(2)}, u32[]{:S(2)}) %collective-permute-start.121) | collective-permute-done | bytes 1048608 | tf_op jit(solution)/shard_map/ppermute | solution.py:573
  947.8 4.4 first_back.1
  953.7 8.1 collective-permute-done.124
  974.6 23.8 %collective-permute-done.128 = bf16[4,64,1280]{2,1,0:T(8,128)(2,1)S(1)} collective-permute-done((bf16[4,64,1280]{2,1,0:T(8,128)(2,1)S(1)}, bf16[4,64,1280]{2,1,0:T(8,128)(2,1)S(1)}, u32[]{:S(2)}, u32[]{:S(2)}) %collective-permute-start.128) | collective-permute-done | bytes 655392 | tf_op jit(solution)/shard_map/ppermute | solution.py:573
  (671 shorter events, 351.0 us)
Async XLA Ops:
  70.2 30.8 %collective-permute-start.12 = (bf16[256,1280]{1,0:T(8,128)(2,1)}, bf16[256,1280]{1,0:T(8,128)(2,1)S(1)}, u32[]{:S(2)}, u32[]{:S(2)}) collective-permute-start(bf16[256,1280]{1,0:T(8,128)(2,1)} %copy-done.75), channel_id=1, source_target_pairs={{0,4},{1,5},{2,6},{3,7},{4,0},{5,1},{6,2},{7,3},{8,12},{9,13},{10,... | collective-permute-start | bytes 1966088 | tf_op jit(solution)/shard_map/ppermute | solution.py:573
  103.2 31.2 %collective-permute-start.15 = (bf16[256,2048]{1,0:T(8,128)(2,1)}, bf16[256,2048]{1,0:T(8,128)(2,1)S(1)}, u32[]{:S(2)}, u32[]{:S(2)}) collective-permute-start(bf16[256,2048]{1,0:T(8,128)(2,1)} %collective-permute-done), channel_id=1, source_target_pairs={{0,8},{1,9},{2,10},{3,11},{4,12},{5,13},{6,14},{7,15},{8,0},{9,1},... | collective-permute-start | bytes 3145736 | tf_op jit(solution)/shard_map/ppermute | solution.py:573
  103.7 30.7 %collective-permute-start.18 = (bf16[256,1280]{1,0:T(8,128)(2,1)S(1)}, bf16[256,1280]{1,0:T(8,128)(2,1)S(1)}, u32[]{:S(2)}, u32[]{:S(2)}) collective-permute-start(bf16[256,1280]{1,0:T(8,128)(2,1)S(1)} %collective-permute-done.12), channel_id=1, source_target_pairs={{0,1},{1,0},{2,3},{3,2},{4,5},{5,4},{6,7},{7,6},{8,9},{9,8},{10,11... | collective-permute-start | bytes 1966088 | tf_op jit(solution)/shard_map/ppermute | solution.py:573
  162.8 32.6 %collective-permute-start.25 = (bf16[1024,512]{1,0:T(8,128)(2,1)}, bf16[1024,512]{1,0:T(8,128)(2,1)S(1)}, u32[]{:S(2)}, u32[]{:S(2)}) collective-permute-start(bf16[1024,512]{1,0:T(8,128)(2,1)} %bitcast.11), channel_id=1, source_target_pairs={{0,24},{1,25},{2,26},{3,27},{4,28},{5,29},{6,30},{7,31},{8,16},{9,... | collective-permute-start | bytes 3145736 | tf_op jit(solution)/shard_map/ppermute | solution.py:573
  163.9 32.8 %collective-permute-start.26 = (bf16[1024,512]{1,0:T(8,128)(2,1)}, bf16[1024,512]{1,0:T(8,128)(2,1)S(1)}, u32[]{:S(2)}, u32[]{:S(2)}) collective-permute-start(bf16[1024,512]{1,0:T(8,128)(2,1)} %bitcast.12), channel_id=1, source_target_pairs={{0,8},{1,9},{2,10},{3,11},{4,12},{5,13},{6,14},{7,15},{8,0},{9,1},... | collective-permute-start | bytes 3145736 | tf_op jit(solution)/shard_map/ppermute | solution.py:573
  234.4 45.6 %collective-permute-start.36 = (bf16[160,2048]{1,0:T(8,128)(2,1)}, bf16[160,2048]{1,0:T(8,128)(2,1)S(1)}, u32[]{:S(2)}, u32[]{:S(2)}) collective-permute-start(bf16[160,2048]{1,0:T(8,128)(2,1)} %get-tuple-element.373), channel_id=1, source_target_pairs={{0,1},{1,0},{2,3},{3,2},{4,5},{5,4},{6,7},{7,6},{8,9},{9,8},{10,11... | collective-permute-start | bytes 1966088 | tf_op jit(solution)/shard_map/ppermute | solution.py:573
  241.1 38.9 %collective-permute-start.37 = (bf16[256,1024]{1,0:T(8,128)(2,1)S(1)}, bf16[256,1024]{1,0:T(8,128)(2,1)S(1)}, u32[]{:S(2)}, u32[]{:S(2)}) collective-permute-start(bf16[256,1024]{1,0:T(8,128)(2,1)S(1)} %get-tuple-element.394), channel_id=1, source_target_pairs={{0,4},{1,5},{2,6},{3,7},{4,0},{5,1},{6,2},{7,3},{8,12},{9,13},{10,... | collective-permute-start | bytes 1572872 | tf_op jit(solution)/shard_map/ppermute | solution.py:573
  280.0 34.4 %collective-permute-start.41 = (bf16[320,2048]{1,0:T(8,128)(2,1)}, bf16[320,2048]{1,0:T(8,128)(2,1)}, u32[]{:S(2)}, u32[]{:S(2)}) collective-permute-start(bf16[320,2048]{1,0:T(8,128)(2,1)} %pad_maximum_fusion), channel_id=1, source_target_pairs={{0,8},{1,9},{2,10},{3,11},{4,12},{5,13},{6,14},{7,15},{8,0},{9,1},... | collective-permute-start | bytes 3932168 | tf_op jit(solution)/shard_map/ppermute | solution.py:573
  282.6 30.4 %collective-permute-start.39 = (bf16[160,2048]{1,0:T(8,128)(2,1)}, bf16[160,2048]{1,0:T(8,128)(2,1)S(1)}, u32[]{:S(2)}, u32[]{:S(2)}) collective-permute-start(bf16[160,2048]{1,0:T(8,128)(2,1)} %get-tuple-element.378), channel_id=1, source_target_pairs={{0,16},{1,17},{2,18},{3,19},{4,20},{5,21},{6,22},{7,23},{8,24},{9,... | collective-permute-start | bytes 1966088 | tf_op jit(solution)/shard_map/ppermute | solution.py:573
  314.5 34.5 %collective-permute-start.48 = (bf16[320,2048]{1,0:T(8,128)(2,1)}, bf16[320,2048]{1,0:T(8,128)(2,1)}, u32[]{:S(2)}, u32[]{:S(2)}) collective-permute-start(bf16[320,2048]{1,0:T(8,128)(2,1)} %pad_maximum_fusion.1), channel_id=1, source_target_pairs={{0,8},{1,9},{2,10},{3,11},{4,12},{5,13},{6,14},{7,15},{8,0},{9,1},... | collective-permute-start | bytes 3932168 | tf_op jit(solution)/shard_map/ppermute | solution.py:573
  315.9 31.0 %collective-permute-start.44 = (bf16[160,2048]{1,0:T(8,128)(2,1)}, bf16[160,2048]{1,0:T(8,128)(2,1)}, u32[]{:S(2)}, u32[]{:S(2)}) collective-permute-start(bf16[160,2048]{1,0:T(8,128)(2,1)} %get-tuple-element.391), channel_id=1, source_target_pairs={{0,16},{1,17},{2,18},{3,19},{4,20},{5,21},{6,22},{7,23},{8,24},{9,... | collective-permute-start | bytes 1966088 | tf_op jit(solution)/shard_map/ppermute | solution.py:573
  317.5 31.5 %collective-permute-start.46 = (bf16[160,2048]{1,0:T(8,128)(2,1)}, bf16[160,2048]{1,0:T(8,128)(2,1)S(1)}, u32[]{:S(2)}, u32[]{:S(2)}) collective-permute-start(bf16[160,2048]{1,0:T(8,128)(2,1)} %get-tuple-element.393), channel_id=1, source_target_pairs={{0,1},{1,0},{2,3},{3,2},{4,5},{5,4},{6,7},{7,6},{8,9},{9,8},{10,11... | collective-permute-start | bytes 1966088 | tf_op jit(solution)/shard_map/ppermute | solution.py:573
  318.9 30.1 %collective-permute-start.47 = (bf16[256,1024]{1,0:T(8,128)(2,1)}, bf16[256,1024]{1,0:T(8,128)(2,1)}, u32[]{:S(2)}, u32[]{:S(2)}) collective-permute-start(bf16[256,1024]{1,0:T(8,128)(2,1)} %copy-done.103), channel_id=1, source_target_pairs={{0,6},{1,7},{2,4},{3,5},{4,2},{5,3},{6,0},{7,1},{8,14},{9,15},{10,... | collective-permute-start | bytes 1572872 | tf_op jit(solution)/shard_map/ppermute | solution.py:573
  349.0 32.8 %collective-permute-start.52 = (bf16[320,2048]{1,0:T(8,128)(2,1)}, bf16[320,2048]{1,0:T(8,128)(2,1)}, u32[]{:S(2)}, u32[]{:S(2)}) collective-permute-start(bf16[320,2048]{1,0:T(8,128)(2,1)} %pad_maximum_fusion.2), channel_id=1, source_target_pairs={{0,8},{1,9},{2,10},{3,11},{4,12},{5,13},{6,14},{7,15},{8,0},{9,1},... | collective-permute-start | bytes 3932168 | tf_op jit(solution)/shard_map/ppermute | solution.py:573
  349.1 32.2 %collective-permute-start.49 = (bf16[160,2048]{1,0:T(8,128)(2,1)}, bf16[160,2048]{1,0:T(8,128)(2,1)S(1)}, u32[]{:S(2)}, u32[]{:S(2)}) collective-permute-start(bf16[160,2048]{1,0:T(8,128)(2,1)} %get-tuple-element.407), channel_id=1, source_target_pairs={{0,1},{1,0},{2,3},{3,2},{4,5},{5,4},{6,7},{7,6},{8,9},{9,8},{10,11... | collective-permute-start | bytes 1966088 | tf_op jit(solution)/shard_map/ppermute | solution.py:573
  349.9 31.5 %collective-permute-start.50 = (bf16[160,2048]{1,0:T(8,128)(2,1)}, bf16[160,2048]{1,0:T(8,128)(2,1)}, u32[]{:S(2)}, u32[]{:S(2)}) collective-permute-start(bf16[160,2048]{1,0:T(8,128)(2,1)} %get-tuple-element.408), channel_id=1, source_target_pairs={{0,16},{1,17},{2,18},{3,19},{4,20},{5,21},{6,22},{7,23},{8,24},{9,... | collective-permute-start | bytes 1966088 | tf_op jit(solution)/shard_map/ppermute | solution.py:573
  350.4 31.4 %collective-permute-start.51 = (bf16[160,2048]{1,0:T(8,128)(2,1)}, bf16[160,2048]{1,0:T(8,128)(2,1)}, u32[]{:S(2)}, u32[]{:S(2)}) collective-permute-start(bf16[160,2048]{1,0:T(8,128)(2,1)} %get-tuple-element.409), channel_id=1, source_target_pairs={{0,17},{1,16},{2,19},{3,18},{4,21},{5,20},{6,23},{7,22},{8,25},{9,... | collective-permute-start | bytes 1966088 | tf_op jit(solution)/shard_map/ppermute | solution.py:573
  382.2 37.7 %collective-permute-start.58 = (bf16[320,4224]{1,0:T(8,128)(2,1)}, bf16[320,4224]{1,0:T(8,128)(2,1)S(1)}, u32[]{:S(2)}, u32[]{:S(2)}) collective-permute-start(bf16[320,4224]{1,0:T(8,128)(2,1)} %get-tuple-element.423), channel_id=1, source_target_pairs={{0,8},{1,9},{2,10},{3,11},{4,12},{5,13},{6,14},{7,15},{8,0},{9,1},... | collective-permute-start | bytes 8110088 | tf_op jit(solution)/shard_map/ppermute | solution.py:573
  385.5 34.3 %collective-permute-start.57 = (bf16[320,2048]{1,0:T(8,128)(2,1)}, bf16[320,2048]{1,0:T(8,128)(2,1)}, u32[]{:S(2)}, u32[]{:S(2)}) collective-permute-start(bf16[320,2048]{1,0:T(8,128)(2,1)} %pad_maximum_fusion.3), channel_id=1, source_target_pairs={{0,8},{1,9},{2,10},{3,11},{4,12},{5,13},{6,14},{7,15},{8,0},{9,1},... | collective-permute-start | bytes 3932168 | tf_op jit(solution)/shard_map/ppermute | solution.py:573
  385.9 33.9 %collective-permute-start.56 = (bf16[256,2048]{1,0:T(8,128)(2,1)S(1)}, bf16[256,2048]{1,0:T(8,128)(2,1)}, u32[]{:S(2)}, u32[]{:S(2)}) collective-permute-start(bf16[256,2048]{1,0:T(8,128)(2,1)S(1)} %bitcast.223), channel_id=1, source_target_pairs={{0,2},{1,3},{2,0},{3,1},{4,6},{5,7},{6,4},{7,5},{8,10},{9,11},{10,... | collective-permute-start | bytes 3145736 | tf_op jit(solution)/shard_map/ppermute | solution.py:573
  419.8 35.7 %collective-permute-start.62 = (bf16[320,2048]{1,0:T(8,128)(2,1)}, bf16[320,2048]{1,0:T(8,128)(2,1)}, u32[]{:S(2)}, u32[]{:S(2)}) collective-permute-start(bf16[320,2048]{1,0:T(8,128)(2,1)} %pad_maximum_fusion.4), channel_id=1, source_target_pairs={{0,8},{1,9},{2,10},{3,11},{4,12},{5,13},{6,14},{7,15},{8,0},{9,1},... | collective-permute-start | bytes 3932168 | tf_op jit(solution)/shard_map/ppermute | solution.py:573
  419.9 35.6 %collective-permute-start.63 = (bf16[256,2048]{1,0:T(8,128)(2,1)S(1)}, bf16[256,2048]{1,0:T(8,128)(2,1)}, u32[]{:S(2)}, u32[]{:S(2)}) collective-permute-start(bf16[256,2048]{1,0:T(8,128)(2,1)S(1)} %copy-done.18), channel_id=1, source_target_pairs={{0,2},{1,3},{2,0},{3,1},{4,6},{5,7},{6,4},{7,5},{8,10},{9,11},{10,... | collective-permute-start | bytes 3145736 | tf_op jit(solution)/shard_map/ppermute | solution.py:573
  421.7 33.8 %collective-permute-start.59 = (bf16[160,2048]{1,0:T(8,128)(2,1)}, bf16[160,2048]{1,0:T(8,128)(2,1)S(1)}, u32[]{:S(2)}, u32[]{:S(2)}) collective-permute-start(bf16[160,2048]{1,0:T(8,128)(2,1)} %get-tuple-element.424), channel_id=1, source_target_pairs={{0,1},{1,0},{2,3},{3,2},{4,5},{5,4},{6,7},{7,6},{8,9},{9,8},{10,11... | collective-permute-start | bytes 1966088 | tf_op jit(solution)/shard_map/ppermute | solution.py:573
  422.6 33.0 %collective-permute-start.60 = (bf16[160,2048]{1,0:T(8,128)(2,1)}, bf16[160,2048]{1,0:T(8,128)(2,1)S(1)}, u32[]{:S(2)}, u32[]{:S(2)}) collective-permute-start(bf16[160,2048]{1,0:T(8,128)(2,1)} %get-tuple-element.425), channel_id=1, source_target_pairs={{0,16},{1,17},{2,18},{3,19},{4,20},{5,21},{6,22},{7,23},{8,24},{9,... | collective-permute-start | bytes 1966088 | tf_op jit(solution)/shard_map/ppermute | solution.py:573
  423.7 31.8 %collective-permute-start.61 = (bf16[160,2048]{1,0:T(8,128)(2,1)}, bf16[160,2048]{1,0:T(8,128)(2,1)}, u32[]{:S(2)}, u32[]{:S(2)}) collective-permute-start(bf16[160,2048]{1,0:T(8,128)(2,1)} %get-tuple-element.426), channel_id=1, source_target_pairs={{0,17},{1,16},{2,19},{3,18},{4,21},{5,20},{6,23},{7,22},{8,25},{9,... | collective-permute-start | bytes 1966088 | tf_op jit(solution)/shard_map/ppermute | solution.py:573
  456.4 35.9 %collective-permute-start.68 = (bf16[320,4224]{1,0:T(8,128)(2,1)}, bf16[320,4224]{1,0:T(8,128)(2,1)S(1)}, u32[]{:S(2)}, u32[]{:S(2)}) collective-permute-start(bf16[320,4224]{1,0:T(8,128)(2,1)} %get-tuple-element.451), channel_id=1, source_target_pairs={{0,8},{1,9},{2,10},{3,11},{4,12},{5,13},{6,14},{7,15},{8,0},{9,1},... | collective-permute-start | bytes 8110088 | tf_op jit(solution)/shard_map/ppermute | solution.py:573
  458.7 33.6 %collective-permute-start.67 = (bf16[320,2048]{1,0:T(8,128)(2,1)}, bf16[320,2048]{1,0:T(8,128)(2,1)}, u32[]{:S(2)}, u32[]{:S(2)}) collective-permute-start(bf16[320,2048]{1,0:T(8,128)(2,1)} %pad_maximum_fusion.5), channel_id=1, source_target_pairs={{0,8},{1,9},{2,10},{3,11},{4,12},{5,13},{6,14},{7,15},{8,0},{9,1},... | collective-permute-start | bytes 3932168 | tf_op jit(solution)/shard_map/ppermute | solution.py:573
  492.3 35.5 %collective-permute-start.72 = (bf16[320,2048]{1,0:T(8,128)(2,1)}, bf16[320,2048]{1,0:T(8,128)(2,1)}, u32[]{:S(2)}, u32[]{:S(2)}) collective-permute-start(bf16[320,2048]{1,0:T(8,128)(2,1)} %pad_maximum_fusion.6), channel_id=1, source_target_pairs={{0,8},{1,9},{2,10},{3,11},{4,12},{5,13},{6,14},{7,15},{8,0},{9,1},... | collective-permute-start | bytes 3932168 | tf_op jit(solution)/shard_map/ppermute | solution.py:573
  492.4 35.4 %collective-permute-start.69 = (bf16[160,2048]{1,0:T(8,128)(2,1)}, bf16[160,2048]{1,0:T(8,128)(2,1)}, u32[]{:S(2)}, u32[]{:S(2)}) collective-permute-start(bf16[160,2048]{1,0:T(8,128)(2,1)} %get-tuple-element.459), channel_id=1, source_target_pairs={{0,1},{1,0},{2,3},{3,2},{4,5},{5,4},{6,7},{7,6},{8,9},{9,8},{10,11... | collective-permute-start | bytes 1966088 | tf_op jit(solution)/shard_map/ppermute | solution.py:573
  493.3 34.5 %collective-permute-start.70 = (bf16[160,2048]{1,0:T(8,128)(2,1)}, bf16[160,2048]{1,0:T(8,128)(2,1)}, u32[]{:S(2)}, u32[]{:S(2)}) collective-permute-start(bf16[160,2048]{1,0:T(8,128)(2,1)} %get-tuple-element.460), channel_id=1, source_target_pairs={{0,16},{1,17},{2,18},{3,19},{4,20},{5,21},{6,22},{7,23},{8,24},{9,... | collective-permute-start | bytes 1966088 | tf_op jit(solution)/shard_map/ppermute | solution.py:573
  494.6 33.2 %collective-permute-start.71 = (bf16[160,2048]{1,0:T(8,128)(2,1)}, bf16[160,2048]{1,0:T(8,128)(2,1)}, u32[]{:S(2)}, u32[]{:S(2)}) collective-permute-start(bf16[160,2048]{1,0:T(8,128)(2,1)} %get-tuple-element.461), channel_id=1, source_target_pairs={{0,17},{1,16},{2,19},{3,18},{4,21},{5,20},{6,23},{7,22},{8,25},{9,... | collective-permute-start | bytes 1966088 | tf_op jit(solution)/shard_map/ppermute | solution.py:573
  531.1 34.6 %collective-permute-start.76 = (bf16[320,2048]{1,0:T(8,128)(2,1)S(1)}, bf16[320,2048]{1,0:T(8,128)(2,1)}, u32[]{:S(2)}, u32[]{:S(2)}) collective-permute-start(bf16[320,2048]{1,0:T(8,128)(2,1)S(1)} %pad_maximum_fusion.7), channel_id=1, source_target_pairs={{0,8},{1,9},{2,10},{3,11},{4,12},{5,13},{6,14},{7,15},{8,0},{9,1},... | collective-permute-start | bytes 3932168 | tf_op jit(solution)/shard_map/ppermute | solution.py:573
  533.7 31.9 %collective-permute-start.75 = (bf16[160,2176]{1,0:T(8,128)(2,1)}, bf16[160,2176]{1,0:T(8,128)(2,1)}, u32[]{:S(2)}, u32[]{:S(2)}) collective-permute-start(bf16[160,2176]{1,0:T(8,128)(2,1)} %get-tuple-element.474), channel_id=1, source_target_pairs={{0,17},{1,16},{2,19},{3,18},{4,21},{5,20},{6,23},{7,22},{8,25},{9,... | collective-permute-start | bytes 2088968 | tf_op jit(solution)/shard_map/ppermute | solution.py:573
  565.7 35.2 %collective-permute-start.78 = (bf16[160,2176]{1,0:T(8,128)(2,1)}, bf16[160,2176]{1,0:T(8,128)(2,1)S(1)}, u32[]{:S(2)}, u32[]{:S(2)}) collective-permute-start(bf16[160,2176]{1,0:T(8,128)(2,1)} %get-tuple-element.492), channel_id=1, source_target_pairs={{0,1},{1,0},{2,3},{3,2},{4,5},{5,4},{6,7},{7,6},{8,9},{9,8},{10,11... | collective-permute-start | bytes 2088968 | tf_op jit(solution)/shard_map/ppermute | solution.py:573
  566.5 34.4 %collective-permute-start.79 = (bf16[160,2176]{1,0:T(8,128)(2,1)}, bf16[160,2176]{1,0:T(8,128)(2,1)S(1)}, u32[]{:S(2)}, u32[]{:S(2)}) collective-permute-start(bf16[160,2176]{1,0:T(8,128)(2,1)} %get-tuple-element.494), channel_id=1, source_target_pairs={{0,16},{1,17},{2,18},{3,19},{4,20},{5,21},{6,22},{7,23},{8,24},{9,... | collective-permute-start | bytes 2088968 | tf_op jit(solution)/shard_map/ppermute | solution.py:573
  567.7 33.2 %collective-permute-start.80 = (bf16[160,2176]{1,0:T(8,128)(2,1)}, bf16[160,2176]{1,0:T(8,128)(2,1)S(1)}, u32[]{:S(2)}, u32[]{:S(2)}) collective-permute-start(bf16[160,2176]{1,0:T(8,128)(2,1)} %get-tuple-element.496), channel_id=1, source_target_pairs={{0,17},{1,16},{2,19},{3,18},{4,21},{5,20},{6,23},{7,22},{8,25},{9,... | collective-permute-start | bytes 2088968 | tf_op jit(solution)/shard_map/ppermute | solution.py:573
  601.9 30.8 %collective-permute-start.83 = (bf16[160,2176]{1,0:T(8,128)(2,1)}, bf16[160,2176]{1,0:T(8,128)(2,1)S(1)}, u32[]{:S(2)}, u32[]{:S(2)}) collective-permute-start(bf16[160,2176]{1,0:T(8,128)(2,1)} %get-tuple-element.504), channel_id=1, source_target_pairs={{0,1},{1,0},{2,3},{3,2},{4,5},{5,4},{6,7},{7,6},{8,9},{9,8},{10,11... | collective-permute-start | bytes 2088968 | tf_op jit(solution)/shard_map/ppermute | solution.py:573
  603.7 32.6 %collective-permute-start.85 = (bf16[160,2176]{1,0:T(8,128)(2,1)}, bf16[160,2176]{1,0:T(8,128)(2,1)}, u32[]{:S(2)}, u32[]{:S(2)}) collective-permute-start(bf16[160,2176]{1,0:T(8,128)(2,1)} %get-tuple-element.508), channel_id=1, source_target_pairs={{0,17},{1,16},{2,19},{3,18},{4,21},{5,20},{6,23},{7,22},{8,25},{9,... | collective-permute-start | bytes 2088968 | tf_op jit(solution)/shard_map/ppermute | solution.py:573
  638.1 31.4 %collective-permute-start.90 = (bf16[160,2176]{1,0:T(8,128)(2,1)}, bf16[160,2176]{1,0:T(8,128)(2,1)S(1)}, u32[]{:S(2)}, u32[]{:S(2)}) collective-permute-start(bf16[160,2176]{1,0:T(8,128)(2,1)} %get-tuple-element.522), channel_id=1, source_target_pairs={{0,17},{1,16},{2,19},{3,18},{4,21},{5,20},{6,23},{7,22},{8,25},{9,... | collective-permute-start | bytes 2088968 | tf_op jit(solution)/shard_map/ppermute | solution.py:573
  639.8 54.2 %collective-permute-start.87 = (bf16[256,2176]{1,0:T(8,128)(2,1)S(1)}, bf16[256,2176]{1,0:T(8,128)(2,1)S(1)}, u32[]{:S(2)}, u32[]{:S(2)}) collective-permute-start(bf16[256,2176]{1,0:T(8,128)(2,1)S(1)} %copy-done.56), channel_id=1, source_target_pairs={{0,6},{1,7},{2,4},{3,5},{4,2},{5,3},{6,0},{7,1},{8,14},{9,15},{10,... | collective-permute-start | bytes 3342344 | tf_op jit(solution)/shard_map/ppermute | solution.py:573
  674.3 31.8 %collective-permute-start.91 = (bf16[256,2176]{1,0:T(8,128)(2,1)}, bf16[256,2176]{1,0:T(8,128)(2,1)S(1)}, u32[]{:S(2)}, u32[]{:S(2)}) collective-permute-start(bf16[256,2176]{1,0:T(8,128)(2,1)} %combine.11), channel_id=1, source_target_pairs={{0,2},{1,3},{2,0},{3,1},{4,6},{5,7},{6,4},{7,5},{8,10},{9,11},{10,... | collective-permute-start | bytes 3342344 | tf_op jit(solution)/shard_map/ppermute | solution.py:573
  710.4 41.3 %collective-permute-start.96 = (bf16[256,2048]{1,0:T(8,128)(2,1)}, bf16[256,2048]{1,0:T(8,128)(2,1)}, u32[]{:S(2)}, u32[]{:S(2)}) collective-permute-start(bf16[256,2048]{1,0:T(8,128)(2,1)} %combine.12), channel_id=1, source_target_pairs={{0,6},{1,7},{2,4},{3,5},{4,2},{5,3},{6,0},{7,1},{8,14},{9,15},{10,... | collective-permute-start | bytes 3145736 | tf_op jit(solution)/shard_map/ppermute | solution.py:573
  719.0 32.7 %collective-permute-start.95 = (bf16[256,2048]{1,0:T(8,128)(2,1)}, bf16[256,2048]{1,0:T(8,128)(2,1)}, u32[]{:S(2)}, u32[]{:S(2)}) collective-permute-start(bf16[256,2048]{1,0:T(8,128)(2,1)} %get-tuple-element.543), channel_id=1, source_target_pairs={{0,16},{1,17},{2,18},{3,19},{4,20},{5,21},{6,22},{7,23},{8,24},{9,... | collective-permute-start | bytes 3145736 | tf_op jit(solution)/shard_map/ppermute | solution.py:573
  720.3 31.3 %collective-permute-start.97 = (bf16[256,2048]{1,0:T(8,128)(2,1)}, bf16[256,2048]{1,0:T(8,128)(2,1)}, u32[]{:S(2)}, u32[]{:S(2)}) collective-permute-start(bf16[256,2048]{1,0:T(8,128)(2,1)} %get-tuple-element.543), channel_id=1, source_target_pairs={{0,8},{1,9},{2,10},{3,11},{4,12},{5,13},{6,14},{7,15},{8,0},{9,1},... | collective-permute-start | bytes 3145736 | tf_op jit(solution)/shard_map/ppermute | solution.py:573
  721.1 30.5 %collective-permute-start.99 = (bf16[160,2048]{1,0:T(8,128)(2,1)S(1)}, bf16[160,2048]{1,0:T(8,128)(2,1)}, u32[]{:S(2)}, u32[]{:S(2)}) collective-permute-start(bf16[160,2048]{1,0:T(8,128)(2,1)S(1)} %copy-done.118), channel_id=1, source_target_pairs={{0,1},{1,0},{2,3},{3,2},{4,5},{5,4},{6,7},{7,6},{8,9},{9,8},{10,11... | collective-permute-start | bytes 1966088 | tf_op jit(solution)/shard_map/ppermute | solution.py:573
  757.6 30.1 %collective-permute-start.101 = (bf16[160,2048]{1,0:T(8,128)(2,1)}, bf16[160,2048]{1,0:T(8,128)(2,1)S(1)}, u32[]{:S(2)}, u32[]{:S(2)}) collective-permute-start(bf16[160,2048]{1,0:T(8,128)(2,1)} %get-tuple-element.555), channel_id=1, source_target_pairs={{0,16},{1,17},{2,18},{3,19},{4,20},{5,21},{6,22},{7,23},{8,24},{9,... | collective-permute-start | bytes 1966088 | tf_op jit(solution)/shard_map/ppermute | solution.py:573
  758.4 31.3 %collective-permute-start.102 = (bf16[160,2048]{1,0:T(8,128)(2,1)}, bf16[160,2048]{1,0:T(8,128)(2,1)S(1)}, u32[]{:S(2)}, u32[]{:S(2)}) collective-permute-start(bf16[160,2048]{1,0:T(8,128)(2,1)} %get-tuple-element.557), channel_id=1, source_target_pairs={{0,17},{1,16},{2,19},{3,18},{4,21},{5,20},{6,23},{7,22},{8,25},{9,... | collective-permute-start | bytes 1966088 | tf_op jit(solution)/shard_map/ppermute | solution.py:573
  759.9 44.3 %collective-permute-start.104 = (bf16[160,2048]{1,0:T(8,128)(2,1)}, bf16[160,2048]{1,0:T(8,128)(2,1)}, u32[]{:S(2)}, u32[]{:S(2)}) collective-permute-start(bf16[160,2048]{1,0:T(8,128)(2,1)} %get-tuple-element.561), channel_id=1, source_target_pairs={{0,16},{1,17},{2,18},{3,19},{4,20},{5,21},{6,22},{7,23},{8,24},{9,... | collective-permute-start | bytes 1966088 | tf_op jit(solution)/shard_map/ppermute | solution.py:573
  760.7 43.5 %collective-permute-start.105 = (bf16[160,2048]{1,0:T(8,128)(2,1)}, bf16[160,2048]{1,0:T(8,128)(2,1)}, u32[]{:S(2)}, u32[]{:S(2)}) collective-permute-start(bf16[160,2048]{1,0:T(8,128)(2,1)} %get-tuple-element.563), channel_id=1, source_target_pairs={{0,1},{1,0},{2,3},{3,2},{4,5},{5,4},{6,7},{7,6},{8,9},{9,8},{10,11... | collective-permute-start | bytes 1966088 | tf_op jit(solution)/shard_map/ppermute | solution.py:573
  794.3 49.2 %collective-permute-start.103 = (bf16[256,2048]{1,0:T(8,128)(2,1)}, bf16[256,2048]{1,0:T(8,128)(2,1)}, u32[]{:S(2)}, u32[]{:S(2)}) collective-permute-start(bf16[256,2048]{1,0:T(8,128)(2,1)} %combine.13), channel_id=1, source_target_pairs={{0,4},{1,5},{2,6},{3,7},{4,0},{5,1},{6,2},{7,3},{8,12},{9,13},{10,... | collective-permute-start | bytes 3145736 | tf_op jit(solution)/shard_map/ppermute | solution.py:573
  804.2 38.6 %collective-permute-start.109 = (bf16[160,2048]{1,0:T(8,128)(2,1)}, bf16[160,2048]{1,0:T(8,128)(2,1)}, u32[]{:S(2)}, u32[]{:S(2)}) collective-permute-start(bf16[160,2048]{1,0:T(8,128)(2,1)} %get-tuple-element.568), channel_id=1, source_target_pairs={{0,16},{1,17},{2,18},{3,19},{4,20},{5,21},{6,22},{7,23},{8,24},{9,... | collective-permute-start | bytes 1966088 | tf_op jit(solution)/shard_map/ppermute | solution.py:573
  805.5 32.3 %collective-permute-start.106 = (bf16[132,2048]{1,0:T(8,128)(2,1)}, bf16[132,2048]{1,0:T(8,128)(2,1)}, u32[]{:S(2)}, u32[]{:S(2)}) collective-permute-start(bf16[132,2048]{1,0:T(8,128)(2,1)} %pad_maximum_fusion.10), channel_id=1, source_target_pairs={{0,1},{1,0},{2,3},{3,2},{4,5},{5,4},{6,7},{7,6},{8,9},{9,8},{10,11... | collective-permute-start | bytes 1622024 | tf_op jit(solution)/shard_map/ppermute | solution.py:573
  806.7 31.0 %collective-permute-start.107 = (bf16[132,2048]{1,0:T(8,128)(2,1)}, bf16[132,2048]{1,0:T(8,128)(2,1)}, u32[]{:S(2)}, u32[]{:S(2)}) collective-permute-start(bf16[132,2048]{1,0:T(8,128)(2,1)} %pad_maximum_fusion.11), channel_id=1, source_target_pairs={{0,1},{1,0},{2,3},{3,2},{4,5},{5,4},{6,7},{7,6},{8,9},{9,8},{10,11... | collective-permute-start | bytes 1622024 | tf_op jit(solution)/shard_map/ppermute | solution.py:573
  807.5 35.3 %collective-permute-start.108 = (bf16[132,2048]{1,0:T(8,128)(2,1)}, bf16[132,2048]{1,0:T(8,128)(2,1)}, u32[]{:S(2)}, u32[]{:S(2)}) collective-permute-start(bf16[132,2048]{1,0:T(8,128)(2,1)} %pad_maximum_fusion.12), channel_id=1, source_target_pairs={{0,1},{1,0},{2,3},{3,2},{4,5},{5,4},{6,7},{7,6},{8,9},{9,8},{10,11... | collective-permute-start | bytes 1622024 | tf_op jit(solution)/shard_map/ppermute | solution.py:573
  843.5 42.4 %collective-permute-start.110 = (bf16[160,2048]{1,0:T(8,128)(2,1)}, bf16[160,2048]{1,0:T(8,128)(2,1)}, u32[]{:S(2)}, u32[]{:S(2)}) collective-permute-start(bf16[160,2048]{1,0:T(8,128)(2,1)} %get-tuple-element.574), channel_id=1, source_target_pairs={{0,17},{1,16},{2,19},{3,18},{4,21},{5,20},{6,23},{7,22},{8,25},{9,... | collective-permute-start | bytes 1966088 | tf_op jit(solution)/shard_map/ppermute | solution.py:573
  845.5 40.5 %collective-permute-start.111 = (bf16[160,2048]{1,0:T(8,128)(2,1)S(1)}, bf16[160,2048]{1,0:T(8,128)(2,1)}, u32[]{:S(2)}, u32[]{:S(2)}) collective-permute-start(bf16[160,2048]{1,0:T(8,128)(2,1)S(1)} %copy-done.116), channel_id=1, source_target_pairs={{0,17},{1,16},{2,19},{3,18},{4,21},{5,20},{6,23},{7,22},{8,25},{9,... | collective-permute-start | bytes 1966088 | tf_op jit(solution)/shard_map/ppermute | solution.py:573
  846.5 39.4 %collective-permute-start.112 = (bf16[132,2048]{1,0:T(8,128)(2,1)S(1)}, bf16[132,2048]{1,0:T(8,128)(2,1)}, u32[]{:S(2)}, u32[]{:S(2)}) collective-permute-start(bf16[132,2048]{1,0:T(8,128)(2,1)S(1)} %copy-done.95), channel_id=1, source_target_pairs={{0,1},{1,0},{2,3},{3,2},{4,5},{5,4},{6,7},{7,6},{8,9},{9,8},{10,11... | collective-permute-start | bytes 1622024 | tf_op jit(solution)/shard_map/ppermute | solution.py:573
  848.8 37.1 %collective-permute-start.113 = (bf16[132,2048]{1,0:T(8,128)(2,1)S(1)}, bf16[132,2048]{1,0:T(8,128)(2,1)S(1)}, u32[]{:S(2)}, u32[]{:S(2)}) collective-permute-start(bf16[132,2048]{1,0:T(8,128)(2,1)S(1)} %fusion.10), channel_id=1, source_target_pairs={{0,6},{1,7},{2,4},{3,5},{4,2},{5,3},{6,0},{7,1},{8,14},{9,15},{10,... | collective-permute-start | bytes 1622024 | tf_op jit(solution)/shard_map/ppermute | solution.py:573
  888.1 31.2 %collective-permute-start.114 = (bf16[4,64,1280]{2,1,0:T(8,128)(2,1)}, bf16[4,64,1280]{2,1,0:T(8,128)(2,1)S(1)}, u32[]{:S(2)}, u32[]{:S(2)}) collective-permute-start(bf16[4,64,1280]{2,1,0:T(8,128)(2,1)} %get-tuple-element.584), channel_id=1, source_target_pairs={{0,1},{1,0},{2,3},{3,2},{4,5},{5,4},{6,7},{7,6},{8,9},{9,8},{10,11... | collective-permute-start | bytes 1966088 | tf_op jit(solution)/shard_map/ppermute | solution.py:573
  889.4 30.2 %collective-permute-start.115 = (bf16[4,64,1280]{2,1,0:T(8,128)(2,1)}, bf16[4,64,1280]{2,1,0:T(8,128)(2,1)S(1)}, u32[]{:S(2)}, u32[]{:S(2)}) collective-permute-start(bf16[4,64,1280]{2,1,0:T(8,128)(2,1)} %get-tuple-element.585), channel_id=1, source_target_pairs={{0,1},{1,0},{2,3},{3,2},{4,5},{5,4},{6,7},{7,6},{8,9},{9,8},{10,11... | collective-permute-start | bytes 1966088 | tf_op jit(solution)/shard_map/ppermute | solution.py:573
  920.4 41.4 %collective-permute-start.120 = (bf16[256,2048]{1,0:T(8,128)(2,1)}, bf16[256,2048]{1,0:T(8,128)(2,1)S(1)}, u32[]{:S(2)}, u32[]{:S(2)}) collective-permute-start(bf16[256,2048]{1,0:T(8,128)(2,1)} %combine.15), channel_id=1, source_target_pairs={{0,2},{1,3},{2,0},{3,1},{4,6},{5,7},{6,4},{7,5},{8,10},{9,11},{10,... | collective-permute-start | bytes 3145736 | tf_op jit(solution)/shard_map/ppermute | solution.py:573
  927.9 33.9 %collective-permute-start.124 = (bf16[4,64,1280]{2,1,0:T(8,128)(2,1)}, bf16[4,64,1280]{2,1,0:T(8,128)(2,1)}, u32[]{:S(2)}, u32[]{:S(2)}) collective-permute-start(bf16[4,64,1280]{2,1,0:T(8,128)(2,1)} %fusion.9), channel_id=1, source_target_pairs={{0,6},{1,7},{2,4},{3,5},{4,2},{5,3},{6,0},{7,1},{8,14},{9,15},{10,... | collective-permute-start | bytes 1966088 | tf_op jit(solution)/shard_map/ppermute | solution.py:573
  967.8 30.6 %collective-permute-start.128 = (bf16[4,64,1280]{2,1,0:T(8,128)(2,1)S(1)}, bf16[4,64,1280]{2,1,0:T(8,128)(2,1)S(1)}, u32[]{:S(2)}, u32[]{:S(2)}) collective-permute-start(bf16[4,64,1280]{2,1,0:T(8,128)(2,1)S(1)} %get-tuple-element.609), channel_id=1, source_target_pairs={{0,4},{1,5},{2,6},{3,7},{4,0},{5,1},{6,2},{7,3},{8,12},{9,13},{10,... | collective-permute-start | bytes 1966088 | tf_op jit(solution)/shard_map/ppermute | solution.py:573
  967.8 30.7 %collective-permute-start.129 = (bf16[4,64,1280]{2,1,0:T(8,128)(2,1)S(1)}, bf16[4,64,1280]{2,1,0:T(8,128)(2,1)S(1)}, u32[]{:S(2)}, u32[]{:S(2)}) collective-permute-start(bf16[4,64,1280]{2,1,0:T(8,128)(2,1)S(1)} %get-tuple-element.611), channel_id=1, source_target_pairs={{0,2},{1,3},{2,0},{3,1},{4,6},{5,7},{6,4},{7,5},{8,10},{9,11},{10,... | collective-permute-start | bytes 1966088 | tf_op jit(solution)/shard_map/ppermute | solution.py:573
  (194 other events, 3153.7 us)

commit v4 on v3

--- a/solution.py
+++ b/solution.py
@@ -418,6 +418,30 @@
     )(own, routes, upto)
 
 
+def join_kernel(at, *refs):
+    pieces, out = refs[:-1], refs[-1]
+    for i, piece in enumerate(pieces):
+
+        @pl.when((at[0] ^ pl.program_id(0)) == i)
+        def _(piece=piece):
+            out[...] = piece[...]
+
+
+def join(pieces, at):
+    deep, width = pieces[0].shape
+    return pl.pallas_call(
+        join_kernel,
+        grid=(len(pieces),),
+        in_specs=[pl.BlockSpec(memory_space=pltpu.SMEM)]
+        + [pl.BlockSpec((deep, width), lambda i: (0, 0))] * len(pieces),
+        out_specs=pl.BlockSpec((deep, width), lambda i: (i, 0)),
+        out_shape=jax.ShapeDtypeStruct((len(pieces) * deep, width), pieces[0].dtype),
+        compiler_params=pltpu.CompilerParams(vmem_limit_bytes=VMEM_MOST),
+        cost_estimate=LIGHT,
+        name="join",
+    )(at, *pieces)
+
+
 def product_kernel(kind, dtype, a, b, *rest):
     out = rest[-1]
     dims = {"nn": ((1,), (0,)), "nt": ((1,), (1,)), "tn": ((0,), (0,))}[kind]
@@ -742,7 +766,7 @@
     cos_full = jnp.concatenate([cosine, cosine], axis=1)
     sin_full = jnp.concatenate([-sine, sine], axis=1)
     q_gain_row, k_gain_row = q_gain[None, :], key_norm_gain[None, :]
-    h_full = place(h_pieces, lambda i: at_ctx ^ i)
+    h_full = join(h_pieces, at_ctx[None])
     flat_routes = now(jnp.concatenate(there))
     plane_routes = [flat_routes] + [swap(flat_routes, b & ~1, b & 1) for b in range(1, nb)]
     tick()
@@ -910,11 +934,11 @@
     tick()
     low_pieces[3] = swap(low_pieces[2], 1, 0)
     post(outs, made, 2, 2, 3, rounds=2)
-    post(outs, made, 1, 2, rounds=2)
+    post(outs, made, 1, 3, rounds=2)
     post(outs, made, 0, 1, rounds=2)
     tick()
 
-    branch_full = now(place(low_pieces, lambda i: at_ctx ^ i))
+    branch_full = now(join(low_pieces, at_ctx[None]))
     o_own = q_cols // nep
     own_width = width // devices
     o_part = product(attn, branch_full, "tn", F32, 256)
@@ -937,15 +961,14 @@
     tick()
 
     o_near = {j: swap(o_sent[j], 0, 1) for j in last_steps[:-1]}
-    post(outs, made, 0, 2)
+    post(outs, made, 1, 2)
     grad_qkv, q_gain_part, k_gain_part = attend_back(
         qkv, turned_q, turned_k, attn, lse, now(grad_attn), cos_full, sin_full, q_gain_row, k_gain_row, heads
     )
     did(grad_qkv)
     tick()
 
-    post(outs, made, 1, 3)
-    post(outs, made, 0, 3)
+    post(outs, made, 0, 2, 3)
     o_near[0] = swap(o_sent[0], 0, 1)
     o_far = {}
     o_mid = {j: (o_term(j, 0) + now(o_near[j]).astype(F32)).astype(BF16) for j in last_steps[:-1]}

time: 1030 us -> 1020 us (level)
  local copies, waits for them, and re-layouts: 88.9 us -> 73.7 us
    dynamic_update_slice x28 -> x21, local copies, waits for them, and re-layouts: 24.7 us -> 10 us  [place(): whole = lax.dynamic_update_slice_in_dim(whole, piece, at(i) * size, axis)]
    unnamed x242 -> x248, local copies, waits for them, and re-layouts: 23.9 us -> 23.9 us
  transfers between devices with their start and end apart: 135 -> 135, of which waited for: 54 -> 52; matrix products, arithmetic and copies ran while one was open for 12% -> 10% of each run, Pallas kernels for 33% -> 34%
where the time goes in v4:
time: 1020 us; the launch traced here: 1010 us
  waiting for transfers between devices  374 us (37%)
  Pallas kernels  350 us (34%)
  starting transfers between devices  146 us (14%)
  local copies, waits for them, and re-layouts  73.7 us (7%)
  other arithmetic  41.2 us (4%)
  matrix products  23.5 us (2%)
    ppermute x135, waiting for transfers between devices, swap(): got = lax.ppermute(now(v) if rounds else v, AXES, pairs)  374 us
    ppermute x135, starting transfers between devices, swap(): got = lax.ppermute(now(v) if rounds else v, AXES, pairs)  146 us
    pallas_call x4, Pallas kernels, expert_step(): pl.pallas_call(lambda *refs: expert_kernel(chips, ff_tiles, len(args), *r...  107 us
    pallas_call x10, Pallas kernels, product(): pl.pallas_call(lambda *refs: product_kernel(kind, dtype, *refs), grid=((m...  87.8 us
    pallas_call x8, Pallas kernels, combine(): pl.pallas_call(lambda *refs: combine_kernel(len(pieces), *refs), out_shap...  31.9 us
    pallas_call x8, Pallas kernels, select(): pl.pallas_call(lambda *refs: select_kernel(len(parts), *refs), out_shape=...  28.6 us
    unnamed x248, local copies, waits for them, and re-layouts  23.9 us
    pallas_call x1, Pallas kernels, attend_back(): pl.pallas_call(attend_back_kernel, grid=(heads + 2,), in_specs=[moving, m...  23.6 us
  transfers between devices with their start and end apart: 135, of which 52 were waited for; matrix products, arithmetic and copies ran while one was open for 10% of the time, Pallas kernels for 34%

profile of v4, /device:TPU:0, one launch (start us, length us, event | category | flops | bytes accessed | tf_op | source)
XLA Modules:
  0.0 1011.3 jit_solution(17207565094776614875)
XLA Ops:
  15.7 15.3 %collective-permute-done.4 = s32[8,256]{1,0:T(8,128)S(1)} collective-permute-done((s32[8,256]{1,0:T(8,128)}, s32[8,256]{1,0:T(8,128)S(1)}, u32[]{:S(2)}, u32[]{:S(2)}) %collective-permute-start.4) | collective-permute-done | bytes 8224 | tf_op jit(solution)/shard_map/ppermute | solution.py:597
  43.6 20.4 %collective-permute-done.10 = s32[8,256]{1,0:T(8,128)S(1)} collective-permute-done((s32[8,256]{1,0:T(8,128)S(1)}, s32[8,256]{1,0:T(8,128)S(1)}, u32[]{:S(2)}, u32[]{:S(2)}) %collective-permute-start.10) | collective-permute-done | bytes 8224 | tf_op jit(solution)/shard_map/ppermute | solution.py:597
  73.9 5.3 collective-permute-done.13
  88.8 10.4 %collective-permute-done.11 = bf16[256,1280]{1,0:T(8,128)(2,1)S(1)} collective-permute-done((bf16[256,1280]{1,0:T(8,128)(2,1)}, bf16[256,1280]{1,0:T(8,128)(2,1)S(1)}, u32[]{:S(2)}, u32[]{:S(2)}) %collective-permute-start.11) | collective-permute-done | bytes 655392 | tf_op jit(solution)/shard_map/ppermute | solution.py:597
  107.2 9.7 collective-permute-done.16
  120.4 13.7 %collective-permute-done.18 = bf16[256,1280]{1,0:T(8,128)(2,1)S(1)} collective-permute-done((bf16[256,1280]{1,0:T(8,128)(2,1)S(1)}, bf16[256,1280]{1,0:T(8,128)(2,1)S(1)}, u32[]{:S(2)}, u32[]{:S(2)}) %collective-permute-start.18) | collective-permute-done | bytes 655392 | tf_op jit(solution)/shard_map/ppermute | solution.py:597
  144.5 4.9 join.2.refs_0_
  153.1 7.7 collective-permute-done.21.refs_1_
  167.5 5.6 fusion.55.q_ref.k_ref.v_ref
  173.2 17.5 %attend.1 = (bf16[1024,1024]{1,0:T(8,128)(2,1)S(1)}, bf16[1024,1024]{1,0:T(8,128)(2,1)S(1)}, bf16[1024,128]{1,0:T(8,128)(2,1)S(1)}, f32[8,1,1024]{2,1,0:T(1,128)S(1)}) custom-call(f32[1024,1280]{1,0:T(8,128)S(1)} %fusion.55.q_ref.k_ref.v_ref, f32[1024,1280]{1,0:T(8,128)S(1)} %fusion.55.q_ref.k_ref.v_ref, f32[1024,1280]{1,0:T(8,128)S(1)} %fusion.55.q_ref.k_ref.v_ref, ...), custom_call_target="tpu_custom_call" | custom-call | flops 1 | bytes 1 | tf_op jit(solution)/shard_map/attend/pallas_call | solution.py:171
  198.8 4.6 convolution_convert_fusion.1
  215.2 5.1 convolution_add_fusion.1.held
  220.3 4.6 collective-permute-done.32.refs_1_
  225.0 7.9 collective-permute-done.31.arrived
  239.0 4.1 second_norm.1
  251.5 11.4 %collective-permute-done.34.refs_7_ = bf16[160,2048]{1,0:T(8,128)(2,1)S(1)} collective-permute-done((bf16[160,2048]{1,0:T(8,128)(2,1)}, bf16[160,2048]{1,0:T(8,128)(2,1)S(1)}, u32[]{:S(2)}, u32[]{:S(2)}) %collective-permute-start.34) | collective-permute-done | bytes 655392 | tf_op jit(solution)/shard_map/ppermute | solution.py:597
  264.1 18.9 %collective-permute-done.37.refs_1_ = bf16[256,1024]{1,0:T(8,128)(2,1)S(1)} collective-permute-done((bf16[256,1024]{1,0:T(8,128)(2,1)S(1)}, bf16[256,1024]{1,0:T(8,128)(2,1)S(1)}, u32[]{:S(2)}, u32[]{:S(2)}) %collective-permute-start.37) | collective-permute-done | bytes 524320 | tf_op jit(solution)/shard_map/ppermute | solution.py:597
  291.0 11.6 %collective-permute-done.40.refs_3_ = bf16[160,2048]{1,0:T(8,128)(2,1)S(1)} collective-permute-done((bf16[160,2048]{1,0:T(8,128)(2,1)}, bf16[160,2048]{1,0:T(8,128)(2,1)S(1)}, u32[]{:S(2)}, u32[]{:S(2)}) %collective-permute-start.40) | collective-permute-done | bytes 655392 | tf_op jit(solution)/shard_map/ppermute | solution.py:597
  302.6 13.0 %collective-permute-done.39.refs_2_ = bf16[160,2048]{1,0:T(8,128)(2,1)S(1)} collective-permute-done((bf16[160,2048]{1,0:T(8,128)(2,1)}, bf16[160,2048]{1,0:T(8,128)(2,1)S(1)}, u32[]{:S(2)}, u32[]{:S(2)}) %collective-permute-start.39) | collective-permute-done | bytes 655392 | tf_op jit(solution)/shard_map/ppermute | solution.py:597
  334.0 6.3 picks.1.refs_17_
  344.3 5.2 collective-permute-done.44.refs_7_
  358.4 26.7 %expert.4 = (bf16[320,4224]{1,0:T(8,128)(2,1)}, bf16[320,4224]{1,0:T(8,128)(2,1)}, bf16[2560,2048]{1,0:T(8,128)(2,1)}, bf16[2560,2048]{1,0:T(8,128)(2,1)}, bf16[...) custom-call(bf16[160,2048]{1,0:T(8,128)(2,1)} %get-tuple-element.402.refs_0_, ...), custom_call_target="tpu_custom_call" | custom-call | flops 1 | bytes 1 | tf_op jit(solution)/shard_map/expert/pallas_call | solution.py:377
  395.5 12.8 %collective-permute-done.55.refs_8_ = bf16[160,2048]{1,0:T(8,128)(2,1)S(1)} collective-permute-done((bf16[160,2048]{1,0:T(8,128)(2,1)}, bf16[160,2048]{1,0:T(8,128)(2,1)S(1)}, u32[]{:S(2)}, u32[]{:S(2)}) %collective-permute-start.55) | collective-permute-done | bytes 655392 | tf_op jit(solution)/shard_map/ppermute | solution.py:597
  408.3 12.6 %collective-permute-done.54.refs_7_ = bf16[160,2048]{1,0:T(8,128)(2,1)} collective-permute-done((bf16[160,2048]{1,0:T(8,128)(2,1)}, bf16[160,2048]{1,0:T(8,128)(2,1)}, u32[]{:S(2)}, u32[]{:S(2)}) %collective-permute-start.54) | collective-permute-done | bytes 655392 | tf_op jit(solution)/shard_map/ppermute | solution.py:597
  432.0 26.7 %expert.5 = (bf16[320,4224]{1,0:T(8,128)(2,1)}, bf16[320,4224]{1,0:T(8,128)(2,1)}, bf16[2560,2048]{1,0:T(8,128)(2,1)}, bf16[2560,2048]{1,0:T(8,128)(2,1)}, bf16[...) custom-call(bf16[160,2048]{1,0:T(8,128)(2,1)} %get-tuple-element.432, ...), custom_call_target="tpu_custom_call", output_to_operand_aliasing={{2}: (19, {}), {3}: (20, {}), {4}: (21, {}), {5}: (22, {}),... | custom-call | flops 1 | bytes 1 | tf_op jit(solution)/shard_map/expert/pallas_call | solution.py:377
  469.4 5.0 pack.4
  474.4 6.7 collective-permute-done.66.refs_8_
  481.1 13.0 %collective-permute-done.65.refs_7_ = bf16[160,2048]{1,0:T(8,128)(2,1)S(1)} collective-permute-done((bf16[160,2048]{1,0:T(8,128)(2,1)}, bf16[160,2048]{1,0:T(8,128)(2,1)S(1)}, u32[]{:S(2)}, u32[]{:S(2)}) %collective-permute-start.65) | collective-permute-done | bytes 655392 | tf_op jit(solution)/shard_map/ppermute | solution.py:597
  499.3 5.0 pack.5
  504.3 26.6 %expert.6 = (bf16[320,4224]{1,0:T(8,128)(2,1)}, bf16[320,4224]{1,0:T(8,128)(2,1)}, bf16[2560,2048]{1,0:T(8,128)(2,1)}, bf16[2560,2048]{1,0:T(8,128)(2,1)}, bf16[...) custom-call(bf16[160,2048]{1,0:T(8,128)(2,1)} %get-tuple-element.457, ...), custom_call_target="tpu_custom_call", output_to_operand_aliasing={{2}: (19, {}), {3}: (20, {}), {4}: (21, {}), {5}: (22, {}),... | custom-call | flops 1 | bytes 1 | tf_op jit(solution)/shard_map/expert/pallas_call | solution.py:377
  539.8 5.0 pack.6
  544.8 7.8 collective-permute-done.74.refs_2_
  554.8 14.0 %collective-permute-done.76.refs_4_ = bf16[160,2176]{1,0:T(8,128)(2,1)} collective-permute-done((bf16[160,2176]{1,0:T(8,128)(2,1)}, bf16[160,2176]{1,0:T(8,128)(2,1)}, u32[]{:S(2)}, u32[]{:S(2)}) %collective-permute-start.76) | collective-permute-done | bytes 696352 | tf_op jit(solution)/shard_map/ppermute | solution.py:597
  576.3 27.0 %expert.7 = (bf16[320,4224]{1,0:T(8,128)(2,1)}, bf16[320,4224]{1,0:T(8,128)(2,1)}, bf16[2560,2048]{1,0:T(8,128)(2,1)}, bf16[2560,2048]{1,0:T(8,128)(2,1)}, bf16[...) custom-call(bf16[160,2048]{1,0:T(8,128)(2,1)} %get-tuple-element.491, ...), custom_call_target="tpu_custom_call", output_to_operand_aliasing={{2}: (19, {}), {3}: (20, {}), {4}: (21, {}), {5}: (22, {}),... | custom-call | flops 1 | bytes 1 | tf_op jit(solution)/shard_map/expert/pallas_call | solution.py:377
  610.6 13.1 %product.10 = f32[2048,768]{1,0:T(8,128)} custom-call(bf16[2560,2048]{1,0:T(8,128)(2,1)} %get-tuple-element.509.refs_0_, bf16[2560,768]{1,0:T(8,128)(2,1)} %get-tuple-element.511.refs_1_), custom_call_target="tpu_custom_call" | custom-call | flops 1 | bytes 1 | tf_op jit(solution)/shard_map/product/pallas_call | solution.py:468
  629.2 5.0 pack.7
  644.7 13.3 %product.11 = f32[2048,768]{1,0:T(8,128)} custom-call(bf16[2560,2048]{1,0:T(8,128)(2,1)} %get-tuple-element.509.refs_0_, bf16[2560,768]{1,0:T(8,128)(2,1)} %get-tuple-element.521.refs_1_), custom_call_target="tpu_custom_call" | custom-call | flops 1 | bytes 1 | tf_op jit(solution)/shard_map/product/pallas_call | solution.py:468
  658.0 4.3 combine.10.refs_0_
  662.4 9.6 collective-permute-done.90.refs_4_
  682.0 14.5 %product.12 = f32[768,2048]{1,0:T(8,128)} custom-call(bf16[2560,768]{1,0:T(8,128)(2,1)} %get-tuple-element.531.refs_0_, bf16[2560,2048]{1,0:T(8,128)(2,1)} %get-tuple-element.532.refs_1_), custom_call_target="tpu_custom_call" | custom-call | flops 1 | bytes 1 | tf_op jit(solution)/shard_map/product/pallas_call | solution.py:468
  697.6 11.0 %collective-permute-done.94.refs_4_ = bf16[160,2048]{1,0:T(8,128)(2,1)} collective-permute-done((bf16[160,2048]{1,0:T(8,128)(2,1)}, bf16[160,2048]{1,0:T(8,128)(2,1)}, u32[]{:S(2)}, u32[]{:S(2)}) %collective-permute-start.94) | collective-permute-done | bytes 655392 | tf_op jit(solution)/shard_map/ppermute | solution.py:597
  708.6 4.2 combine.12
  715.3 6.7 second_back.1
  725.3 15.8 %collective-permute-done.98.refs_2_ = bf16[160,2048]{1,0:T(8,128)(2,1)S(1)} collective-permute-done((bf16[160,2048]{1,0:T(8,128)(2,1)}, bf16[160,2048]{1,0:T(8,128)(2,1)S(1)}, u32[]{:S(2)}, u32[]{:S(2)}) %collective-permute-start.98) | collective-permute-done | bytes 655392 | tf_op jit(solution)/shard_map/ppermute | solution.py:597
  741.0 13.3 %collective-permute-done.99.refs_2_ = bf16[160,2048]{1,0:T(8,128)(2,1)S(1)} collective-permute-done((bf16[160,2048]{1,0:T(8,128)(2,1)}, bf16[160,2048]{1,0:T(8,128)(2,1)S(1)}, u32[]{:S(2)}, u32[]{:S(2)}) %collective-permute-start.99) | collective-permute-done | bytes 655392 | tf_op jit(solution)/shard_map/ppermute | solution.py:597
  766.4 4.7 join.3.refs_0_.refs_1_
  771.0 8.5 product.13.do_ref
  779.6 9.3 product.14
  792.7 4.5 collective-permute-start.103
  803.2 6.7 collective-permute-done.105.refs_2_
  818.4 23.6 %attend_back.1 = (bf16[1024,1280]{1,0:T(8,128)(2,1)S(1)}, f32[1,128]{1,0:T(1,128)S(1)}, f32[1,128]{1,0:T(1,128)S(1)}) custom-call(bf16[1024,1024]{1,0:T(8,128)(2,1)S(1)} %copy-done.8, f32[1024,1280]{1,0:T(8,128)} %copy-done.2, bf16[1024,1024]{1,0:T(8,128)(2,1)S(1)} %copy-done.6, bf16[1024,1024]{1,0:T(8,128)(2,1)S(1)} %copy-done.5, ...), custom_call_target="tpu_custom_call" | custom-call | flops 1 | bytes 1 | tf_op jit(solution)/shard_map/attend_back/pallas_call | solution.py:195
  843.3 5.0 collective-permute-done.108
  855.7 4.4 product.16
  860.2 4.4 product.17
  864.6 10.5 %product.15 = f32[2048,1280]{1,0:T(8,128)} custom-call(bf16[1024,2048]{1,0:T(8,128)(2,1)} %join.2.refs_0_, bf16[1024,1280]{1,0:T(8,128)(2,1)} %copy-done.3), custom_call_target="tpu_custom_call" | custom-call | flops 1 | bytes 1 | tf_op jit(solution)/shard_map/product/pallas_call | solution.py:468
  875.1 4.1 fusion.20
  892.0 4.2 combine.14
  896.2 4.8 product.18.held
  902.0 4.9 product.19
  906.8 5.8 collective-permute-done.118
  927.9 13.9 %collective-permute-done.121.arrived = bf16[256,2048]{1,0:T(8,128)(2,1)S(1)} collective-permute-done((bf16[256,2048]{1,0:T(8,128)(2,1)}, bf16[256,2048]{1,0:T(8,128)(2,1)S(1)}, u32[]{:S(2)}, u32[]{:S(2)}) %collective-permute-start.121) | collective-permute-done | bytes 1048608 | tf_op jit(solution)/shard_map/ppermute | solution.py:597
  942.8 4.4 first_back.1
  948.4 7.1 collective-permute-done.124
  969.3 24.2 %collective-permute-done.128 = bf16[4,64,1280]{2,1,0:T(8,128)(2,1)S(1)} collective-permute-done((bf16[4,64,1280]{2,1,0:T(8,128)(2,1)S(1)}, bf16[4,64,1280]{2,1,0:T(8,128)(2,1)S(1)}, u32[]{:S(2)}, u32[]{:S(2)}) %collective-permute-start.128) | collective-permute-done | bytes 655392 | tf_op jit(solution)/shard_map/ppermute | solution.py:597
  (671 shorter events, 350.9 us)
Async XLA Ops:
  70.3 31.1 %collective-permute-start.12 = (bf16[256,1280]{1,0:T(8,128)(2,1)}, bf16[256,1280]{1,0:T(8,128)(2,1)S(1)}, u32[]{:S(2)}, u32[]{:S(2)}) collective-permute-start(bf16[256,1280]{1,0:T(8,128)(2,1)} %copy-done.76), channel_id=1, source_target_pairs={{0,4},{1,5},{2,6},{3,7},{4,0},{5,1},{6,2},{7,3},{8,12},{9,13},{10,... | collective-permute-start | bytes 1966088 | tf_op jit(solution)/shard_map/ppermute | solution.py:597
  102.9 31.2 %collective-permute-start.15 = (bf16[256,2048]{1,0:T(8,128)(2,1)}, bf16[256,2048]{1,0:T(8,128)(2,1)S(1)}, u32[]{:S(2)}, u32[]{:S(2)}) collective-permute-start(bf16[256,2048]{1,0:T(8,128)(2,1)} %collective-permute-done.6.refs_2_), channel_id=1, source_target_pairs={{0,8},{1,9},{2,10},{3,11},{4,12},{5,13},{6,14},{7,15},{8,0},{9,1},... | collective-permute-start | bytes 3145736 | tf_op jit(solution)/shard_map/ppermute | solution.py:597
  103.4 30.7 %collective-permute-start.18 = (bf16[256,1280]{1,0:T(8,128)(2,1)S(1)}, bf16[256,1280]{1,0:T(8,128)(2,1)S(1)}, u32[]{:S(2)}, u32[]{:S(2)}) collective-permute-start(bf16[256,1280]{1,0:T(8,128)(2,1)S(1)} %collective-permute-done.12), channel_id=1, source_target_pairs={{0,1},{1,0},{2,3},{3,2},{4,5},{5,4},{6,7},{7,6},{8,9},{9,8},{10,11... | collective-permute-start | bytes 1966088 | tf_op jit(solution)/shard_map/ppermute | solution.py:597
  160.8 29.9 %collective-permute-start.25 = (bf16[1024,512]{1,0:T(8,128)(2,1)S(1)}, bf16[1024,512]{1,0:T(8,128)(2,1)S(1)}, u32[]{:S(2)}, u32[]{:S(2)}) collective-permute-start(bf16[1024,512]{1,0:T(8,128)(2,1)S(1)} %bitcast.228), channel_id=1, source_target_pairs={{0,24},{1,25},{2,26},{3,27},{4,28},{5,29},{6,30},{7,31},{8,16},{9,... | collective-permute-start | bytes 3145736 | tf_op jit(solution)/shard_map/ppermute | solution.py:597
  161.8 30.5 %collective-permute-start.26 = (bf16[1024,512]{1,0:T(8,128)(2,1)S(1)}, bf16[1024,512]{1,0:T(8,128)(2,1)S(1)}, u32[]{:S(2)}, u32[]{:S(2)}) collective-permute-start(bf16[1024,512]{1,0:T(8,128)(2,1)S(1)} %bitcast.227), channel_id=1, source_target_pairs={{0,8},{1,9},{2,10},{3,11},{4,12},{5,13},{6,14},{7,15},{8,0},{9,1},... | collective-permute-start | bytes 3145736 | tf_op jit(solution)/shard_map/ppermute | solution.py:597
  237.5 45.5 %collective-permute-start.36 = (bf16[160,2048]{1,0:T(8,128)(2,1)}, bf16[160,2048]{1,0:T(8,128)(2,1)S(1)}, u32[]{:S(2)}, u32[]{:S(2)}) collective-permute-start(bf16[160,2048]{1,0:T(8,128)(2,1)} %get-tuple-element.370), channel_id=1, source_target_pairs={{0,1},{1,0},{2,3},{3,2},{4,5},{5,4},{6,7},{7,6},{8,9},{9,8},{10,11... | collective-permute-start | bytes 1966088 | tf_op jit(solution)/shard_map/ppermute | solution.py:597
  245.2 37.8 %collective-permute-start.37 = (bf16[256,1024]{1,0:T(8,128)(2,1)S(1)}, bf16[256,1024]{1,0:T(8,128)(2,1)S(1)}, u32[]{:S(2)}, u32[]{:S(2)}) collective-permute-start(bf16[256,1024]{1,0:T(8,128)(2,1)S(1)} %get-tuple-element.391), channel_id=1, source_target_pairs={{0,4},{1,5},{2,6},{3,7},{4,0},{5,1},{6,2},{7,3},{8,12},{9,13},{10,... | collective-permute-start | bytes 1572872 | tf_op jit(solution)/shard_map/ppermute | solution.py:597
  283.0 34.0 %collective-permute-start.41 = (bf16[320,2048]{1,0:T(8,128)(2,1)}, bf16[320,2048]{1,0:T(8,128)(2,1)}, u32[]{:S(2)}, u32[]{:S(2)}) collective-permute-start(bf16[320,2048]{1,0:T(8,128)(2,1)} %pad_maximum_fusion), channel_id=1, source_target_pairs={{0,8},{1,9},{2,10},{3,11},{4,12},{5,13},{6,14},{7,15},{8,0},{9,1},... | collective-permute-start | bytes 3932168 | tf_op jit(solution)/shard_map/ppermute | solution.py:597
  285.7 29.9 %collective-permute-start.39 = (bf16[160,2048]{1,0:T(8,128)(2,1)}, bf16[160,2048]{1,0:T(8,128)(2,1)S(1)}, u32[]{:S(2)}, u32[]{:S(2)}) collective-permute-start(bf16[160,2048]{1,0:T(8,128)(2,1)} %get-tuple-element.375), channel_id=1, source_target_pairs={{0,16},{1,17},{2,18},{3,19},{4,20},{5,21},{6,22},{7,23},{8,24},{9,... | collective-permute-start | bytes 1966088 | tf_op jit(solution)/shard_map/ppermute | solution.py:597
  317.1 34.5 %collective-permute-start.48 = (bf16[320,2048]{1,0:T(8,128)(2,1)}, bf16[320,2048]{1,0:T(8,128)(2,1)}, u32[]{:S(2)}, u32[]{:S(2)}) collective-permute-start(bf16[320,2048]{1,0:T(8,128)(2,1)} %pad_maximum_fusion.1), channel_id=1, source_target_pairs={{0,8},{1,9},{2,10},{3,11},{4,12},{5,13},{6,14},{7,15},{8,0},{9,1},... | collective-permute-start | bytes 3932168 | tf_op jit(solution)/shard_map/ppermute | solution.py:597
  319.0 30.4 %collective-permute-start.44 = (bf16[160,2048]{1,0:T(8,128)(2,1)}, bf16[160,2048]{1,0:T(8,128)(2,1)}, u32[]{:S(2)}, u32[]{:S(2)}) collective-permute-start(bf16[160,2048]{1,0:T(8,128)(2,1)} %get-tuple-element.388), channel_id=1, source_target_pairs={{0,16},{1,17},{2,18},{3,19},{4,20},{5,21},{6,22},{7,23},{8,24},{9,... | collective-permute-start | bytes 1966088 | tf_op jit(solution)/shard_map/ppermute | solution.py:597
  320.1 31.5 %collective-permute-start.46 = (bf16[160,2048]{1,0:T(8,128)(2,1)}, bf16[160,2048]{1,0:T(8,128)(2,1)S(1)}, u32[]{:S(2)}, u32[]{:S(2)}) collective-permute-start(bf16[160,2048]{1,0:T(8,128)(2,1)} %get-tuple-element.390), channel_id=1, source_target_pairs={{0,1},{1,0},{2,3},{3,2},{4,5},{5,4},{6,7},{7,6},{8,9},{9,8},{10,11... | collective-permute-start | bytes 1966088 | tf_op jit(solution)/shard_map/ppermute | solution.py:597
  321.5 30.1 %collective-permute-start.47 = (bf16[256,1024]{1,0:T(8,128)(2,1)}, bf16[256,1024]{1,0:T(8,128)(2,1)}, u32[]{:S(2)}, u32[]{:S(2)}) collective-permute-start(bf16[256,1024]{1,0:T(8,128)(2,1)} %copy-done.107), channel_id=1, source_target_pairs={{0,6},{1,7},{2,4},{3,5},{4,2},{5,3},{6,0},{7,1},{8,14},{9,15},{10,... | collective-permute-start | bytes 1572872 | tf_op jit(solution)/shard_map/ppermute | solution.py:597
  351.6 33.5 %collective-permute-start.52 = (bf16[320,2048]{1,0:T(8,128)(2,1)}, bf16[320,2048]{1,0:T(8,128)(2,1)}, u32[]{:S(2)}, u32[]{:S(2)}) collective-permute-start(bf16[320,2048]{1,0:T(8,128)(2,1)} %pad_maximum_fusion.2), channel_id=1, source_target_pairs={{0,8},{1,9},{2,10},{3,11},{4,12},{5,13},{6,14},{7,15},{8,0},{9,1},... | collective-permute-start | bytes 3932168 | tf_op jit(solution)/shard_map/ppermute | solution.py:597
  351.7 33.4 %collective-permute-start.49 = (bf16[160,2048]{1,0:T(8,128)(2,1)}, bf16[160,2048]{1,0:T(8,128)(2,1)S(1)}, u32[]{:S(2)}, u32[]{:S(2)}) collective-permute-start(bf16[160,2048]{1,0:T(8,128)(2,1)} %get-tuple-element.404), channel_id=1, source_target_pairs={{0,1},{1,0},{2,3},{3,2},{4,5},{5,4},{6,7},{7,6},{8,9},{9,8},{10,11... | collective-permute-start | bytes 1966088 | tf_op jit(solution)/shard_map/ppermute | solution.py:597
  352.5 32.6 %collective-permute-start.50 = (bf16[160,2048]{1,0:T(8,128)(2,1)}, bf16[160,2048]{1,0:T(8,128)(2,1)}, u32[]{:S(2)}, u32[]{:S(2)}) collective-permute-start(bf16[160,2048]{1,0:T(8,128)(2,1)} %get-tuple-element.405), channel_id=1, source_target_pairs={{0,16},{1,17},{2,18},{3,19},{4,20},{5,21},{6,22},{7,23},{8,24},{9,... | collective-permute-start | bytes 1966088 | tf_op jit(solution)/shard_map/ppermute | solution.py:597
  353.5 31.6 %collective-permute-start.51 = (bf16[160,2048]{1,0:T(8,128)(2,1)}, bf16[160,2048]{1,0:T(8,128)(2,1)}, u32[]{:S(2)}, u32[]{:S(2)}) collective-permute-start(bf16[160,2048]{1,0:T(8,128)(2,1)} %get-tuple-element.406), channel_id=1, source_target_pairs={{0,17},{1,16},{2,19},{3,18},{4,21},{5,20},{6,23},{7,22},{8,25},{9,... | collective-permute-start | bytes 1966088 | tf_op jit(solution)/shard_map/ppermute | solution.py:597
  385.9 37.2 %collective-permute-start.58 = (bf16[320,4224]{1,0:T(8,128)(2,1)}, bf16[320,4224]{1,0:T(8,128)(2,1)S(1)}, u32[]{:S(2)}, u32[]{:S(2)}) collective-permute-start(bf16[320,4224]{1,0:T(8,128)(2,1)} %get-tuple-element.420), channel_id=1, source_target_pairs={{0,8},{1,9},{2,10},{3,11},{4,12},{5,13},{6,14},{7,15},{8,0},{9,1},... | collective-permute-start | bytes 8110088 | tf_op jit(solution)/shard_map/ppermute | solution.py:597
  389.2 33.8 %collective-permute-start.57 = (bf16[320,2048]{1,0:T(8,128)(2,1)}, bf16[320,2048]{1,0:T(8,128)(2,1)}, u32[]{:S(2)}, u32[]{:S(2)}) collective-permute-start(bf16[320,2048]{1,0:T(8,128)(2,1)} %pad_maximum_fusion.3), channel_id=1, source_target_pairs={{0,8},{1,9},{2,10},{3,11},{4,12},{5,13},{6,14},{7,15},{8,0},{9,1},... | collective-permute-start | bytes 3932168 | tf_op jit(solution)/shard_map/ppermute | solution.py:597
  389.6 33.4 %collective-permute-start.56 = (bf16[256,2048]{1,0:T(8,128)(2,1)S(1)}, bf16[256,2048]{1,0:T(8,128)(2,1)}, u32[]{:S(2)}, u32[]{:S(2)}) collective-permute-start(bf16[256,2048]{1,0:T(8,128)(2,1)S(1)} %bitcast.222), channel_id=1, source_target_pairs={{0,2},{1,3},{2,0},{3,1},{4,6},{5,7},{6,4},{7,5},{8,10},{9,11},{10,... | collective-permute-start | bytes 3145736 | tf_op jit(solution)/shard_map/ppermute | solution.py:597
  390.9 30.0 %collective-permute-start.54 = (bf16[160,2048]{1,0:T(8,128)(2,1)}, bf16[160,2048]{1,0:T(8,128)(2,1)}, u32[]{:S(2)}, u32[]{:S(2)}) collective-permute-start(bf16[160,2048]{1,0:T(8,128)(2,1)} %get-tuple-element.412), channel_id=1, source_target_pairs={{0,16},{1,17},{2,18},{3,19},{4,20},{5,21},{6,22},{7,23},{8,24},{9,... | collective-permute-start | bytes 1966088 | tf_op jit(solution)/shard_map/ppermute | solution.py:597
  423.1 35.7 %collective-permute-start.62 = (bf16[320,2048]{1,0:T(8,128)(2,1)}, bf16[320,2048]{1,0:T(8,128)(2,1)}, u32[]{:S(2)}, u32[]{:S(2)}) collective-permute-start(bf16[320,2048]{1,0:T(8,128)(2,1)} %pad_maximum_fusion.4), channel_id=1, source_target_pairs={{0,8},{1,9},{2,10},{3,11},{4,12},{5,13},{6,14},{7,15},{8,0},{9,1},... | collective-permute-start | bytes 3932168 | tf_op jit(solution)/shard_map/ppermute | solution.py:597
  423.1 35.6 %collective-permute-start.63 = (bf16[256,2048]{1,0:T(8,128)(2,1)S(1)}, bf16[256,2048]{1,0:T(8,128)(2,1)}, u32[]{:S(2)}, u32[]{:S(2)}) collective-permute-start(bf16[256,2048]{1,0:T(8,128)(2,1)S(1)} %copy-done.17), channel_id=1, source_target_pairs={{0,2},{1,3},{2,0},{3,1},{4,6},{5,7},{6,4},{7,5},{8,10},{9,11},{10,... | collective-permute-start | bytes 3145736 | tf_op jit(solution)/shard_map/ppermute | solution.py:597
  424.9 33.8 %collective-permute-start.59 = (bf16[160,2048]{1,0:T(8,128)(2,1)}, bf16[160,2048]{1,0:T(8,128)(2,1)S(1)}, u32[]{:S(2)}, u32[]{:S(2)}) collective-permute-start(bf16[160,2048]{1,0:T(8,128)(2,1)} %get-tuple-element.421), channel_id=1, source_target_pairs={{0,1},{1,0},{2,3},{3,2},{4,5},{5,4},{6,7},{7,6},{8,9},{9,8},{10,11... | collective-permute-start | bytes 1966088 | tf_op jit(solution)/shard_map/ppermute | solution.py:597
  426.3 32.5 %collective-permute-start.60 = (bf16[160,2048]{1,0:T(8,128)(2,1)}, bf16[160,2048]{1,0:T(8,128)(2,1)S(1)}, u32[]{:S(2)}, u32[]{:S(2)}) collective-permute-start(bf16[160,2048]{1,0:T(8,128)(2,1)} %get-tuple-element.422), channel_id=1, source_target_pairs={{0,16},{1,17},{2,18},{3,19},{4,20},{5,21},{6,22},{7,23},{8,24},{9,... | collective-permute-start | bytes 1966088 | tf_op jit(solution)/shard_map/ppermute | solution.py:597
  427.4 31.4 %collective-permute-start.61 = (bf16[160,2048]{1,0:T(8,128)(2,1)}, bf16[160,2048]{1,0:T(8,128)(2,1)}, u32[]{:S(2)}, u32[]{:S(2)}) collective-permute-start(bf16[160,2048]{1,0:T(8,128)(2,1)} %get-tuple-element.423), channel_id=1, source_target_pairs={{0,17},{1,16},{2,19},{3,18},{4,21},{5,20},{6,23},{7,22},{8,25},{9,... | collective-permute-start | bytes 1966088 | tf_op jit(solution)/shard_map/ppermute | solution.py:597
  459.6 36.0 %collective-permute-start.68 = (bf16[320,4224]{1,0:T(8,128)(2,1)}, bf16[320,4224]{1,0:T(8,128)(2,1)S(1)}, u32[]{:S(2)}, u32[]{:S(2)}) collective-permute-start(bf16[320,4224]{1,0:T(8,128)(2,1)} %get-tuple-element.447), channel_id=1, source_target_pairs={{0,8},{1,9},{2,10},{3,11},{4,12},{5,13},{6,14},{7,15},{8,0},{9,1},... | collective-permute-start | bytes 8110088 | tf_op jit(solution)/shard_map/ppermute | solution.py:597
  462.0 33.7 %collective-permute-start.67 = (bf16[320,2048]{1,0:T(8,128)(2,1)}, bf16[320,2048]{1,0:T(8,128)(2,1)}, u32[]{:S(2)}, u32[]{:S(2)}) collective-permute-start(bf16[320,2048]{1,0:T(8,128)(2,1)} %pad_maximum_fusion.5), channel_id=1, source_target_pairs={{0,8},{1,9},{2,10},{3,11},{4,12},{5,13},{6,14},{7,15},{8,0},{9,1},... | collective-permute-start | bytes 3932168 | tf_op jit(solution)/shard_map/ppermute | solution.py:597
  464.3 29.9 %collective-permute-start.65 = (bf16[160,2048]{1,0:T(8,128)(2,1)}, bf16[160,2048]{1,0:T(8,128)(2,1)S(1)}, u32[]{:S(2)}, u32[]{:S(2)}) collective-permute-start(bf16[160,2048]{1,0:T(8,128)(2,1)} %get-tuple-element.443), channel_id=1, source_target_pairs={{0,16},{1,17},{2,18},{3,19},{4,20},{5,21},{6,22},{7,23},{8,24},{9,... | collective-permute-start | bytes 1966088 | tf_op jit(solution)/shard_map/ppermute | solution.py:597
  495.7 35.3 %collective-permute-start.72 = (bf16[320,2048]{1,0:T(8,128)(2,1)}, bf16[320,2048]{1,0:T(8,128)(2,1)}, u32[]{:S(2)}, u32[]{:S(2)}) collective-permute-start(bf16[320,2048]{1,0:T(8,128)(2,1)} %pad_maximum_fusion.6), channel_id=1, source_target_pairs={{0,8},{1,9},{2,10},{3,11},{4,12},{5,13},{6,14},{7,15},{8,0},{9,1},... | collective-permute-start | bytes 3932168 | tf_op jit(solution)/shard_map/ppermute | solution.py:597
  495.8 35.1 %collective-permute-start.69 = (bf16[160,2048]{1,0:T(8,128)(2,1)}, bf16[160,2048]{1,0:T(8,128)(2,1)}, u32[]{:S(2)}, u32[]{:S(2)}) collective-permute-start(bf16[160,2048]{1,0:T(8,128)(2,1)} %get-tuple-element.464), channel_id=1, source_target_pairs={{0,1},{1,0},{2,3},{3,2},{4,5},{5,4},{6,7},{7,6},{8,9},{9,8},{10,11... | collective-permute-start | bytes 1966088 | tf_op jit(solution)/shard_map/ppermute | solution.py:597
  497.0 33.9 %collective-permute-start.70 = (bf16[160,2048]{1,0:T(8,128)(2,1)}, bf16[160,2048]{1,0:T(8,128)(2,1)}, u32[]{:S(2)}, u32[]{:S(2)}) collective-permute-start(bf16[160,2048]{1,0:T(8,128)(2,1)} %get-tuple-element.465), channel_id=1, source_target_pairs={{0,16},{1,17},{2,18},{3,19},{4,20},{5,21},{6,22},{7,23},{8,24},{9,... | collective-permute-start | bytes 1966088 | tf_op jit(solution)/shard_map/ppermute | solution.py:597
  498.2 32.7 %collective-permute-start.71 = (bf16[160,2048]{1,0:T(8,128)(2,1)}, bf16[160,2048]{1,0:T(8,128)(2,1)}, u32[]{:S(2)}, u32[]{:S(2)}) collective-permute-start(bf16[160,2048]{1,0:T(8,128)(2,1)} %get-tuple-element.466), channel_id=1, source_target_pairs={{0,17},{1,16},{2,19},{3,18},{4,21},{5,20},{6,23},{7,22},{8,25},{9,... | collective-permute-start | bytes 1966088 | tf_op jit(solution)/shard_map/ppermute | solution.py:597
  534.2 34.6 %collective-permute-start.77 = (bf16[320,2048]{1,0:T(8,128)(2,1)S(1)}, bf16[320,2048]{1,0:T(8,128)(2,1)}, u32[]{:S(2)}, u32[]{:S(2)}) collective-permute-start(bf16[320,2048]{1,0:T(8,128)(2,1)S(1)} %pad_maximum_fusion.7), channel_id=1, source_target_pairs={{0,8},{1,9},{2,10},{3,11},{4,12},{5,13},{6,14},{7,15},{8,0},{9,1},... | collective-permute-start | bytes 3932168 | tf_op jit(solution)/shard_map/ppermute | solution.py:597
  537.1 31.6 %collective-permute-start.76 = (bf16[160,2176]{1,0:T(8,128)(2,1)}, bf16[160,2176]{1,0:T(8,128)(2,1)}, u32[]{:S(2)}, u32[]{:S(2)}) collective-permute-start(bf16[160,2176]{1,0:T(8,128)(2,1)} %get-tuple-element.478), channel_id=1, source_target_pairs={{0,17},{1,16},{2,19},{3,18},{4,21},{5,20},{6,23},{7,22},{8,25},{9,... | collective-permute-start | bytes 2088968 | tf_op jit(solution)/shard_map/ppermute | solution.py:597
  568.8 34.5 %collective-permute-start.78 = (bf16[160,2176]{1,0:T(8,128)(2,1)}, bf16[160,2176]{1,0:T(8,128)(2,1)S(1)}, u32[]{:S(2)}, u32[]{:S(2)}) collective-permute-start(bf16[160,2176]{1,0:T(8,128)(2,1)} %get-tuple-element.481), channel_id=1, source_target_pairs={{0,1},{1,0},{2,3},{3,2},{4,5},{5,4},{6,7},{7,6},{8,9},{9,8},{10,11... | collective-permute-start | bytes 2088968 | tf_op jit(solution)/shard_map/ppermute | solution.py:597
  570.0 33.3 %collective-permute-start.79 = (bf16[160,2176]{1,0:T(8,128)(2,1)}, bf16[160,2176]{1,0:T(8,128)(2,1)S(1)}, u32[]{:S(2)}, u32[]{:S(2)}) collective-permute-start(bf16[160,2176]{1,0:T(8,128)(2,1)} %get-tuple-element.483), channel_id=1, source_target_pairs={{0,16},{1,17},{2,18},{3,19},{4,20},{5,21},{6,22},{7,23},{8,24},{9,... | collective-permute-start | bytes 2088968 | tf_op jit(solution)/shard_map/ppermute | solution.py:597
  571.1 32.2 %collective-permute-start.80 = (bf16[160,2176]{1,0:T(8,128)(2,1)}, bf16[160,2176]{1,0:T(8,128)(2,1)S(1)}, u32[]{:S(2)}, u32[]{:S(2)}) collective-permute-start(bf16[160,2176]{1,0:T(8,128)(2,1)} %get-tuple-element.485), channel_id=1, source_target_pairs={{0,17},{1,16},{2,19},{3,18},{4,21},{5,20},{6,23},{7,22},{8,25},{9,... | collective-permute-start | bytes 2088968 | tf_op jit(solution)/shard_map/ppermute | solution.py:597
  604.3 31.0 %collective-permute-start.82 = (bf16[160,2176]{1,0:T(8,128)(2,1)}, bf16[160,2176]{1,0:T(8,128)(2,1)S(1)}, u32[]{:S(2)}, u32[]{:S(2)}) collective-permute-start(bf16[160,2176]{1,0:T(8,128)(2,1)} %get-tuple-element.498), channel_id=1, source_target_pairs={{0,1},{1,0},{2,3},{3,2},{4,5},{5,4},{6,7},{7,6},{8,9},{9,8},{10,11... | collective-permute-start | bytes 2088968 | tf_op jit(solution)/shard_map/ppermute | solution.py:597
  606.5 32.2 %collective-permute-start.84 = (bf16[160,2176]{1,0:T(8,128)(2,1)}, bf16[160,2176]{1,0:T(8,128)(2,1)}, u32[]{:S(2)}, u32[]{:S(2)}) collective-permute-start(bf16[160,2176]{1,0:T(8,128)(2,1)} %get-tuple-element.502), channel_id=1, source_target_pairs={{0,17},{1,16},{2,19},{3,18},{4,21},{5,20},{6,23},{7,22},{8,25},{9,... | collective-permute-start | bytes 2088968 | tf_op jit(solution)/shard_map/ppermute | solution.py:597
  641.0 31.0 %collective-permute-start.90 = (bf16[160,2176]{1,0:T(8,128)(2,1)}, bf16[160,2176]{1,0:T(8,128)(2,1)S(1)}, u32[]{:S(2)}, u32[]{:S(2)}) collective-permute-start(bf16[160,2176]{1,0:T(8,128)(2,1)} %get-tuple-element.519), channel_id=1, source_target_pairs={{0,17},{1,16},{2,19},{3,18},{4,21},{5,20},{6,23},{7,22},{8,25},{9,... | collective-permute-start | bytes 2088968 | tf_op jit(solution)/shard_map/ppermute | solution.py:597
  642.2 54.2 %collective-permute-start.87 = (bf16[256,2176]{1,0:T(8,128)(2,1)S(1)}, bf16[256,2176]{1,0:T(8,128)(2,1)S(1)}, u32[]{:S(2)}, u32[]{:S(2)}) collective-permute-start(bf16[256,2176]{1,0:T(8,128)(2,1)S(1)} %copy-done.55), channel_id=1, source_target_pairs={{0,6},{1,7},{2,4},{3,5},{4,2},{5,3},{6,0},{7,1},{8,14},{9,15},{10,... | collective-permute-start | bytes 3342344 | tf_op jit(solution)/shard_map/ppermute | solution.py:597
  676.7 31.8 %collective-permute-start.91 = (bf16[256,2176]{1,0:T(8,128)(2,1)}, bf16[256,2176]{1,0:T(8,128)(2,1)S(1)}, u32[]{:S(2)}, u32[]{:S(2)}) collective-permute-start(bf16[256,2176]{1,0:T(8,128)(2,1)} %combine.11), channel_id=1, source_target_pairs={{0,2},{1,3},{2,0},{3,1},{4,6},{5,7},{6,4},{7,5},{8,10},{9,11},{10,... | collective-permute-start | bytes 3342344 | tf_op jit(solution)/shard_map/ppermute | solution.py:597
  712.8 41.6 %collective-permute-start.97 = (bf16[256,2048]{1,0:T(8,128)(2,1)}, bf16[256,2048]{1,0:T(8,128)(2,1)S(1)}, u32[]{:S(2)}, u32[]{:S(2)}) collective-permute-start(bf16[256,2048]{1,0:T(8,128)(2,1)} %combine.12), channel_id=1, source_target_pairs={{0,6},{1,7},{2,4},{3,5},{4,2},{5,3},{6,0},{7,1},{8,14},{9,15},{10,... | collective-permute-start | bytes 3145736 | tf_op jit(solution)/shard_map/ppermute | solution.py:597
  721.9 32.4 %collective-permute-start.95 = (bf16[256,2048]{1,0:T(8,128)(2,1)}, bf16[256,2048]{1,0:T(8,128)(2,1)S(1)}, u32[]{:S(2)}, u32[]{:S(2)}) collective-permute-start(bf16[256,2048]{1,0:T(8,128)(2,1)} %get-tuple-element.540.refs_0_), channel_id=1, source_target_pairs={{0,8},{1,9},{2,10},{3,11},{4,12},{5,13},{6,14},{7,15},{8,0},{9,1},... | collective-permute-start | bytes 3145736 | tf_op jit(solution)/shard_map/ppermute | solution.py:597
  722.0 33.3 %collective-permute-start.96 = (bf16[256,2048]{1,0:T(8,128)(2,1)}, bf16[256,2048]{1,0:T(8,128)(2,1)}, u32[]{:S(2)}, u32[]{:S(2)}) collective-permute-start(bf16[256,2048]{1,0:T(8,128)(2,1)} %get-tuple-element.540.refs_0_), channel_id=1, source_target_pairs={{0,16},{1,17},{2,18},{3,19},{4,20},{5,21},{6,22},{7,23},{8,24},{9,... | collective-permute-start | bytes 3145736 | tf_op jit(solution)/shard_map/ppermute | solution.py:597
  724.5 29.8 %collective-permute-start.99 = (bf16[160,2048]{1,0:T(8,128)(2,1)}, bf16[160,2048]{1,0:T(8,128)(2,1)S(1)}, u32[]{:S(2)}, u32[]{:S(2)}) collective-permute-start(bf16[160,2048]{1,0:T(8,128)(2,1)} %get-tuple-element.545), channel_id=1, source_target_pairs={{0,1},{1,0},{2,3},{3,2},{4,5},{5,4},{6,7},{7,6},{8,9},{9,8},{10,11... | collective-permute-start | bytes 1966088 | tf_op jit(solution)/shard_map/ppermute | solution.py:597
  755.5 33.3 %collective-permute-start.101 = (bf16[160,2048]{1,0:T(8,128)(2,1)}, bf16[160,2048]{1,0:T(8,128)(2,1)}, u32[]{:S(2)}, u32[]{:S(2)}) collective-permute-start(bf16[160,2048]{1,0:T(8,128)(2,1)} %get-tuple-element.551), channel_id=1, source_target_pairs={{0,16},{1,17},{2,18},{3,19},{4,20},{5,21},{6,22},{7,23},{8,24},{9,... | collective-permute-start | bytes 1966088 | tf_op jit(solution)/shard_map/ppermute | solution.py:597
  756.4 32.5 %collective-permute-start.102 = (bf16[160,2048]{1,0:T(8,128)(2,1)}, bf16[160,2048]{1,0:T(8,128)(2,1)}, u32[]{:S(2)}, u32[]{:S(2)}) collective-permute-start(bf16[160,2048]{1,0:T(8,128)(2,1)} %get-tuple-element.553), channel_id=1, source_target_pairs={{0,17},{1,16},{2,19},{3,18},{4,21},{5,20},{6,23},{7,22},{8,25},{9,... | collective-permute-start | bytes 1966088 | tf_op jit(solution)/shard_map/ppermute | solution.py:597
  764.1 39.1 %collective-permute-start.104 = (bf16[160,2048]{1,0:T(8,128)(2,1)}, bf16[160,2048]{1,0:T(8,128)(2,1)}, u32[]{:S(2)}, u32[]{:S(2)}) collective-permute-start(bf16[160,2048]{1,0:T(8,128)(2,1)} %get-tuple-element.557), channel_id=1, source_target_pairs={{0,17},{1,16},{2,19},{3,18},{4,21},{5,20},{6,23},{7,22},{8,25},{9,... | collective-permute-start | bytes 1966088 | tf_op jit(solution)/shard_map/ppermute | solution.py:597
  765.2 44.7 %collective-permute-start.105 = (bf16[160,2048]{1,0:T(8,128)(2,1)}, bf16[160,2048]{1,0:T(8,128)(2,1)}, u32[]{:S(2)}, u32[]{:S(2)}) collective-permute-start(bf16[160,2048]{1,0:T(8,128)(2,1)} %get-tuple-element.559), channel_id=1, source_target_pairs={{0,1},{1,0},{2,3},{3,2},{4,5},{5,4},{6,7},{7,6},{8,9},{9,8},{10,11... | collective-permute-start | bytes 1966088 | tf_op jit(solution)/shard_map/ppermute | solution.py:597
  792.7 55.6 %collective-permute-start.103 = (bf16[256,2048]{1,0:T(8,128)(2,1)}, bf16[256,2048]{1,0:T(8,128)(2,1)}, u32[]{:S(2)}, u32[]{:S(2)}) collective-permute-start(bf16[256,2048]{1,0:T(8,128)(2,1)} %combine.13), channel_id=1, source_target_pairs={{0,4},{1,5},{2,6},{3,7},{4,0},{5,1},{6,2},{7,3},{8,12},{9,13},{10,... | collective-permute-start | bytes 3145736 | tf_op jit(solution)/shard_map/ppermute | solution.py:597
  809.9 38.4 %collective-permute-start.109 = (bf16[160,2048]{1,0:T(8,128)(2,1)}, bf16[160,2048]{1,0:T(8,128)(2,1)}, u32[]{:S(2)}, u32[]{:S(2)}) collective-permute-start(bf16[160,2048]{1,0:T(8,128)(2,1)} %get-tuple-element.564), channel_id=1, source_target_pairs={{0,16},{1,17},{2,18},{3,19},{4,20},{5,21},{6,22},{7,23},{8,24},{9,... | collective-permute-start | bytes 1966088 | tf_op jit(solution)/shard_map/ppermute | solution.py:597
  811.0 32.3 %collective-permute-start.106 = (bf16[132,2048]{1,0:T(8,128)(2,1)}, bf16[132,2048]{1,0:T(8,128)(2,1)}, u32[]{:S(2)}, u32[]{:S(2)}) collective-permute-start(bf16[132,2048]{1,0:T(8,128)(2,1)} %pad_maximum_fusion.10), channel_id=1, source_target_pairs={{0,1},{1,0},{2,3},{3,2},{4,5},{5,4},{6,7},{7,6},{8,9},{9,8},{10,11... | collective-permute-start | bytes 1622024 | tf_op jit(solution)/shard_map/ppermute | solution.py:597
  812.3 31.0 %collective-permute-start.107 = (bf16[132,2048]{1,0:T(8,128)(2,1)}, bf16[132,2048]{1,0:T(8,128)(2,1)}, u32[]{:S(2)}, u32[]{:S(2)}) collective-permute-start(bf16[132,2048]{1,0:T(8,128)(2,1)} %pad_maximum_fusion.11), channel_id=1, source_target_pairs={{0,1},{1,0},{2,3},{3,2},{4,5},{5,4},{6,7},{7,6},{8,9},{9,8},{10,11... | collective-permute-start | bytes 1622024 | tf_op jit(solution)/shard_map/ppermute | solution.py:597
  813.1 35.2 %collective-permute-start.108 = (bf16[132,2048]{1,0:T(8,128)(2,1)}, bf16[132,2048]{1,0:T(8,128)(2,1)}, u32[]{:S(2)}, u32[]{:S(2)}) collective-permute-start(bf16[132,2048]{1,0:T(8,128)(2,1)} %pad_maximum_fusion.12), channel_id=1, source_target_pairs={{0,1},{1,0},{2,3},{3,2},{4,5},{5,4},{6,7},{7,6},{8,9},{9,8},{10,11... | collective-permute-start | bytes 1622024 | tf_op jit(solution)/shard_map/ppermute | solution.py:597
  848.3 31.0 %collective-permute-start.110 = (bf16[160,2048]{1,0:T(8,128)(2,1)}, bf16[160,2048]{1,0:T(8,128)(2,1)}, u32[]{:S(2)}, u32[]{:S(2)}) collective-permute-start(bf16[160,2048]{1,0:T(8,128)(2,1)} %get-tuple-element.570), channel_id=1, source_target_pairs={{0,16},{1,17},{2,18},{3,19},{4,20},{5,21},{6,22},{7,23},{8,24},{9,... | collective-permute-start | bytes 1966088 | tf_op jit(solution)/shard_map/ppermute | solution.py:597
  849.1 30.1 %collective-permute-start.111 = (bf16[160,2048]{1,0:T(8,128)(2,1)S(1)}, bf16[160,2048]{1,0:T(8,128)(2,1)}, u32[]{:S(2)}, u32[]{:S(2)}) collective-permute-start(bf16[160,2048]{1,0:T(8,128)(2,1)S(1)} %copy-done.120), channel_id=1, source_target_pairs={{0,17},{1,16},{2,19},{3,18},{4,21},{5,20},{6,23},{7,22},{8,25},{9,... | collective-permute-start | bytes 1966088 | tf_op jit(solution)/shard_map/ppermute | solution.py:597
  881.4 31.2 %collective-permute-start.114 = (bf16[4,64,1280]{2,1,0:T(8,128)(2,1)}, bf16[4,64,1280]{2,1,0:T(8,128)(2,1)S(1)}, u32[]{:S(2)}, u32[]{:S(2)}) collective-permute-start(bf16[4,64,1280]{2,1,0:T(8,128)(2,1)} %get-tuple-element.580), channel_id=1, source_target_pairs={{0,1},{1,0},{2,3},{3,2},{4,5},{5,4},{6,7},{7,6},{8,9},{9,8},{10,11... | collective-permute-start | bytes 1966088 | tf_op jit(solution)/shard_map/ppermute | solution.py:597
  882.7 30.2 %collective-permute-start.115 = (bf16[4,64,1280]{2,1,0:T(8,128)(2,1)}, bf16[4,64,1280]{2,1,0:T(8,128)(2,1)S(1)}, u32[]{:S(2)}, u32[]{:S(2)}) collective-permute-start(bf16[4,64,1280]{2,1,0:T(8,128)(2,1)} %get-tuple-element.581), channel_id=1, source_target_pairs={{0,1},{1,0},{2,3},{3,2},{4,5},{5,4},{6,7},{7,6},{8,9},{9,8},{10,11... | collective-permute-start | bytes 1966088 | tf_op jit(solution)/shard_map/ppermute | solution.py:597
  913.8 41.7 %collective-permute-start.120 = (bf16[256,2048]{1,0:T(8,128)(2,1)}, bf16[256,2048]{1,0:T(8,128)(2,1)S(1)}, u32[]{:S(2)}, u32[]{:S(2)}) collective-permute-start(bf16[256,2048]{1,0:T(8,128)(2,1)} %combine.15), channel_id=1, source_target_pairs={{0,2},{1,3},{2,0},{3,1},{4,6},{5,7},{6,4},{7,5},{8,10},{9,11},{10,... | collective-permute-start | bytes 3145736 | tf_op jit(solution)/shard_map/ppermute | solution.py:597
  922.6 32.9 %collective-permute-start.124 = (bf16[4,64,1280]{2,1,0:T(8,128)(2,1)}, bf16[4,64,1280]{2,1,0:T(8,128)(2,1)}, u32[]{:S(2)}, u32[]{:S(2)}) collective-permute-start(bf16[4,64,1280]{2,1,0:T(8,128)(2,1)} %fusion.9), channel_id=1, source_target_pairs={{0,6},{1,7},{2,4},{3,5},{4,2},{5,3},{6,0},{7,1},{8,14},{9,15},{10,... | collective-permute-start | bytes 1966088 | tf_op jit(solution)/shard_map/ppermute | solution.py:597
  961.8 31.6 %collective-permute-start.128 = (bf16[4,64,1280]{2,1,0:T(8,128)(2,1)S(1)}, bf16[4,64,1280]{2,1,0:T(8,128)(2,1)S(1)}, u32[]{:S(2)}, u32[]{:S(2)}) collective-permute-start(bf16[4,64,1280]{2,1,0:T(8,128)(2,1)S(1)} %get-tuple-element.605), channel_id=1, source_target_pairs={{0,4},{1,5},{2,6},{3,7},{4,0},{5,1},{6,2},{7,3},{8,12},{9,13},{10,... | collective-permute-start | bytes 1966088 | tf_op jit(solution)/shard_map/ppermute | solution.py:597
  961.9 31.6 %collective-permute-start.129 = (bf16[4,64,1280]{2,1,0:T(8,128)(2,1)S(1)}, bf16[4,64,1280]{2,1,0:T(8,128)(2,1)S(1)}, u32[]{:S(2)}, u32[]{:S(2)}) collective-permute-start(bf16[4,64,1280]{2,1,0:T(8,128)(2,1)S(1)} %get-tuple-element.607), channel_id=1, source_target_pairs={{0,2},{1,3},{2,0},{3,1},{4,6},{5,7},{6,4},{7,5},{8,10},{9,11},{10,... | collective-permute-start | bytes 1966088 | tf_op jit(solution)/shard_map/ppermute | solution.py:597
  (198 other events, 2943.1 us)

commit v5 on v4

--- a/solution.py
+++ b/solution.py
@@ -969,6 +969,7 @@
     tick()
 
     post(outs, made, 0, 2, 3)
+    total_1 = gather(made, 1, 1)
     o_near[0] = swap(o_sent[0], 0, 1)
     o_far = {}
     o_mid = {j: (o_term(j, 0) + now(o_near[j]).astype(F32)).astype(BF16) for j in last_steps[:-1]}
@@ -989,9 +990,10 @@
     first_steps, other_steps = last_steps[::2], last_steps[1::2]
     qkv_near = {j: swap(qkv_sent[j], 0, 1) for j in first_steps}
     sent = [swap(v, 1, 0) for v in sent]
-    for j in last_steps[nz // 4 : -1]:
+    for j in last_steps[nz // 4 : -2]:
         o_far[j] = swap_z(o_mid[j], j)
-    total_1, total_0 = gather(made, 1, 1), gather(made, 0, 1)
+    home(total_1, homes, 0)
+    total_0 = gather(made, 0, 1)
     held = [did(one_term(0, sent[1], F32)), did(one_term(2, sent[0], BF16))]
     tick()
 
@@ -999,12 +1001,7 @@
     one_far = swap(held[1], 2, 0)
     qkv_mid = lambda j: (qkv_term(j, 0) + now(qkv_near[j]).astype(F32)).astype(BF16)
     qkv_far = {j: swap_z(qkv_mid(j), j) for j in last_steps[: nz // 4]}
-    home(total_1, homes, 0)
-    o_sum = o_term(0, 0) + o_near[0].astype(F32)
-    for j in range(1, nz):
-        o_sum = o_sum + now(o_far[j]).astype(F32)
-    o_grad = did(o_sum[:o_own])
-    router_sum = did(o_sum[o_own:].reshape(experts, nctx, own_width).transpose(1, 2, 0))
+    o_far[1] = swap_z(o_mid[1], 1)
     input_grad, attn_gain_part = by_rows(
         first_back_kernel,
         [held[0], one_far, layer_input[0], scale_one, attn_gain[None], grad_resid],
@@ -1016,6 +1013,11 @@
 
     qkv_far.update({j: swap_z(qkv_mid(j), j) for j in last_steps[nz // 4 : -1]})
     home(total_0, homes, 0)
+    o_sum = o_term(0, 0) + o_near[0].astype(F32)
+    for j in range(1, nz):
+        o_sum = o_sum + now(o_far[j]).astype(F32)
+    o_grad = did(o_sum[:o_own])
+    router_sum = did(o_sum[o_own:].reshape(experts, nctx, own_width).transpose(1, 2, 0))
     late = jnp.concatenate([now(attn_gain_part)[0], ffn_gain_part[0], q_gain_part[0], k_gain_part[0]])
     late = did(sum_over(late, [(1 << b, 0) for b in range(nctx.bit_length() - 1)] + [(0, 1)]))
     tick()

time: 1020 us -> 1020 us (level)
    unnamed x248 -> x256, local copies, waits for them, and re-layouts: 23.9 us -> 24.4 us
  transfers between devices with their start and end apart: 135 -> 135, of which waited for: 52 -> 48; matrix products, arithmetic and copies ran while one was open for 10% -> 11% of each run, Pallas kernels for 34% -> 34%
where the time goes in v5:
time: 1020 us
  waiting for transfers between devices  375 us (37%)
  Pallas kernels  350 us (34%)
  starting transfers between devices  148 us (15%)
  local copies, waits for them, and re-layouts  74.5 us (7%)
  other arithmetic  42.3 us (4%)
  matrix products  23.5 us (2%)
    ppermute x135, waiting for transfers between devices, swap(): got = lax.ppermute(now(v) if rounds else v, AXES, pairs)  375 us
    ppermute x135, starting transfers between devices, swap(): got = lax.ppermute(now(v) if rounds else v, AXES, pairs)  148 us
    pallas_call x4, Pallas kernels, expert_step(): pl.pallas_call(lambda *refs: expert_kernel(chips, ff_tiles, len(args), *r...  107 us
    pallas_call x10, Pallas kernels, product(): pl.pallas_call(lambda *refs: product_kernel(kind, dtype, *refs), grid=((m...  87.8 us
    pallas_call x8, Pallas kernels, combine(): pl.pallas_call(lambda *refs: combine_kernel(len(pieces), *refs), out_shap...  31.9 us
    pallas_call x8, Pallas kernels, select(): pl.pallas_call(lambda *refs: select_kernel(len(parts), *refs), out_shape=...  28.5 us
    unnamed x256, local copies, waits for them, and re-layouts  24.4 us
    pallas_call x1, Pallas kernels, attend_back(): pl.pallas_call(attend_back_kernel, grid=(heads + 2,), in_specs=[moving, m...  23.6 us
  transfers between devices with their start and end apart: 135, of which 48 were waited for; matrix products, arithmetic and copies ran while one was open for 11% of the time, Pallas kernels for 34%

profile of v5, /device:TPU:0, one launch (start us, length us, event | category | flops | bytes accessed | tf_op | source)
XLA Modules:
  0.0 1016.0 jit_solution(1475331405633118670)
XLA Ops:
  15.7 15.3 %collective-permute-done.4 = s32[8,256]{1,0:T(8,128)S(1)} collective-permute-done((s32[8,256]{1,0:T(8,128)}, s32[8,256]{1,0:T(8,128)S(1)}, u32[]{:S(2)}, u32[]{:S(2)}) %collective-permute-start.4) | collective-permute-done | bytes 8224 | tf_op jit(solution)/shard_map/ppermute | solution.py:597
  43.6 20.4 %collective-permute-done.10 = s32[8,256]{1,0:T(8,128)S(1)} collective-permute-done((s32[8,256]{1,0:T(8,128)S(1)}, s32[8,256]{1,0:T(8,128)S(1)}, u32[]{:S(2)}, u32[]{:S(2)}) %collective-permute-start.10) | collective-permute-done | bytes 8224 | tf_op jit(solution)/shard_map/ppermute | solution.py:597
  73.8 5.4 collective-permute-done.13
  88.8 10.3 %collective-permute-done.11 = bf16[256,1280]{1,0:T(8,128)(2,1)S(1)} collective-permute-done((bf16[256,1280]{1,0:T(8,128)(2,1)}, bf16[256,1280]{1,0:T(8,128)(2,1)S(1)}, u32[]{:S(2)}, u32[]{:S(2)}) %collective-permute-start.11) | collective-permute-done | bytes 655392 | tf_op jit(solution)/shard_map/ppermute | solution.py:597
  107.1 9.7 collective-permute-done.16
  120.3 13.7 %collective-permute-done.18 = bf16[256,1280]{1,0:T(8,128)(2,1)S(1)} collective-permute-done((bf16[256,1280]{1,0:T(8,128)(2,1)S(1)}, bf16[256,1280]{1,0:T(8,128)(2,1)S(1)}, u32[]{:S(2)}, u32[]{:S(2)}) %collective-permute-start.18) | collective-permute-done | bytes 655392 | tf_op jit(solution)/shard_map/ppermute | solution.py:597
  144.3 4.9 join.2.refs_0_
  153.0 7.7 collective-permute-done.21.refs_1_
  167.4 5.6 fusion.55.q_ref.k_ref.v_ref
  173.1 17.5 %attend.1 = (bf16[1024,1024]{1,0:T(8,128)(2,1)S(1)}, bf16[1024,1024]{1,0:T(8,128)(2,1)S(1)}, bf16[1024,128]{1,0:T(8,128)(2,1)S(1)}, f32[8,1,1024]{2,1,0:T(1,128)S(1)}) custom-call(f32[1024,1280]{1,0:T(8,128)S(1)} %fusion.55.q_ref.k_ref.v_ref, f32[1024,1280]{1,0:T(8,128)S(1)} %fusion.55.q_ref.k_ref.v_ref, f32[1024,1280]{1,0:T(8,128)S(1)} %fusion.55.q_ref.k_ref.v_ref, ...), custom_call_target="tpu_custom_call" | custom-call | flops 1 | bytes 1 | tf_op jit(solution)/shard_map/attend/pallas_call | solution.py:171
  198.7 4.6 convolution_convert_fusion.1
  215.1 5.1 convolution_add_fusion.1.held
  220.2 4.6 collective-permute-done.32.refs_1_
  224.9 7.9 collective-permute-done.31.arrived
  238.9 4.1 second_norm.1
  251.4 11.4 %collective-permute-done.34.refs_7_ = bf16[160,2048]{1,0:T(8,128)(2,1)S(1)} collective-permute-done((bf16[160,2048]{1,0:T(8,128)(2,1)}, bf16[160,2048]{1,0:T(8,128)(2,1)S(1)}, u32[]{:S(2)}, u32[]{:S(2)}) %collective-permute-start.34) | collective-permute-done | bytes 655392 | tf_op jit(solution)/shard_map/ppermute | solution.py:597
  264.1 18.9 %collective-permute-done.37.refs_1_ = bf16[256,1024]{1,0:T(8,128)(2,1)S(1)} collective-permute-done((bf16[256,1024]{1,0:T(8,128)(2,1)S(1)}, bf16[256,1024]{1,0:T(8,128)(2,1)S(1)}, u32[]{:S(2)}, u32[]{:S(2)}) %collective-permute-start.37) | collective-permute-done | bytes 524320 | tf_op jit(solution)/shard_map/ppermute | solution.py:597
  290.9 11.6 %collective-permute-done.40.refs_3_ = bf16[160,2048]{1,0:T(8,128)(2,1)S(1)} collective-permute-done((bf16[160,2048]{1,0:T(8,128)(2,1)}, bf16[160,2048]{1,0:T(8,128)(2,1)S(1)}, u32[]{:S(2)}, u32[]{:S(2)}) %collective-permute-start.40) | collective-permute-done | bytes 655392 | tf_op jit(solution)/shard_map/ppermute | solution.py:597
  302.5 13.0 %collective-permute-done.39.refs_2_ = bf16[160,2048]{1,0:T(8,128)(2,1)S(1)} collective-permute-done((bf16[160,2048]{1,0:T(8,128)(2,1)}, bf16[160,2048]{1,0:T(8,128)(2,1)S(1)}, u32[]{:S(2)}, u32[]{:S(2)}) %collective-permute-start.39) | collective-permute-done | bytes 655392 | tf_op jit(solution)/shard_map/ppermute | solution.py:597
  333.9 6.3 picks.1.refs_17_
  344.2 5.1 collective-permute-done.44.refs_7_
  358.3 26.7 %expert.4 = (bf16[320,4224]{1,0:T(8,128)(2,1)}, bf16[320,4224]{1,0:T(8,128)(2,1)}, bf16[2560,2048]{1,0:T(8,128)(2,1)}, bf16[2560,2048]{1,0:T(8,128)(2,1)}, bf16[...) custom-call(bf16[160,2048]{1,0:T(8,128)(2,1)} %get-tuple-element.402.refs_0_, ...), custom_call_target="tpu_custom_call" | custom-call | flops 1 | bytes 1 | tf_op jit(solution)/shard_map/expert/pallas_call | solution.py:377
  395.4 12.8 %collective-permute-done.55.refs_8_ = bf16[160,2048]{1,0:T(8,128)(2,1)S(1)} collective-permute-done((bf16[160,2048]{1,0:T(8,128)(2,1)}, bf16[160,2048]{1,0:T(8,128)(2,1)S(1)}, u32[]{:S(2)}, u32[]{:S(2)}) %collective-permute-start.55) | collective-permute-done | bytes 655392 | tf_op jit(solution)/shard_map/ppermute | solution.py:597
  408.2 12.6 %collective-permute-done.54.refs_7_ = bf16[160,2048]{1,0:T(8,128)(2,1)} collective-permute-done((bf16[160,2048]{1,0:T(8,128)(2,1)}, bf16[160,2048]{1,0:T(8,128)(2,1)}, u32[]{:S(2)}, u32[]{:S(2)}) %collective-permute-start.54) | collective-permute-done | bytes 655392 | tf_op jit(solution)/shard_map/ppermute | solution.py:597
  431.9 26.7 %expert.5 = (bf16[320,4224]{1,0:T(8,128)(2,1)}, bf16[320,4224]{1,0:T(8,128)(2,1)}, bf16[2560,2048]{1,0:T(8,128)(2,1)}, bf16[2560,2048]{1,0:T(8,128)(2,1)}, bf16[...) custom-call(bf16[160,2048]{1,0:T(8,128)(2,1)} %get-tuple-element.432, ...), custom_call_target="tpu_custom_call", output_to_operand_aliasing={{2}: (19, {}), {3}: (20, {}), {4}: (21, {}), {5}: (22, {}),... | custom-call | flops 1 | bytes 1 | tf_op jit(solution)/shard_map/expert/pallas_call | solution.py:377
  469.3 5.0 pack.4
  474.3 6.7 collective-permute-done.66.refs_8_
  481.0 13.0 %collective-permute-done.65.refs_7_ = bf16[160,2048]{1,0:T(8,128)(2,1)S(1)} collective-permute-done((bf16[160,2048]{1,0:T(8,128)(2,1)}, bf16[160,2048]{1,0:T(8,128)(2,1)S(1)}, u32[]{:S(2)}, u32[]{:S(2)}) %collective-permute-start.65) | collective-permute-done | bytes 655392 | tf_op jit(solution)/shard_map/ppermute | solution.py:597
  499.1 5.0 pack.5
  504.1 26.6 %expert.6 = (bf16[320,4224]{1,0:T(8,128)(2,1)}, bf16[320,4224]{1,0:T(8,128)(2,1)}, bf16[2560,2048]{1,0:T(8,128)(2,1)}, bf16[2560,2048]{1,0:T(8,128)(2,1)}, bf16[...) custom-call(bf16[160,2048]{1,0:T(8,128)(2,1)} %get-tuple-element.457, ...), custom_call_target="tpu_custom_call", output_to_operand_aliasing={{2}: (19, {}), {3}: (20, {}), {4}: (21, {}), {5}: (22, {}),... | custom-call | flops 1 | bytes 1 | tf_op jit(solution)/shard_map/expert/pallas_call | solution.py:377
  539.6 5.0 pack.6
  544.6 7.8 collective-permute-done.74.refs_2_
  554.6 13.9 %collective-permute-done.76.refs_4_ = bf16[160,2176]{1,0:T(8,128)(2,1)} collective-permute-done((bf16[160,2176]{1,0:T(8,128)(2,1)}, bf16[160,2176]{1,0:T(8,128)(2,1)}, u32[]{:S(2)}, u32[]{:S(2)}) %collective-permute-start.76) | collective-permute-done | bytes 696352 | tf_op jit(solution)/shard_map/ppermute | solution.py:597
  576.1 27.0 %expert.7 = (bf16[320,4224]{1,0:T(8,128)(2,1)}, bf16[320,4224]{1,0:T(8,128)(2,1)}, bf16[2560,2048]{1,0:T(8,128)(2,1)}, bf16[2560,2048]{1,0:T(8,128)(2,1)}, bf16[...) custom-call(bf16[160,2048]{1,0:T(8,128)(2,1)} %get-tuple-element.491, ...), custom_call_target="tpu_custom_call", output_to_operand_aliasing={{2}: (19, {}), {3}: (20, {}), {4}: (21, {}), {5}: (22, {}),... | custom-call | flops 1 | bytes 1 | tf_op jit(solution)/shard_map/expert/pallas_call | solution.py:377
  610.4 13.1 %product.10 = f32[2048,768]{1,0:T(8,128)} custom-call(bf16[2560,2048]{1,0:T(8,128)(2,1)} %get-tuple-element.509.refs_0_, bf16[2560,768]{1,0:T(8,128)(2,1)} %get-tuple-element.511.refs_1_), custom_call_target="tpu_custom_call" | custom-call | flops 1 | bytes 1 | tf_op jit(solution)/shard_map/product/pallas_call | solution.py:468
  629.0 5.1 pack.7
  644.6 13.3 %product.11 = f32[2048,768]{1,0:T(8,128)} custom-call(bf16[2560,2048]{1,0:T(8,128)(2,1)} %get-tuple-element.509.refs_0_, bf16[2560,768]{1,0:T(8,128)(2,1)} %get-tuple-element.521.refs_1_), custom_call_target="tpu_custom_call" | custom-call | flops 1 | bytes 1 | tf_op jit(solution)/shard_map/product/pallas_call | solution.py:468
  657.9 4.3 combine.10.refs_0_
  662.2 9.6 collective-permute-done.90.refs_4_
  681.8 14.5 %product.12 = f32[768,2048]{1,0:T(8,128)} custom-call(bf16[2560,768]{1,0:T(8,128)(2,1)} %get-tuple-element.531.refs_0_, bf16[2560,2048]{1,0:T(8,128)(2,1)} %get-tuple-element.532.refs_1_), custom_call_target="tpu_custom_call" | custom-call | flops 1 | bytes 1 | tf_op jit(solution)/shard_map/product/pallas_call | solution.py:468
  697.4 10.9 %collective-permute-done.94.refs_4_ = bf16[160,2048]{1,0:T(8,128)(2,1)} collective-permute-done((bf16[160,2048]{1,0:T(8,128)(2,1)}, bf16[160,2048]{1,0:T(8,128)(2,1)}, u32[]{:S(2)}, u32[]{:S(2)}) %collective-permute-start.94) | collective-permute-done | bytes 655392 | tf_op jit(solution)/shard_map/ppermute | solution.py:597
  708.4 4.2 combine.12
  715.1 6.7 second_back.1
  725.1 15.8 %collective-permute-done.98.refs_2_ = bf16[160,2048]{1,0:T(8,128)(2,1)S(1)} collective-permute-done((bf16[160,2048]{1,0:T(8,128)(2,1)}, bf16[160,2048]{1,0:T(8,128)(2,1)S(1)}, u32[]{:S(2)}, u32[]{:S(2)}) %collective-permute-start.98) | collective-permute-done | bytes 655392 | tf_op jit(solution)/shard_map/ppermute | solution.py:597
  740.9 13.3 %collective-permute-done.99.refs_2_ = bf16[160,2048]{1,0:T(8,128)(2,1)S(1)} collective-permute-done((bf16[160,2048]{1,0:T(8,128)(2,1)}, bf16[160,2048]{1,0:T(8,128)(2,1)S(1)}, u32[]{:S(2)}, u32[]{:S(2)}) %collective-permute-start.99) | collective-permute-done | bytes 655392 | tf_op jit(solution)/shard_map/ppermute | solution.py:597
  766.3 4.7 join.3.refs_0_.refs_1_
  770.9 8.5 product.13.do_ref
  779.5 9.3 product.14
  792.5 4.4 collective-permute-start.103
  802.9 6.9 collective-permute-done.105.refs_2_
  818.3 23.6 %attend_back.1 = (bf16[1024,1280]{1,0:T(8,128)(2,1)S(1)}, f32[1,128]{1,0:T(1,128)S(1)}, f32[1,128]{1,0:T(1,128)S(1)}) custom-call(bf16[1024,1024]{1,0:T(8,128)(2,1)S(1)} %copy-done.8, f32[1024,1280]{1,0:T(8,128)} %copy-done.2, bf16[1024,1024]{1,0:T(8,128)(2,1)S(1)} %copy-done.6, bf16[1024,1024]{1,0:T(8,128)(2,1)S(1)} %copy-done.5, ...), custom_call_target="tpu_custom_call" | custom-call | flops 1 | bytes 1 | tf_op jit(solution)/shard_map/attend_back/pallas_call | solution.py:195
  843.5 4.6 collective-permute-done.108
  856.3 4.4 product.16
  860.8 4.4 product.17
  865.2 10.5 %product.15 = f32[2048,1280]{1,0:T(8,128)} custom-call(bf16[1024,2048]{1,0:T(8,128)(2,1)} %join.2.refs_0_, bf16[1024,1280]{1,0:T(8,128)(2,1)} %copy-done.3), custom_call_target="tpu_custom_call" | custom-call | flops 1 | bytes 1 | tf_op jit(solution)/shard_map/product/pallas_call | solution.py:468
  879.4 4.1 fusion.20
  892.9 4.1 combine.15
  897.0 4.9 product.18.held
  902.8 4.9 product.19
  907.7 15.9 %collective-permute-done.119 = bf16[132,2048]{1,0:T(8,128)(2,1)S(1)} collective-permute-done((bf16[132,2048]{1,0:T(8,128)(2,1)}, bf16[132,2048]{1,0:T(8,128)(2,1)S(1)}, u32[]{:S(2)}, u32[]{:S(2)}) %collective-permute-start.119) | collective-permute-done | bytes 540704 | tf_op jit(solution)/shard_map/ppermute | solution.py:597
  936.9 12.4 %collective-permute-done.120.arrived = bf16[256,2048]{1,0:T(8,128)(2,1)S(1)} collective-permute-done((bf16[256,2048]{1,0:T(8,128)(2,1)}, bf16[256,2048]{1,0:T(8,128)(2,1)S(1)}, u32[]{:S(2)}, u32[]{:S(2)}) %collective-permute-start.120) | collective-permute-done | bytes 1048608 | tf_op jit(solution)/shard_map/ppermute | solution.py:597
  950.2 4.3 first_back.1
  954.6 4.9 collective-permute-done.124
  974.3 21.9 %collective-permute-done.128 = bf16[4,64,1280]{2,1,0:T(8,128)(2,1)S(1)} collective-permute-done((bf16[4,64,1280]{2,1,0:T(8,128)(2,1)}, bf16[4,64,1280]{2,1,0:T(8,128)(2,1)S(1)}, u32[]{:S(2)}, u32[]{:S(2)}) %collective-permute-start.128) | collective-permute-done | bytes 655392 | tf_op jit(solution)/shard_map/ppermute | solution.py:597
  (679 shorter events, 351.9 us)
Async XLA Ops:
  70.2 31.1 %collective-permute-start.12 = (bf16[256,1280]{1,0:T(8,128)(2,1)}, bf16[256,1280]{1,0:T(8,128)(2,1)S(1)}, u32[]{:S(2)}, u32[]{:S(2)}) collective-permute-start(bf16[256,1280]{1,0:T(8,128)(2,1)} %copy-done.78), channel_id=1, source_target_pairs={{0,4},{1,5},{2,6},{3,7},{4,0},{5,1},{6,2},{7,3},{8,12},{9,13},{10,... | collective-permute-start | bytes 1966088 | tf_op jit(solution)/shard_map/ppermute | solution.py:597
  102.8 31.2 %collective-permute-start.15 = (bf16[256,2048]{1,0:T(8,128)(2,1)}, bf16[256,2048]{1,0:T(8,128)(2,1)S(1)}, u32[]{:S(2)}, u32[]{:S(2)}) collective-permute-start(bf16[256,2048]{1,0:T(8,128)(2,1)} %collective-permute-done.6.refs_2_), channel_id=1, source_target_pairs={{0,8},{1,9},{2,10},{3,11},{4,12},{5,13},{6,14},{7,15},{8,0},{9,1},... | collective-permute-start | bytes 3145736 | tf_op jit(solution)/shard_map/ppermute | solution.py:597
  103.3 30.7 %collective-permute-start.18 = (bf16[256,1280]{1,0:T(8,128)(2,1)S(1)}, bf16[256,1280]{1,0:T(8,128)(2,1)S(1)}, u32[]{:S(2)}, u32[]{:S(2)}) collective-permute-start(bf16[256,1280]{1,0:T(8,128)(2,1)S(1)} %collective-permute-done.12), channel_id=1, source_target_pairs={{0,1},{1,0},{2,3},{3,2},{4,5},{5,4},{6,7},{7,6},{8,9},{9,8},{10,11... | collective-permute-start | bytes 1966088 | tf_op jit(solution)/shard_map/ppermute | solution.py:597
  161.7 30.5 %collective-permute-start.26 = (bf16[1024,512]{1,0:T(8,128)(2,1)S(1)}, bf16[1024,512]{1,0:T(8,128)(2,1)S(1)}, u32[]{:S(2)}, u32[]{:S(2)}) collective-permute-start(bf16[1024,512]{1,0:T(8,128)(2,1)S(1)} %bitcast.227), channel_id=1, source_target_pairs={{0,8},{1,9},{2,10},{3,11},{4,12},{5,13},{6,14},{7,15},{8,0},{9,1},... | collective-permute-start | bytes 3145736 | tf_op jit(solution)/shard_map/ppermute | solution.py:597
  237.4 45.5 %collective-permute-start.36 = (bf16[160,2048]{1,0:T(8,128)(2,1)}, bf16[160,2048]{1,0:T(8,128)(2,1)S(1)}, u32[]{:S(2)}, u32[]{:S(2)}) collective-permute-start(bf16[160,2048]{1,0:T(8,128)(2,1)} %get-tuple-element.370), channel_id=1, source_target_pairs={{0,1},{1,0},{2,3},{3,2},{4,5},{5,4},{6,7},{7,6},{8,9},{9,8},{10,11... | collective-permute-start | bytes 1966088 | tf_op jit(solution)/shard_map/ppermute | solution.py:597
  245.1 37.8 %collective-permute-start.37 = (bf16[256,1024]{1,0:T(8,128)(2,1)S(1)}, bf16[256,1024]{1,0:T(8,128)(2,1)S(1)}, u32[]{:S(2)}, u32[]{:S(2)}) collective-permute-start(bf16[256,1024]{1,0:T(8,128)(2,1)S(1)} %get-tuple-element.391), channel_id=1, source_target_pairs={{0,4},{1,5},{2,6},{3,7},{4,0},{5,1},{6,2},{7,3},{8,12},{9,13},{10,... | collective-permute-start | bytes 1572872 | tf_op jit(solution)/shard_map/ppermute | solution.py:597
  282.9 33.9 %collective-permute-start.41 = (bf16[320,2048]{1,0:T(8,128)(2,1)}, bf16[320,2048]{1,0:T(8,128)(2,1)}, u32[]{:S(2)}, u32[]{:S(2)}) collective-permute-start(bf16[320,2048]{1,0:T(8,128)(2,1)} %pad_maximum_fusion), channel_id=1, source_target_pairs={{0,8},{1,9},{2,10},{3,11},{4,12},{5,13},{6,14},{7,15},{8,0},{9,1},... | collective-permute-start | bytes 3932168 | tf_op jit(solution)/shard_map/ppermute | solution.py:597
  317.0 34.5 %collective-permute-start.48 = (bf16[320,2048]{1,0:T(8,128)(2,1)}, bf16[320,2048]{1,0:T(8,128)(2,1)}, u32[]{:S(2)}, u32[]{:S(2)}) collective-permute-start(bf16[320,2048]{1,0:T(8,128)(2,1)} %pad_maximum_fusion.1), channel_id=1, source_target_pairs={{0,8},{1,9},{2,10},{3,11},{4,12},{5,13},{6,14},{7,15},{8,0},{9,1},... | collective-permute-start | bytes 3932168 | tf_op jit(solution)/shard_map/ppermute | solution.py:597
  318.9 30.4 %collective-permute-start.44 = (bf16[160,2048]{1,0:T(8,128)(2,1)}, bf16[160,2048]{1,0:T(8,128)(2,1)}, u32[]{:S(2)}, u32[]{:S(2)}) collective-permute-start(bf16[160,2048]{1,0:T(8,128)(2,1)} %get-tuple-element.388), channel_id=1, source_target_pairs={{0,16},{1,17},{2,18},{3,19},{4,20},{5,21},{6,22},{7,23},{8,24},{9,... | collective-permute-start | bytes 1966088 | tf_op jit(solution)/shard_map/ppermute | solution.py:597
  320.0 31.5 %collective-permute-start.46 = (bf16[160,2048]{1,0:T(8,128)(2,1)}, bf16[160,2048]{1,0:T(8,128)(2,1)S(1)}, u32[]{:S(2)}, u32[]{:S(2)}) collective-permute-start(bf16[160,2048]{1,0:T(8,128)(2,1)} %get-tuple-element.390), channel_id=1, source_target_pairs={{0,1},{1,0},{2,3},{3,2},{4,5},{5,4},{6,7},{7,6},{8,9},{9,8},{10,11... | collective-permute-start | bytes 1966088 | tf_op jit(solution)/shard_map/ppermute | solution.py:597
  321.4 30.1 %collective-permute-start.47 = (bf16[256,1024]{1,0:T(8,128)(2,1)}, bf16[256,1024]{1,0:T(8,128)(2,1)}, u32[]{:S(2)}, u32[]{:S(2)}) collective-permute-start(bf16[256,1024]{1,0:T(8,128)(2,1)} %copy-done.111), channel_id=1, source_target_pairs={{0,6},{1,7},{2,4},{3,5},{4,2},{5,3},{6,0},{7,1},{8,14},{9,15},{10,... | collective-permute-start | bytes 1572872 | tf_op jit(solution)/shard_map/ppermute | solution.py:597
  351.5 33.5 %collective-permute-start.52 = (bf16[320,2048]{1,0:T(8,128)(2,1)}, bf16[320,2048]{1,0:T(8,128)(2,1)}, u32[]{:S(2)}, u32[]{:S(2)}) collective-permute-start(bf16[320,2048]{1,0:T(8,128)(2,1)} %pad_maximum_fusion.2), channel_id=1, source_target_pairs={{0,8},{1,9},{2,10},{3,11},{4,12},{5,13},{6,14},{7,15},{8,0},{9,1},... | collective-permute-start | bytes 3932168 | tf_op jit(solution)/shard_map/ppermute | solution.py:597
  351.6 33.4 %collective-permute-start.49 = (bf16[160,2048]{1,0:T(8,128)(2,1)}, bf16[160,2048]{1,0:T(8,128)(2,1)S(1)}, u32[]{:S(2)}, u32[]{:S(2)}) collective-permute-start(bf16[160,2048]{1,0:T(8,128)(2,1)} %get-tuple-element.404), channel_id=1, source_target_pairs={{0,1},{1,0},{2,3},{3,2},{4,5},{5,4},{6,7},{7,6},{8,9},{9,8},{10,11... | collective-permute-start | bytes 1966088 | tf_op jit(solution)/shard_map/ppermute | solution.py:597
  352.3 32.6 %collective-permute-start.50 = (bf16[160,2048]{1,0:T(8,128)(2,1)}, bf16[160,2048]{1,0:T(8,128)(2,1)}, u32[]{:S(2)}, u32[]{:S(2)}) collective-permute-start(bf16[160,2048]{1,0:T(8,128)(2,1)} %get-tuple-element.405), channel_id=1, source_target_pairs={{0,16},{1,17},{2,18},{3,19},{4,20},{5,21},{6,22},{7,23},{8,24},{9,... | collective-permute-start | bytes 1966088 | tf_op jit(solution)/shard_map/ppermute | solution.py:597
  353.4 31.6 %collective-permute-start.51 = (bf16[160,2048]{1,0:T(8,128)(2,1)}, bf16[160,2048]{1,0:T(8,128)(2,1)}, u32[]{:S(2)}, u32[]{:S(2)}) collective-permute-start(bf16[160,2048]{1,0:T(8,128)(2,1)} %get-tuple-element.406), channel_id=1, source_target_pairs={{0,17},{1,16},{2,19},{3,18},{4,21},{5,20},{6,23},{7,22},{8,25},{9,... | collective-permute-start | bytes 1966088 | tf_op jit(solution)/shard_map/ppermute | solution.py:597
  385.8 37.2 %collective-permute-start.58 = (bf16[320,4224]{1,0:T(8,128)(2,1)}, bf16[320,4224]{1,0:T(8,128)(2,1)S(1)}, u32[]{:S(2)}, u32[]{:S(2)}) collective-permute-start(bf16[320,4224]{1,0:T(8,128)(2,1)} %get-tuple-element.420), channel_id=1, source_target_pairs={{0,8},{1,9},{2,10},{3,11},{4,12},{5,13},{6,14},{7,15},{8,0},{9,1},... | collective-permute-start | bytes 8110088 | tf_op jit(solution)/shard_map/ppermute | solution.py:597
  389.1 33.8 %collective-permute-start.57 = (bf16[320,2048]{1,0:T(8,128)(2,1)}, bf16[320,2048]{1,0:T(8,128)(2,1)}, u32[]{:S(2)}, u32[]{:S(2)}) collective-permute-start(bf16[320,2048]{1,0:T(8,128)(2,1)} %pad_maximum_fusion.3), channel_id=1, source_target_pairs={{0,8},{1,9},{2,10},{3,11},{4,12},{5,13},{6,14},{7,15},{8,0},{9,1},... | collective-permute-start | bytes 3932168 | tf_op jit(solution)/shard_map/ppermute | solution.py:597
  389.5 33.4 %collective-permute-start.56 = (bf16[256,2048]{1,0:T(8,128)(2,1)S(1)}, bf16[256,2048]{1,0:T(8,128)(2,1)}, u32[]{:S(2)}, u32[]{:S(2)}) collective-permute-start(bf16[256,2048]{1,0:T(8,128)(2,1)S(1)} %bitcast.222), channel_id=1, source_target_pairs={{0,2},{1,3},{2,0},{3,1},{4,6},{5,7},{6,4},{7,5},{8,10},{9,11},{10,... | collective-permute-start | bytes 3145736 | tf_op jit(solution)/shard_map/ppermute | solution.py:597
  390.8 30.0 %collective-permute-start.54 = (bf16[160,2048]{1,0:T(8,128)(2,1)}, bf16[160,2048]{1,0:T(8,128)(2,1)}, u32[]{:S(2)}, u32[]{:S(2)}) collective-permute-start(bf16[160,2048]{1,0:T(8,128)(2,1)} %get-tuple-element.412), channel_id=1, source_target_pairs={{0,16},{1,17},{2,18},{3,19},{4,20},{5,21},{6,22},{7,23},{8,24},{9,... | collective-permute-start | bytes 1966088 | tf_op jit(solution)/shard_map/ppermute | solution.py:597
  423.0 35.7 %collective-permute-start.62 = (bf16[320,2048]{1,0:T(8,128)(2,1)}, bf16[320,2048]{1,0:T(8,128)(2,1)}, u32[]{:S(2)}, u32[]{:S(2)}) collective-permute-start(bf16[320,2048]{1,0:T(8,128)(2,1)} %pad_maximum_fusion.4), channel_id=1, source_target_pairs={{0,8},{1,9},{2,10},{3,11},{4,12},{5,13},{6,14},{7,15},{8,0},{9,1},... | collective-permute-start | bytes 3932168 | tf_op jit(solution)/shard_map/ppermute | solution.py:597
  423.1 35.6 %collective-permute-start.63 = (bf16[256,2048]{1,0:T(8,128)(2,1)S(1)}, bf16[256,2048]{1,0:T(8,128)(2,1)}, u32[]{:S(2)}, u32[]{:S(2)}) collective-permute-start(bf16[256,2048]{1,0:T(8,128)(2,1)S(1)} %copy-done.17), channel_id=1, source_target_pairs={{0,2},{1,3},{2,0},{3,1},{4,6},{5,7},{6,4},{7,5},{8,10},{9,11},{10,... | collective-permute-start | bytes 3145736 | tf_op jit(solution)/shard_map/ppermute | solution.py:597
  424.8 33.8 %collective-permute-start.59 = (bf16[160,2048]{1,0:T(8,128)(2,1)}, bf16[160,2048]{1,0:T(8,128)(2,1)S(1)}, u32[]{:S(2)}, u32[]{:S(2)}) collective-permute-start(bf16[160,2048]{1,0:T(8,128)(2,1)} %get-tuple-element.421), channel_id=1, source_target_pairs={{0,1},{1,0},{2,3},{3,2},{4,5},{5,4},{6,7},{7,6},{8,9},{9,8},{10,11... | collective-permute-start | bytes 1966088 | tf_op jit(solution)/shard_map/ppermute | solution.py:597
  426.2 32.5 %collective-permute-start.60 = (bf16[160,2048]{1,0:T(8,128)(2,1)}, bf16[160,2048]{1,0:T(8,128)(2,1)S(1)}, u32[]{:S(2)}, u32[]{:S(2)}) collective-permute-start(bf16[160,2048]{1,0:T(8,128)(2,1)} %get-tuple-element.422), channel_id=1, source_target_pairs={{0,16},{1,17},{2,18},{3,19},{4,20},{5,21},{6,22},{7,23},{8,24},{9,... | collective-permute-start | bytes 1966088 | tf_op jit(solution)/shard_map/ppermute | solution.py:597
  427.3 31.3 %collective-permute-start.61 = (bf16[160,2048]{1,0:T(8,128)(2,1)}, bf16[160,2048]{1,0:T(8,128)(2,1)}, u32[]{:S(2)}, u32[]{:S(2)}) collective-permute-start(bf16[160,2048]{1,0:T(8,128)(2,1)} %get-tuple-element.423), channel_id=1, source_target_pairs={{0,17},{1,16},{2,19},{3,18},{4,21},{5,20},{6,23},{7,22},{8,25},{9,... | collective-permute-start | bytes 1966088 | tf_op jit(solution)/shard_map/ppermute | solution.py:597
  459.5 36.0 %collective-permute-start.68 = (bf16[320,4224]{1,0:T(8,128)(2,1)}, bf16[320,4224]{1,0:T(8,128)(2,1)S(1)}, u32[]{:S(2)}, u32[]{:S(2)}) collective-permute-start(bf16[320,4224]{1,0:T(8,128)(2,1)} %get-tuple-element.447), channel_id=1, source_target_pairs={{0,8},{1,9},{2,10},{3,11},{4,12},{5,13},{6,14},{7,15},{8,0},{9,1},... | collective-permute-start | bytes 8110088 | tf_op jit(solution)/shard_map/ppermute | solution.py:597
  461.8 33.7 %collective-permute-start.67 = (bf16[320,2048]{1,0:T(8,128)(2,1)}, bf16[320,2048]{1,0:T(8,128)(2,1)}, u32[]{:S(2)}, u32[]{:S(2)}) collective-permute-start(bf16[320,2048]{1,0:T(8,128)(2,1)} %pad_maximum_fusion.5), channel_id=1, source_target_pairs={{0,8},{1,9},{2,10},{3,11},{4,12},{5,13},{6,14},{7,15},{8,0},{9,1},... | collective-permute-start | bytes 3932168 | tf_op jit(solution)/shard_map/ppermute | solution.py:597
  495.5 35.2 %collective-permute-start.72 = (bf16[320,2048]{1,0:T(8,128)(2,1)}, bf16[320,2048]{1,0:T(8,128)(2,1)}, u32[]{:S(2)}, u32[]{:S(2)}) collective-permute-start(bf16[320,2048]{1,0:T(8,128)(2,1)} %pad_maximum_fusion.6), channel_id=1, source_target_pairs={{0,8},{1,9},{2,10},{3,11},{4,12},{5,13},{6,14},{7,15},{8,0},{9,1},... | collective-permute-start | bytes 3932168 | tf_op jit(solution)/shard_map/ppermute | solution.py:597
  495.6 35.1 %collective-permute-start.69 = (bf16[160,2048]{1,0:T(8,128)(2,1)}, bf16[160,2048]{1,0:T(8,128)(2,1)}, u32[]{:S(2)}, u32[]{:S(2)}) collective-permute-start(bf16[160,2048]{1,0:T(8,128)(2,1)} %get-tuple-element.464), channel_id=1, source_target_pairs={{0,1},{1,0},{2,3},{3,2},{4,5},{5,4},{6,7},{7,6},{8,9},{9,8},{10,11... | collective-permute-start | bytes 1966088 | tf_op jit(solution)/shard_map/ppermute | solution.py:597
  496.9 33.8 %collective-permute-start.70 = (bf16[160,2048]{1,0:T(8,128)(2,1)}, bf16[160,2048]{1,0:T(8,128)(2,1)}, u32[]{:S(2)}, u32[]{:S(2)}) collective-permute-start(bf16[160,2048]{1,0:T(8,128)(2,1)} %get-tuple-element.465), channel_id=1, source_target_pairs={{0,16},{1,17},{2,18},{3,19},{4,20},{5,21},{6,22},{7,23},{8,24},{9,... | collective-permute-start | bytes 1966088 | tf_op jit(solution)/shard_map/ppermute | solution.py:597
  498.0 32.7 %collective-permute-start.71 = (bf16[160,2048]{1,0:T(8,128)(2,1)}, bf16[160,2048]{1,0:T(8,128)(2,1)}, u32[]{:S(2)}, u32[]{:S(2)}) collective-permute-start(bf16[160,2048]{1,0:T(8,128)(2,1)} %get-tuple-element.466), channel_id=1, source_target_pairs={{0,17},{1,16},{2,19},{3,18},{4,21},{5,20},{6,23},{7,22},{8,25},{9,... | collective-permute-start | bytes 1966088 | tf_op jit(solution)/shard_map/ppermute | solution.py:597
  534.0 34.6 %collective-permute-start.77 = (bf16[320,2048]{1,0:T(8,128)(2,1)S(1)}, bf16[320,2048]{1,0:T(8,128)(2,1)}, u32[]{:S(2)}, u32[]{:S(2)}) collective-permute-start(bf16[320,2048]{1,0:T(8,128)(2,1)S(1)} %pad_maximum_fusion.7), channel_id=1, source_target_pairs={{0,8},{1,9},{2,10},{3,11},{4,12},{5,13},{6,14},{7,15},{8,0},{9,1},... | collective-permute-start | bytes 3932168 | tf_op jit(solution)/shard_map/ppermute | solution.py:597
  536.9 31.6 %collective-permute-start.76 = (bf16[160,2176]{1,0:T(8,128)(2,1)}, bf16[160,2176]{1,0:T(8,128)(2,1)}, u32[]{:S(2)}, u32[]{:S(2)}) collective-permute-start(bf16[160,2176]{1,0:T(8,128)(2,1)} %get-tuple-element.478), channel_id=1, source_target_pairs={{0,17},{1,16},{2,19},{3,18},{4,21},{5,20},{6,23},{7,22},{8,25},{9,... | collective-permute-start | bytes 2088968 | tf_op jit(solution)/shard_map/ppermute | solution.py:597
  568.6 34.5 %collective-permute-start.78 = (bf16[160,2176]{1,0:T(8,128)(2,1)}, bf16[160,2176]{1,0:T(8,128)(2,1)S(1)}, u32[]{:S(2)}, u32[]{:S(2)}) collective-permute-start(bf16[160,2176]{1,0:T(8,128)(2,1)} %get-tuple-element.481), channel_id=1, source_target_pairs={{0,1},{1,0},{2,3},{3,2},{4,5},{5,4},{6,7},{7,6},{8,9},{9,8},{10,11... | collective-permute-start | bytes 2088968 | tf_op jit(solution)/shard_map/ppermute | solution.py:597
  569.8 33.3 %collective-permute-start.79 = (bf16[160,2176]{1,0:T(8,128)(2,1)}, bf16[160,2176]{1,0:T(8,128)(2,1)S(1)}, u32[]{:S(2)}, u32[]{:S(2)}) collective-permute-start(bf16[160,2176]{1,0:T(8,128)(2,1)} %get-tuple-element.483), channel_id=1, source_target_pairs={{0,16},{1,17},{2,18},{3,19},{4,20},{5,21},{6,22},{7,23},{8,24},{9,... | collective-permute-start | bytes 2088968 | tf_op jit(solution)/shard_map/ppermute | solution.py:597
  571.0 32.2 %collective-permute-start.80 = (bf16[160,2176]{1,0:T(8,128)(2,1)}, bf16[160,2176]{1,0:T(8,128)(2,1)S(1)}, u32[]{:S(2)}, u32[]{:S(2)}) collective-permute-start(bf16[160,2176]{1,0:T(8,128)(2,1)} %get-tuple-element.485), channel_id=1, source_target_pairs={{0,17},{1,16},{2,19},{3,18},{4,21},{5,20},{6,23},{7,22},{8,25},{9,... | collective-permute-start | bytes 2088968 | tf_op jit(solution)/shard_map/ppermute | solution.py:597
  604.1 31.0 %collective-permute-start.82 = (bf16[160,2176]{1,0:T(8,128)(2,1)}, bf16[160,2176]{1,0:T(8,128)(2,1)S(1)}, u32[]{:S(2)}, u32[]{:S(2)}) collective-permute-start(bf16[160,2176]{1,0:T(8,128)(2,1)} %get-tuple-element.498), channel_id=1, source_target_pairs={{0,1},{1,0},{2,3},{3,2},{4,5},{5,4},{6,7},{7,6},{8,9},{9,8},{10,11... | collective-permute-start | bytes 2088968 | tf_op jit(solution)/shard_map/ppermute | solution.py:597
  606.4 32.1 %collective-permute-start.84 = (bf16[160,2176]{1,0:T(8,128)(2,1)}, bf16[160,2176]{1,0:T(8,128)(2,1)}, u32[]{:S(2)}, u32[]{:S(2)}) collective-permute-start(bf16[160,2176]{1,0:T(8,128)(2,1)} %get-tuple-element.502), channel_id=1, source_target_pairs={{0,17},{1,16},{2,19},{3,18},{4,21},{5,20},{6,23},{7,22},{8,25},{9,... | collective-permute-start | bytes 2088968 | tf_op jit(solution)/shard_map/ppermute | solution.py:597
  640.9 30.9 %collective-permute-start.90 = (bf16[160,2176]{1,0:T(8,128)(2,1)}, bf16[160,2176]{1,0:T(8,128)(2,1)S(1)}, u32[]{:S(2)}, u32[]{:S(2)}) collective-permute-start(bf16[160,2176]{1,0:T(8,128)(2,1)} %get-tuple-element.519), channel_id=1, source_target_pairs={{0,17},{1,16},{2,19},{3,18},{4,21},{5,20},{6,23},{7,22},{8,25},{9,... | collective-permute-start | bytes 2088968 | tf_op jit(solution)/shard_map/ppermute | solution.py:597
  642.0 54.2 %collective-permute-start.87 = (bf16[256,2176]{1,0:T(8,128)(2,1)S(1)}, bf16[256,2176]{1,0:T(8,128)(2,1)S(1)}, u32[]{:S(2)}, u32[]{:S(2)}) collective-permute-start(bf16[256,2176]{1,0:T(8,128)(2,1)S(1)} %copy-done.55), channel_id=1, source_target_pairs={{0,6},{1,7},{2,4},{3,5},{4,2},{5,3},{6,0},{7,1},{8,14},{9,15},{10,... | collective-permute-start | bytes 3342344 | tf_op jit(solution)/shard_map/ppermute | solution.py:597
  676.6 31.8 %collective-permute-start.91 = (bf16[256,2176]{1,0:T(8,128)(2,1)}, bf16[256,2176]{1,0:T(8,128)(2,1)S(1)}, u32[]{:S(2)}, u32[]{:S(2)}) collective-permute-start(bf16[256,2176]{1,0:T(8,128)(2,1)} %combine.11), channel_id=1, source_target_pairs={{0,2},{1,3},{2,0},{3,1},{4,6},{5,7},{6,4},{7,5},{8,10},{9,11},{10,... | collective-permute-start | bytes 3342344 | tf_op jit(solution)/shard_map/ppermute | solution.py:597
  712.5 41.6 %collective-permute-start.97 = (bf16[256,2048]{1,0:T(8,128)(2,1)}, bf16[256,2048]{1,0:T(8,128)(2,1)S(1)}, u32[]{:S(2)}, u32[]{:S(2)}) collective-permute-start(bf16[256,2048]{1,0:T(8,128)(2,1)} %combine.12), channel_id=1, source_target_pairs={{0,6},{1,7},{2,4},{3,5},{4,2},{5,3},{6,0},{7,1},{8,14},{9,15},{10,... | collective-permute-start | bytes 3145736 | tf_op jit(solution)/shard_map/ppermute | solution.py:597
  721.8 32.4 %collective-permute-start.95 = (bf16[256,2048]{1,0:T(8,128)(2,1)}, bf16[256,2048]{1,0:T(8,128)(2,1)S(1)}, u32[]{:S(2)}, u32[]{:S(2)}) collective-permute-start(bf16[256,2048]{1,0:T(8,128)(2,1)} %get-tuple-element.540.refs_0_), channel_id=1, source_target_pairs={{0,8},{1,9},{2,10},{3,11},{4,12},{5,13},{6,14},{7,15},{8,0},{9,1},... | collective-permute-start | bytes 3145736 | tf_op jit(solution)/shard_map/ppermute | solution.py:597
  721.9 33.3 %collective-permute-start.96 = (bf16[256,2048]{1,0:T(8,128)(2,1)}, bf16[256,2048]{1,0:T(8,128)(2,1)}, u32[]{:S(2)}, u32[]{:S(2)}) collective-permute-start(bf16[256,2048]{1,0:T(8,128)(2,1)} %get-tuple-element.540.refs_0_), channel_id=1, source_target_pairs={{0,16},{1,17},{2,18},{3,19},{4,20},{5,21},{6,22},{7,23},{8,24},{9,... | collective-permute-start | bytes 3145736 | tf_op jit(solution)/shard_map/ppermute | solution.py:597
  755.4 33.4 %collective-permute-start.101 = (bf16[160,2048]{1,0:T(8,128)(2,1)}, bf16[160,2048]{1,0:T(8,128)(2,1)}, u32[]{:S(2)}, u32[]{:S(2)}) collective-permute-start(bf16[160,2048]{1,0:T(8,128)(2,1)} %get-tuple-element.551), channel_id=1, source_target_pairs={{0,16},{1,17},{2,18},{3,19},{4,20},{5,21},{6,22},{7,23},{8,24},{9,... | collective-permute-start | bytes 1966088 | tf_op jit(solution)/shard_map/ppermute | solution.py:597
  756.3 32.5 %collective-permute-start.102 = (bf16[160,2048]{1,0:T(8,128)(2,1)}, bf16[160,2048]{1,0:T(8,128)(2,1)}, u32[]{:S(2)}, u32[]{:S(2)}) collective-permute-start(bf16[160,2048]{1,0:T(8,128)(2,1)} %get-tuple-element.553), channel_id=1, source_target_pairs={{0,17},{1,16},{2,19},{3,18},{4,21},{5,20},{6,23},{7,22},{8,25},{9,... | collective-permute-start | bytes 1966088 | tf_op jit(solution)/shard_map/ppermute | solution.py:597
  763.9 38.9 %collective-permute-start.104 = (bf16[160,2048]{1,0:T(8,128)(2,1)}, bf16[160,2048]{1,0:T(8,128)(2,1)}, u32[]{:S(2)}, u32[]{:S(2)}) collective-permute-start(bf16[160,2048]{1,0:T(8,128)(2,1)} %get-tuple-element.557), channel_id=1, source_target_pairs={{0,17},{1,16},{2,19},{3,18},{4,21},{5,20},{6,23},{7,22},{8,25},{9,... | collective-permute-start | bytes 1966088 | tf_op jit(solution)/shard_map/ppermute | solution.py:597
  765.0 44.7 %collective-permute-start.105 = (bf16[160,2048]{1,0:T(8,128)(2,1)}, bf16[160,2048]{1,0:T(8,128)(2,1)}, u32[]{:S(2)}, u32[]{:S(2)}) collective-permute-start(bf16[160,2048]{1,0:T(8,128)(2,1)} %get-tuple-element.559), channel_id=1, source_target_pairs={{0,1},{1,0},{2,3},{3,2},{4,5},{5,4},{6,7},{7,6},{8,9},{9,8},{10,11... | collective-permute-start | bytes 1966088 | tf_op jit(solution)/shard_map/ppermute | solution.py:597
  792.5 55.6 %collective-permute-start.103 = (bf16[256,2048]{1,0:T(8,128)(2,1)}, bf16[256,2048]{1,0:T(8,128)(2,1)}, u32[]{:S(2)}, u32[]{:S(2)}) collective-permute-start(bf16[256,2048]{1,0:T(8,128)(2,1)} %combine.13), channel_id=1, source_target_pairs={{0,4},{1,5},{2,6},{3,7},{4,0},{5,1},{6,2},{7,3},{8,12},{9,13},{10,... | collective-permute-start | bytes 3145736 | tf_op jit(solution)/shard_map/ppermute | solution.py:597
  809.7 38.4 %collective-permute-start.109 = (bf16[160,2048]{1,0:T(8,128)(2,1)}, bf16[160,2048]{1,0:T(8,128)(2,1)}, u32[]{:S(2)}, u32[]{:S(2)}) collective-permute-start(bf16[160,2048]{1,0:T(8,128)(2,1)} %get-tuple-element.564), channel_id=1, source_target_pairs={{0,16},{1,17},{2,18},{3,19},{4,20},{5,21},{6,22},{7,23},{8,24},{9,... | collective-permute-start | bytes 1966088 | tf_op jit(solution)/shard_map/ppermute | solution.py:597
  810.9 32.6 %collective-permute-start.106 = (bf16[132,2048]{1,0:T(8,128)(2,1)}, bf16[132,2048]{1,0:T(8,128)(2,1)}, u32[]{:S(2)}, u32[]{:S(2)}) collective-permute-start(bf16[132,2048]{1,0:T(8,128)(2,1)} %pad_maximum_fusion.10), channel_id=1, source_target_pairs={{0,1},{1,0},{2,3},{3,2},{4,5},{5,4},{6,7},{7,6},{8,9},{9,8},{10,11... | collective-permute-start | bytes 1622024 | tf_op jit(solution)/shard_map/ppermute | solution.py:597
  812.1 31.3 %collective-permute-start.107 = (bf16[132,2048]{1,0:T(8,128)(2,1)}, bf16[132,2048]{1,0:T(8,128)(2,1)}, u32[]{:S(2)}, u32[]{:S(2)}) collective-permute-start(bf16[132,2048]{1,0:T(8,128)(2,1)} %pad_maximum_fusion.11), channel_id=1, source_target_pairs={{0,1},{1,0},{2,3},{3,2},{4,5},{5,4},{6,7},{7,6},{8,9},{9,8},{10,11... | collective-permute-start | bytes 1622024 | tf_op jit(solution)/shard_map/ppermute | solution.py:597
  812.9 35.2 %collective-permute-start.108 = (bf16[132,2048]{1,0:T(8,128)(2,1)}, bf16[132,2048]{1,0:T(8,128)(2,1)}, u32[]{:S(2)}, u32[]{:S(2)}) collective-permute-start(bf16[132,2048]{1,0:T(8,128)(2,1)} %pad_maximum_fusion.12), channel_id=1, source_target_pairs={{0,1},{1,0},{2,3},{3,2},{4,5},{5,4},{6,7},{7,6},{8,9},{9,8},{10,11... | collective-permute-start | bytes 1622024 | tf_op jit(solution)/shard_map/ppermute | solution.py:597
  848.1 35.5 %collective-permute-start.110 = (bf16[160,2048]{1,0:T(8,128)(2,1)}, bf16[160,2048]{1,0:T(8,128)(2,1)S(1)}, u32[]{:S(2)}, u32[]{:S(2)}) collective-permute-start(bf16[160,2048]{1,0:T(8,128)(2,1)} %get-tuple-element.570), channel_id=1, source_target_pairs={{0,16},{1,17},{2,18},{3,19},{4,20},{5,21},{6,22},{7,23},{8,24},{9,... | collective-permute-start | bytes 1966088 | tf_op jit(solution)/shard_map/ppermute | solution.py:597
  849.0 34.6 %collective-permute-start.111 = (bf16[160,2048]{1,0:T(8,128)(2,1)}, bf16[160,2048]{1,0:T(8,128)(2,1)S(1)}, u32[]{:S(2)}, u32[]{:S(2)}) collective-permute-start(bf16[160,2048]{1,0:T(8,128)(2,1)} %get-tuple-element.572), channel_id=1, source_target_pairs={{0,17},{1,16},{2,19},{3,18},{4,21},{5,20},{6,23},{7,22},{8,25},{9,... | collective-permute-start | bytes 1966088 | tf_op jit(solution)/shard_map/ppermute | solution.py:597
  850.8 32.8 %collective-permute-start.112 = (bf16[132,2048]{1,0:T(8,128)(2,1)}, bf16[132,2048]{1,0:T(8,128)(2,1)S(1)}, u32[]{:S(2)}, u32[]{:S(2)}) collective-permute-start(bf16[132,2048]{1,0:T(8,128)(2,1)} %pad_maximum_fusion.13), channel_id=1, source_target_pairs={{0,1},{1,0},{2,3},{3,2},{4,5},{5,4},{6,7},{7,6},{8,9},{9,8},{10,11... | collective-permute-start | bytes 1622024 | tf_op jit(solution)/shard_map/ppermute | solution.py:597
  853.6 30.0 %collective-permute-start.113 = (bf16[132,2048]{1,0:T(8,128)(2,1)}, bf16[132,2048]{1,0:T(8,128)(2,1)S(1)}, u32[]{:S(2)}, u32[]{:S(2)}) collective-permute-start(bf16[132,2048]{1,0:T(8,128)(2,1)} %fusion.10), channel_id=1, source_target_pairs={{0,6},{1,7},{2,4},{3,5},{4,2},{5,3},{6,0},{7,1},{8,14},{9,15},{10,... | collective-permute-start | bytes 1622024 | tf_op jit(solution)/shard_map/ppermute | solution.py:597
  885.2 39.2 %collective-permute-start.114 = (bf16[256,2048]{1,0:T(8,128)(2,1)}, bf16[256,2048]{1,0:T(8,128)(2,1)}, u32[]{:S(2)}, u32[]{:S(2)}) collective-permute-start(bf16[256,2048]{1,0:T(8,128)(2,1)} %combine.14), channel_id=1, source_target_pairs={{0,2},{1,3},{2,0},{3,1},{4,6},{5,7},{6,4},{7,5},{8,10},{9,11},{10,... | collective-permute-start | bytes 3145736 | tf_op jit(solution)/shard_map/ppermute | solution.py:597
  888.7 34.9 %collective-permute-start.117 = (bf16[4,64,1280]{2,1,0:T(8,128)(2,1)}, bf16[4,64,1280]{2,1,0:T(8,128)(2,1)}, u32[]{:S(2)}, u32[]{:S(2)}) collective-permute-start(bf16[4,64,1280]{2,1,0:T(8,128)(2,1)} %get-tuple-element.583), channel_id=1, source_target_pairs={{0,1},{1,0},{2,3},{3,2},{4,5},{5,4},{6,7},{7,6},{8,9},{9,8},{10,11... | collective-permute-start | bytes 1966088 | tf_op jit(solution)/shard_map/ppermute | solution.py:597
  890.0 33.6 %collective-permute-start.118 = (bf16[4,64,1280]{2,1,0:T(8,128)(2,1)}, bf16[4,64,1280]{2,1,0:T(8,128)(2,1)}, u32[]{:S(2)}, u32[]{:S(2)}) collective-permute-start(bf16[4,64,1280]{2,1,0:T(8,128)(2,1)} %get-tuple-element.584), channel_id=1, source_target_pairs={{0,1},{1,0},{2,3},{3,2},{4,5},{5,4},{6,7},{7,6},{8,9},{9,8},{10,11... | collective-permute-start | bytes 1966088 | tf_op jit(solution)/shard_map/ppermute | solution.py:597
  892.7 30.8 %collective-permute-start.119 = (bf16[132,2048]{1,0:T(8,128)(2,1)}, bf16[132,2048]{1,0:T(8,128)(2,1)S(1)}, u32[]{:S(2)}, u32[]{:S(2)}) collective-permute-start(bf16[132,2048]{1,0:T(8,128)(2,1)} %fusion.11), channel_id=1, source_target_pairs={{0,4},{1,5},{2,6},{3,7},{4,0},{5,1},{6,2},{7,3},{8,12},{9,13},{10,... | collective-permute-start | bytes 1622024 | tf_op jit(solution)/shard_map/ppermute | solution.py:597
  925.6 33.9 %collective-permute-start.121 = (bf16[4,64,1280]{2,1,0:T(8,128)(2,1)}, bf16[4,64,1280]{2,1,0:T(8,128)(2,1)}, u32[]{:S(2)}, u32[]{:S(2)}) collective-permute-start(bf16[4,64,1280]{2,1,0:T(8,128)(2,1)} %get-tuple-element.591), channel_id=1, source_target_pairs={{0,1},{1,0},{2,3},{3,2},{4,5},{5,4},{6,7},{7,6},{8,9},{9,8},{10,11... | collective-permute-start | bytes 1966088 | tf_op jit(solution)/shard_map/ppermute | solution.py:597
  926.8 32.6 %collective-permute-start.122 = (bf16[4,64,1280]{2,1,0:T(8,128)(2,1)}, bf16[4,64,1280]{2,1,0:T(8,128)(2,1)S(1)}, u32[]{:S(2)}, u32[]{:S(2)}) collective-permute-start(bf16[4,64,1280]{2,1,0:T(8,128)(2,1)} %get-tuple-element.592), channel_id=1, source_target_pairs={{0,1},{1,0},{2,3},{3,2},{4,5},{5,4},{6,7},{7,6},{8,9},{9,8},{10,11... | collective-permute-start | bytes 1966088 | tf_op jit(solution)/shard_map/ppermute | solution.py:597
  963.8 32.4 %collective-permute-start.128 = (bf16[4,64,1280]{2,1,0:T(8,128)(2,1)}, bf16[4,64,1280]{2,1,0:T(8,128)(2,1)S(1)}, u32[]{:S(2)}, u32[]{:S(2)}) collective-permute-start(bf16[4,64,1280]{2,1,0:T(8,128)(2,1)} %get-tuple-element.602), channel_id=1, source_target_pairs={{0,4},{1,5},{2,6},{3,7},{4,0},{5,1},{6,2},{7,3},{8,12},{9,13},{10,... | collective-permute-start | bytes 1966088 | tf_op jit(solution)/shard_map/ppermute | solution.py:597
  966.0 30.1 %collective-permute-start.129 = (bf16[4,64,1280]{2,1,0:T(8,128)(2,1)S(1)}, bf16[4,64,1280]{2,1,0:T(8,128)(2,1)S(1)}, u32[]{:S(2)}, u32[]{:S(2)}) collective-permute-start(bf16[4,64,1280]{2,1,0:T(8,128)(2,1)S(1)} %get-tuple-element.604), channel_id=1, source_target_pairs={{0,2},{1,3},{2,0},{3,1},{4,6},{5,7},{6,4},{7,5},{8,10},{9,11},{10,... | collective-permute-start | bytes 1966088 | tf_op jit(solution)/shard_map/ppermute | solution.py:597
  (202 other events, 2939.0 us)
